TPU v7x, 32 devices: a whole 2x2x4 slice. The times are simulated.
32 devices in a mesh: dp: 4 (over y, core), heads: 8 (over z, x).
Axes of the slice: x: 2, y: 2, z: 4, core: 2. Of those that a mesh axis runs over, the one named last changes fastest.
Arguments:
- block_in: bfloat16 [8192, 2048], P(('dp', 'heads')), may hold values from -6 to 6
- seq_counts: int32 [4, 2], P('dp'), may hold values from 0 to 4, as said below
- norm1_gain: float32 [2048], replicated, may hold values from 0.5 to 1.5
- w_qkvg: bfloat16 [2048, 4, 2048], P(None, None, 'heads'), may hold values from -0.125 to 0.125
- conv_weight: float32 [3, 4, 2048], P(None, None, 'heads'), may hold values from -3 to 3
- w_gates: bfloat16 [2048, 2, 16], P(None, None, 'heads'), may hold values from -0.125 to 0.125
- gate_params: float32 [2, 16], P(None, 'heads'), may hold values from -9 to 1, as said below
- out_gain: float32 [128], replicated, may hold values from 0.5 to 1.5
- w_out: bfloat16 [2048, 2048], P('heads'), may hold values from -0.25 to 0.25
- norm2_gain: float32 [2048], replicated, may hold values from 0.5 to 1.5
- w_gate_up: bfloat16 [2048, 2, 5632], P(None, None, 'heads'), may hold values from -0.125 to 0.125
- w_down: bfloat16 [5632, 2048], P('heads'), may hold values from -0.078125 to 0.078125
- cotangent: bfloat16 [8192, 2048], P(('dp', 'heads')), may hold values from -6 to 6
Outputs:
- layer_out: bfloat16 [8192, 2048], P(('dp', 'heads'))
- grad_in: float32 [8192, 2048], P(('dp', 'heads'))
- grad_norm1_gain: float32 [2048], replicated
- grad_w_qkvg: float32 [2048, 4, 2048], P(None, None, 'heads')
- grad_conv_weight: float32 [3, 4, 2048], P(None, None, 'heads')
- grad_w_gates: float32 [2048, 2, 16], P(None, None, 'heads')
- grad_gate_params: float32 [2, 16], P(None, 'heads')
- grad_out_gain: float32 [128], replicated
- grad_w_out: float32 [2048, 2048], P('heads')
- grad_norm2_gain: float32 [2048], replicated
- grad_w_gate_up: float32 [2048, 2, 5632], P(None, None, 'heads')
- grad_w_down: float32 [5632, 2048], P('heads')
Inputs may be any that keep to these rules, and one draw needn't show every extreme that they name: `seq_counts`: column 0 counts sequences of 512 tokens, column 1 sequence of 2048 tokens. A replica holds either one long sequence and no short one, or 1 to 4 short ones and no long one. In every draw some replica holds a long sequence and some other replica holds 4 short ones. `gate_params`: row 0 is a log decay rate, row 1 a bias.
All inputs are finite; a program needn't handle non-finite values.
Results may differ from a plain program's by a relative error of at most 0.017.
Values may be sent and summed in bfloat16 or wider, within the bound.
A program may use at most 256 MiB of HBM per device.

v0:
```python
import jax
import jax.numpy as jnp
from jax import lax
from jax.sharding import PartitionSpec as P

BLOCK_LEN = 64
SEQ_SHORT = 512


epsilon = 1e-06
highest = lax.Precision.HIGHEST


def rms_rows(values, gain):
    return values * lax.rsqrt(jnp.mean(values * values, axis=-1, keepdims=True) + epsilon) * gain


def layout(counts_row, row_count):
    row_index = jnp.arange(row_count, dtype=jnp.int32)
    longer = counts_row[1] > 0
    position = jnp.where(longer, row_index, row_index % SEQ_SHORT)
    live_rows = jnp.where(longer, True, row_index < counts_row[0] * SEQ_SHORT).astype(jnp.float32)
    return (position, live_rows)


def block_step(state_in, inputs):
    query, key_vec, value, log_decay, beta_gate, keep_flag = inputs
    state_in = state_in * keep_flag
    block_rows = query.shape[0]
    cumulative = jnp.cumsum(log_decay, axis=0)
    row_index = jnp.arange(block_rows)[:, None]
    col_index = jnp.arange(block_rows)[None, :]
    lower_mask = row_index > col_index
    lower_incl = row_index >= col_index
    log_ratio = cumulative.T[:, :, None] - cumulative.T[:, None, :]
    strict = jnp.where(lower_mask, jnp.exp(jnp.where(lower_mask, log_ratio, 0.0)), 0.0)
    inclusive = jnp.where(lower_incl, jnp.exp(jnp.where(lower_incl, log_ratio, 0.0)), 0.0)
    decay_in = jnp.exp(cumulative).T[:, :, None]
    beta_rows = beta_gate.T[:, :, None]
    key_gram = jnp.einsum("ihd,jhd->hij", key_vec, key_vec, precision=highest)
    link_matrix = beta_rows * key_gram * strict
    right_side = beta_rows * (
        jnp.transpose(value, (1, 0, 2))
        - decay_in * jnp.einsum("ihk,hvk->hiv", key_vec, state_in, precision=highest)
    )
    power_term = -link_matrix
    delta_rows = right_side
    for doubling in range(block_rows.bit_length() - 1):
        delta_rows = delta_rows + jnp.einsum(
            "hij,hjv->hiv", power_term, delta_rows, precision=highest
        )
        power_term = jnp.einsum("hij,hjk->hik", power_term, power_term, precision=highest)
    query_gram = jnp.einsum("ihd,jhd->hij", query, key_vec, precision=highest) * inclusive
    carried = decay_in * jnp.einsum("ihk,hvk->hiv", query, state_in, precision=highest)
    block_out = carried + jnp.einsum("hij,hjv->hiv", query_gram, delta_rows, precision=highest)
    tail_decay = jnp.exp(cumulative[-1][None, :] - cumulative)
    new_state = jnp.exp(cumulative[-1])[:, None, None] * state_in + jnp.einsum(
        "hjv,jhk->hvk", delta_rows * tail_decay.T[:, :, None], key_vec, precision=highest
    )
    return (new_state, jnp.transpose(block_out, (1, 0, 2)))


def mixer(pre_main, pre_gates, conv_weight, gate_params, out_gain, position):
    row_count = pre_main.shape[0]
    channels = pre_main.shape[1] // 4
    heads_here = pre_gates.shape[1] // 2
    head_size = channels // heads_here
    triple = pre_main[:, : 3 * channels].reshape(row_count, 3, channels)
    convolved = jnp.zeros_like(triple)
    for lag_step in range(conv_weight.shape[1]):
        shifted = jnp.pad(triple, ((lag_step, 0), (0, 0), (0, 0)))[:row_count]
        valid_rows = (position >= lag_step).astype(jnp.float32)[:, None, None]
        convolved = convolved + shifted * valid_rows * conv_weight[:, lag_step, :][None]
    convolved = jax.nn.silu(convolved)
    query = convolved[:, 0].reshape(row_count, heads_here, head_size)
    key_vec = convolved[:, 1].reshape(row_count, heads_here, head_size)
    value = convolved[:, 2].reshape(row_count, heads_here, head_size)
    query = (
        query
        * lax.rsqrt(jnp.sum(query * query, axis=-1, keepdims=True) + epsilon)
        * head_size ** (-0.5)
    )
    key_vec = key_vec * lax.rsqrt(jnp.sum(key_vec * key_vec, axis=-1, keepdims=True) + epsilon)
    log_decay = -jnp.exp(gate_params[0])[None] * jax.nn.softplus(
        pre_gates[:, :heads_here] + gate_params[1][None]
    )
    beta_gate = jax.nn.sigmoid(pre_gates[:, heads_here:])
    keep_flags = (position[::BLOCK_LEN] > 0).astype(jnp.float32)
    blocks = row_count // BLOCK_LEN

    def to_blocks(array):
        return array.reshape((blocks, BLOCK_LEN) + array.shape[1:])

    start_state = jnp.zeros((heads_here, head_size, head_size), jnp.float32)
    final, block_outs = lax.scan(
        jax.checkpoint(block_step),
        start_state,
        (
            to_blocks(query),
            to_blocks(key_vec),
            to_blocks(value),
            to_blocks(log_decay),
            to_blocks(beta_gate),
            keep_flags,
        ),
    )
    raw_out = block_outs.reshape(row_count, heads_here, head_size)
    normed = rms_rows(raw_out, out_gain)
    gate_out = jax.nn.silu(pre_main[:, 3 * channels :]).reshape(row_count, heads_here, head_size)
    return (normed * gate_out).reshape(row_count, channels)


def contract_last(left, right):
    return lax.dot_general(
        left, right, (((1,), (1,)), ((), ())), preferred_element_type=jnp.float32
    )


def contract_first(left, right):
    return lax.dot_general(
        left, right, (((0,), (0,)), ((), ())), preferred_element_type=jnp.float32
    )


def on_device(
    block_in,
    seq_counts,
    norm1_gain,
    w_qkvg,
    conv_weight,
    w_gates,
    gate_params,
    out_gain,
    w_out,
    norm2_gain,
    w_gate_up,
    w_down,
    cotangent,
):
    own_rows = block_in.shape[0]
    group_size = lax.axis_size("heads")
    all_rows = own_rows * group_size
    features = block_in.shape[1]
    position, live_rows = layout(seq_counts[0], all_rows)
    first_row = lax.axis_index("heads") * own_rows
    live_own = lax.dynamic_slice_in_dim(live_rows, first_row, own_rows, 0)[:, None]
    input_rows = block_in.astype(jnp.float32)
    normed1, pull_norm1 = jax.vjp(rms_rows, input_rows, norm1_gain)
    normed1 = normed1.astype(jnp.bfloat16)
    main_weight = w_qkvg.reshape(features, -1)
    gates_weight = w_gates.reshape(features, -1)
    main_cols = main_weight.shape[1]
    full_normed1 = lax.all_gather(normed1, "heads", axis=0, tiled=True)
    projected = jnp.concatenate(
        [
            jnp.dot(full_normed1, main_weight, preferred_element_type=jnp.float32),
            jnp.dot(full_normed1, gates_weight, preferred_element_type=jnp.float32),
        ],
        1,
    )

    def mixer_local(pre_main, pre_gates, conv_local, params_local, gain_local):
        return mixer(pre_main, pre_gates, conv_local, params_local, gain_local, position)

    mixed_f32, pull_mixer = jax.vjp(
        mixer_local,
        projected[:, :main_cols],
        projected[:, main_cols:],
        conv_weight,
        gate_params,
        out_gain,
    )
    mixed_out = mixed_f32.astype(jnp.bfloat16)
    branch = lax.psum_scatter(
        jnp.dot(mixed_out, w_out, preferred_element_type=jnp.float32),
        "heads",
        scatter_dimension=0,
        tiled=True,
    )
    middle = input_rows + live_own * branch
    normed2, pull_norm2 = jax.vjp(rms_rows, middle, norm2_gain)
    full_normed2 = lax.all_gather(normed2.astype(jnp.bfloat16), "heads", axis=0, tiled=True)
    feed_weight = w_gate_up.reshape(features, -1)
    hidden_cols = feed_weight.shape[1] // 2
    gate_up = jnp.dot(full_normed2, feed_weight, preferred_element_type=jnp.float32)
    gate_pre = gate_up[:, :hidden_cols]
    up_pre = gate_up[:, hidden_cols:]
    hidden = (jax.nn.silu(gate_pre) * up_pre).astype(jnp.bfloat16)
    feed = lax.psum_scatter(
        jnp.dot(hidden, w_down, preferred_element_type=jnp.float32).astype(jnp.bfloat16),
        "heads",
        scatter_dimension=0,
        tiled=True,
    ).astype(jnp.float32)
    layer_out = (middle + live_own * feed).astype(jnp.bfloat16)
    grad_top = cotangent.astype(jnp.float32)
    grad_feed = (live_own * grad_top).astype(jnp.bfloat16)
    piece_rows = lax.all_gather(grad_feed, "heads", axis=0, tiled=True)
    grad_hidden = contract_last(piece_rows, w_down)
    grad_hidden, grad_down = (grad_hidden, contract_first(hidden, piece_rows))
    sigmoid_gate = jax.nn.sigmoid(gate_pre)
    grad_gate = grad_hidden * up_pre * sigmoid_gate * (1.0 + gate_pre * (1.0 - sigmoid_gate))
    grad_up = grad_hidden * gate_pre * sigmoid_gate
    grad_gate_up = jnp.concatenate([grad_gate, grad_up], 1).astype(jnp.bfloat16)
    grad_feed_weight = contract_first(full_normed2, grad_gate_up)
    grad_normed2 = lax.psum_scatter(
        contract_last(grad_gate_up, feed_weight).astype(jnp.bfloat16),
        "heads",
        scatter_dimension=0,
        tiled=True,
    ).astype(jnp.float32)
    grad_middle_part, grad_gain2 = pull_norm2(grad_normed2)
    grad_middle = grad_top + grad_middle_part
    grad_mix = (live_own * grad_middle).astype(jnp.bfloat16)
    piece_rows = lax.all_gather(grad_mix, "heads", axis=0, tiled=True)
    grad_mixed = contract_last(piece_rows, w_out)
    grad_mixed, grad_wout = (grad_mixed, contract_first(mixed_out, piece_rows))
    grad_main, grad_gates_pre, grad_conv, grad_params, grad_ogain = pull_mixer(grad_mixed)
    grad_projected = jnp.concatenate([grad_main, grad_gates_pre], 1).astype(jnp.bfloat16)
    grad_proj_weight = contract_first(full_normed1, grad_projected)
    grad_normed1 = lax.psum_scatter(
        (
            contract_last(grad_projected[:, :main_cols], main_weight)
            + contract_last(grad_projected[:, main_cols:], gates_weight)
        ).astype(jnp.bfloat16),
        "heads",
        scatter_dimension=0,
        tiled=True,
    ).astype(jnp.float32)
    grad_input_part, grad_gain1 = pull_norm1(grad_normed1)
    grad_in = grad_middle + grad_input_part
    summed = (
        lax.psum(
            grad_proj_weight[:, :main_cols].reshape(w_qkvg.shape).astype(jnp.bfloat16), "dp"
        ).astype(jnp.float32),
        lax.psum(grad_conv.astype(jnp.bfloat16), "dp").astype(jnp.float32),
        lax.psum(
            grad_proj_weight[:, main_cols:].reshape(w_gates.shape).astype(jnp.bfloat16), "dp"
        ).astype(jnp.float32),
        lax.psum(grad_params.astype(jnp.bfloat16), "dp").astype(jnp.float32),
        lax.psum(grad_wout.astype(jnp.bfloat16), "dp").astype(jnp.float32),
        lax.psum(grad_feed_weight.reshape(w_gate_up.shape).astype(jnp.bfloat16), "dp").astype(
            jnp.float32
        ),
        lax.psum(grad_down.astype(jnp.bfloat16), "dp").astype(jnp.float32),
    )
    gains = lax.psum((grad_gain1, grad_gain2, grad_ogain), ("dp", "heads"))
    return (
        layer_out,
        grad_in,
        gains[0],
        summed[0],
        summed[1],
        summed[2],
        summed[3],
        gains[2],
        summed[4],
        gains[1],
        summed[5],
        summed[6],
    )


def solution(mesh):
    return jax.shard_map(
        on_device,
        mesh=mesh,
        in_specs=(
            P(("dp", "heads"), None),
            P("dp", None),
            P(),
            P(None, None, "heads"),
            P(None, None, "heads"),
            P(None, None, "heads"),
            P(None, "heads"),
            P(),
            P("heads", None),
            P(),
            P(None, None, "heads"),
            P("heads", None),
            P(("dp", "heads"), None),
        ),
        out_specs=(
            P(("dp", "heads"), None),
            P(("dp", "heads"), None),
            P(),
            P(None, None, "heads"),
            P(None, None, "heads"),
            P(None, None, "heads"),
            P(None, "heads"),
            P(),
            P("heads", None),
            P(),
            P(None, None, "heads"),
            P("heads", None),
        ),
        check_vma=False,
    )
```

profile of v0, /device:TPU:1, one launch (start us, length us, event | category | flops | bytes accessed | tf_op | source)
XLA Modules:
  0.0 3170.5 jit_solution(16703043459884027135)
XLA Ops:
  12.7 5.2 copy.530
  19.6 119.7 %all-gather.5.cloned.1.call-done = bf16[2048,2048]{1,0:T(8,128)(2,1)} async-done(((bf16[256,2048]{1,0:T(8,128)(2,1)}), bf16[2048,2048]{1,0:T(8,128)(2,1)}) %all-gather.5.cloned.1.call-update) | async-done | bytes 8388624 | tf_op jit(solution)/shard_map/all_gather | solution.py:153
  139.4 13.1 fusion.220
  152.5 3.4 slice.130
  157.8 6.6 copy.416
  164.4 13.9 fusion.148
  182.8 3.3 squeeze.142
  189.3 3.3 squeeze.144
  192.7 3.3 squeeze.143
  195.9 6.0 multiply_reduce_fusion.14
  204.8 4.1 broadcast_multiply_fusion.1
  211.3 4.4 multiply_reduce_fusion.13
  223.9 5.6 fusion.219
  235.3 409.1 %while.44 = (s32[]{:T(128)}, f32[2,128,128]{2,1,0:T(8,128)S(1)}, f32[32,64,2,128]{3,1,2,0:T(8,128)}, f32[32,2,128,128]{3,2,1,0:T(8,128)}, f32[32,64,2]{1,2,0:T(2...) while((s32[]{:T(128)}, f32[2,128,128]{2,1,0:T(8,128)S(1)}, ...), condition=%wide.region_5.6_spmd.clone.clone, body=%wide.region_3.5_spmd.clone.clone.sunk | while | flops 220782592 | bytes 3086046 | solution.py:95
  644.4 5.6 copy.480
  652.2 5.1 reshape.421
  661.5 8.1 fusion.221
  670.4 280.8 %reduce-scatter.5.cloned.1.call-done = f32[256,2048]{1,0:T(8,128)} async-done(((f32[2048,2048]{1,0:T(8,128)}), f32[256,2048]{1,0:T(8,128)}) %reduce-scatter.5.cloned.1.call-update) | async-done | bytes 2097168 | tf_op jit(solution)/shard_map/reduce_scatter | solution.py:174
  951.1 3.8 multiply_reduce_fusion.11
  958.1 123.1 %all-gather.7.cloned.1.call-done = bf16[2048,2048]{1,0:T(8,128)(2,1)} async-done(((bf16[256,2048]{1,0:T(8,128)(2,1)}), bf16[2048,2048]{1,0:T(8,128)(2,1)}) %all-gather.7.cloned.1.call-update) | async-done | bytes 8388624 | tf_op jit(solution)/shard_map/all_gather | solution.py:182
  1081.2 18.8 fusion.222
  1100.0 107.1 %all-gather.9.cloned.1.call-done = bf16[2048,2048]{1,0:T(8,128)(2,1)} async-done(((bf16[256,2048]{1,0:T(8,128)(2,1)}), bf16[2048,2048]{1,0:T(8,128)(2,1)}) %all-gather.9.cloned.1.call-update) | async-done | bytes 8388624 | tf_op jit(solution)/shard_map/all_gather | solution.py:198
  1207.1 14.6 multiply_convert_fusion.1
  1224.2 18.1 convolution_convert_fusion.2
  1242.4 10.9 convolution_convert_fusion.3
  1253.4 136.8 %reduce-scatter.9.cloned.1.call-done = bf16[256,2048]{1,0:T(8,128)(2,1)} async-done(((bf16[2048,2048]{1,0:T(8,128)(2,1)}), bf16[256,2048]{1,0:T(8,128)(2,1)}) %reduce-scatter.9.cloned.1.call-update) | async-done | bytes 1048592 | tf_op jit(solution)/shard_map/reduce_scatter | solution.py:206
  1392.7 149.0 %reduce-scatter.7.cloned.1.call-done = bf16[256,2048]{1,0:T(8,128)(2,1)} async-done(((bf16[2048,2048]{1,0:T(8,128)(2,1)}), bf16[256,2048]{1,0:T(8,128)(2,1)}) %reduce-scatter.7.cloned.1.call-update) | async-done | bytes 1048592 | tf_op jit(solution)/shard_map/reduce_scatter | solution.py:189
  1541.7 4.1 multiply_convert_fusion.3
  1547.3 5.2 mul.1168
  1555.1 10.7 convolution_convert_fusion.4
  1565.8 16.4 convolution_convert_fusion
  1582.2 87.2 %all-gather.11.cloned.1.call-done = bf16[2048,2048]{1,0:T(8,128)(2,1)} async-done(((bf16[256,2048]{1,0:T(8,128)(2,1)}), bf16[2048,2048]{1,0:T(8,128)(2,1)}) %all-gather.11.cloned.1.call-update) | async-done | bytes 8388624 | tf_op jit(solution)/shard_map/all_gather | solution.py:215
  1669.4 9.4 fusion.162
  1681.9 3.4 mul.1159
  1685.3 8.3 multiply_reduce_fusion.9
  1696.6 8.4 add_add_fusion.3
  1711.5 878.4 %while.43 = (s32[]{:T(128)}, f32[2,128,128]{2,1,0:T(8,128)S(1)}, f32[32,64,2,128]{3,1,2,0:T(8,128)}, f32[32,64,2,128]{3,1,2,0:T(8,128)}, f32[32,64,2,128]{3,2,1,...) while((s32[]{:T(128)}, f32[2,128,128]{2,1,0:T(8,128)S(1)}, ...), condition=%wide.region_25.26_spmd.clone, body=%wide.region_13.25_spmd.clone.sunk | while | flops 624780160 | bytes 11836839 | solution.py:95
  2589.9 3.3 copy.447
  2606.6 5.0 broadcast_in_dim.217
  2615.6 6.2 mul.1177
  2621.8 3.9 mul.1178
  2629.3 6.2 broadcast_in_dim.215
  2635.5 3.9 broadcast_in_dim.216
  2642.2 3.9 reshape.415
  2646.1 4.1 reshape.412
  2650.3 6.5 add_add_fusion.2
  2656.8 13.2 multiply_reduce_fusion.8
  2670.1 3.9 multiply_multiply_fusion
  2673.9 6.1 fusion.145
  2680.1 6.8 copy.455
  2687.2 3.4 add_convert_fusion.1
  2690.7 13.0 convolution_convert_fusion.1
  2706.9 7.6 copy.458
  2714.5 6.7 convolution_convert_fusion.5
  2721.2 15.6 fusion.223
  2736.9 11.6 add_convert_fusion
  2749.3 12.5 all-reduce.22
  2763.6 199.5 %all-reduce.26.cloned.1.call-done = (bf16[2048,4,256]{2,1,0:T(4,128)(2,1)}, bf16[256,2048]{1,0:T(8,128)(2,1)}, bf16[2048,2,704]{0,2,1:T(8,128)(2,1)}, bf16[704,2048]{1,0:T(8,128)(2,1)}) async-done(((bf16[2048,4,256]{2,1,0:T(4,128)(2,1)}, bf16[256,2048]{1,0:T(8,128)(2,1)}, bf16[2048,2,704]{0,2,1:T(8,128)(2,1)}, bf16[704,2048]{1,0:T(8,128)(2,1)}), (bf16[2048,4,256]{2,1,0:T(4,128)(2,1)}, ...) | async-done | bytes 13893648 | tf_op jit(solution)/shard_map/psum | solution.py:233
  2963.1 8.8 convert_element_type.167
  2971.9 4.4 convert_element_type.156
  2976.3 3.3 convert_element_type.169
  2981.3 135.5 %reduce-scatter.11.cloned.1.call-done = bf16[256,2048]{1,0:T(8,128)(2,1)} async-done(((bf16[2048,2048]{1,0:T(8,128)(2,1)}), bf16[256,2048]{1,0:T(8,128)(2,1)}) %reduce-scatter.11.cloned.1.call-update) | async-done | bytes 1048592 | tf_op jit(solution)/shard_map/reduce_scatter | solution.py:221
  3119.1 39.1 %all-reduce.21 = (f32[2048]{0:T(1024)}, f32[128]{0:T(128)}, f32[2048]{0:T(1024)}) all-reduce(f32[2048]{0:T(1024)S(1)} %get-tuple-element.850, f32[128]{0:T(128)S(1)} %get-tuple-element.846, f32[2048]{0:T(1024)S(1)} %copy-done.58), channel_id=1, replica_groups=mesh['dp'=4,'heads'=8] {'dp','heads'}, use_global_device_ids=true, to_apply=%region_31.32 | all-reduce | flops 4224 | bytes 33792 | tf_op jit(solution)/shard_map/psum | solution.py:247
  3158.2 5.3 fusion.163
  (3603 shorter events, 1369.7 us)
Async XLA Ops:
  7.2 1199.9 %copy-start = (bf16[704,2048]{1,0:T(8,128)(2,1)S(1)}, bf16[704,2048]{1,0:T(8,128)(2,1)}, u32[]{:S(2)}) copy-start(bf16[704,2048]{1,0:T(8,128)(2,1)} %param.28) | copy-start | bytes 8650756
  7.2 132.2 %all-gather.5.cloned.1.call-start = ((), (), s32[]{:S(2)}) async-start(), calls=%async_computation.4 | async-start | bytes 9437184 | tf_op jit(solution)/shard_map/all_gather | solution.py:153
  12.6 938.5 %reduce-scatter.5.cloned.1.call-start = ((), (), s32[]{:S(2)}) async-start(), calls=%async_computation.5 | async-start | bytes 18874368 | tf_op jit(solution)/shard_map/reduce_scatter | solution.py:174
  12.7 6.8 copy-start.74
  12.7 6.8 copy-start.76
  12.7 6.8 copy-start.64
  18.0 205.9 %copy-start.28 = (bf16[2048,4]{0,1:T(4,128)(2,1)}, bf16[2048,4]{0,1:T(4,128)(2,1)S(1)}, u32[]{:S(2)}) copy-start(bf16[2048,4]{0,1:T(4,128)(2,1)S(1)} %reshape.405) | copy-start | bytes 49156
  19.4 145.0 %copy-start.38 = (f32[2048]{0:T(1024)}, f32[2048]{0:T(1024)S(1)}, u32[]{:S(2)}) copy-start(f32[2048]{0:T(1024)S(1)} %get-tuple-element.990) | copy-start | bytes 24580
  19.4 145.0 %copy-start.40 = (f32[2048]{0:T(1024)}, f32[2048]{0:T(1024)S(1)}, u32[]{:S(2)}) copy-start(f32[2048]{0:T(1024)S(1)} %get-tuple-element.991) | copy-start | bytes 24580
  19.4 145.0 %copy-start.36 = (f32[2048]{0:T(1024)}, f32[2048]{0:T(1024)S(1)}, u32[]{:S(2)}) copy-start(f32[2048]{0:T(1024)S(1)} %get-tuple-element.993) | copy-start | bytes 24580
  19.4 145.0 %copy-start.42 = (f32[2048]{0:T(1024)}, f32[2048]{0:T(1024)S(1)}, u32[]{:S(2)}) copy-start(f32[2048]{0:T(1024)S(1)} %get-tuple-element.992) | copy-start | bytes 24580
  19.5 210.0 %copy-start.69 = (f32[2]{0:T(128)}, f32[2]{0:T(128)S(1)}, u32[]{:S(2)}) copy-start(f32[2]{0:T(128)S(1)} %get-tuple-element.986) | copy-start | bytes 28
  19.5 210.0 %copy-start.71 = (f32[2]{0:T(128)}, f32[2]{0:T(128)S(1)}, u32[]{:S(2)}) copy-start(f32[2]{0:T(128)S(1)} %get-tuple-element.987) | copy-start | bytes 28
  19.6 144.8 %copy-start.52 = (f32[3,256]{1,0:T(4,128)}, f32[3,256]{1,0:T(4,128)S(1)}, u32[]{:S(2)}) copy-start(f32[3,256]{1,0:T(4,128)S(1)} %get-tuple-element.994) | copy-start | bytes 9220
  19.6 144.8 %copy-start.54 = (f32[3,256]{1,0:T(4,128)}, f32[3,256]{1,0:T(4,128)S(1)}, u32[]{:S(2)}) copy-start(f32[3,256]{1,0:T(4,128)S(1)} %get-tuple-element.995) | copy-start | bytes 9220
  19.6 144.8 %copy-start.50 = (f32[3,256]{1,0:T(4,128)}, f32[3,256]{1,0:T(4,128)S(1)}, u32[]{:S(2)}) copy-start(f32[3,256]{1,0:T(4,128)S(1)} %get-tuple-element.997) | copy-start | bytes 9220
  19.6 144.8 %copy-start.56 = (f32[3,256]{1,0:T(4,128)}, f32[3,256]{1,0:T(4,128)S(1)}, u32[]{:S(2)}) copy-start(f32[3,256]{1,0:T(4,128)S(1)} %get-tuple-element.996) | copy-start | bytes 9220
  203.4 5.5 copy-start.30
  229.5 5.7 copy-start.26
  644.4 5.6 copy-start.48
  644.4 5.6 copy-start.49
  644.4 5.6 copy-start.78
  669.6 411.6 %all-gather.7.cloned.1.call-start = ((), (), s32[]{:S(2)}) async-start(), calls=%async_computation.6 | async-start | bytes 9437184 | tf_op jit(solution)/shard_map/all_gather | solution.py:182
  670.3 285.9 %copy-start.44 = (f32[2048]{0:T(1024)S(1)}, f32[2048]{0:T(1024)}, u32[]{:S(2)}) copy-start(f32[2048]{0:T(1024)} %param.26) | copy-start | bytes 24580
  954.9 586.8 %copy-start.59 = (f32[256]{0:T(256)}, f32[256]{0:T(256)S(1)}, u32[]{:S(2)}) copy-start(f32[256]{0:T(256)S(1)} %fusion.186) | copy-start | bytes 3076
  957.5 249.6 %all-gather.9.cloned.1.call-start = ((), (), s32[]{:S(2)}) async-start(), calls=%async_computation.8 | async-start | bytes 9437184 | tf_op jit(solution)/shard_map/all_gather | solution.py:198
  958.1 432.1 %reduce-scatter.9.cloned.1.call-start = ((), (), s32[]{:S(2)}) async-start(), calls=%async_computation.9 | async-start | bytes 9437184 | tf_op jit(solution)/shard_map/reduce_scatter | solution.py:206
  1242.4 299.3 %reduce-scatter.7.cloned.1.call-start = ((), (), s32[]{:S(2)}) async-start(), calls=%async_computation.7 | async-start | bytes 9437184 | tf_op jit(solution)/shard_map/reduce_scatter | solution.py:189
  1253.3 136.9 %copy-start.4 = (f32[256,2048]{1,0:T(8,128)S(1)}, f32[256,2048]{1,0:T(8,128)}, u32[]{:S(2)}) copy-start(f32[256,2048]{1,0:T(8,128)} %copy-done.3) | copy-start | bytes 6291460
  1253.3 416.1 %all-gather.11.cloned.1.call-start = ((), (), s32[]{:S(2)}) async-start(), calls=%async_computation.10 | async-start | bytes 9437184 | tf_op jit(solution)/shard_map/all_gather | solution.py:215
  1392.7 153.1 %copy-start.67 = (f32[256]{0:T(256)}, f32[256]{0:T(256)S(1)}, u32[]{:S(2)}) copy-start(f32[256]{0:T(256)S(1)} %multiply_multiply_fusion.7) | copy-start | bytes 3076
  1545.8 1417.3 %all-reduce.26.cloned.1.call-start = ((), (), s32[]{:S(2)}) async-start(), calls=%async_computation.12 | async-start | bytes 27787264 | tf_op jit(solution)/shard_map/psum | solution.py:233
  1555.1 10.7 copy-start.81
  1555.1 10.7 copy-start.83
  1565.8 103.6 %copy-start.12 = (f32[2048,256]{0,1:T(8,128)S(1)}, f32[2048,256]{0,1:T(8,128)}, u32[]{:S(2)}) copy-start(f32[2048,256]{0,1:T(8,128)} %reshape.421) | copy-start | bytes 6291460
  2615.6 10.1 copy-start.7
  2629.3 10.1 copy-start.15
  2650.2 6.5 copy-start.16
  2650.2 6.5 copy-start.37
  2650.2 6.5 copy-start.39
  2650.2 6.5 copy-start.41
  2650.2 6.5 copy-start.43
  2656.8 13.2 copy-start.53
  2656.8 13.2 copy-start.55
  2656.8 13.2 copy-start.57
  2680.1 6.8 copy-start.27
  2680.1 6.8 copy-start.47
  2680.1 6.8 copy-start.70
  2680.1 6.8 copy-start.72
  2680.1 7.1 copy-start.17
  2690.6 13.0 copy-start.20
  2706.9 7.6 copy-start.22
  2721.2 15.7 copy-start.29
  2721.2 395.6 %reduce-scatter.11.cloned.1.call-start = ((), (), s32[]{:S(2)}) async-start(), calls=%async_computation.11 | async-start | bytes 9437184 | tf_op jit(solution)/shard_map/reduce_scatter | solution.py:221
  2963.1 8.8 copy-start.19
  2979.6 137.1 %copy-start.6 = (bf16[256,2048]{1,0:T(8,128)(2,1)S(1)}, bf16[256,2048]{1,0:T(8,128)(2,1)}, u32[]{:S(2)}) copy-start(bf16[256,2048]{1,0:T(8,128)(2,1)} %param.17) | copy-start | bytes 3145732
  2979.6 137.1 %copy-start.46 = (f32[2048]{0:T(1024)S(1)}, f32[2048]{0:T(1024)}, u32[]{:S(2)}) copy-start(f32[2048]{0:T(1024)} %param.19) | copy-start | bytes 24580
  2979.6 137.1 %copy-start.63 = (f32[256]{0:T(256)S(1)}, f32[256]{0:T(256)}, u32[]{:S(2)}) copy-start(f32[256]{0:T(256)} %copy-done.62) | copy-start | bytes 3076
  2979.6 139.4 %copy-start.66 = (f32[256]{0:T(256)S(1)}, f32[256]{0:T(256)}, u32[]{:S(2)}) copy-start(f32[256]{0:T(256)} %copy-done.65) | copy-start | bytes 3076
  2979.6 139.4 %copy-start.58 = (f32[2048]{0:T(1024)S(1)}, f32[2048]{0:T(1024)}, u32[]{:S(2)}) copy-start(f32[2048]{0:T(1024)} %get-tuple-element.848) | copy-start | bytes 24580
  2979.7 178.5 %copy-start.45 = (f32[2048]{0:T(1024)S(1)}, f32[2048]{0:T(1024)}, u32[]{:S(2)}) copy-start(f32[2048]{0:T(1024)} %param.26) | copy-start | bytes 24580
  2979.7 178.5 %copy-start.60 = (f32[256]{0:T(256)S(1)}, f32[256]{0:T(256)}, u32[]{:S(2)}) copy-start(f32[256]{0:T(256)} %copy-done.59) | copy-start | bytes 3076
  2979.7 178.5 %copy-start.68 = (f32[256]{0:T(256)S(1)}, f32[256]{0:T(256)}, u32[]{:S(2)}) copy-start(f32[256]{0:T(256)} %copy-done.67) | copy-start | bytes 3076
  3119.0 44.5 %copy-start.1 = (bf16[704,2048]{1,0:T(8,128)(2,1)S(1)}, bf16[704,2048]{1,0:T(8,128)(2,1)}, u32[]{:S(2)}) copy-start(bf16[704,2048]{1,0:T(8,128)(2,1)} %param.28) | copy-start | bytes 8650756
  (30 other events, 92.7 us)
Sparse Core Ops, SparseCore 0:
  12.7 126.5 all-gather.4
  669.8 281.3 reduce-scatter.4
  957.6 123.5 all-gather.6
  1084.0 123.1 all-gather.8
  1242.5 147.6 reduce-scatter.8
  1393.7 147.9 reduce-scatter.6
  1545.9 123.4 all-gather.10
  2721.3 241.7 all-reduce.25
  2967.2 149.5 reduce-scatter.10
where the time goes:
time: 3200 us; the launch traced here: 3170 us
  waiting for transfers between devices  1340 us (42%)
  matrix products  1120 us (35%)
  local copies, waits for them, and re-layouts  406 us (13%)
  other arithmetic  223 us (7%)
  blocking collectives  51.7 us (2%)
    reduce_scatter x1, waiting for transfers between devices, on_device(): lax.psum_scatter(jnp.dot(mixed_out, w_out, preferred_element_type=jnp.flo...  281 us
    psum x1, waiting for transfers between devices, on_device(): lax.psum(grad_proj_weight[:, :main_cols].reshape(w_qkvg.shape).astype(jnp...  200 us
    dot_general x768, matrix products, block_step(): jnp.einsum('hij,hjv->hiv', power_term, delta_rows, precision=highest)  189 us
    dot_general x128, matrix products, block_step(): jnp.einsum('ihk,hvk->hiv', key_vec, state_in, precision=highest)  162 us
    dot_general x640, matrix products, block_step(): jnp.einsum('hij,hjk->hik', power_term, power_term, precision=highest)  154 us
    reduce_scatter x1, waiting for transfers between devices, on_device(): lax.psum_scatter(jnp.dot(hidden, w_down, preferred_element_type=jnp.float...  149 us
    dot_general x128, matrix products, block_step(): jnp.einsum('ihk,hvk->hiv', query, state_in, precision=highest)  139 us
    reduce_scatter x1, waiting for transfers between devices, on_device(): lax.psum_scatter(contract_last(grad_gate_up, feed_weight).astype(jnp.bflo...  137 us
  transfers between devices with their start and end apart: 9, of which 9 were waited for; matrix products, arithmetic and copies ran while one was open for 4% of the time, Pallas kernels for 0%

commit v1 on v0

v1 whole, which is shorter than its diff:
```python
import functools
import jax
import jax.numpy as jnp
from jax import lax
from jax.experimental import pallas as pl
from jax.experimental.pallas import tpu as pltpu
from jax.sharding import PartitionSpec as P

SEQ_SHORT = 512
CHUNK = 256
HEAD = 128
EPS = 1e-06
F32 = jnp.float32
BF16 = jnp.bfloat16
LOW, MID, TOP = lax.Precision.DEFAULT, lax.Precision.HIGH, lax.Precision.HIGHEST
NN, NT, TN = ((1,), (0,)), ((1,), (1,)), ((0,), (0,))
P_INV, P_FWD, P_BWD = MID, MID, MID


def dot(left, right, dims, precision):
    if precision is LOW:
        left, right = left.astype(BF16), right.astype(BF16)
        return lax.dot_general(left, right, (dims, ((), ())), preferred_element_type=F32)
    return lax.dot_general(
        left, right, (dims, ((), ())), precision=precision, preferred_element_type=F32
    )


def grid_index(shape, axis):
    return lax.broadcasted_iota(jnp.int32, shape, axis)


def positions(longer, first_row, count):
    rows = grid_index((count, 1), 0) + first_row
    return jnp.where(longer > 0, rows, rows % SEQ_SHORT)


def keeps(longer, first_row):
    start = jnp.where(longer > 0, first_row, first_row % SEQ_SHORT)
    return jnp.where(start > 0, 1.0, 0.0).astype(F32)


def softplus(x):
    return jnp.maximum(x, 0.0) + jnp.log1p(jnp.exp(-jnp.abs(x)))


def gate_values(gates, params, heads):
    lane = grid_index(gates.shape, 1)
    rate = jnp.exp(params[0:1])
    shifted = gates + params[1:2]
    log_decay = jnp.where(lane < heads, -rate * softplus(shifted), 0.0)
    return rate, shifted, log_decay


def lane_column(values, index):
    return values[:, index : index + 1]


def decays(cumulative, cumulative_rows, head, masks):
    column = lane_column(cumulative, head)
    row = cumulative_rows[head : head + 1, :]
    inclusive = masks[0]
    ratio = jnp.where(inclusive, jnp.exp(jnp.where(inclusive, column - row, 0.0)), 0.0)
    last = column[CHUNK - 1 : CHUNK, :]
    return ratio, jnp.exp(column), jnp.exp(last - column), jnp.exp(last)


def unit(values):
    scale = lax.rsqrt(jnp.sum(values * values, axis=-1, keepdims=True) + EPS)
    return values * scale, scale


def inverse(link, row, col):
    apart = row ^ col

    def level(size):
        return (apart >= size) & (apart < 2 * size)

    out = jnp.where(row == col, 1.0, 0.0) - jnp.where(level(1), link, 0.0)
    size = 2
    while size < CHUNK // 2:
        part = jnp.where(level(size), link, 0.0)
        out = out - dot(out, dot(part, out, NN, P_INV), NN, P_INV)
        size *= 2
    half = CHUNK // 2
    corner = dot(link[half:, :half], out[:half, :half], NN, P_INV)
    corner = -dot(out[half:, half:], corner, NN, P_INV)
    return jnp.concatenate(
        [out[:half], jnp.concatenate([corner, out[half:, half:]], axis=1)], axis=0
    )


def forward_kernel(
    heads, longer_ref, main_ref, conv_ref, params_ref, gain_ref,
    mixed_ref, conv_out_ref, raw_ref, delta_ref, solve_ref, state_ref, state, tail_rows,
):
    step = pl.program_id(0)
    first_row = step * CHUNK
    longer = longer_ref[0]
    width = heads * HEAD

    @pl.when(step == 0)
    def _():
        state[...] = jnp.zeros_like(state)
        tail_rows[...] = jnp.zeros_like(tail_rows)

    position = positions(longer, first_row, CHUNK)
    keep = keeps(longer, first_row)
    triple = main_ref[:, : 3 * width]
    padded = jnp.concatenate([tail_rows[...], triple], axis=0)
    taps = conv_ref[...]
    convolved = triple * taps[0:1]
    for lag in range(1, 4):
        shifted = padded[8 - lag : 8 - lag + CHUNK]
        convolved = convolved + jnp.where(position >= lag, shifted, 0.0) * taps[lag : lag + 1]
    tail_rows[...] = triple[CHUNK - 8 :]
    conv_out_ref[...] = convolved
    active = convolved * jax.nn.sigmoid(convolved)
    gates = main_ref[:, 4 * width :]
    rate, shifted_gate, log_decay = gate_values(gates, params_ref[...], heads)
    beta_all = jax.nn.sigmoid(gates)
    row = grid_index((CHUNK, CHUNK), 0)
    col = grid_index((CHUNK, CHUNK), 1)
    masks = (row >= col, row > col)
    cumulative = dot(jnp.where(masks[0], 1.0, 0.0), log_decay, NN, TOP)
    cumulative_rows = jnp.transpose(cumulative)
    for head in range(heads):
        cols = slice(head * HEAD, (head + 1) * HEAD)
        query = unit(active[:, head * HEAD : (head + 1) * HEAD])[0] * HEAD**-0.5
        key = unit(active[:, width + head * HEAD : width + (head + 1) * HEAD])[0]
        value = active[:, 2 * width + head * HEAD : 2 * width + (head + 1) * HEAD]
        beta = lane_column(beta_all, heads + head)
        ratio, decay_in, decay_out, decay_all = decays(cumulative, cumulative_rows, head, masks)
        grams = dot(jnp.concatenate([key, query], axis=0), key, NT, P_FWD)
        link = jnp.where(masks[1], beta * ratio * grams[:CHUNK], 0.0)
        solve = inverse(link, row, col)
        solve_ref[head] = solve
        both = dot(
            solve, jnp.concatenate([beta * value, (beta * decay_in) * key], axis=1), NN, P_FWD
        )
        entry = state[head] * keep
        state_ref[0, head] = entry
        carried = dot(
            jnp.concatenate([both[:, HEAD:], decay_in * query], axis=0), entry, NT, P_FWD
        )
        delta = both[:, :HEAD] - carried[:CHUNK]
        delta_ref[:, cols] = delta
        raw = carried[CHUNK:] + dot(grams[CHUNK:] * ratio, delta, NN, P_FWD)
        state[head] = decay_all * entry + dot(delta * decay_out, key, TN, P_FWD)
        raw_ref[:, cols] = raw
        scale = lax.rsqrt(jnp.mean(raw * raw, axis=-1, keepdims=True) + EPS)
        gate = main_ref[:, 3 * width + head * HEAD : 3 * width + (head + 1) * HEAD]
        mixed = raw * scale * gain_ref[...] * (gate * jax.nn.sigmoid(gate))
        mixed_ref[:, cols] = mixed.astype(mixed_ref.dtype)


def backward_kernel(
    heads, chunks, longer_ref, grad_ref, main_ref, conv_out_ref, raw_ref, delta_ref,
    solve_ref, state_ref, conv_ref, params_ref, gain_ref,
    dmain_ref, dconv_ref, dparams_ref, dgain_ref, dstate, head_rows,
):
    step = pl.program_id(0)
    first_row = (chunks - 1 - step) * CHUNK
    longer = longer_ref[0]
    width = heads * HEAD

    @pl.when(step == 0)
    def _():
        dstate[...] = jnp.zeros_like(dstate)
        head_rows[...] = jnp.zeros_like(head_rows)
        dconv_ref[...] = jnp.zeros_like(dconv_ref)
        dparams_ref[...] = jnp.zeros_like(dparams_ref)
        dgain_ref[...] = jnp.zeros_like(dgain_ref)

    keep = keeps(longer, first_row)
    convolved = conv_out_ref[...]
    sigmoid_conv = jax.nn.sigmoid(convolved)
    active = convolved * sigmoid_conv
    slope = sigmoid_conv * (1.0 + convolved * (1.0 - sigmoid_conv))
    gates = main_ref[:, 4 * width :]
    params = params_ref[...]
    rate, shifted_gate, log_decay = gate_values(gates, params, heads)
    beta_all = jax.nn.sigmoid(gates)
    row = grid_index((CHUNK, CHUNK), 0)
    col = grid_index((CHUNK, CHUNK), 1)
    masks = (row >= col, row > col)
    cumulative = dot(jnp.where(masks[0], 1.0, 0.0), log_decay, NN, TOP)
    cumulative_rows = jnp.transpose(cumulative)
    lane = grid_index((CHUNK, 128), 1)
    last_row = grid_index((CHUNK, 1), 0) == CHUNK - 1
    dcumulative = jnp.zeros((CHUNK, 128), F32)
    dbeta_all = jnp.zeros((CHUNK, 128), F32)
    gain = gain_ref[...]
    dgain = jnp.zeros((1, HEAD), F32)
    dconv_parts = [[], [], []]
    for head in range(heads):
        cols = slice(head * HEAD, (head + 1) * HEAD)
        gate = main_ref[:, 3 * width + head * HEAD : 3 * width + (head + 1) * HEAD]
        raw = raw_ref[:, cols]
        grad = grad_ref[:, cols]
        scale = lax.rsqrt(jnp.mean(raw * raw, axis=-1, keepdims=True) + EPS)
        normed = raw * scale
        sigmoid_gate = jax.nn.sigmoid(gate)
        gated = gate * sigmoid_gate
        product = grad * normed
        dgain = dgain + jnp.sum(product * gated, axis=0, keepdims=True)
        dgate = product * gain * (sigmoid_gate * (1.0 + gate * (1.0 - sigmoid_gate)))
        dmain_ref[:, 3 * width + head * HEAD : 3 * width + (head + 1) * HEAD] = dgate.astype(
            dmain_ref.dtype
        )
        dnormed = grad * gain * gated
        draw = scale * (dnormed - normed * jnp.mean(dnormed * normed, axis=-1, keepdims=True))
        query_unit, query_scale = unit(active[:, head * HEAD : (head + 1) * HEAD])
        query = query_unit * HEAD**-0.5
        key, key_scale = unit(active[:, width + head * HEAD : width + (head + 1) * HEAD])
        value = active[:, 2 * width + head * HEAD : 2 * width + (head + 1) * HEAD]
        beta = lane_column(beta_all, heads + head)
        ratio, decay_in, decay_out, decay_all = decays(cumulative, cumulative_rows, head, masks)
        entry = state_ref[0, head]
        delta = delta_ref[:, cols]
        dlater = dstate[head]
        gram = dot(query, key, NT, P_BWD) * ratio
        key_dlater = dot(key, dlater, NT, P_BWD)
        ddelta = dot(gram, draw, TN, P_BWD) + decay_out * key_dlater
        dright = dot(solve_ref[head], ddelta, TN, P_BWD)
        pairs = dot(jnp.concatenate([dright, draw], axis=0), delta, NT, P_BWD)
        dlink = jnp.where(masks[1], -pairs[:CHUNK] * ratio, 0.0)
        dgram = pairs[CHUNK:] * ratio
        on_entry = dot(jnp.concatenate([dright, draw], axis=0), entry, NN, P_BWD)
        key_entry = dot(key, entry, NT, P_BWD)
        on_key = dot(jnp.concatenate([dlink, dgram], axis=0), key, NN, P_BWD)
        dquery = decay_in * on_entry[CHUNK:] + on_key[CHUNK:]
        link_key = on_key[:CHUNK]
        key_read = beta * (link_key - decay_in * on_entry[:CHUNK])
        key_tail = decay_out * dot(delta, dlater, NN, P_BWD)
        key_write = (
            dot(beta * dlink, key, TN, P_BWD) + dot(dgram, query, TN, P_BWD) + key_tail
        )
        dkey = key_read + key_write
        dvalue = beta * dright
        dbeta = jnp.sum(
            dright * (value - decay_in * key_entry) + key * link_key, axis=-1, keepdims=True
        )
        dlog = jnp.sum(query * dquery + key * (key_read - key_write), axis=-1, keepdims=True)
        ending = decay_all * jnp.sum(
            jnp.sum(entry * dlater, axis=-1, keepdims=True), axis=0, keepdims=True
        ) + jnp.sum(jnp.sum(key * key_tail, axis=-1, keepdims=True), axis=0, keepdims=True)
        dlog = dlog + jnp.where(last_row, ending, 0.0)
        dcumulative = jnp.where(lane == head, dlog, dcumulative)
        dbeta_all = jnp.where(lane == heads + head, dbeta, dbeta_all)
        dstate[head] = keep * (
            decay_all * dlater
            + dot(decay_in * draw, query, TN, P_BWD)
            - dot((beta * decay_in) * dright, key, TN, P_BWD)
        )
        dquery = (HEAD**-0.5 * query_scale) * (
            dquery - query_unit * jnp.sum(dquery * query_unit, axis=-1, keepdims=True)
        )
        dkey = key_scale * (dkey - key * jnp.sum(dkey * key, axis=-1, keepdims=True))
        for kind, part in enumerate((dquery, dkey, dvalue)):
            dconv_parts[kind].append(part)
    dactive = jnp.concatenate([p for parts in dconv_parts for p in parts], axis=1)
    dconvolved = dactive * slope
    padded = jnp.concatenate([dconvolved, head_rows[...]], axis=0)
    position = positions(longer, first_row, CHUNK + 8)
    taps = conv_ref[...]
    triple = main_ref[:, : 3 * width]
    dtriple = dconvolved * taps[0:1]
    dconv_ref[0:1] += jnp.sum(dconvolved * triple, axis=0, keepdims=True)
    for lag in range(1, 4):
        moved = jnp.where(position >= lag, padded, 0.0)[lag : lag + CHUNK]
        dtriple = dtriple + moved * taps[lag : lag + 1]
        dconv_ref[lag : lag + 1] += jnp.sum(moved * triple, axis=0, keepdims=True)
    head_rows[...] = dconvolved[:8]
    dmain_ref[:, : 3 * width] = dtriple.astype(dmain_ref.dtype)
    dlog_decay = dot(jnp.where(row <= col, 1.0, 0.0), dcumulative, NN, TOP)
    dshifted = -dlog_decay * rate * jax.nn.sigmoid(shifted_gate)
    dshifted = jnp.where(lane < heads, dshifted, 0.0)
    dparams_ref[0:1] += jnp.sum(dlog_decay * log_decay, axis=0, keepdims=True)
    dparams_ref[1:2] += jnp.sum(dshifted, axis=0, keepdims=True)
    dmain_ref[:, 4 * width :] = (dshifted + dbeta_all * beta_all * (1.0 - beta_all)).astype(
        dmain_ref.dtype
    )
    dgain_ref[...] += dgain


def row_block(width, chunks, backward):
    if backward:
        return pl.BlockSpec((CHUNK, width), lambda i: (chunks - 1 - i, 0))
    return pl.BlockSpec((CHUNK, width), lambda i: (i, 0))


def whole_block(shape):
    return pl.BlockSpec(shape, lambda i: (0,) * len(shape))


def mixer_forward(longer, main, conv, params, gain):
    rows, width = main.shape[0], conv.shape[1] // 3
    heads, chunks = width // HEAD, rows // CHUNK
    rowed = functools.partial(row_block, chunks=chunks, backward=False)
    shape = jax.ShapeDtypeStruct
    return pl.pallas_call(
        functools.partial(forward_kernel, heads),
        grid=(chunks,),
        in_specs=[
            pl.BlockSpec(memory_space=pltpu.SMEM),
            rowed(4 * width + 128),
            whole_block((4, 3 * width)),
            whole_block((2, 128)),
            whole_block((1, HEAD)),
        ],
        out_specs=[
            rowed(width),
            rowed(3 * width),
            rowed(width),
            rowed(width),
            pl.BlockSpec((heads, CHUNK, CHUNK), lambda i: (0, i, 0)),
            pl.BlockSpec((1, heads, HEAD, HEAD), lambda i: (i, 0, 0, 0)),
        ],
        out_shape=[
            shape((rows, width), BF16),
            shape((rows, 3 * width), F32),
            shape((rows, width), F32),
            shape((rows, width), F32),
            shape((heads, rows, CHUNK), F32),
            shape((chunks, heads, HEAD, HEAD), F32),
        ],
        scratch_shapes=[
            pltpu.VMEM((heads, HEAD, HEAD), F32),
            pltpu.VMEM((8, 3 * width), F32),
        ],
        compiler_params=pltpu.CompilerParams(vmem_limit_bytes=48 * 2**20),
        name="mixer_forward",
    )(longer, main, conv, params, gain)


def mixer_backward(longer, grad, main, saved, conv, params, gain):
    rows, width = main.shape[0], conv.shape[1] // 3
    heads, chunks = width // HEAD, rows // CHUNK
    rowed = functools.partial(row_block, chunks=chunks, backward=True)
    shape = jax.ShapeDtypeStruct
    return pl.pallas_call(
        functools.partial(backward_kernel, heads, chunks),
        grid=(chunks,),
        in_specs=[
            pl.BlockSpec(memory_space=pltpu.SMEM),
            rowed(width),
            rowed(4 * width + 128),
            rowed(3 * width),
            rowed(width),
            rowed(width),
            pl.BlockSpec((heads, CHUNK, CHUNK), lambda i: (0, chunks - 1 - i, 0)),
            pl.BlockSpec((1, heads, HEAD, HEAD), lambda i: (chunks - 1 - i, 0, 0, 0)),
            whole_block((4, 3 * width)),
            whole_block((2, 128)),
            whole_block((1, HEAD)),
        ],
        out_specs=[
            rowed(4 * width + 128),
            whole_block((4, 3 * width)),
            whole_block((2, 128)),
            whole_block((1, HEAD)),
        ],
        out_shape=[
            shape((rows, 4 * width + 128), BF16),
            shape((4, 3 * width), F32),
            shape((2, 128), F32),
            shape((1, HEAD), F32),
        ],
        scratch_shapes=[
            pltpu.VMEM((heads, HEAD, HEAD), F32),
            pltpu.VMEM((8, 3 * width), F32),
        ],
        compiler_params=pltpu.CompilerParams(vmem_limit_bytes=48 * 2**20),
        name="mixer_backward",
    )(longer, grad, main, *saved, conv, params, gain)


def rms_rows(values, gain):
    return values * lax.rsqrt(jnp.mean(values * values, axis=-1, keepdims=True) + EPS) * gain


def matmul(left, right, dims):
    return lax.dot_general(left, right, (dims, ((), ())), preferred_element_type=F32)


def gather_rows(values):
    return lax.all_gather(values, "heads", axis=0, tiled=True)


def scatter_rows(values):
    return lax.psum_scatter(
        values.astype(BF16), "heads", scatter_dimension=0, tiled=True
    ).astype(F32)


def sum_replicas(values):
    return lax.psum(values.astype(BF16), "dp").astype(F32)


def on_device(
    block_in,
    seq_counts,
    norm1_gain,
    w_qkvg,
    conv_weight,
    w_gates,
    gate_params,
    out_gain,
    w_out,
    norm2_gain,
    w_gate_up,
    w_down,
    cotangent,
):
    own_rows, features = block_in.shape
    all_rows = own_rows * lax.axis_size("heads")
    width = conv_weight.shape[2]
    heads = gate_params.shape[1]
    longer = seq_counts[0, 1:2]
    first_row = lax.axis_index("heads") * own_rows
    row_index = first_row + jnp.arange(own_rows, dtype=jnp.int32)
    live_own = jnp.where(longer[0] > 0, True, row_index < seq_counts[0, 0] * SEQ_SHORT)
    live_own = live_own.astype(F32)[:, None]
    input_rows = block_in.astype(F32)
    normed1, pull_norm1 = jax.vjp(rms_rows, input_rows, norm1_gain)
    full_normed1 = gather_rows(normed1.astype(BF16))
    weight = jnp.concatenate(
        [
            w_qkvg.reshape(features, 4 * width),
            w_gates.reshape(features, 2 * heads),
            jnp.zeros((features, 128 - 2 * heads), BF16),
        ],
        axis=1,
    )
    projected = matmul(full_normed1, weight, NN)
    taps = jnp.transpose(conv_weight, (1, 0, 2)).reshape(4, 3 * width)
    params = jnp.pad(gate_params, ((0, 0), (0, 128 - heads)))
    gain_row = out_gain[None]
    mixed, *saved = mixer_forward(longer, projected, taps, params, gain_row)
    branch = scatter_rows(matmul(mixed, w_out, NN))
    grad_top = cotangent.astype(F32)
    grad_feed = gather_rows((live_own * grad_top).astype(BF16))
    middle = input_rows + live_own * branch
    normed2, pull_norm2 = jax.vjp(rms_rows, middle, norm2_gain)
    full_normed2 = gather_rows(normed2.astype(BF16))
    feed_weight = w_gate_up.reshape(features, -1)
    hidden_cols = w_down.shape[0]
    gate_up = matmul(full_normed2, feed_weight, NN)
    gate_pre = gate_up[:, :hidden_cols]
    up_pre = gate_up[:, hidden_cols:]
    hidden = (jax.nn.silu(gate_pre) * up_pre).astype(BF16)
    grad_hidden = matmul(grad_feed, w_down, NT)
    sigmoid_gate = jax.nn.sigmoid(gate_pre)
    grad_gate = grad_hidden * up_pre * sigmoid_gate * (1.0 + gate_pre * (1.0 - sigmoid_gate))
    grad_up = grad_hidden * gate_pre * sigmoid_gate
    grad_gate_up = jnp.concatenate([grad_gate, grad_up], 1).astype(BF16)
    grad_normed2 = scatter_rows(matmul(grad_gate_up, feed_weight, NT))
    feed = scatter_rows(matmul(hidden, w_down, NN))
    layer_out = (middle + live_own * feed).astype(BF16)
    grad_middle_part, grad_gain2 = pull_norm2(grad_normed2)
    grad_middle = grad_top + grad_middle_part
    grad_mix = gather_rows((live_own * grad_middle).astype(BF16))
    grad_feed_weight = matmul(full_normed2, grad_gate_up, TN)
    grad_down = matmul(hidden, grad_feed, TN)
    grad_mixed = matmul(grad_mix, w_out, NT)
    grad_wout = matmul(mixed, grad_mix, TN)
    dprojected, dtaps, dparams, dgain = mixer_backward(
        longer, grad_mixed, projected, saved, taps, params, gain_row
    )
    grad_normed1 = scatter_rows(matmul(dprojected, weight, NT))
    grad_weight = matmul(full_normed1, dprojected, TN)
    grad_input_part, grad_gain1 = pull_norm1(grad_normed1)
    grad_in = grad_middle + grad_input_part
    grad_conv = jnp.transpose(dtaps.reshape(4, 3, width), (1, 0, 2))
    summed_ff = (
        sum_replicas(grad_feed_weight.reshape(w_gate_up.shape)),
        sum_replicas(grad_down),
    )
    summed_out = sum_replicas(grad_wout)
    small = lax.psum(
        (grad_conv, grad_weight[:, 4 * width : 4 * width + 2 * heads], dparams[:, :heads]), "dp"
    )
    gains = lax.psum((grad_gain1, grad_gain2, dgain[0]), ("dp", "heads"))
    return (
        layer_out,
        grad_in,
        gains[0],
        sum_replicas(grad_weight[:, : 4 * width]).reshape(w_qkvg.shape),
        small[0],
        small[1].reshape(w_gates.shape),
        small[2],
        gains[2],
        summed_out,
        gains[1],
        summed_ff[0],
        summed_ff[1],
    )


def solution(mesh):
    return jax.shard_map(
        on_device,
        mesh=mesh,
        in_specs=(
            P(("dp", "heads"), None),
            P("dp", None),
            P(),
            P(None, None, "heads"),
            P(None, None, "heads"),
            P(None, None, "heads"),
            P(None, "heads"),
            P(),
            P("heads", None),
            P(),
            P(None, None, "heads"),
            P("heads", None),
            P(("dp", "heads"), None),
        ),
        out_specs=(
            P(("dp", "heads"), None),
            P(("dp", "heads"), None),
            P(),
            P(None, None, "heads"),
            P(None, None, "heads"),
            P(None, None, "heads"),
            P(None, "heads"),
            P(),
            P("heads", None),
            P(),
            P(None, None, "heads"),
            P("heads", None),
        ),
        check_vma=False,
    )
```

time: 3200 us -> 1650 us (0.52)
  matrix products: 1120 us -> 156 us
  local copies, waits for them, and re-layouts: 406 us -> 36.9 us
  other arithmetic: 223 us -> 43.8 us
  waiting for transfers between devices: 1340 us -> 1170 us
  Pallas kernels: 0 us -> 152 us
    dot_general x2126 -> x12, matrix products: 1120 us -> 156 us  [matmul(): lax.dot_general(left, right, (dims, ((), ())), preferred_element_type=F32)]
    reduce_scatter x4, waiting for transfers between devices: 702 us -> 536 us  [scatter_rows(): lax.psum_scatter(values.astype(BF16), 'heads', scatter_dimension=0, tiled...]
    pallas_call x0 -> x2, Pallas kernels: none -> 152 us  [the longest x1 96 us: mixer_forward(): pl.pallas_call(functools.partial(forward_kernel, heads), grid=(chunks,),...]
    squeeze x229 -> x0, local copies, waits for them, and re-layouts: 127 us -> none  [the longest x192 110 us: mixer(): lax.scan(jax.checkpoint(block_step), start_state, (to_blocks(query), to_b...]
    reduce_sum x108 -> x4, other arithmetic: 81 us -> 9.33 us  [the longest x2 5.57 us: rms_rows(): values * lax.rsqrt(jnp.mean(values * values, axis=-1, keepdims=True) + EPS)]
    dynamic_slice x96 -> x0, local copies, waits for them, and re-layouts: 65.2 us -> none  [mixer(): lax.scan(jax.checkpoint(block_step), start_state, (to_blocks(query), to_b...]
    dynamic_update_slice x96 -> x0, local copies, waits for them, and re-layouts: 42.6 us -> none  [mixer(): lax.scan(jax.checkpoint(block_step), start_state, (to_blocks(query), to_b...]
    mul x42 -> x0, other arithmetic: 33.3 us -> none  [the longest x1 13.9 us: mixer(): convolved = jax.nn.silu(convolved)]
  transfers between devices with their start and end apart: 9 -> 9, of which waited for: 9 -> 9; matrix products, arithmetic and copies ran while one was open for 4% -> 7% of each run, Pallas kernels for 0% -> 0%
where the time goes in v1:
time: 1650 us; the launch traced here: 1640 us
  waiting for transfers between devices  1170 us (71%)
  matrix products  156 us (9%)
  Pallas kernels  152 us (9%)
  blocking collectives  57.1 us (3%)
  other arithmetic  43.8 us (3%)
  local copies, waits for them, and re-layouts  36.9 us (2%)
    reduce_scatter x4, waiting for transfers between devices, scatter_rows(): lax.psum_scatter(values.astype(BF16), 'heads', scatter_dimension=0, tiled...  536 us
    all_gather x4, waiting for transfers between devices, gather_rows(): return lax.all_gather(values, 'heads', axis=0, tiled=True)  438 us
    psum x1, waiting for transfers between devices, sum_replicas(): return lax.psum(values.astype(BF16), 'dp').astype(F32)  200 us
    dot_general x12, matrix products, matmul(): lax.dot_general(left, right, (dims, ((), ())), preferred_element_type=F32)  156 us
    pallas_call x1, Pallas kernels, mixer_forward(): pl.pallas_call(functools.partial(forward_kernel, heads), grid=(chunks,),...  96 us
    pallas_call x1, Pallas kernels, mixer_backward(): pl.pallas_call(functools.partial(backward_kernel, heads, chunks), grid=(c...  56.2 us
    psum x1, blocking collectives, on_device(): gains = lax.psum((grad_gain1, grad_gain2, dgain[0]), ('dp', 'heads'))  43.2 us
  transfers between devices with their start and end apart: 9, of which 9 were waited for; matrix products, arithmetic and copies ran while one was open for 7% of the time, Pallas kernels for 0%

profile of v1, /device:TPU:1, one launch (start us, length us, event | category | flops | bytes accessed | tf_op | source)
XLA Modules:
  0.0 1636.2 jit_solution(118062890734715463)
XLA Ops:
  7.2 0.0 all-gather.5.cloned.1.call-start
  7.2 1.7 fusion.10
  8.9 0.6 copy-done.19
  9.5 0.6 copy-done.16
  10.1 2.5 fusion.4
  12.6 0.0 reduce-scatter.5.cloned.1.call-start
  12.7 0.4 copy.28
  13.0 5.3 copy.30
  18.3 0.9 broadcast_in_dim.22
  19.2 8.0 concatenate.7
  27.2 0.6 fusion.16
  27.8 111.6 %all-gather.5.cloned.1.call-done = bf16[2048,2048]{1,0:T(8,128)(2,1)} async-done(((bf16[256,2048]{1,0:T(8,128)(2,1)}), bf16[2048,2048]{1,0:T(8,128)(2,1)}) %all-gather.5.cloned.1.call-update) | async-done | bytes 8388624 | tf_op jit(solution)/shard_map/all_gather | solution.py:388
  139.3 16.3 fusion.17.main_ref
  155.7 96.0 %mixer_forward.1 = (bf16[2048,256]{1,0:T(8,128)(2,1)S(1)}, f32[2048,768]{1,0:T(8,128)}, f32[2048,256]{1,0:T(8,128)S(1)}, f32[2048,256]{1,0:T(8,128)}, f32[2,2048...) custom-call(s32[1]{0:T(128)} %bitcast.2.longer_ref, f32[2048,1152]{1,0:T(8,128)} %fusion.17.main_ref, ...), custom_call_target="tpu_custom_call" | custom-call | tf_op jit(solution)/shard_map/mixer_forward/pallas_call | solution.py:302
  251.6 1.3 copy-done.2
  253.0 1.0 copy-done.4
  254.0 1.0 copy-done.1
  254.9 5.8 convolution_convert_fusion.4
  260.7 0.0 all-gather.7.cloned.1.call-start
  262.1 146.4 %reduce-scatter.5.cloned.1.call-done = bf16[256,2048]{1,0:T(8,128)(2,1)} async-done(((bf16[2048,2048]{1,0:T(8,128)(2,1)}), bf16[256,2048]{1,0:T(8,128)(2,1)}) %reduce-scatter.5.cloned.1.call-update) | async-done | bytes 1048592 | tf_op jit(solution)/shard_map/reduce_scatter | solution.py:392
  408.5 2.1 multiply_reduce_fusion
  410.6 3.7 fusion.6
  414.3 0.0 all-gather.7.cloned.1.call-update
  414.4 0.0 all-gather.9.cloned.1.call-start
  414.4 0.5 all-gather.9.cloned.1.call-update
  415.0 0.0 reduce-scatter.9.cloned.1.call-start
  415.0 123.0 %all-gather.7.cloned.1.call-done = bf16[2048,2048]{1,0:T(8,128)(2,1)} async-done(((bf16[256,2048]{1,0:T(8,128)(2,1)}), bf16[2048,2048]{1,0:T(8,128)(2,1)}) %all-gather.7.cloned.1.call-update) | async-done | bytes 8388624 | tf_op jit(solution)/shard_map/all_gather | solution.py:388
  538.0 18.8 %fusion.18 = f32[2048,1408]{0,1:T(8,128)} fusion(bf16[2048,2048]{1,0:T(8,128)(2,1)} %all-gather.7.cloned.1.call-done, bf16[2048,1408]{0,1:T(8,128)(2,1)} %bitcast.56), kind=kOutput, calls=%fused_computation.53 | convolution fusion | flops 11811160064 | bytes 25690112 | tf_op jit(solution)/shard_map/dot_general | solution.py:384
  556.8 107.1 %all-gather.9.cloned.1.call-done = bf16[2048,2048]{1,0:T(8,128)(2,1)} async-done(((bf16[256,2048]{1,0:T(8,128)(2,1)}), bf16[2048,2048]{1,0:T(8,128)(2,1)}) %all-gather.9.cloned.1.call-update) | async-done | bytes 8388624 | tf_op jit(solution)/shard_map/all_gather | solution.py:388
  663.9 14.6 multiply_convert_fusion.1
  678.5 1.6 copy-done.23
  680.1 0.9 copy-done.25
  681.0 17.9 %convolution_convert_fusion.2 = bf16[2048,2048]{1,0:T(8,128)(2,1)} fusion(bf16[2048,1408]{0,1:T(8,128)(2,1)} %bitcast.57, bf16[2048,704]{0,1:T(8,128)(2,1)S(1)} %get-tuple-element.47, bf16[2048,704]{0,1:T(8,128)(2,1)S(1)} %get-tuple-element.46), kind=kOutput, calls=%fused_computation.3 | convolution fusion | flops 11826888704 | bytes 19922944 | tf_op jit(solution)/shard_map/dot_general | solution.py:384
  699.0 0.0 all-gather.11.cloned.1.call-start
  699.0 147.8 %reduce-scatter.9.cloned.1.call-done = bf16[256,2048]{1,0:T(8,128)(2,1)} async-done(((bf16[2048,2048]{1,0:T(8,128)(2,1)}), bf16[256,2048]{1,0:T(8,128)(2,1)}) %reduce-scatter.9.cloned.1.call-update) | async-done | bytes 1048592 | tf_op jit(solution)/shard_map/reduce_scatter | solution.py:392
  846.8 3.0 fusion.7
  849.9 3.2 multiply_convert_fusion.3
  853.1 0.0 all-reduce.6.cloned.1.call-start
  853.2 11.2 convolution_convert_fusion.5
  864.3 16.2 convolution_convert_fusion
  880.5 96.2 %all-gather.11.cloned.1.call-done = bf16[2048,2048]{1,0:T(8,128)(2,1)} async-done(((bf16[256,2048]{1,0:T(8,128)(2,1)}), bf16[2048,2048]{1,0:T(8,128)(2,1)}) %all-gather.11.cloned.1.call-update) | async-done | bytes 8388624 | tf_op jit(solution)/shard_map/all_gather | solution.py:388
  976.7 6.2 fusion.19.grad_ref
  982.9 56.2 %mixer_backward.1 = (bf16[2048,1152]{1,0:T(8,128)(2,1)}, f32[4,768]{1,0:T(4,128)S(1)}, f32[2,128]{1,0:T(2,128)S(1)}, f32[1,128]{1,0:T(1,128)S(1)}) custom-call(s32[1]{0:T(128)} %bitcast.2.longer_ref, f32[2048,256]{1,0:T(8,128)S(1)} %fusion.19.grad_ref, f32[2048,1152]{1,0:T(8,128)} %fusion.17.main_ref, f32[2048,768]{1,0:T(8,128)} %get-tuple-element.23.conv_out_ref, ...), custom_call_target="tpu_custom_call" | custom-call | tf_op jit(solution)/shard_map/mixer_backward/pallas_call | solution.py:342
  1039.1 14.5 fusion.20
  1053.6 3.7 copy-done.12
  1057.3 2.6 slice.39
  1059.9 7.6 copy.29
  1067.5 7.0 convolution_convert_fusion.6
  1074.6 0.0 reduce-scatter.11.cloned.1.call-start
  1074.7 16.5 %convolution_convert_fusion.1 = bf16[2048,2048]{1,0:T(8,128)(2,1)} fusion(bf16[2048,1152]{1,0:T(8,128)(2,1)} %get-tuple-element.28, bf16[2048,1152]{1,0:T(8,128)(2,1)} %concatenate.7), kind=kOutput, calls=%fused_computation.2 | convolution fusion | flops 9667870720 | bytes 17825792 | tf_op jit(solution)/shard_map/dot_general | solution.py:384
  1091.2 0.0 reduce-scatter.7.cloned.1.call-start
  1091.2 10.9 convolution_convert_fusion.3
  1102.2 0.7 slice-done.2
  1102.9 13.9 all-reduce.2
  1116.8 200.0 %all-reduce.6.cloned.1.call-done = (bf16[2048,4,256]{2,1,0:T(4,128)(2,1)}, bf16[256,2048]{1,0:T(8,128)(2,1)}, bf16[2048,2,704]{0,2,1:T(8,128)(2,1)}, bf16[704,2048]{1,0:T(8,128)(2,1)}) async-done(((bf16[2048,4,256]{2,1,0:T(4,128)(2,1)}, bf16[256,2048]{1,0:T(8,128)(2,1)}, bf16[2048,2,704]{0,2,1:T(8,128)(2,1)}, bf16[704,2048]{1,0:T(8,128)(2,1)}), (bf16[2048,4,256]{2,1,0:T(4,128)(2,1)}, ...) | async-done | bytes 13893648 | tf_op jit(solution)/shard_map/psum | solution.py:398
  1316.8 2.9 convert_element_type.99
  1319.7 6.4 reshape.106
  1326.2 3.4 convert_element_type.104
  1329.7 6.0 convert_element_type.102
  1335.7 134.3 %reduce-scatter.11.cloned.1.call-done = bf16[256,2048]{1,0:T(8,128)(2,1)} async-done(((bf16[2048,2048]{1,0:T(8,128)(2,1)}), bf16[256,2048]{1,0:T(8,128)(2,1)}) %reduce-scatter.11.cloned.1.call-update) | async-done | bytes 1048592 | tf_op jit(solution)/shard_map/reduce_scatter | solution.py:392
  1470.0 2.6 fusion.8
  1472.6 43.2 %all-reduce.1 = (f32[2048]{0:T(1024)}, f32[128]{0:T(128)}, f32[2048]{0:T(1024)}) all-reduce(f32[2048]{0:T(1024)S(1)} %get-tuple-element.34, f32[128]{0:T(128)S(1)} %bitcast.49, f32[2048]{0:T(1024)S(1)} %get-tuple-element.32), channel_id=1, replica_groups=mesh['dp'=4,'heads'=8] {'dp','heads'}, use_global_device_ids=true, to_apply=%region_9.10 | all-reduce | flops 4224 | bytes 33792 | tf_op jit(solution)/shard_map/psum | solution.py:484
  1515.8 107.2 %reduce-scatter.7.cloned.1.call-done = bf16[256,2048]{1,0:T(8,128)(2,1)} async-done(((bf16[2048,2048]{1,0:T(8,128)(2,1)}), bf16[256,2048]{1,0:T(8,128)(2,1)}) %reduce-scatter.7.cloned.1.call-update) | async-done | bytes 1048592 | tf_op jit(solution)/shard_map/reduce_scatter | solution.py:392
  1623.0 6.2 fusion.9
  (67 shorter events, 0.3 us)
Async XLA Ops:
  7.2 656.7 %copy-start = (bf16[704,2048]{1,0:T(8,128)(2,1)S(1)}, bf16[704,2048]{1,0:T(8,128)(2,1)}, u32[]{:S(2)}) copy-start(bf16[704,2048]{1,0:T(8,128)(2,1)} %param.24) | copy-start | bytes 8650756
  7.2 5.4 copy-start.18
  7.2 132.1 %all-gather.5.cloned.1.call-start = ((), (), s32[]{:S(2)}) async-start(), calls=%async_computation.4 | async-start | bytes 9437184 | tf_op jit(solution)/shard_map/all_gather | solution.py:388
  8.9 0.6 copy-start.19
  9.5 0.6 copy-start.16
  12.6 395.9 %reduce-scatter.5.cloned.1.call-start = ((), (), s32[]{:S(2)}) async-start(), calls=%async_computation.5 | async-start | bytes 9437184 | tf_op jit(solution)/shard_map/reduce_scatter | solution.py:392
  13.0 5.3 copy-start.22
  19.2 8.0 copy-start.21
  27.8 127.9 %copy-start.6 = (f32[3,4,256]{2,1,0:T(4,128)S(1)}, f32[3,4,256]{2,1,0:T(4,128)}, u32[]{:S(2)}) copy-start(f32[3,4,256]{2,1,0:T(4,128)} %param.17) | copy-start | bytes 36868
  27.8 127.9 %copy-start.7 = (f32[128]{0:T(128)S(1)}, f32[128]{0:T(128)}, u32[]{:S(2)}) copy-start(f32[128]{0:T(128)} %param.20) | copy-start | bytes 1540
  155.7 99.3 %copy-start.13 = (bf16[256,2048]{1,0:T(8,128)(2,1)S(1)}, bf16[256,2048]{1,0:T(8,128)(2,1)}, u32[]{:S(2)}) copy-start(bf16[256,2048]{1,0:T(8,128)(2,1)} %param.21) | copy-start | bytes 3145732
  251.6 1.3 copy-start.2
  253.0 1.0 copy-start.4
  254.0 1.0 copy-start.1
  260.7 149.9 %copy-start.14 = (f32[2048]{0:T(1024)S(1)}, f32[2048]{0:T(1024)}, u32[]{:S(2)}) copy-start(f32[2048]{0:T(1024)} %param.22) | copy-start | bytes 24580
  260.7 277.3 %all-gather.7.cloned.1.call-start = ((), (), s32[]{:S(2)}) async-start(), calls=%async_computation.6 | async-start | bytes 9437184 | tf_op jit(solution)/shard_map/all_gather | solution.py:388
  414.4 249.5 %all-gather.9.cloned.1.call-start = ((), (), s32[]{:S(2)}) async-start(), calls=%async_computation.8 | async-start | bytes 9437184 | tf_op jit(solution)/shard_map/all_gather | solution.py:388
  415.0 431.9 %reduce-scatter.9.cloned.1.call-start = ((), (), s32[]{:S(2)}) async-start(), calls=%async_computation.9 | async-start | bytes 9437184 | tf_op jit(solution)/shard_map/reduce_scatter | solution.py:392
  678.5 1.6 copy-start.23
  678.5 2.5 copy-start.25
  699.0 277.7 %all-gather.11.cloned.1.call-start = ((), (), s32[]{:S(2)}) async-start(), calls=%async_computation.10 | async-start | bytes 9437184 | tf_op jit(solution)/shard_map/all_gather | solution.py:388
  846.8 3.0 copy-start.8
  846.8 3.0 copy-start.9
  846.8 3.0 copy-start.10
  853.1 463.7 %all-reduce.6.cloned.1.call-start = ((), (), s32[]{:S(2)}) async-start(), calls=%async_computation.12 | async-start | bytes 27787264 | tf_op jit(solution)/shard_map/psum | solution.py:398
  853.1 11.2 copy-start.24
  853.1 11.2 copy-start.26
  976.7 6.2 copy-start.3
  976.7 6.2 copy-start.5
  1053.6 3.7 copy-start.12
  1074.6 395.4 %reduce-scatter.11.cloned.1.call-start = ((), (), s32[]{:S(2)}) async-start(), calls=%async_computation.11 | async-start | bytes 9437184 | tf_op jit(solution)/shard_map/reduce_scatter | solution.py:392
  1091.2 531.8 %reduce-scatter.7.cloned.1.call-start = ((), (), s32[]{:S(2)}) async-start(), calls=%async_computation.7 | async-start | bytes 9437184 | tf_op jit(solution)/shard_map/reduce_scatter | solution.py:392
  1102.1 0.8 slice-start.2
  1316.8 12.8 slice-start
  1319.7 6.4 copy-start.11
  1319.7 9.9 slice-start.1
  1329.6 140.4 %copy-start.15 = (f32[2048]{0:T(1024)S(1)}, f32[2048]{0:T(1024)}, u32[]{:S(2)}) copy-start(f32[2048]{0:T(1024)} %param.15) | copy-start | bytes 24580
  1329.6 140.4 %copy-start.17 = (f32[256]{0:T(256)S(1)}, f32[256]{0:T(256)}, u32[]{:S(2)}) copy-start(f32[256]{0:T(256)} %copy-done.16) | copy-start | bytes 3076
  1329.6 186.1 %copy-start.20 = (f32[256]{0:T(256)S(1)}, f32[256]{0:T(256)}, u32[]{:S(2)}) copy-start(f32[256]{0:T(256)} %copy-done.19) | copy-start | bytes 3076
Sparse Core Ops, SparseCore 0:
  12.7 126.5 all-gather.4
  260.8 147.6 reduce-scatter.4
  414.5 123.4 all-gather.6
  540.8 123.1 all-gather.8
  699.1 147.6 reduce-scatter.8
  853.2 123.4 all-gather.10
  1074.7 242.0 all-reduce.5
  1320.4 149.5 reduce-scatter.10
  1474.1 148.8 reduce-scatter.6

commit v2 on v1

--- a/solution.py
+++ b/solution.py
@@ -376,8 +376,491 @@
     )(longer, grad, main, *saved, conv, params, gain)
 
 
-def rms_rows(values, gain):
-    return values * lax.rsqrt(jnp.mean(values * values, axis=-1, keepdims=True) + EPS) * gain
+MESH = pl.DeviceIdType.MESH
+PIECES = 4
+
+
+class Group:
+    def __init__(self, count, deep):
+        self.nz = 4 if count % 4 == 0 else 1
+        self.nx = count // self.nz
+        self.deep = min(deep, self.nz)
+        self.size = self.deep * self.nx
+        me = lax.axis_index("heads")
+        self.z, self.x = me // self.nx, me % self.nx
+        self.base = (self.z // self.deep) * self.deep
+        self.own = (self.z - self.base) * self.nx + self.x
+
+    def along_z(self, k):
+        return (self.z - self.base + k) % self.deep
+
+    def along_x(self, j):
+        return (self.x + j) % self.nx
+
+    def slot(self, k, j):
+        return self.along_z(k) * self.nx + self.along_x(j)
+
+    def device(self, k, j):
+        return {"heads": self.base * self.nx + self.slot(k, j)}
+
+
+def meet(count, wide):
+    me = lax.axis_index("heads")
+    replica = lax.axis_index("dp")
+    replicas = lax.axis_size("dp")
+    barrier = pltpu.get_barrier_semaphore()
+
+    def greet(k, _):
+        pl.semaphore_signal(
+            barrier, inc=1, device_id={"heads": (me + k) % count}, device_id_type=MESH
+        )
+        return 0
+
+    def greet_replica(k, _):
+        pl.semaphore_signal(
+            barrier, inc=1, device_id={"dp": (replica + k) % replicas}, device_id_type=MESH
+        )
+        return 0
+
+    lax.fori_loop(1, count, greet, 0)
+    if wide:
+        lax.fori_loop(1, replicas, greet_replica, 0)
+    pl.semaphore_wait(barrier, count - 1 + (replicas - 1 if wide else 0))
+
+
+def arrived(ref, sem):
+    pltpu.make_async_copy(ref, ref, sem).wait()
+
+
+class Gather:
+    def __init__(self, group, full, send_sems, recv_sems):
+        self.group, self.full = group, full
+        self.part = full.shape[1] // PIECES
+        self.send_sems, self.recv_sems = send_sems, recv_sems
+        self.sent = []
+
+    @staticmethod
+    def scratch(deep, nx, rows, cols):
+        size = deep * nx
+        return [
+            pltpu.VMEM((size, rows, cols), BF16),
+            pltpu.SemaphoreType.DMA((PIECES, deep + deep * nx)),
+            pltpu.SemaphoreType.DMA((PIECES, size)),
+        ]
+
+    def rows(self, piece):
+        return pl.ds(piece * self.part, self.part)
+
+    def send(self, slot, piece, which, target):
+        place = self.full.at[slot, self.rows(piece)]
+        copy = pltpu.make_async_remote_copy(
+            place, place, self.send_sems.at[piece, which], self.recv_sems.at[piece, slot],
+            device_id=target, device_id_type=MESH,
+        )
+        copy.start()
+        self.sent.append(copy)
+
+    def receive(self, slot, piece):
+        arrived(self.full.at[slot, self.rows(piece)], self.recv_sems.at[piece, slot])
+
+    def start(self, piece):
+        group = self.group
+        for k in range(1, group.deep):
+            self.send(group.own, piece, k, group.device(k, 0))
+        for j in range(1, group.nx):
+            self.send(group.own, piece, group.deep + j, group.device(0, j))
+
+    def relay(self, piece):
+        group = self.group
+        for k in range(1, group.deep):
+            self.receive(group.slot(k, 0), piece)
+            for j in range(1, group.nx):
+                self.send(
+                    group.slot(k, 0), piece, group.deep + k * group.nx + j, group.device(0, j)
+                )
+
+    def finish(self, piece):
+        group = self.group
+        for j in range(1, group.nx):
+            for k in range(group.deep):
+                self.receive(group.slot(k, j), piece)
+
+    def drain(self):
+        for copy in self.sent:
+            copy.wait_send()
+
+
+class Scatter:
+    def __init__(self, group, parts, over_x, sums, over_z, sems):
+        self.group, self.parts = group, parts
+        self.over_x, self.sums, self.over_z = over_x, sums, over_z
+        self.part = parts.shape[1] // PIECES
+        self.x_send, self.x_recv, self.z_send, self.z_recv = sems
+        self.sent = []
+
+    @staticmethod
+    def scratch(deep, nx, rows, cols):
+        return [
+            pltpu.VMEM((deep * nx, rows, cols), BF16),
+            pltpu.VMEM((deep, max(nx - 1, 1), rows, cols), BF16),
+            pltpu.VMEM((deep, rows, cols), BF16),
+            pltpu.VMEM((max(deep - 1, 1), rows, cols), BF16),
+            pltpu.SemaphoreType.DMA((PIECES, deep, nx)),
+            pltpu.SemaphoreType.DMA((PIECES, deep, nx)),
+            pltpu.SemaphoreType.DMA((PIECES, deep)),
+            pltpu.SemaphoreType.DMA((PIECES, deep)),
+        ]
+
+    def rows(self, piece):
+        return pl.ds(piece * self.part, self.part)
+
+    def copy(self, source, target, send_sem, recv_sem, device):
+        copy = pltpu.make_async_remote_copy(
+            source, target, send_sem, recv_sem, device_id=device, device_id_type=MESH
+        )
+        copy.start()
+        self.sent.append(copy)
+
+    def start(self, piece):
+        group, rows = self.group, self.rows(piece)
+        for k in range(group.deep):
+            for j in range(1, group.nx):
+                self.copy(
+                    self.parts.at[group.slot(k + 1, j), rows],
+                    self.over_x.at[k, j - 1, rows],
+                    self.x_send.at[piece, k, j],
+                    self.x_recv.at[piece, k, j],
+                    group.device(0, j),
+                )
+
+    def relay(self, piece):
+        group, rows = self.group, self.rows(piece)
+        for k in range(group.deep):
+            total = self.parts[group.slot(k + 1, 0), rows].astype(F32)
+            for j in range(1, group.nx):
+                arrived(self.over_x.at[k, j - 1, rows], self.x_recv.at[piece, k, j])
+                total = total + self.over_x[k, j - 1, rows].astype(F32)
+            self.sums[k, rows] = total.astype(BF16)
+            if k < group.deep - 1:
+                self.copy(
+                    self.sums.at[k, rows],
+                    self.over_z.at[k, rows],
+                    self.z_send.at[piece, k],
+                    self.z_recv.at[piece, k],
+                    group.device(k + 1, 0),
+                )
+
+    def finish(self, piece):
+        group, rows = self.group, self.rows(piece)
+        total = self.sums[group.deep - 1, rows].astype(F32)
+        for k in range(group.deep - 1):
+            arrived(self.over_z.at[k, rows], self.z_recv.at[piece, k])
+            total = total + self.over_z[k, rows].astype(F32)
+        return total
+
+    def drain(self):
+        for copy in self.sent:
+            copy.wait_send()
+
+
+def inverse_rms(rows):
+    return lax.rsqrt(jnp.mean(rows * rows, axis=-1, keepdims=True) + EPS)
+
+
+def wide_dot(left, right_ref, dims, tile, store):
+    total = right_ref.shape[0] if dims is NT else right_ref.shape[1]
+    for first in range(0, total, tile):
+        cols = slice(first, min(first + tile, total))
+        right = right_ref[cols, :] if dims is NT else right_ref[:, cols]
+        store(cols, lax.dot_general(left, right, (dims, ((), ())), preferred_element_type=F32))
+
+
+def project_kernel(
+    count, rows_ref, gain_ref, weight_ref, full_out, projected_out,
+    full, gather_send, gather_recv, staged, full_sems, staged_sems,
+):
+    group = Group(count, 4)
+    gather = Gather(group, full, gather_send, gather_recv)
+    part = gather.part
+    meet(count, False)
+    for piece in range(PIECES):
+        rows = rows_ref[gather.rows(piece)].astype(F32)
+        full[group.own, gather.rows(piece)] = (
+            rows * inverse_rms(rows) * gain_ref[...]
+        ).astype(BF16)
+        gather.start(piece)
+    outs = []
+    for piece in range(PIECES):
+        gather.relay(piece)
+        gather.finish(piece)
+        rows = gather.rows(piece)
+        copy = pltpu.make_async_copy(full.at[:, rows], full_out.at[:, rows], full_sems.at[piece])
+        copy.start()
+        outs.append(copy)
+        left = full[:, rows].reshape(count * part, full.shape[2])
+
+        def store(cols, value, rows=rows):
+            staged[:, rows, cols] = value.reshape(count, part, value.shape[1])
+
+        wide_dot(left, weight_ref, NN, 256, store)
+        copy = pltpu.make_async_copy(
+            staged.at[:, rows], projected_out.at[:, rows], staged_sems.at[piece]
+        )
+        copy.start()
+        outs.append(copy)
+    gather.drain()
+    for copy in outs:
+        copy.wait()
+
+
+VMEM_SPEC = pl.BlockSpec(memory_space=pltpu.VMEM)
+ANY_SPEC = pl.BlockSpec(memory_space=pl.ANY)
+
+
+def grid_sizes(count):
+    nz = 4 if count % 4 == 0 else 1
+    return nz, count // nz
+
+
+def linked(collective):
+    return pltpu.CompilerParams(
+        collective_id=collective, has_side_effects=True, vmem_limit_bytes=60 * 2**20
+    )
+
+
+def project(rows, gain, weight, count):
+    own, features = rows.shape
+    cols = weight.shape[1]
+    nz, nx = grid_sizes(count)
+    return pl.pallas_call(
+        functools.partial(project_kernel, count),
+        out_shape=[
+            jax.ShapeDtypeStruct((count, own, features), BF16),
+            jax.ShapeDtypeStruct((count, own, cols), F32),
+        ],
+        in_specs=[VMEM_SPEC] * 3,
+        out_specs=[ANY_SPEC] * 2,
+        scratch_shapes=[
+            *Gather.scratch(nz, nx, own, features),
+            pltpu.VMEM((count, own, cols), F32),
+            pltpu.SemaphoreType.DMA((PIECES,)),
+            pltpu.SemaphoreType.DMA((PIECES,)),
+        ],
+        compiler_params=linked(0),
+        name="project",
+    )(rows, gain, weight)
+
+
+def branch_kernel(
+    count, deep, mixed_ref, weight_ref, input_ref, live_ref, gain_ref, middle_out, full_out,
+    parts, over_x, sums, over_z, x_send, x_recv, z_send, z_recv,
+    full, gather_send, gather_recv, out_sems,
+):
+    scatter = Scatter(
+        Group(count, 4), parts, over_x, sums, over_z, (x_send, x_recv, z_send, z_recv)
+    )
+    near = Group(count, deep)
+    gather = Gather(near, full, gather_send, gather_recv)
+    part = gather.part
+    meet(count, False)
+    for piece in range(PIECES):
+        rows = gather.rows(piece)
+        left = mixed_ref[:, rows].reshape(count * part, mixed_ref.shape[2])
+
+        def store(cols, value, rows=rows):
+            parts[:, rows, cols] = value.astype(BF16).reshape(count, part, value.shape[1])
+
+        wide_dot(left, weight_ref, NN, 512, store)
+        scatter.start(piece)
+    for piece in range(PIECES):
+        scatter.relay(piece)
+    outs = []
+
+    def pass_on(piece):
+        gather.relay(piece)
+
+    for piece in range(PIECES):
+        rows = gather.rows(piece)
+        middle = input_ref[rows].astype(F32) + live_ref[rows] * scatter.finish(piece)
+        middle_out[rows] = middle
+        full[near.own, rows] = (middle * inverse_rms(middle) * gain_ref[...]).astype(BF16)
+        gather.start(piece)
+        if piece > 0:
+            pass_on(piece - 1)
+    pass_on(PIECES - 1)
+    for piece in range(PIECES):
+        gather.finish(piece)
+        rows = gather.rows(piece)
+        copy = pltpu.make_async_copy(full.at[:, rows], full_out.at[:, rows], out_sems.at[piece])
+        copy.start()
+        outs.append(copy)
+    scatter.drain()
+    gather.drain()
+    for copy in outs:
+        copy.wait()
+
+
+def branch_and_norm(mixed, weight, rows, live, gain, count, deep):
+    own, features = rows.shape
+    nz, nx = grid_sizes(count)
+    deep = min(deep, nz)
+    return pl.pallas_call(
+        functools.partial(branch_kernel, count, deep),
+        out_shape=[
+            jax.ShapeDtypeStruct((own, features), F32),
+            jax.ShapeDtypeStruct((deep * nx, own, features), BF16),
+        ],
+        in_specs=[VMEM_SPEC] * 5,
+        out_specs=[VMEM_SPEC, ANY_SPEC],
+        scratch_shapes=[
+            *Scatter.scratch(nz, nx, own, features),
+            *Gather.scratch(deep, nx, own, features),
+            pltpu.SemaphoreType.DMA((PIECES,)),
+        ],
+        compiler_params=linked(1),
+        name="branch_and_norm",
+    )(mixed.reshape(count, own, -1), weight, rows, live, gain)
+
+
+def feed_back_kernel(
+    count, deep, grad_ref, weight_ref, top_ref, middle_ref, live_ref, gain_ref, out_weight_ref,
+    dmiddle_out, dgain_out, full_out, dmixed_out,
+    parts, over_x, sums, over_z, x_send, x_recv, z_send, z_recv,
+    full, gather_send, gather_recv, out_sems,
+):
+    near = Group(count, deep)
+    scatter = Scatter(near, parts, over_x, sums, over_z, (x_send, x_recv, z_send, z_recv))
+    group = Group(count, 4)
+    gather = Gather(group, full, gather_send, gather_recv)
+    part = gather.part
+    meet(count, False)
+    for piece in range(PIECES):
+        rows = gather.rows(piece)
+        left = grad_ref[:, rows].reshape(near.size * part, grad_ref.shape[2])
+
+        def store(cols, value, rows=rows):
+            parts[:, rows, cols] = value.astype(BF16).reshape(near.size, part, value.shape[1])
+
+        wide_dot(left, weight_ref, NT, 256, store)
+        scatter.start(piece)
+    for piece in range(PIECES):
+        scatter.relay(piece)
+    dgain = jnp.zeros(dgain_out.shape, F32)
+    gain = gain_ref[...]
+    for piece in range(PIECES):
+        rows = gather.rows(piece)
+        dnormed = scatter.finish(piece)
+        middle = middle_ref[rows]
+        scale = inverse_rms(middle)
+        normed = middle * scale
+        dgain = dgain + jnp.sum(dnormed * normed, axis=0, keepdims=True)
+        scaled = dnormed * gain
+        dmiddle = top_ref[rows].astype(F32) + scale * (
+            scaled - normed * jnp.mean(scaled * normed, axis=-1, keepdims=True)
+        )
+        dmiddle_out[rows] = dmiddle
+        full[group.own, rows] = (live_ref[rows] * dmiddle).astype(BF16)
+        gather.start(piece)
+        if piece > 0:
+            gather.relay(piece - 1)
+    dgain_out[...] = dgain
+    gather.relay(PIECES - 1)
+    outs = []
+    for piece in range(PIECES):
+        gather.finish(piece)
+        rows = gather.rows(piece)
+        copy = pltpu.make_async_copy(full.at[:, rows], full_out.at[:, rows], out_sems.at[piece])
+        copy.start()
+        outs.append(copy)
+        left = full[:, rows].reshape(count * part, full.shape[2])
+
+        def store(cols, value, rows=rows):
+            dmixed_out[:, rows, cols] = value.reshape(count, part, value.shape[1])
+
+        wide_dot(left, out_weight_ref, NT, 256, store)
+    scatter.drain()
+    gather.drain()
+    for copy in outs:
+        copy.wait()
+
+
+def feed_back(grad, weight, top, middle, live, gain, out_weight, count, deep):
+    own, features = middle.shape
+    nz, nx = grid_sizes(count)
+    deep = min(deep, nz)
+    width = out_weight.shape[0]
+    return pl.pallas_call(
+        functools.partial(feed_back_kernel, count, deep),
+        out_shape=[
+            jax.ShapeDtypeStruct((own, features), F32),
+            jax.ShapeDtypeStruct((1, features), F32),
+            jax.ShapeDtypeStruct((count, own, features), BF16),
+            jax.ShapeDtypeStruct((count, own, width), F32),
+        ],
+        in_specs=[VMEM_SPEC] * 7,
+        out_specs=[VMEM_SPEC, VMEM_SPEC, ANY_SPEC, VMEM_SPEC],
+        scratch_shapes=[
+            *Scatter.scratch(deep, nx, own, features),
+            *Gather.scratch(nz, nx, own, features),
+            pltpu.SemaphoreType.DMA((PIECES,)),
+        ],
+        compiler_params=linked(2),
+        name="feed_back",
+    )(grad.reshape(deep * nx, own, -1), weight, top, middle, live, gain, out_weight)
+
+
+def input_back_kernel(
+    count, grad_ref, weight_ref, later_ref, input_ref, gain_ref, grad_out, dgain_out,
+    parts, over_x, sums, over_z, x_send, x_recv, z_send, z_recv,
+):
+    scatter = Scatter(
+        Group(count, 4), parts, over_x, sums, over_z, (x_send, x_recv, z_send, z_recv)
+    )
+    part = scatter.part
+    meet(count, False)
+    for piece in range(PIECES):
+        rows = scatter.rows(piece)
+        left = grad_ref[:, rows].reshape(count * part, grad_ref.shape[2])
+
+        def store(cols, value, rows=rows):
+            parts[:, rows, cols] = value.astype(BF16).reshape(count, part, value.shape[1])
+
+        wide_dot(left, weight_ref, NT, 256, store)
+        scatter.start(piece)
+    for piece in range(PIECES):
+        scatter.relay(piece)
+    dgain = jnp.zeros(dgain_out.shape, F32)
+    gain = gain_ref[...]
+    for piece in range(PIECES):
+        rows = scatter.rows(piece)
+        dnormed = scatter.finish(piece)
+        values = input_ref[rows].astype(F32)
+        scale = inverse_rms(values)
+        normed = values * scale
+        dgain = dgain + jnp.sum(dnormed * normed, axis=0, keepdims=True)
+        scaled = dnormed * gain
+        grad_out[rows] = later_ref[rows] + scale * (
+            scaled - normed * jnp.mean(scaled * normed, axis=-1, keepdims=True)
+        )
+    dgain_out[...] = dgain
+    scatter.drain()
+
+
+def input_back(grad, weight, later, rows, gain, count):
+    own, features = rows.shape
+    nz, nx = grid_sizes(count)
+    return pl.pallas_call(
+        functools.partial(input_back_kernel, count),
+        out_shape=[
+            jax.ShapeDtypeStruct((own, features), F32),
+            jax.ShapeDtypeStruct((1, features), F32),
+        ],
+        in_specs=[VMEM_SPEC] * 5,
+        out_specs=[VMEM_SPEC, VMEM_SPEC],
+        scratch_shapes=Scatter.scratch(nz, nx, own, features),
+        compiler_params=linked(3),
+        name="input_back",
+    )(grad.reshape(count, own, -1), weight, later, rows, gain)
 
 
 def matmul(left, right, dims):
@@ -414,7 +897,8 @@
     cotangent,
 ):
     own_rows, features = block_in.shape
-    all_rows = own_rows * lax.axis_size("heads")
+    count = lax.axis_size("heads")
+    all_rows = own_rows * count
     width = conv_weight.shape[2]
     heads = gate_params.shape[1]
     longer = seq_counts[0, 1:2]
@@ -422,9 +906,8 @@
     row_index = first_row + jnp.arange(own_rows, dtype=jnp.int32)
     live_own = jnp.where(longer[0] > 0, True, row_index < seq_counts[0, 0] * SEQ_SHORT)
     live_own = live_own.astype(F32)[:, None]
-    input_rows = block_in.astype(F32)
-    normed1, pull_norm1 = jax.vjp(rms_rows, input_rows, norm1_gain)
-    full_normed1 = gather_rows(normed1.astype(BF16))
+    grad_top = cotangent.astype(F32)
+    grad_feed = gather_rows((live_own * grad_top).astype(BF16))
     weight = jnp.concatenate(
         [
             w_qkvg.reshape(features, 4 * width),
@@ -433,17 +916,18 @@
         ],
         axis=1,
     )
-    projected = matmul(full_normed1, weight, NN)
+    full_normed1, projected = project(block_in, norm1_gain[None], weight, count)
+    full_normed1 = full_normed1.reshape(all_rows, features)
+    projected = projected.reshape(all_rows, -1)
     taps = jnp.transpose(conv_weight, (1, 0, 2)).reshape(4, 3 * width)
     params = jnp.pad(gate_params, ((0, 0), (0, 128 - heads)))
     gain_row = out_gain[None]
     mixed, *saved = mixer_forward(longer, projected, taps, params, gain_row)
-    branch = scatter_rows(matmul(mixed, w_out, NN))
-    grad_top = cotangent.astype(F32)
-    grad_feed = gather_rows((live_own * grad_top).astype(BF16))
-    middle = input_rows + live_own * branch
-    normed2, pull_norm2 = jax.vjp(rms_rows, middle, norm2_gain)
-    full_normed2 = gather_rows(normed2.astype(BF16))
+    mixed, grad_feed = lax.optimization_barrier((mixed, grad_feed))
+    middle, full_normed2 = branch_and_norm(
+        mixed, w_out, block_in, live_own, norm2_gain[None], count, 4
+    )
+    full_normed2 = full_normed2.reshape(all_rows, features)
     feed_weight = w_gate_up.reshape(features, -1)
     hidden_cols = w_down.shape[0]
     gate_up = matmul(full_normed2, feed_weight, NN)
@@ -455,33 +939,40 @@
     grad_gate = grad_hidden * up_pre * sigmoid_gate * (1.0 + gate_pre * (1.0 - sigmoid_gate))
     grad_up = grad_hidden * gate_pre * sigmoid_gate
     grad_gate_up = jnp.concatenate([grad_gate, grad_up], 1).astype(BF16)
-    grad_normed2 = scatter_rows(matmul(grad_gate_up, feed_weight, NT))
+    grad_middle, grad_gain2, grad_mix, grad_mixed = feed_back(
+        grad_gate_up,
+        feed_weight,
+        cotangent,
+        middle,
+        live_own,
+        norm2_gain[None],
+        w_out,
+        count,
+        4,
+    )
+    grad_mix = grad_mix.reshape(all_rows, features)
     feed = scatter_rows(matmul(hidden, w_down, NN))
     layer_out = (middle + live_own * feed).astype(BF16)
-    grad_middle_part, grad_gain2 = pull_norm2(grad_normed2)
-    grad_middle = grad_top + grad_middle_part
-    grad_mix = gather_rows((live_own * grad_middle).astype(BF16))
     grad_feed_weight = matmul(full_normed2, grad_gate_up, TN)
     grad_down = matmul(hidden, grad_feed, TN)
-    grad_mixed = matmul(grad_mix, w_out, NT)
     grad_wout = matmul(mixed, grad_mix, TN)
-    dprojected, dtaps, dparams, dgain = mixer_backward(
-        longer, grad_mixed, projected, saved, taps, params, gain_row
-    )
-    grad_normed1 = scatter_rows(matmul(dprojected, weight, NT))
-    grad_weight = matmul(full_normed1, dprojected, TN)
-    grad_input_part, grad_gain1 = pull_norm1(grad_normed1)
-    grad_in = grad_middle + grad_input_part
-    grad_conv = jnp.transpose(dtaps.reshape(4, 3, width), (1, 0, 2))
     summed_ff = (
         sum_replicas(grad_feed_weight.reshape(w_gate_up.shape)),
         sum_replicas(grad_down),
-    )
-    summed_out = sum_replicas(grad_wout)
+        sum_replicas(grad_wout),
+    )
+    dprojected, dtaps, dparams, dgain = mixer_backward(
+        longer, grad_mixed.reshape(all_rows, width), projected, saved, taps, params, gain_row
+    )
+    grad_weight = matmul(full_normed1, dprojected, TN)
+    grad_in, grad_gain1 = input_back(
+        dprojected, weight, grad_middle, block_in, norm1_gain[None], count
+    )
+    grad_conv = jnp.transpose(dtaps.reshape(4, 3, width), (1, 0, 2))
     small = lax.psum(
         (grad_conv, grad_weight[:, 4 * width : 4 * width + 2 * heads], dparams[:, :heads]), "dp"
     )
-    gains = lax.psum((grad_gain1, grad_gain2, dgain[0]), ("dp", "heads"))
+    gains = lax.psum((grad_gain1[0], grad_gain2[0], dgain[0]), ("dp", "heads"))
     return (
         layer_out,
         grad_in,
@@ -491,7 +982,7 @@
         small[1].reshape(w_gates.shape),
         small[2],
         gains[2],
-        summed_out,
+        summed_ff[2],
         gains[1],
         summed_ff[0],
         summed_ff[1],

time: 1650 us -> 1390 us (0.84)
  waiting for transfers between devices: 1170 us -> 200 us
  Pallas kernels: 152 us -> 920 us
  matrix products: 156 us -> 93.3 us
  local copies, waits for them, and re-layouts: 36.9 us -> 55.9 us
    pallas_call x0 -> x4, Pallas kernels: none -> 768 us  [the longest x1 232 us: feed_back(): pl.pallas_call(functools.partial(feed_back_kernel, count, deep), out_shap...]
    all_gather x4 -> x1, waiting for transfers between devices: 438 us -> 0.01 us  [gather_rows(): return lax.all_gather(values, 'heads', axis=0, tiled=True)]
    reduce_scatter x4 -> x1, waiting for transfers between devices: 536 us -> 135 us  [scatter_rows(): lax.psum_scatter(values.astype(BF16), 'heads', scatter_dimension=0, tiled...]
    psum x1, waiting for transfers between devices: 200 us -> 64.6 us  [sum_replicas(): return lax.psum(values.astype(BF16), 'dp').astype(F32)]
    dot_general x12 -> x7, matrix products: 156 us -> 93.3 us  [matmul(): lax.dot_general(left, right, (dims, ((), ())), preferred_element_type=F32)]
  transfers between devices with their start and end apart: 9 -> 3, of which waited for: 9 -> 2; matrix products, arithmetic and copies ran while one was open for 7% -> 4% of each run, Pallas kernels for 0% -> 29%
where the time goes in v2:
time: 1390 us; the launch traced here: 1380 us
  Pallas kernels  920 us (66%)
  waiting for transfers between devices  200 us (14%)
  matrix products  93.3 us (7%)
  blocking collectives  58.9 us (4%)
  local copies, waits for them, and re-layouts  55.9 us (4%)
  other arithmetic  37.6 us (3%)
  between operations  15.7 us (1%)
    pallas_call x1, Pallas kernels, feed_back(): pl.pallas_call(functools.partial(feed_back_kernel, count, deep), out_shap...  232 us
    pallas_call x1, Pallas kernels, branch_and_norm(): pl.pallas_call(functools.partial(branch_kernel, count, deep), out_shape=[...  228 us
    pallas_call x1, Pallas kernels, project(): pl.pallas_call(functools.partial(project_kernel, count), out_shape=[jax.S...  189 us
    reduce_scatter x1, waiting for transfers between devices, scatter_rows(): lax.psum_scatter(values.astype(BF16), 'heads', scatter_dimension=0, tiled...  135 us
    pallas_call x1, Pallas kernels, input_back(): pl.pallas_call(functools.partial(input_back_kernel, count), out_shape=[ja...  119 us
    pallas_call x1, Pallas kernels, mixer_forward(): pl.pallas_call(functools.partial(forward_kernel, heads), grid=(chunks,),...  96 us
    dot_general x7, matrix products, matmul(): lax.dot_general(left, right, (dims, ((), ())), preferred_element_type=F32)  93.3 us
    psum x1, waiting for transfers between devices, sum_replicas(): return lax.psum(values.astype(BF16), 'dp').astype(F32)  64.6 us
  transfers between devices with their start and end apart: 3, of which 2 were waited for; matrix products, arithmetic and copies ran while one was open for 4% of the time, Pallas kernels for 29%

profile of v2, /device:TPU:1, one launch (start us, length us, event | category | flops | bytes accessed | tf_op | source)
XLA Modules:
  0.0 1381.3 jit_solution(6545341639908196795)
XLA Ops:
  7.2 0.0 copy-start
  7.2 0.0 all-gather.2.cloned.1.call-start
  7.2 1.4 fusion.2
  10.0 0.0 copy-start.15
  10.0 0.6 copy-done.15
  10.6 2.4 multiply_convert_fusion.3
  13.0 0.0 all-gather.2.cloned.1.call-update
  13.0 0.0 all-reduce.6.cloned.1.call-start
  13.1 5.2 copy.36
  18.3 0.0 copy-done.14
  18.3 1.1 copy.31
  19.4 8.5 copy.34.weight_ref
  27.9 0.0 copy-done.18
  27.9 0.9 broadcast_in_dim.22
  28.8 8.0 concatenate.15.weight_ref
  36.7 188.7 %project.1 = (bf16[8,256,2048]{2,1,0:T(8,128)(2,1)}, f32[8,256,1152]{2,1,0:T(8,128)}) custom-call(bf16[256,2048]{1,0:T(8,128)(2,1)} %input_ref.3, f32[1,2048]{1,0:T(1,128)} %bitcast.75, bf16[2048,1152]{1,0:T(8,128)(2,1)} %concatenate.15.weight_ref), custom_call_target="tpu_custom_call" | custom-call | tf_op jit(solution)/shard_map/project/pallas_call | solution.py:635
  225.4 0.0 copy-done.8
  225.4 0.0 copy-done.9
  225.4 96.0 %mixer_forward.1 = (bf16[2048,256]{1,0:T(8,128)(2,1)S(1)}, f32[2048,768]{1,0:T(8,128)}, f32[2048,256]{1,0:T(8,128)S(1)}, f32[2048,256]{1,0:T(8,128)}, f32[2,2048...) custom-call(s32[1]{0:T(128)} %bitcast.longer_ref, f32[2048,1152]{1,0:T(8,128)} %bitcast.61, f32[4,768]{1,0:T(4,128)S(1)} %bitcast.54, ...), custom_call_target="tpu_custom_call" | custom-call | tf_op jit(solution)/shard_map/mixer_forward/pallas_call | solution.py:302
  321.5 1.0 copy-done.1
  322.4 1.3 copy-done.3
  323.8 1.0 copy-done.6
  324.7 0.7 fusion.1.live_ref
  325.4 227.8 %branch_and_norm.1 = (f32[256,2048]{1,0:T(8,128)}, bf16[8,256,2048]{2,1,0:T(8,128)(2,1)}) custom-call(bf16[8,256,256]{2,1,0:T(8,128)(2,1)} %bitcast.52, bf16[256,2048]{1,0:T(8,128)(2,1)} %out_weight_ref.1, bf16[256,2048]{1,0:T(8,128)(2,1)} %input_ref.3, f32[256,1]{1,0:T(8,128)} %fusion.1.live_ref, f32[1,2048]{1,0:T(1,128)} %bitcast.73), custom_call_target="tpu_custom_call" | custom-call | tf_op jit(solution)/shard_map/branch_and_norm/pallas_call | solution.py:707
  553.2 0.0 copy-start.19
  553.2 19.0 %fusion.3 = f32[2048,1408]{0,1:T(8,128)} fusion(bf16[2048,2048]{1,0:T(8,128)(2,1)} %bitcast.80, bf16[2048,1408]{0,1:T(8,128)(2,1)} %bitcast.69), kind=kOutput, calls=%fused_computation.18 | convolution fusion | flops 11811160064 | bytes 25690112 | tf_op jit(solution)/shard_map/dot_general | solution.py:867
  572.2 0.0 copy-done
  572.2 0.0 copy-done.19
  572.2 13.5 multiply_convert_fusion.1
  585.6 4.6 copy.32
  590.2 6.2 pad_maximum_fusion.1
  596.4 4.6 copy.33
  601.0 7.2 pad_maximum_fusion.grad_ref
  608.2 232.3 %feed_back.1 = (f32[256,2048]{1,0:T(8,128)}, f32[1,2048]{1,0:T(1,128)}, bf16[8,256,2048]{2,1,0:T(8,128)(2,1)}, f32[8,256,256]{2,1,0:T(8,128)}) custom-call(bf16[8,256,1408]{2,1,0:T(8,128)(2,1)} %pad_maximum_fusion.grad_ref, bf16[2048,1408]{1,0:T(8,128)(2,1)} %copy.34.weight_ref, bf16[256,2048]{1,0:T(8,128)(2,1)} %top_ref.1, ...), custom_call_target="tpu_custom_call" | custom-call | tf_op jit(solution)/shard_map/feed_back/pallas_call | solution.py:792
  840.5 0.0 copy-done.2
  840.5 0.0 copy-start.4
  840.5 0.0 copy-start.5
  840.6 0.0 copy-start.7
  840.6 6.8 convolution_convert_fusion.3
  847.4 55.9 %mixer_backward.1 = (bf16[2048,1152]{1,0:T(8,128)(2,1)}, f32[4,768]{1,0:T(4,128)S(1)}, f32[2,128]{1,0:T(2,128)S(1)}, f32[1,128]{1,0:T(1,128)S(1)}) custom-call(s32[1]{0:T(128)} %bitcast.longer_ref, f32[2048,256]{1,0:T(8,128)S(1)} %bitcast.53, f32[2048,1152]{1,0:T(8,128)} %bitcast.62, f32[2048,768]{1,0:T(8,128)} %get-tuple-element.41.conv_out_ref, ...), custom_call_target="tpu_custom_call" | custom-call | tf_op jit(solution)/shard_map/mixer_backward/pallas_call | solution.py:342
  903.3 14.6 %fusion.4 = f32[2048,1152]{0,1:T(8,128)S(1)} fusion(bf16[2048,2048]{1,0:T(8,128)(2,1)} %bitcast.79, bf16[2048,1152]{1,0:T(8,128)(2,1)} %get-tuple-element.46), kind=kOutput, calls=%fused_computation.19 | convolution fusion | flops 9663676416 | bytes 22544384 | tf_op jit(solution)/shard_map/dot_general | solution.py:867
  918.0 0.0 copy-start.12
  918.0 3.7 copy-done.12
  921.7 2.7 slice.39
  924.4 7.4 copy.35
  931.8 10.5 convolution_convert_fusion.2
  942.3 18.0 %convolution_convert_fusion.1 = bf16[2048,2,704]{0,2,1:T(8,128)(2,1)} fusion(bf16[2048,2048,1]{1,0,2:T(8,128)(2,1)} %bitcast.81, bf16[2,704,2048]{2,1,0:T(8,128)(2,1)} %bitcast.70), kind=kOutput, calls=%fused_computation.8 | convolution fusion | flops 11814043648 | bytes 19922944 | tf_op jit(solution)/shard_map/dot_general | solution.py:867
  960.3 0.0 all-reduce.6.cloned.1.call-update
  960.3 0.0 reduce-scatter.2.cloned.1.call-start
  960.4 10.9 convolution_convert_fusion
  971.3 0.0 reduce-scatter.2.cloned.1.call-update
  971.3 0.7 slice-done
  972.1 119.1 %input_back.1 = (f32[256,2048]{1,0:T(8,128)}, f32[1,2048]{1,0:T(1,128)}) custom-call(bf16[8,256,1152]{2,1,0:T(8,128)(2,1)} %bitcast.71, bf16[2048,1152]{1,0:T(8,128)(2,1)} %concatenate.15.weight_ref, f32[256,2048]{1,0:T(8,128)} %get-tuple-element.47.later_ref, bf16[256,2048]{1,0:T(8,128)(2,1)} %input_ref.3, f32[1,2048]{1,0:T(1,128)} %bitcast.76), custom_call_target="tpu_custom_call" | custom-call | tf_op jit(solution)/shard_map/input_back/pallas_call | solution.py:852
  1091.2 0.0 copy-done.17
  1091.2 45.3 %all-reduce.1 = (f32[2048]{0:T(1024)}, f32[128]{0:T(128)}, f32[2048]{0:T(1024)}) all-reduce(f32[2048]{0:T(1024)} %bitcast.78, f32[128]{0:T(128)S(1)} %bitcast.60, f32[2048]{0:T(1024)S(1)} %bitcast.77), channel_id=1, replica_groups=mesh['dp'=4,'heads'=8] {'dp','heads'}, use_global_device_ids=true, to_apply=%region_1.2 | all-reduce | flops 4224 | bytes 33792 | tf_op jit(solution)/shard_map/psum | solution.py:975
  1136.6 13.6 all-reduce.2
  1150.1 64.6 %all-reduce.6.cloned.1.call-done = (bf16[2048,4,256]{2,1,0:T(4,128)(2,1)}, bf16[256,2048]{1,0:T(8,128)(2,1)}, bf16[2048,2,704]{0,2,1:T(8,128)(2,1)}, bf16[704,2048]{1,0:T(8,128)(2,1)}) async-done(((bf16[2048,4,256]{2,1,0:T(4,128)(2,1)}, bf16[256,2048]{1,0:T(8,128)(2,1)}, bf16[2048,2,704]{0,2,1:T(8,128)(2,1)}, bf16[704,2048]{1,0:T(8,128)(2,1)}), (bf16[2048,4,256]{2,1,0:T(4,128)(2,1)}, ...) | async-done | bytes 13893648 | tf_op jit(solution)/shard_map/psum | solution.py:881
  1214.8 8.8 convert_element_type.66
  1223.6 4.2 reshape.108
  1227.8 3.3 convert_element_type.68
  1231.2 1.6 convert_element_type.64
  1232.7 135.3 %reduce-scatter.2.cloned.1.call-done = bf16[256,2048]{1,0:T(8,128)(2,1)} async-done(((bf16[2048,2048]{1,0:T(8,128)(2,1)}), bf16[256,2048]{1,0:T(8,128)(2,1)}) %reduce-scatter.2.cloned.1.call-update) | async-done | bytes 1048592 | tf_op jit(solution)/shard_map/reduce_scatter | solution.py:875
  1368.0 3.1 add_convert_fusion
  1371.1 3.1 copy.42
  (26 shorter events, 0.1 us)
Async XLA Ops:
  7.2 565.0 %copy-start = (bf16[704,2048]{1,0:T(8,128)(2,1)S(1)}, bf16[704,2048]{1,0:T(8,128)(2,1)}, u32[]{:S(2)}) copy-start(bf16[704,2048]{1,0:T(8,128)(2,1)} %param.24) | copy-start | bytes 8650756
  7.2 318.2 %all-gather.2.cloned.1.call-start = ((), (), s32[]{:S(2)}) async-start(), calls=%async_computation.1 | async-start | bytes 9437184 | tf_op jit(solution)/shard_map/all_gather | solution.py:871
  10.0 0.6 copy-start.15
  10.6 7.8 copy-start.14
  13.0 1201.8 %all-reduce.6.cloned.1.call-start = ((), (), s32[]{:S(2)}) async-start(), calls=%async_computation.3 | async-start | bytes 27787264 | tf_op jit(solution)/shard_map/psum | solution.py:881
  19.4 8.5 copy-start.18
  28.8 196.6 %copy-start.8 = (f32[3,4,256]{2,1,0:T(4,128)S(1)}, f32[3,4,256]{2,1,0:T(4,128)}, u32[]{:S(2)}) copy-start(f32[3,4,256]{2,1,0:T(4,128)} %param.17) | copy-start | bytes 36868
  28.8 196.7 %copy-start.9 = (f32[128]{0:T(128)S(1)}, f32[128]{0:T(128)}, u32[]{:S(2)}) copy-start(f32[128]{0:T(128)} %param.20) | copy-start | bytes 1540
  321.5 1.0 copy-start.1
  322.4 1.3 copy-start.3
  323.8 1.0 copy-start.6
  553.2 19.0 %copy-start.19 = (bf16[2048,2048]{1,0:T(8,128)(2,1)S(1)}, bf16[2048,2048]{1,0:T(8,128)(2,1)}, u32[]{:S(2)}) copy-start(bf16[2048,2048]{1,0:T(8,128)(2,1)} %all-gather.2.cloned.1.call-done) | copy-start | bytes 25165828
  608.2 232.3 %copy-start.2 = (bf16[2048,256]{1,0:T(8,128)(2,1)S(1)}, bf16[2048,256]{1,0:T(8,128)(2,1)}, u32[]{:S(2)}) copy-start(bf16[2048,256]{1,0:T(8,128)(2,1)} %copy-done.1) | copy-start | bytes 3145732
  840.5 6.9 copy-start.4
  840.5 6.9 copy-start.5
  840.6 6.9 copy-start.7
  918.0 3.7 copy-start.12
  960.3 407.7 %reduce-scatter.2.cloned.1.call-start = ((), (), s32[]{:S(2)}) async-start(), calls=%async_computation.2 | async-start | bytes 9437184 | tf_op jit(solution)/shard_map/reduce_scatter | solution.py:875
  971.3 0.8 slice-start
  972.1 119.1 %copy-start.17 = (f32[1,2048]{1,0:T(1,128)S(1)}, f32[1,2048]{1,0:T(1,128)}, u32[]{:S(2)}) copy-start(f32[1,2048]{1,0:T(1,128)} %get-tuple-element.55) | copy-start | bytes 24580
  1214.8 8.8 copy-start.10
  1223.6 4.2 copy-start.11
  1227.8 3.3 copy-start.13
  1227.8 140.2 %copy-start.16 = (f32[256]{0:T(256)S(1)}, f32[256]{0:T(256)}, u32[]{:S(2)}) copy-start(f32[256]{0:T(256)} %copy-done.15) | copy-start | bytes 3076
Sparse Core Ops, SparseCore 0:
  13.1 206.9 all-gather.1
  960.4 254.3 all-reduce.5
  1218.4 149.5 reduce-scatter.1

commit v3 on v1

--- a/solution.py
+++ b/solution.py
@@ -330,6 +330,9 @@
             pltpu.VMEM((8, 3 * width), F32),
         ],
         compiler_params=pltpu.CompilerParams(vmem_limit_bytes=48 * 2**20),
+        cost_estimate=pl.CostEstimate(
+            flops=10**11, bytes_accessed=2**20, transcendentals=0
+        ),
         name="mixer_forward",
     )(longer, main, conv, params, gain)
 
@@ -372,12 +375,920 @@
             pltpu.VMEM((8, 3 * width), F32),
         ],
         compiler_params=pltpu.CompilerParams(vmem_limit_bytes=48 * 2**20),
+        cost_estimate=pl.CostEstimate(
+            flops=6 * 10**10, bytes_accessed=2**20, transcendentals=0
+        ),
         name="mixer_backward",
     )(longer, grad, main, *saved, conv, params, gain)
 
 
-def rms_rows(values, gain):
-    return values * lax.rsqrt(jnp.mean(values * values, axis=-1, keepdims=True) + EPS) * gain
+MESH = pl.DeviceIdType.MESH
+PIECES = 8
+
+
+def grid_sizes(count):
+    nz = 4 if count % 4 == 0 else 1
+    return nz, count // nz
+
+
+class Group:
+    def __init__(self, count):
+        self.deep, self.nx = grid_sizes(count)
+        self.size = count
+        me = lax.axis_index("heads")
+        self.z, self.x = me // self.nx, me % self.nx
+        self.own = me
+
+    def slot(self, z, j):
+        return z * self.nx + (self.x + j) % self.nx
+
+    def device(self, z, j):
+        return {"heads": self.slot(z, j)}
+
+
+def meet(count, replicas=1):
+    barrier = pltpu.get_barrier_semaphore()
+    for axis, size in (("heads", count), ("dp", replicas)):
+        me = lax.axis_index(axis)
+
+        def greet(k, _, axis=axis, size=size, me=me):
+            pl.semaphore_signal(
+                barrier, inc=1, device_id={axis: (me + k) % size}, device_id_type=MESH
+            )
+            return 0
+
+        lax.fori_loop(1, size, greet, 0)
+    pl.semaphore_wait(barrier, count + replicas - 2)
+
+
+def arrived(ref, sem):
+    pltpu.make_async_copy(ref, ref, sem).wait()
+
+
+def during(piece, work):
+    pl.when((piece >= 0) & (piece < PIECES))(functools.partial(work, piece))
+
+
+class Sender:
+    draining = False
+
+    def push(self, source, target, send_sem, recv_sem, device, condition=None):
+        copy = pltpu.make_async_remote_copy(
+            source, target, send_sem, recv_sem, device_id=device, device_id_type=MESH
+        )
+        act = copy.wait_send if self.draining else copy.start
+        if condition is None:
+            act()
+        else:
+            pl.when(condition)(act)
+
+    def place(self, piece):
+        rows = pl.ds(pl.multiple_of(piece * self.part, self.part), self.part)
+        return rows, self.cols
+
+    def drain(self):
+        def one(piece, _):
+            for step in range(self.last + 1):
+                self.phase(piece, step)
+            return 0
+
+        self.draining = True
+        lax.fori_loop(0, PIECES, one, 0)
+        self.draining = False
+
+
+class Gather(Sender):
+    def __init__(self, group, full, cols, send_sems, recv_sems, x_first):
+        self.group, self.full, self.cols, self.x_first = group, full, cols, x_first
+        self.part = full.shape[1] // PIECES
+        self.send_sems, self.recv_sems = send_sems, recv_sems
+        self.last = group.deep
+
+    @staticmethod
+    def sems(size):
+        return [
+            pltpu.SemaphoreType.DMA((PIECES, 3, size)),
+            pltpu.SemaphoreType.DMA((PIECES, size)),
+        ]
+
+    def send(self, piece, slot, way, mark, device, condition):
+        place = self.full.at[slot, *self.place(piece)]
+        self.push(
+            place,
+            place,
+            self.send_sems.at[piece, way, mark],
+            self.recv_sems.at[piece, slot],
+            device,
+            condition,
+        )
+
+    def receive(self, piece, slot):
+        if not self.draining:
+            arrived(self.full.at[slot, *self.place(piece)], self.recv_sems.at[piece, slot])
+
+    def send_up(self, piece, slot, here=True):
+        group = self.group
+        self.send(
+            piece, slot, 0, slot, group.device(group.z + 1, 0), here & (group.z + 1 < group.deep)
+        )
+
+    def send_down(self, piece, slot, here=True):
+        group = self.group
+        self.send(piece, slot, 1, slot, group.device(group.z - 1, 0), here & (group.z > 0))
+
+    def send_x(self, piece, slot, here=None):
+        group = self.group
+        for j in range(1, group.nx):
+            mark = (slot // group.nx) * group.nx + (slot + j) % group.nx
+            self.send(piece, slot, 2, mark, group.device(group.z, j), here)
+
+    def phase(self, piece, step):
+        group = self.group
+        if step == 0:
+            self.send_up(piece, group.own)
+            self.send_down(piece, group.own)
+            self.send_x(piece, group.own)
+            return
+        if self.x_first and step == 1:
+            for j in range(1, group.nx):
+                slot = group.slot(group.z, j)
+                self.receive(piece, slot)
+                self.send_up(piece, slot)
+                self.send_down(piece, slot)
+        if step < group.deep:
+            for j in range(group.nx if self.x_first else 1):
+                below, above = group.z - step, group.z + step
+                for z, here, forward in (
+                    (below, below >= 0, self.send_up),
+                    (above, above < group.deep, self.send_down),
+                ):
+                    slot = group.slot(z, j)
+                    pl.when(here)(functools.partial(self.receive, piece, slot))
+                    forward(piece, slot, here)
+                    if not self.x_first:
+                        self.send_x(piece, slot, here)
+        elif not self.x_first:
+            for j in range(1, group.nx):
+                for z in range(group.deep):
+                    self.receive(piece, group.slot(z, j))
+
+
+class Scatter(Sender):
+    last = 3
+
+    def __init__(self, group, parts, cols, scratch, z_first):
+        self.group, self.parts, self.cols, self.z_first = group, parts, cols, z_first
+        self.part = parts.shape[1] // PIECES
+        self.over_x, self.line, *sems = scratch
+        self.x_send, self.x_recv, self.z_send, self.z_recv = sems
+
+    @staticmethod
+    def scratch(deep, nx, rows, cols, z_first):
+        dma = pltpu.SemaphoreType.DMA
+        return [
+            pltpu.VMEM((1 if z_first else deep, max(nx - 1, 1), rows, cols), BF16),
+            pltpu.VMEM((deep + 1, nx if z_first else 1, rows, cols), BF16),
+            *[dma((PIECES, deep, nx))] * 2,
+            *[dma((PIECES, 2, deep * nx))] * 2,
+        ]
+
+    def landing(self, piece):
+        return self.place(piece)[0]
+
+    def line_at(self, piece, slot, way):
+        nx = self.group.nx
+        z = slot // nx + (1 if way == 0 else 0)
+        return self.line.at[z, slot % nx if self.z_first else 0, self.landing(piece)]
+
+    def step_line(self, piece, slot, way, device, add):
+        part = (slot, *self.place(piece))
+        if add and not self.draining:
+            landed = self.line_at(piece, slot, way)
+            arrived(landed, self.z_recv.at[piece, way, slot])
+            total = self.parts[part].astype(F32) + landed[...].astype(F32)
+            self.parts[part] = total.astype(BF16)
+        self.push(
+            self.parts.at[part],
+            self.line_at(piece, slot, way),
+            self.z_send.at[piece, way, slot],
+            self.z_recv.at[piece, way, slot],
+            device,
+        )
+
+    def walk(self, piece, columns, ends):
+        group = self.group
+        deep = group.deep
+
+        def one_way(way):
+            for k in range(deep - 1, 0, -1):
+                target = group.z + k if way == 0 else group.z - k
+                inside = target < deep if way == 0 else target >= 0
+                first = group.z == 0 if way == 0 else group.z == deep - 1
+                condition = inside & (first if ends else jnp.logical_not(first))
+                device = group.device(group.z + (1 if way == 0 else -1), 0)
+                for j in range(columns):
+                    slot = group.slot(target, j)
+                    pl.when(condition)(
+                        functools.partial(self.step_line, piece, slot, way, device, not ends)
+                    )
+
+        if ends or self.draining:
+            one_way(0)
+            one_way(1)
+            return
+
+        def both(first, second):
+            one_way(first)
+            one_way(second)
+
+        low = group.z < deep // 2
+        pl.when(low)(functools.partial(both, 0, 1))
+        pl.when(jnp.logical_not(low))(functools.partial(both, 1, 0))
+
+    def total_line(self, piece, slot):
+        group = self.group
+        total = self.parts[(slot, *self.place(piece))].astype(F32)
+        for way, here in ((0, group.z > 0), (1, group.z + 1 < group.deep)):
+            landed = self.line_at(piece, slot, way)
+            pl.when(here)(
+                functools.partial(arrived, landed, self.z_recv.at[piece, way, slot])
+            )
+            total = total + jnp.where(here, landed[...].astype(F32), 0.0)
+        return total
+
+    def send_x(self, piece, index, z, j):
+        group = self.group
+        self.push(
+            self.parts.at[group.slot(z, j), *self.place(piece)],
+            self.over_x.at[index, j - 1, self.landing(piece)],
+            self.x_send.at[piece, index, j],
+            self.x_recv.at[piece, index, j],
+            group.device(group.z, j),
+        )
+
+    def add_x(self, piece, index, total):
+        for j in range(1, self.group.nx):
+            landed = self.over_x.at[index, j - 1, self.landing(piece)]
+            arrived(landed, self.x_recv.at[piece, index, j])
+            total = total + landed[...].astype(F32)
+        return total
+
+    def phase(self, piece, step):
+        group = self.group
+        if self.z_first:
+            if step == 0:
+                self.walk(piece, group.nx, True)
+            elif step == 1:
+                self.walk(piece, group.nx, False)
+            elif step == 2:
+                for j in range(1, group.nx):
+                    slot = group.slot(group.z, j)
+                    if not self.draining:
+                        total = self.total_line(piece, slot)
+                        self.parts[(slot, *self.place(piece))] = total.astype(BF16)
+                    self.send_x(piece, 0, group.z, j)
+            elif not self.draining:
+                return self.add_x(piece, 0, self.total_line(piece, group.own))
+        elif step == 0:
+            for z in range(group.deep):
+                for j in range(1, group.nx):
+                    self.send_x(piece, z, z, j)
+        elif step == 1:
+            for z in range(group.deep):
+                part = (group.slot(z, 0), *self.place(piece))
+                if not self.draining:
+                    total = self.add_x(piece, z, self.parts[part].astype(F32))
+                    self.parts[part] = total.astype(BF16)
+            self.walk(piece, 1, True)
+        elif step == 2:
+            self.walk(piece, 1, False)
+        elif not self.draining:
+            return self.total_line(piece, group.own)
+        return None
+
+
+class Both:
+    def __init__(self, first, second):
+        self.both = (first, second)
+        self.part, self.last = first.part, first.last
+
+    def rows(self, piece):
+        return pl.ds(pl.multiple_of(piece * self.part, self.part), self.part)
+
+    def phase(self, piece, step):
+        out = [each.phase(piece, step) for each in self.both]
+        return None if out[0] is None else jnp.concatenate(out, axis=1)
+
+    def drain(self):
+        for each in self.both:
+            each.drain()
+
+
+def cut(cols, share):
+    edge = cols - cols * share // 8
+    return pl.ds(0, edge), pl.ds(edge, cols - edge)
+
+
+def gather_of(group, share, scratch):
+    full, *sems = scratch
+    first, second = cut(full.shape[2], share)
+    return Both(
+        Gather(group, full, first, *sems[:2], False), Gather(group, full, second, *sems[2:], True)
+    )
+
+
+def scatter_of(group, share, scratch):
+    parts, *rest = scratch
+    first, second = cut(parts.shape[2], share)
+    return Both(
+        Scatter(group, parts, first, rest[:6], False),
+        Scatter(group, parts, second, rest[6:], True),
+    )
+
+
+def gather_scratch(nz, nx, rows, cols):
+    return [pltpu.VMEM((nz * nx, rows, cols), BF16), *Gather.sems(nz * nx), *Gather.sems(nz * nx)]
+
+
+def scatter_scratch(nz, nx, rows, cols, share):
+    first, second = cut(cols, share)
+    return [
+        pltpu.VMEM((nz * nx, rows, cols), BF16),
+        *Scatter.scratch(nz, nx, rows, first.size, False),
+        *Scatter.scratch(nz, nx, rows, second.size, True),
+    ]
+
+
+SCATTER_COUNT, GATHER_COUNT = 13, 5
+
+
+def inverse_rms(rows):
+    return lax.rsqrt(jnp.mean(rows * rows, axis=-1, keepdims=True) + EPS)
+
+
+def wide_dot(terms, dims, tile, store):
+    total = terms[0][1].shape[0 if dims is NT else 1]
+    for first in range(0, total, tile):
+        cols = slice(first, min(first + tile, total))
+        products = [
+            lax.dot_general(
+                left,
+                right[cols, :] if dims is NT else right[:, cols],
+                (dims, ((), ())),
+                preferred_element_type=F32,
+            )
+            for left, right in terms
+        ]
+        store(cols, functools.reduce(jnp.add, products))
+
+
+VMEM_SPEC = pl.BlockSpec(memory_space=pltpu.VMEM)
+ANY_SPEC = pl.BlockSpec(memory_space=pl.ANY)
+PAIR_SHARE, GATHER_SHARE, SCATTER_SHARE = 3, 1, 2
+
+
+def lasting(microseconds):
+    return pl.CostEstimate(
+        flops=int(microseconds * 1.1e9), bytes_accessed=2**20, transcendentals=0
+    )
+
+
+def linked(collective):
+    return pltpu.CompilerParams(
+        collective_id=collective, has_side_effects=True, vmem_limit_bytes=62 * 2**20
+    )
+
+
+def joined(values):
+    return values.reshape(values.shape[0] * values.shape[1], values.shape[2])
+
+
+def split(values, parts):
+    return values.reshape(parts, values.shape[0] // parts, values.shape[1])
+
+
+def project_kernel(count, rows_ref, gain_ref, weight_ref, full_out, projected_out, *scratch):
+    full, staged, full_sems, staged_sems = scratch[0], *scratch[GATHER_COUNT:]
+    group = Group(count)
+    gather = gather_of(group, GATHER_SHARE, scratch[:GATHER_COUNT])
+    meet(count)
+
+    shares, share = full_out.shape[0], full_out.shape[3]
+
+    def full_copy(piece, index):
+        rows = gather.rows(piece)
+        return pltpu.make_async_copy(
+            full.at[:, rows, pl.ds(index * share, share)],
+            full_out.at[index, :, rows],
+            full_sems.at[piece, index],
+        )
+
+    def staged_copy(piece):
+        rows = gather.rows(piece)
+        return pltpu.make_async_copy(
+            staged.at[:, rows], projected_out.at[:, rows], staged_sems.at[piece]
+        )
+
+    def begin(piece):
+        rows = rows_ref[gather.rows(piece)].astype(F32)
+        full[group.own, gather.rows(piece)] = (
+            rows * inverse_rms(rows) * gain_ref[...]
+        ).astype(BF16)
+        gather.phase(piece, 0)
+
+    def ready(piece):
+        gather.phase(piece, gather.last)
+        rows = gather.rows(piece)
+        for index in range(shares):
+            full_copy(piece, index).start()
+
+        def store(cols, value):
+            staged[:, rows, cols] = split(value, count)
+
+        wide_dot([(joined(full[:, rows]), weight_ref)], NN, 256, store)
+        staged_copy(piece).start()
+
+    def tick(time, _):
+        during(time, begin)
+        for step in range(1, gather.last):
+            during(time - step, functools.partial(gather.phase, step=step))
+        during(time - gather.last, ready)
+        return 0
+
+    lax.fori_loop(0, PIECES + gather.last, tick, 0)
+    gather.drain()
+
+    def finish(piece, _):
+        for index in range(shares):
+            full_copy(piece, index).wait()
+        staged_copy(piece).wait()
+        return 0
+
+    lax.fori_loop(0, PIECES, finish, 0)
+
+
+def project(rows, gain, weight, count, shares):
+    own, features = rows.shape
+    cols = weight.shape[1]
+    nz, nx = grid_sizes(count)
+    return pl.pallas_call(
+        functools.partial(project_kernel, count),
+        out_shape=[
+            jax.ShapeDtypeStruct((shares, count, own, features // shares), BF16),
+            jax.ShapeDtypeStruct((count, own, cols), F32),
+        ],
+        in_specs=[VMEM_SPEC] * 3,
+        out_specs=[ANY_SPEC] * 2,
+        scratch_shapes=[
+            *gather_scratch(nz, nx, own, features),
+            pltpu.VMEM((count, own, cols), F32),
+            pltpu.SemaphoreType.DMA((PIECES, shares)),
+            pltpu.SemaphoreType.DMA((PIECES,)),
+        ],
+        compiler_params=linked(0),
+        cost_estimate=lasting(100),
+        name="project",
+    )(rows, gain, weight)
+
+
+def sum_and_gather(scatter, gather, full, full_out, out_sems, prepare, middle, ready):
+    own = lax.axis_index("heads")
+
+    def out(piece):
+        rows = gather.rows(piece)
+        return pltpu.make_async_copy(full.at[:, rows], full_out.at[:, rows], out_sems.at[piece])
+
+    def begin(piece):
+        prepare(piece)
+        scatter.phase(piece, 0)
+
+    def turn(piece):
+        total = scatter.phase(piece, scatter.last)
+        full[own, gather.rows(piece)] = middle(piece, total).astype(BF16)
+        gather.phase(piece, 0)
+
+    def end(piece):
+        gather.phase(piece, gather.last)
+        out(piece).start()
+        ready(piece)
+
+    def tick(time, _):
+        during(time + 1, begin)
+        for step in range(1, scatter.last):
+            during(time - step + 1, functools.partial(scatter.phase, step=step))
+        during(time - scatter.last + 1, turn)
+        for step in range(1, gather.last):
+            during(
+                time - scatter.last + 1 - step, functools.partial(gather.phase, step=step)
+            )
+        during(time - scatter.last + 1 - gather.last, end)
+        return 0
+
+    lax.fori_loop(-1, PIECES + scatter.last + gather.last - 1, tick, 0)
+    scatter.drain()
+    gather.drain()
+
+    def finish(piece, _):
+        out(piece).wait()
+        return 0
+
+    lax.fori_loop(0, PIECES, finish, 0)
+
+
+def branch_kernel(
+    count, mixed_ref, weight_ref, input_ref, live_ref, gain_ref, middle_out, full_out, *scratch
+):
+    group = Group(count)
+    scatter = scatter_of(group, PAIR_SHARE, scratch[:SCATTER_COUNT])
+    gather = gather_of(group, PAIR_SHARE, scratch[SCATTER_COUNT:-1])
+    parts, full, out_sems = scratch[0], scratch[SCATTER_COUNT], scratch[-1]
+    meet(count)
+
+    def prepare(piece):
+        rows = gather.rows(piece)
+
+        def store(cols, value):
+            parts[:, rows, cols] = split(value.astype(BF16), count)
+
+        wide_dot([(joined(mixed_ref[:, rows]), weight_ref)], NN, 512, store)
+
+    def middle(piece, total):
+        rows = gather.rows(piece)
+        values = input_ref[rows].astype(F32) + live_ref[rows] * total
+        middle_out[rows] = values
+        return values * inverse_rms(values) * gain_ref[...]
+
+    sum_and_gather(
+        scatter, gather, full, full_out, out_sems, prepare, middle, lambda piece: None
+    )
+
+
+def branch_and_norm(mixed, weight, rows, live, gain, count):
+    own, features = rows.shape
+    nz, nx = grid_sizes(count)
+    return pl.pallas_call(
+        functools.partial(branch_kernel, count),
+        out_shape=[
+            jax.ShapeDtypeStruct((own, features), F32),
+            jax.ShapeDtypeStruct((count, own, features), BF16),
+        ],
+        in_specs=[VMEM_SPEC] * 5,
+        out_specs=[VMEM_SPEC, ANY_SPEC],
+        scratch_shapes=[
+            *scatter_scratch(nz, nx, own, features, PAIR_SHARE),
+            *gather_scratch(nz, nx, own, features),
+            pltpu.SemaphoreType.DMA((PIECES,)),
+        ],
+        compiler_params=linked(1),
+        cost_estimate=lasting(180),
+        name="branch_and_norm",
+    )(split(mixed, count), weight, rows, live, gain)
+
+
+def feed_back_kernel(
+    count, dgate_ref, dup_ref, gate_weight_ref, up_weight_ref, top_ref, middle_ref, live_ref,
+    gain_ref, out_weight_ref, dmiddle_out, dgain_out, full_out, dmixed_out, *scratch
+):
+    group = Group(count)
+    scatter = scatter_of(group, PAIR_SHARE, scratch[:SCATTER_COUNT])
+    gather = gather_of(group, PAIR_SHARE, scratch[SCATTER_COUNT:-1])
+    parts, full, out_sems = scratch[0], scratch[SCATTER_COUNT], scratch[-1]
+    meet(count)
+    dgain_out[...] = jnp.zeros(dgain_out.shape, F32)
+
+    def prepare(piece):
+        rows = gather.rows(piece)
+
+        def store(cols, value):
+            parts[:, rows, cols] = split(value.astype(BF16), count)
+
+        wide_dot(
+            [
+                (joined(dgate_ref[:, rows]), gate_weight_ref),
+                (joined(dup_ref[:, rows]), up_weight_ref),
+            ],
+            NT,
+            256,
+            store,
+        )
+
+    def middle(piece, dnormed):
+        rows = gather.rows(piece)
+        values = middle_ref[rows]
+        scale = inverse_rms(values)
+        normed = values * scale
+        dgain_out[...] += jnp.sum(dnormed * normed, axis=0, keepdims=True)
+        scaled = dnormed * gain_ref[...]
+        dmiddle = top_ref[rows].astype(F32) + scale * (
+            scaled - normed * jnp.mean(scaled * normed, axis=-1, keepdims=True)
+        )
+        dmiddle_out[rows] = dmiddle
+        return live_ref[rows] * dmiddle
+
+    def ready(piece):
+        rows = gather.rows(piece)
+
+        def store(cols, value):
+            dmixed_out[:, rows, cols] = split(value, count)
+
+        wide_dot([(joined(full[:, rows]), out_weight_ref)], NT, 256, store)
+
+    sum_and_gather(scatter, gather, full, full_out, out_sems, prepare, middle, ready)
+
+
+def feed_back(dgate, dup, gate_weight, up_weight, top, middle, live, gain, out_weight, count):
+    own, features = middle.shape
+    nz, nx = grid_sizes(count)
+    width = out_weight.shape[0]
+    return pl.pallas_call(
+        functools.partial(feed_back_kernel, count),
+        out_shape=[
+            jax.ShapeDtypeStruct((own, features), F32),
+            jax.ShapeDtypeStruct((1, features), F32),
+            jax.ShapeDtypeStruct((count, own, features), BF16),
+            jax.ShapeDtypeStruct((count, own, width), F32),
+        ],
+        in_specs=[VMEM_SPEC] * 9,
+        out_specs=[VMEM_SPEC, VMEM_SPEC, ANY_SPEC, VMEM_SPEC],
+        scratch_shapes=[
+            *scatter_scratch(nz, nx, own, features, PAIR_SHARE),
+            *gather_scratch(nz, nx, own, features),
+            pltpu.SemaphoreType.DMA((PIECES,)),
+        ],
+        compiler_params=linked(2),
+        cost_estimate=lasting(180),
+        name="feed_back",
+    )(
+        split(dgate, count), split(dup, count), gate_weight, up_weight, top, middle, live, gain,
+        out_weight,
+    )
+
+
+class Replicas(Sender):
+    def __init__(self, values, from_core, from_y, over_back, over_home, sems):
+        self.values, self.from_core, self.from_y = values, from_core, from_y
+        self.over_back, self.over_home = over_back, over_home
+        self.core_sems, self.y_sems, self.back_sems, self.home_sems = sems
+        me = lax.axis_index("dp")
+        self.lines = lax.axis_size("dp") // 2
+        self.y, self.core = me // 2, me % 2
+
+    @staticmethod
+    def scratch(rows, cols, replicas):
+        lines, share = replicas // 2, rows // replicas
+        return [
+            pltpu.VMEM((replicas, share, cols), BF16),
+            pltpu.VMEM((lines, share, cols), BF16),
+            pltpu.VMEM((max(lines - 1, 1), share, cols), BF16),
+            pltpu.VMEM((max(lines - 1, 1), share, cols), BF16),
+            pltpu.VMEM((lines, share, cols), BF16),
+            *[pltpu.SemaphoreType.DMA((2, lines))] * 4,
+        ]
+
+    def share(self, core, y):
+        return core * self.lines + y
+
+    def peer(self, y, core):
+        return {"dp": y * 2 + core}
+
+    def line(self, k):
+        return (self.y + k) % self.lines
+
+    def drain(self):
+        self.draining = True
+        for k in range(self.lines):
+            self.start(k)
+            self.cores(k)
+        self.over_y()
+        self.back()
+        self.draining = False
+
+    def add(self, share, others):
+        step = 64
+
+        def some(block, _):
+            rows = pl.ds(pl.multiple_of(block * step, step), step)
+            total = self.values[share, rows].astype(F32)
+            for ref, index in others:
+                total = total + ref[index, rows].astype(F32)
+            self.values[share, rows] = total.astype(BF16)
+            return 0
+
+        lax.fori_loop(0, self.values.shape[1] // step, some, 0)
+
+    def start(self, k):
+        y = self.line(k)
+        self.push(
+            self.values.at[self.share(1 - self.core, y)],
+            self.from_core.at[y],
+            self.core_sems.at[0, k],
+            self.core_sems.at[1, k],
+            self.peer(self.y, 1 - self.core),
+        )
+
+    def cores(self, k):
+        y = self.line(k)
+        share = self.share(self.core, y)
+        if not self.draining:
+            arrived(self.from_core.at[y], self.core_sems.at[1, k])
+            self.add(share, [(self.from_core, y)])
+        if k > 0:
+            self.push(
+                self.values.at[share],
+                self.from_y.at[self.lines - k - 1],
+                self.y_sems.at[0, k],
+                self.y_sems.at[1, self.lines - k],
+                self.peer(y, self.core),
+            )
+
+    def over_y(self):
+        share = self.share(self.core, self.y)
+        if not self.draining:
+            for k in range(1, self.lines):
+                arrived(self.from_y.at[k - 1], self.y_sems.at[1, k])
+            self.add(share, [(self.from_y, k) for k in range(self.lines - 1)])
+        for k in range(1, self.lines):
+            self.push(
+                self.values.at[share],
+                self.over_back.at[self.lines - k - 1],
+                self.back_sems.at[0, k],
+                self.back_sems.at[1, self.lines - k],
+                self.peer(self.line(k), self.core),
+            )
+        self.send_home(0)
+
+    def own(self, k):
+        return self.values.at[self.share(self.core, self.y)] if k == 0 else self.over_back.at[k - 1]
+
+    def send_home(self, k):
+        self.push(
+            self.own(k),
+            self.over_home.at[k],
+            self.home_sems.at[0, k],
+            self.home_sems.at[1, k],
+            self.peer(self.y, 1 - self.core),
+        )
+
+    def back(self):
+        for k in range(1, self.lines):
+            if not self.draining:
+                arrived(self.over_back.at[k - 1], self.back_sems.at[1, k])
+            self.send_home(k)
+
+    def home(self):
+        for k in range(self.lines):
+            arrived(self.over_home.at[k], self.home_sems.at[1, k])
+
+    def totals(self):
+        for k in range(self.lines):
+            yield self.own(k), self.share(self.core, self.line(k))
+            yield self.over_home.at[k], self.share(1 - self.core, self.line(k))
+
+
+def sum_small(small, seen, send_sems, recv_sems, axis, rows):
+    me, size = lax.axis_index(axis), lax.axis_size(axis)
+    copies = []
+    seen[me] = small[...]
+    for k in range(1, size):
+        copy = pltpu.make_async_remote_copy(
+            seen.at[me], seen.at[me], send_sems.at[k], recv_sems.at[size - k],
+            device_id={axis: (me + k) % size}, device_id_type=MESH,
+        )
+        copy.start()
+        copies.append(copy)
+    for k in range(1, size):
+        arrived(seen.at[(me + k) % size], recv_sems.at[k])
+    total = seen[0]
+    for other in range(1, size):
+        total = total + seen[other]
+    small[...] = jnp.where(grid_index(total.shape, 0) < rows, total, small[...])
+    return copies
+
+
+def input_back_kernel(
+    count, grad_ref, weight_ref, normed_ref, later_ref, input_ref, gain_ref, small_ref,
+    wout_ref, grad_out, small_out, dweight_out, *scratch
+):
+    parts, rest = scratch[0], scratch[SCATTER_COUNT:]
+    values = rest[0]
+    near, near_send, near_recv, far, far_send, far_recv, staged, out_sems = rest[9:]
+    scatter = scatter_of(Group(count), SCATTER_SHARE, scratch[:SCATTER_COUNT])
+    replicas = Replicas(*rest[:5], rest[5:9])
+    meet(count, lax.axis_size("dp"))
+    small_out[...] = small_ref[...]
+    width = grad_ref.shape[2]
+    values[:, :, width:] = split(wout_ref[...], values.shape[0])
+
+    def begin(piece):
+        rows = scatter.rows(piece)
+
+        def store(cols, value):
+            parts[:, rows, cols] = split(value.astype(BF16), count)
+
+        wide_dot([(joined(grad_ref[:, rows]), weight_ref)], NT, 256, store)
+        scatter.phase(piece, 0)
+
+    def end(piece):
+        dnormed = scatter.phase(piece, scatter.last)
+        rows = scatter.rows(piece)
+        given = input_ref[rows].astype(F32)
+        scale = inverse_rms(given)
+        normed = given * scale
+        small_out[0:1] += jnp.sum(dnormed * normed, axis=0, keepdims=True)
+        scaled = dnormed * gain_ref[...]
+        grad_out[rows] = later_ref[rows] + scale * (
+            scaled - normed * jnp.mean(scaled * normed, axis=-1, keepdims=True)
+        )
+
+    def weight_share(core, y):
+        share = replicas.share(core, y)
+        left = joined(normed_ref[share])
+        grads = joined(grad_ref[...])
+        for first in range(0, width, 384):
+            cols = slice(first, min(first + 384, width))
+            staged[:, cols] = lax.dot_general(
+                left, grads[:, cols], (TN, ((), ())), preferred_element_type=F32
+            ).astype(BF16)
+
+        def some(block, _):
+            rows = pl.ds(pl.multiple_of(block * 64, 64), 64)
+            values[share, rows, :width] = staged[rows]
+            return 0
+
+        lax.fori_loop(0, staged.shape[0] // 64, some, 0)
+
+    def other_core(k):
+        weight_share(1 - replicas.core, replicas.line(k))
+        replicas.start(k)
+
+    def this_core(k):
+        weight_share(replicas.core, replicas.line(k))
+        replicas.cores(k)
+
+    order = range(replicas.lines - 1, -1, -1)
+    steps = [functools.partial(other_core, k) for k in order]
+    steps += [functools.partial(this_core, k) for k in order]
+    steps += [replicas.over_y, replicas.back]
+
+    def tick(time, _):
+        during(time + 1, begin)
+        for step in range(1, scatter.last):
+            during(time - step + 1, functools.partial(scatter.phase, step=step))
+        during(time - scatter.last + 1, end)
+        for index, step in enumerate(steps):
+            pl.when(time == index)(step)
+        return 0
+
+    lax.fori_loop(-1, max(PIECES + scatter.last - 1, len(steps)), tick, 0)
+    copies = sum_small(small_out, near, near_send, near_recv, "heads", 3)
+    copies += sum_small(small_out, far, far_send, far_recv, "dp", 8)
+    replicas.home()
+    outs = [
+        pltpu.make_async_copy(total, dweight_out.at[share], out_sems.at[index])
+        for index, (total, share) in enumerate(replicas.totals())
+    ]
+    for copy in outs:
+        copy.start()
+    scatter.drain()
+    replicas.drain()
+    for copy in copies:
+        copy.wait_send()
+    for copy in outs:
+        copy.wait()
+
+
+def input_back(
+    grad, weight, normed, later, rows, gain, small, grad_wout, count, replica_count
+):
+    own, features = rows.shape
+    nz, nx = grid_sizes(count)
+    cols = weight.shape[1] + grad_wout.shape[1]
+    dma = pltpu.SemaphoreType.DMA
+    return pl.pallas_call(
+        functools.partial(input_back_kernel, count),
+        out_shape=[
+            jax.ShapeDtypeStruct((own, features), F32),
+            jax.ShapeDtypeStruct(small.shape, F32),
+            jax.ShapeDtypeStruct((replica_count, features // replica_count, cols), BF16),
+        ],
+        in_specs=[VMEM_SPEC] * 8,
+        out_specs=[VMEM_SPEC, VMEM_SPEC, ANY_SPEC],
+        scratch_shapes=[
+            *scatter_scratch(nz, nx, own, features, SCATTER_SHARE),
+            *Replicas.scratch(features, cols, replica_count),
+            pltpu.VMEM((count, *small.shape), F32),
+            dma((count,)),
+            dma((count,)),
+            pltpu.VMEM((replica_count, *small.shape), F32),
+            dma((replica_count,)),
+            dma((replica_count,)),
+            pltpu.VMEM((features // replica_count, weight.shape[1]), BF16),
+            dma((replica_count,)),
+        ],
+        compiler_params=linked(3),
+        cost_estimate=lasting(120),
+        name="input_back",
+    )(split(grad, count), weight, normed, later, rows, gain, small, grad_wout)
 
 
 def matmul(left, right, dims):
@@ -392,10 +1303,6 @@
     return lax.psum_scatter(
         values.astype(BF16), "heads", scatter_dimension=0, tiled=True
     ).astype(F32)
-
-
-def sum_replicas(values):
-    return lax.psum(values.astype(BF16), "dp").astype(F32)
 
 
 def on_device(
@@ -414,7 +1321,8 @@
     cotangent,
 ):
     own_rows, features = block_in.shape
-    all_rows = own_rows * lax.axis_size("heads")
+    count = lax.axis_size("heads")
+    all_rows = own_rows * count
     width = conv_weight.shape[2]
     heads = gate_params.shape[1]
     longer = seq_counts[0, 1:2]
@@ -422,9 +1330,6 @@
     row_index = first_row + jnp.arange(own_rows, dtype=jnp.int32)
     live_own = jnp.where(longer[0] > 0, True, row_index < seq_counts[0, 0] * SEQ_SHORT)
     live_own = live_own.astype(F32)[:, None]
-    input_rows = block_in.astype(F32)
-    normed1, pull_norm1 = jax.vjp(rms_rows, input_rows, norm1_gain)
-    full_normed1 = gather_rows(normed1.astype(BF16))
     weight = jnp.concatenate(
         [
             w_qkvg.reshape(features, 4 * width),
@@ -433,68 +1338,104 @@
         ],
         axis=1,
     )
-    projected = matmul(full_normed1, weight, NN)
+    full_normed1, projected = project(
+        block_in, norm1_gain[None], weight, count, lax.axis_size("dp")
+    )
+    projected, grad_feed = lax.optimization_barrier(
+        (projected, (live_own * cotangent.astype(F32)).astype(BF16))
+    )
+    grad_feed = gather_rows(grad_feed)
+    projected = projected.reshape(all_rows, -1)
     taps = jnp.transpose(conv_weight, (1, 0, 2)).reshape(4, 3 * width)
     params = jnp.pad(gate_params, ((0, 0), (0, 128 - heads)))
     gain_row = out_gain[None]
     mixed, *saved = mixer_forward(longer, projected, taps, params, gain_row)
-    branch = scatter_rows(matmul(mixed, w_out, NN))
-    grad_top = cotangent.astype(F32)
-    grad_feed = gather_rows((live_own * grad_top).astype(BF16))
-    middle = input_rows + live_own * branch
-    normed2, pull_norm2 = jax.vjp(rms_rows, middle, norm2_gain)
-    full_normed2 = gather_rows(normed2.astype(BF16))
-    feed_weight = w_gate_up.reshape(features, -1)
-    hidden_cols = w_down.shape[0]
-    gate_up = matmul(full_normed2, feed_weight, NN)
-    gate_pre = gate_up[:, :hidden_cols]
-    up_pre = gate_up[:, hidden_cols:]
+    mixed, grad_feed = lax.optimization_barrier((mixed, grad_feed))
+    middle, full_normed2 = branch_and_norm(
+        mixed, w_out, block_in, live_own, norm2_gain[None], count
+    )
+    full_normed2 = full_normed2.reshape(all_rows, features)
+    gate_weight, up_weight = w_gate_up[:, 0], w_gate_up[:, 1]
+    gate_pre = matmul(full_normed2, gate_weight, NN)
+    up_pre = matmul(full_normed2, up_weight, NN)
     hidden = (jax.nn.silu(gate_pre) * up_pre).astype(BF16)
     grad_hidden = matmul(grad_feed, w_down, NT)
     sigmoid_gate = jax.nn.sigmoid(gate_pre)
     grad_gate = grad_hidden * up_pre * sigmoid_gate * (1.0 + gate_pre * (1.0 - sigmoid_gate))
-    grad_up = grad_hidden * gate_pre * sigmoid_gate
-    grad_gate_up = jnp.concatenate([grad_gate, grad_up], 1).astype(BF16)
-    grad_normed2 = scatter_rows(matmul(grad_gate_up, feed_weight, NT))
+    grad_gate = grad_gate.astype(BF16)
+    grad_up = (grad_hidden * gate_pre * sigmoid_gate).astype(BF16)
+    early = (
+        matmul(full_normed2, grad_gate, TN).astype(BF16),
+        matmul(full_normed2, grad_up, TN).astype(BF16),
+        matmul(hidden, grad_feed, TN).astype(BF16),
+    )
+    grad_gate, grad_up, early, hidden = lax.optimization_barrier(
+        (grad_gate, grad_up, early, hidden)
+    )
+    grad_middle, grad_gain2, grad_mix, grad_mixed = feed_back(
+        grad_gate,
+        grad_up,
+        gate_weight,
+        up_weight,
+        cotangent,
+        middle,
+        live_own,
+        norm2_gain[None],
+        w_out,
+        count,
+    )
+    early = lax.psum(early, "dp")
+    hidden, grad_mixed, early = lax.optimization_barrier((hidden, grad_mixed, early))
     feed = scatter_rows(matmul(hidden, w_down, NN))
+    grad_mix = grad_mix.reshape(all_rows, features)
+    grad_wout = matmul(grad_mix, mixed, TN).astype(BF16)
+    dprojected, dtaps, dparams, dgain = mixer_backward(
+        longer, grad_mixed.reshape(all_rows, width), projected, saved, taps, params, gain_row
+    )
+    dprojected, feed = lax.optimization_barrier((dprojected, feed))
     layer_out = (middle + live_own * feed).astype(BF16)
-    grad_middle_part, grad_gain2 = pull_norm2(grad_normed2)
-    grad_middle = grad_top + grad_middle_part
-    grad_mix = gather_rows((live_own * grad_middle).astype(BF16))
-    grad_feed_weight = matmul(full_normed2, grad_gate_up, TN)
-    grad_down = matmul(hidden, grad_feed, TN)
-    grad_mixed = matmul(grad_mix, w_out, NT)
-    grad_wout = matmul(mixed, grad_mix, TN)
-    dprojected, dtaps, dparams, dgain = mixer_backward(
-        longer, grad_mixed, projected, saved, taps, params, gain_row
-    )
-    grad_normed1 = scatter_rows(matmul(dprojected, weight, NT))
-    grad_weight = matmul(full_normed1, dprojected, TN)
-    grad_input_part, grad_gain1 = pull_norm1(grad_normed1)
-    grad_in = grad_middle + grad_input_part
-    grad_conv = jnp.transpose(dtaps.reshape(4, 3, width), (1, 0, 2))
-    summed_ff = (
-        sum_replicas(grad_feed_weight.reshape(w_gate_up.shape)),
-        sum_replicas(grad_down),
-    )
-    summed_out = sum_replicas(grad_wout)
-    small = lax.psum(
-        (grad_conv, grad_weight[:, 4 * width : 4 * width + 2 * heads], dparams[:, :heads]), "dp"
-    )
-    gains = lax.psum((grad_gain1, grad_gain2, dgain[0]), ("dp", "heads"))
+
+    def row(values):
+        return jnp.pad(values, ((0, 0), (0, features - values.shape[1])))
+
+    small = jnp.concatenate(
+        [
+            jnp.zeros((1, features), F32),
+            grad_gain2,
+            row(dgain),
+            row(dtaps),
+            row(dparams.reshape(1, 256)),
+        ],
+        axis=0,
+    )
+    grad_in, small, grad_weight = input_back(
+        dprojected,
+        weight,
+        full_normed1,
+        grad_middle,
+        block_in,
+        norm1_gain[None],
+        small,
+        grad_wout,
+        count,
+        lax.axis_size("dp"),
+    )
+    cols = weight.shape[1]
+    grad_weight = grad_weight.reshape(features, -1)
+    grad_weight, grad_wout = grad_weight[:, :cols].astype(F32), grad_weight[:, cols:].T
     return (
         layer_out,
         grad_in,
-        gains[0],
-        sum_replicas(grad_weight[:, : 4 * width]).reshape(w_qkvg.shape),
         small[0],
-        small[1].reshape(w_gates.shape),
-        small[2],
-        gains[2],
-        summed_out,
-        gains[1],
-        summed_ff[0],
-        summed_ff[1],
+        grad_weight[:, : 4 * width].reshape(w_qkvg.shape),
+        jnp.transpose(small[3:7, : 3 * width].reshape(4, 3, width), (1, 0, 2)),
+        grad_weight[:, 4 * width : 4 * width + 2 * heads].reshape(w_gates.shape),
+        small[7, :256].reshape(2, 128)[:, :heads],
+        small[2, : out_gain.shape[0]],
+        grad_wout.astype(F32),
+        small[1],
+        jnp.stack([early[0], early[1]], axis=1).astype(F32),
+        early[2].astype(F32),
     )
 
 

time: 1650 us -> 1100 us (0.67)
  waiting for transfers between devices: 1170 us -> 104 us
  Pallas kernels: 152 us -> 796 us
  matrix products: 156 us -> 85.1 us
  blocking collectives: 57.1 us -> 0 us
  local copies, waits for them, and re-layouts: 36.9 us -> 70.9 us
  other arithmetic: 43.8 us -> 20.7 us
    pallas_call x0 -> x4, Pallas kernels: none -> 644 us  [the longest x1 192 us: feed_back(): pl.pallas_call(functools.partial(feed_back_kernel, count), out_shape=[jax...]
    reduce_scatter x4 -> x1, waiting for transfers between devices: 536 us -> 87.8 us  [scatter_rows(): lax.psum_scatter(values.astype(BF16), 'heads', scatter_dimension=0, tiled...]
    all_gather x4 -> x1, waiting for transfers between devices: 438 us -> 16.2 us  [gather_rows(): return lax.all_gather(values, 'heads', axis=0, tiled=True)]
    psum x1, waiting for transfers between devices: 200 us -> 0.02 us  [on_device(): early = lax.psum(early, 'dp')]
    dot_general x12 -> x8, matrix products: 156 us -> 85.1 us  [matmul(): lax.dot_general(left, right, (dims, ((), ())), preferred_element_type=F32)]
    psum x2 -> x0, blocking collectives: 57.1 us -> none  [the longest x1 43.2 us: on_device(): gains = lax.psum((grad_gain1, grad_gain2, dgain[0]), ('dp', 'heads'))]
  transfers between devices with their start and end apart: 9 -> 3, of which waited for: 9 -> 2; matrix products, arithmetic and copies ran while one was open for 7% -> 3% of each run, Pallas kernels for 0% -> 32%
where the time goes in v3:
time: 1100 us; the launch traced here: 1090 us
  Pallas kernels  796 us (72%)
  waiting for transfers between devices  104 us (9%)
  matrix products  85.1 us (8%)
  local copies, waits for them, and re-layouts  70.9 us (6%)
  other arithmetic  20.7 us (2%)
  between operations  15.6 us (1%)
    pallas_call x1, Pallas kernels, feed_back(): pl.pallas_call(functools.partial(feed_back_kernel, count), out_shape=[jax...  192 us
    pallas_call x1, Pallas kernels, branch_and_norm(): pl.pallas_call(functools.partial(branch_kernel, count), out_shape=[jax.Sh...  187 us
    pallas_call x1, Pallas kernels, input_back(): pl.pallas_call(functools.partial(input_back_kernel, count), out_shape=[ja...  167 us
    pallas_call x1, Pallas kernels, project(): pl.pallas_call(functools.partial(project_kernel, count), out_shape=[jax.S...  98.4 us
    pallas_call x1, Pallas kernels, mixer_forward(): pl.pallas_call(functools.partial(forward_kernel, heads), grid=(chunks,),...  95.8 us
    reduce_scatter x1, waiting for transfers between devices, scatter_rows(): lax.psum_scatter(values.astype(BF16), 'heads', scatter_dimension=0, tiled...  87.8 us
    dot_general x8, matrix products, matmul(): lax.dot_general(left, right, (dims, ((), ())), preferred_element_type=F32)  85.1 us
    pallas_call x1, Pallas kernels, mixer_backward(): pl.pallas_call(functools.partial(backward_kernel, heads, chunks), grid=(c...  56.4 us
  transfers between devices with their start and end apart: 3, of which 2 were waited for; matrix products, arithmetic and copies ran while one was open for 3% of the time, Pallas kernels for 32%

profile of v3, /device:TPU:1, one launch (start us, length us, event | category | flops | bytes accessed | tf_op | source)
XLA Modules:
  0.0 1092.8 jit_solution(11348584182355082258)
XLA Ops:
  7.2 0.0 copy-start.18
  7.2 0.0 all-gather.2.cloned.1.call-start
  7.2 1.3 fusion.10
  8.6 5.2 copy.43
  13.8 0.3 copy.33
  15.5 0.6 copy-done.20
  16.0 1.2 multiply_convert_fusion.3
  17.3 0.1 broadcast_in_dim.25
  17.3 7.9 concatenate.6.weight_ref
  25.2 98.4 %project.1 = (bf16[4,8,256,512]{3,2,1,0:T(8,128)(2,1)}, f32[8,256,1152]{2,1,0:T(8,128)}) custom-call(bf16[256,2048]{1,0:T(8,128)(2,1)} %input_ref.3, f32[1,2048]{1,0:T(1,128)} %bitcast.89, bf16[2048,1152]{1,0:T(8,128)(2,1)} %concatenate.6.weight_ref), custom_call_target="tpu_custom_call" | custom-call | flops 109999996928 | bytes 1048576 | tf_op jit(solution)/shard_map/project/pallas_call | solution.py:834
  123.6 0.0 all-gather.2.cloned.1.call-update
  123.6 0.0 all-reduce.7.cloned.1.call-start
  123.7 5.3 fusion.8
  128.9 4.8 copy.41
  133.7 2.8 copy.40
  136.6 0.7 fusion.5.live_ref
  137.3 95.8 %mixer_forward.1 = (bf16[2048,256]{1,0:T(8,128)(2,1)S(1)}, f32[2048,768]{1,0:T(8,128)}, f32[2048,256]{1,0:T(8,128)S(1)}, f32[2048,256]{1,0:T(8,128)}, f32[2,2048...) custom-call(s32[1]{0:T(128)} %bitcast.longer_ref, f32[2048,1152]{1,0:T(8,128)} %bitcast.91, f32[4,768]{1,0:T(4,128)S(1)} %bitcast.63, ...), custom_call_target="tpu_custom_call" | custom-call | flops 99999997952 | bytes 1048576 | tf_op jit(solution)/shard_map/mixer_forward/pallas_call | solution.py:302
  233.0 1.0 copy-done.7
  234.0 1.3 copy-done.9
  235.3 16.2 %all-gather.2.cloned.1.call-done = bf16[2048,2048]{1,0:T(8,128)(2,1)} async-done(((bf16[256,2048]{1,0:T(8,128)(2,1)}), bf16[2048,2048]{1,0:T(8,128)(2,1)}) %all-gather.2.cloned.1.call-update) | async-done | bytes 8388624 | tf_op jit(solution)/shard_map/all_gather | solution.py:1299
  251.5 186.7 %branch_and_norm.1 = (f32[256,2048]{1,0:T(8,128)}, bf16[8,256,2048]{2,1,0:T(8,128)(2,1)}) custom-call(bf16[8,256,256]{2,1,0:T(8,128)(2,1)} %bitcast.68, bf16[256,2048]{1,0:T(8,128)(2,1)} %out_weight_ref.1, bf16[256,2048]{1,0:T(8,128)(2,1)} %input_ref.3, f32[256,1]{1,0:T(8,128)} %fusion.5.live_ref, f32[1,2048]{1,0:T(1,128)} %bitcast.87), custom_call_target="tpu_custom_call" | custom-call | flops 198000001024 | bytes 1048576 | tf_op jit(solution)/shard_map/branch_and_norm/pallas_call | solution.py:929
  438.2 0.0 copy-start.25
  438.2 0.0 slice-start.1
  438.2 11.9 %fusion = f32[2048,704]{0,1:T(8,128)} fusion(bf16[2048,2048]{1,0:T(8,128)(2,1)} %bitcast.94, bf16[2048,2,704]{0,2,1:T(8,128)(2,1)} %param.23), kind=kOutput, calls=%fused_computation.10 | convolution fusion | flops 5905580032 | bytes 17039360 | tf_op jit(solution)/shard_map/dot_general | solution.py:1295
  450.2 8.0 fusion.11
  458.2 15.1 %multiply_convert_fusion = (bf16[2048,704]{0,1:T(8,128)(2,1)}, bf16[2048,704]{0,1:T(8,128)(2,1)S(1)}, bf16[2048,704]{0,1:T(8,128)(2,1)S(1)}) fusion(f32[2048,704]{0,1:T(8,128)} %fusion, f32[2048,704]{0,1:T(8,128)} %fusion.11, bf16[2048,2048]{1,0:T(8,128)(2,1)} %bitcast.95, bf16[2048,2,704]{0,2,1:T(8,128)(2,1)S(1)} %bitcast.73), kind=kOutput, calls=%fused_computation.2 | convolution fusion | flops 5928648704 | bytes 31457280 | tf_op jit(solution)/shard_map/dot_general | solution.py:1295
  473.3 13.1 %convolution_convert_fusion.2 = bf16[2048,704]{0,1:T(8,128)(2,1)} fusion(bf16[2048,704]{0,1:T(8,128)(2,1)S(1)} %get-tuple-element.59, bf16[2048,2048]{1,0:T(8,128)(2,1)} %bitcast.96), kind=kOutput, calls=%fused_computation.8 | convolution fusion | flops 5907021824 | bytes 14155776 | tf_op jit(solution)/shard_map/dot_general | solution.py:1295
  486.4 11.0 %convolution_convert_fusion.1 = bf16[2048,704]{0,1:T(8,128)(2,1)} fusion(bf16[2048,704]{0,1:T(8,128)(2,1)S(1)} %get-tuple-element.60, bf16[2048,2048]{1,0:T(8,128)(2,1)} %bitcast.97), kind=kOutput, calls=%fused_computation.7 | convolution fusion | flops 5907021824 | bytes 14155776 | tf_op jit(solution)/shard_map/dot_general | solution.py:1295
  497.4 7.6 convolution_convert_fusion.3
  504.9 4.6 copy.36
  509.5 4.6 copy.37
  514.1 0.0 all-reduce.7.cloned.1.call-update
  514.1 0.0 reduce-scatter.2.cloned.1.call-start
  514.2 192.4 %feed_back.1 = (f32[256,2048]{1,0:T(8,128)}, f32[1,2048]{1,0:T(1,128)}, bf16[8,256,2048]{2,1,0:T(8,128)(2,1)}, f32[8,256,256]{2,1,0:T(8,128)}) custom-call(bf16[8,256,704]{2,1,0:T(8,128)(2,1)} %bitcast.77, bf16[8,256,704]{2,1,0:T(8,128)(2,1)} %bitcast.78, bf16[2048,704]{1,0:T(8,128)(2,1)} %bitcast.75, bf16[2048,704]{1,0:T(8,128)(2,1)} %bitcast.76, ...), custom_call_target="tpu_custom_call" | custom-call | flops 198000001024 | bytes 1048576 | tf_op jit(solution)/shard_map/feed_back/pallas_call | solution.py:1003
  706.5 0.0 all-reduce.7.cloned.1.call-done
  706.6 11.5 %convolution_convert_fusion = bf16[2048,2048]{1,0:T(8,128)(2,1)} fusion(bf16[2048,704]{0,1:T(8,128)(2,1)} %get-tuple-element.72, bf16[704,2048]{1,0:T(8,128)(2,1)} %param.24), kind=kOutput, calls=%fused_computation | convolution fusion | flops 5909774336 | bytes 14155776 | tf_op jit(solution)/shard_map/dot_general | solution.py:1295
  718.0 0.0 copy-start.8
  718.0 0.0 reduce-scatter.2.cloned.1.call-update
  718.0 1.2 copy-done.8
  719.3 0.0 copy-start.10
  719.3 7.0 convolution_convert_fusion.4.wout_ref
  726.3 56.4 %mixer_backward.1 = (bf16[2048,1152]{1,0:T(8,128)(2,1)}, f32[4,768]{1,0:T(4,128)S(1)}, f32[2,128]{1,0:T(2,128)S(1)}, f32[1,128]{1,0:T(1,128)S(1)}) custom-call(s32[1]{0:T(128)} %bitcast.longer_ref, f32[2048,256]{1,0:T(8,128)S(1)} %bitcast.67, f32[2048,1152]{1,0:T(8,128)} %bitcast.92, f32[2048,768]{1,0:T(8,128)} %get-tuple-element.66.conv_out_ref, ...), custom_call_target="tpu_custom_call" | custom-call | flops 60000002048 | bytes 1048576 | tf_op jit(solution)/shard_map/mixer_backward/pallas_call | solution.py:345
  782.8 3.3 convert_element_type.90
  786.1 0.7 concatenate.7.small_ref
  786.8 7.0 maximum_convert_fusion
  793.8 87.8 %reduce-scatter.2.cloned.1.call-done = bf16[256,2048]{1,0:T(8,128)(2,1)} async-done(((bf16[2048,2048]{1,0:T(8,128)(2,1)}), bf16[256,2048]{1,0:T(8,128)(2,1)}) %reduce-scatter.2.cloned.1.call-update) | async-done | bytes 1048592 | tf_op jit(solution)/shard_map/reduce_scatter | solution.py:1303
  881.6 2.8 convert_element_type.83
  884.4 166.7 %input_back.1 = (f32[256,2048]{1,0:T(8,128)}, f32[8,2048]{1,0:T(8,128)}, bf16[4,512,1408]{2,1,0:T(8,128)(2,1)}) custom-call(bf16[8,256,1152]{2,1,0:T(8,128)(2,1)} %bitcast.98, bf16[2048,1152]{1,0:T(8,128)(2,1)} %concatenate.6.weight_ref, bf16[4,8,256,512]{3,2,1,0:T(8,128)(2,1)} %get-tuple-element.75.normed_ref, f32[256,2048]{1,0:T(8,128)} %get-tuple-element.76.later_ref, ...), custom_call_target="tpu_custom_call" | custom-call | flops 131999997952 | bytes 1048576 | tf_op jit(solution)/shard_map/input_back/pallas_call | solution.py:1267
  1051.2 1.5 fusion.9
  1052.7 1.3 slice.49
  1054.0 2.9 slice_convert_fusion
  1057.0 0.0 copy-start.12
  1057.0 4.9 slice.57
  1061.9 2.3 copy-done.11
  1064.2 1.3 slice.51
  1065.4 1.2 slice_bitcast_fusion
  1066.6 1.3 slice.59
  1067.9 1.2 add_convert_fusion
  1069.2 10.6 reshape.106
  1079.8 0.3 copy.38
  1080.1 0.7 reshape.108
  1080.8 0.6 copy.42
  1081.4 1.6 convert_bitcast_fusion
  1083.0 3.1 copy.48
  (62 shorter events, 0.2 us)
Async XLA Ops:
  7.2 6.7 copy-start.19
  7.2 8.9 copy-start.18
  7.2 244.3 %all-gather.2.cloned.1.call-start = ((), (), s32[]{:S(2)}) async-start(), calls=%async_computation.1 | async-start | bytes 9437184 | tf_op jit(solution)/shard_map/all_gather | solution.py:1299
  15.5 0.6 copy-start.20
  123.6 582.9 %all-reduce.7.cloned.1.call-start = ((), (), s32[]{:S(2)}) async-start(), calls=%async_computation.3 | async-start | bytes 17301504 | tf_op jit(solution)/shard_map/psum | solution.py:1387
  128.9 7.6 copy-start.23
  128.9 8.3 copy-start.2
  128.9 8.3 copy-start.4
  136.6 0.7 copy-start
  233.0 1.0 copy-start.7
  234.0 1.3 copy-start.9
  438.2 12.0 %copy-start.24 = (bf16[2048,2048]{1,0:T(8,128)(2,1)S(1)}, bf16[2048,2048]{1,0:T(8,128)(2,1)}, u32[]{:S(2)}) copy-start(bf16[2048,2048]{1,0:T(8,128)(2,1)} %all-gather.2.cloned.1.call-done) | copy-start | bytes 25165828
  438.2 11.9 %copy-start.25 = (bf16[704,2048]{1,0:T(8,128)(2,1)S(1)}, bf16[704,2048]{1,0:T(8,128)(2,1)}, u32[]{:S(2)}) copy-start(bf16[704,2048]{1,0:T(8,128)(2,1)} %param.24) | copy-start | bytes 8650756
  438.2 19.9 %slice-start.1 = ((s8[5767168]{0:T(1024)(128)(4,1)}), s8[4194304]{0:T(1024)(128)(4,1)S(1)}, s32[]{:S(2)}) async-start(s8[5767168]{0:T(1024)(128)(4,1)} %bitcast.72), calls=%async_computation.5 | async-start | bytes 8388608
  450.1 8.0 slice-start.2
  473.3 13.1 %copy-start.15 = (bf16[2048,704]{0,1:T(8,128)(2,1)}, bf16[2048,704]{0,1:T(8,128)(2,1)S(1)}, u32[]{:S(2)}) copy-start(bf16[2048,704]{0,1:T(8,128)(2,1)S(1)} %get-tuple-element.59) | copy-start | bytes 8650756
  473.3 13.1 %copy-start.14 = (bf16[2048,704]{0,1:T(8,128)(2,1)}, bf16[2048,704]{0,1:T(8,128)(2,1)S(1)}, u32[]{:S(2)}) copy-start(bf16[2048,704]{0,1:T(8,128)(2,1)S(1)} %get-tuple-element.60) | copy-start | bytes 8650756
  473.3 24.1 %slice-start.3 = ((s8[8388608]{0:T(1024)(128)(4,1)}), s8[4194304]{0:T(1024)(128)(4,1)S(1)}, s32[]{:S(2)}) async-start(s8[8388608]{0:T(1024)(128)(4,1)} %bitcast.85), calls=%async_computation.7 | async-start | bytes 8388608
  486.3 11.0 %slice-start.4 = ((s8[8388608]{0:T(1024)(128)(4,1)}), s8[4194304]{0:T(1024)(128)(4,1)S(1)}, s32[]{:S(2)}) async-start(s8[8388608]{0:T(1024)(128)(4,1)} %bitcast.85), calls=%async_computation.8 | async-start | bytes 8388608
  486.3 11.0 %copy-start.26 = (bf16[2048,704]{0,1:T(8,128)(2,1)S(1)}, bf16[2048,704]{0,1:T(8,128)(2,1)}, u32[]{:S(2)}) copy-start(bf16[2048,704]{0,1:T(8,128)(2,1)} %get-tuple-element.72) | copy-start | bytes 8650756
  514.1 367.5 %reduce-scatter.2.cloned.1.call-start = ((), (), s32[]{:S(2)}) async-start(), calls=%async_computation.2 | async-start | bytes 9437184 | tf_op jit(solution)/shard_map/reduce_scatter | solution.py:1303
  718.0 1.2 copy-start.8
  719.2 7.0 copy-start.1
  719.2 7.0 copy-start.3
  719.2 7.0 copy-start.5
  719.2 7.1 copy-start.6
  719.3 7.1 copy-start.10
  726.3 56.5 %copy-start.13 = (bf16[704,2048]{1,0:T(8,128)(2,1)S(1)}, bf16[704,2048]{1,0:T(8,128)(2,1)}, u32[]{:S(2)}) copy-start(bf16[704,2048]{1,0:T(8,128)(2,1)} %get-tuple-element.87) | copy-start | bytes 8650756
  782.8 3.4 copy-start.22
  782.8 4.1 copy-start.16
  1057.0 7.2 copy-start.11
  1057.0 10.9 %copy-start.12 = (f32[256,2048]{1,0:T(8,128)S(1)}, f32[256,2048]{1,0:T(8,128)}, u32[]{:S(2)}) copy-start(f32[256,2048]{1,0:T(8,128)} %convert_element_type.83) | copy-start | bytes 6291460
  1057.0 10.9 copy-start.17
  1057.0 10.9 copy-start.21
  1069.2 10.6 slice-start
Sparse Core Ops, SparseCore 0:
  123.7 127.7 all-gather.1
  514.2 163.0 all-reduce.6
  718.2 163.4 reduce-scatter.1

commit v4 on v3

--- a/solution.py
+++ b/solution.py
@@ -14,7 +14,7 @@
 BF16 = jnp.bfloat16
 LOW, MID, TOP = lax.Precision.DEFAULT, lax.Precision.HIGH, lax.Precision.HIGHEST
 NN, NT, TN = ((1,), (0,)), ((1,), (1,)), ((0,), (0,))
-P_INV, P_FWD, P_BWD = MID, MID, MID
+P_FWD, P_BWD = MID, MID
 
 
 def dot(left, right, dims, precision):
@@ -70,32 +70,53 @@
     return values * scale, scale
 
 
-def inverse(link, row, col):
+def pair_of(values):
+    high = values.astype(BF16)
+    return high, (values - high.astype(F32)).astype(BF16)
+
+
+def pair_dot(left, right):
+    def product(a, b):
+        return lax.dot_general(a, b, (NN, ((), ())), preferred_element_type=F32)
+
+    return product(left[0], right[0]) + (product(left[0], right[1]) + product(left[1], right[0]))
+
+
+def inverses(links, row, col):
     apart = row ^ col
-
-    def level(size):
-        return (apart >= size) & (apart < 2 * size)
-
-    out = jnp.where(row == col, 1.0, 0.0) - jnp.where(level(1), link, 0.0)
-    size = 2
-    while size < CHUNK // 2:
-        part = jnp.where(level(size), link, 0.0)
-        out = out - dot(out, dot(part, out, NN, P_INV), NN, P_INV)
-        size *= 2
-    half = CHUNK // 2
-    corner = dot(link[half:, :half], out[:half, :half], NN, P_INV)
-    corner = -dot(out[half:, half:], corner, NN, P_INV)
-    return jnp.concatenate(
-        [out[:half], jnp.concatenate([corner, out[half:, half:]], axis=1)], axis=0
-    )
+    size = links[0].shape[0]
+    outs = [jnp.where(row == col, 1.0, 0.0) - jnp.where(apart == 1, link, 0.0) for link in links]
+    pairs = [pair_of(link) for link in links]
+    step = 2
+    while step < size // 2:
+        level = (apart >= step) & (apart < 2 * step)
+        parts = [tuple(jnp.where(level, half, 0) for half in pair) for pair in pairs]
+        out_pairs = [pair_of(out) for out in outs]
+        inner = [pair_of(pair_dot(part, out)) for part, out in zip(parts, out_pairs)]
+        outs = [out - pair_dot(pair, mid) for out, pair, mid in zip(outs, out_pairs, inner)]
+        step *= 2
+    half = size // 2
+    uppers = [pair_of(out[:half, :half]) for out in outs]
+    lowers = [pair_of(out[half:, half:]) for out in outs]
+    corners = [tuple(each[half:, :half] for each in pair) for pair in pairs]
+    inner = [pair_of(pair_dot(corner, upper)) for corner, upper in zip(corners, uppers)]
+    corners = [pair_dot(lower, mid) for lower, mid in zip(lowers, inner)]
+    return [
+        jnp.concatenate(
+            [out[:half], jnp.concatenate([-corner, out[half:, half:]], axis=1)], axis=0
+        )
+        for out, corner in zip(outs, corners)
+    ]
 
 
 def forward_kernel(
-    heads, longer_ref, main_ref, conv_ref, params_ref, gain_ref,
-    mixed_ref, conv_out_ref, raw_ref, delta_ref, solve_ref, state_ref, state, tail_rows,
+    heads, count, chunks, longer_ref, main_ref, conv_ref, params_ref, gain_ref, top_ref, live_ref,
+    mixed_ref, conv_out_ref, raw_ref, delta_ref, solve_ref, state_ref, full_out,
+    state, tail_rows, *scratch
 ):
     step = pl.program_id(0)
     first_row = step * CHUNK
+    carry_along(step, chunks, count, top_ref, live_ref, full_out, scratch)
     longer = longer_ref[0]
     width = heads * HEAD
 
@@ -124,34 +145,102 @@
     masks = (row >= col, row > col)
     cumulative = dot(jnp.where(masks[0], 1.0, 0.0), log_decay, NN, TOP)
     cumulative_rows = jnp.transpose(cumulative)
-    for head in range(heads):
-        cols = slice(head * HEAD, (head + 1) * HEAD)
-        query = unit(active[:, head * HEAD : (head + 1) * HEAD])[0] * HEAD**-0.5
-        key = unit(active[:, width + head * HEAD : width + (head + 1) * HEAD])[0]
-        value = active[:, 2 * width + head * HEAD : 2 * width + (head + 1) * HEAD]
-        beta = lane_column(beta_all, heads + head)
-        ratio, decay_in, decay_out, decay_all = decays(cumulative, cumulative_rows, head, masks)
-        grams = dot(jnp.concatenate([key, query], axis=0), key, NT, P_FWD)
-        link = jnp.where(masks[1], beta * ratio * grams[:CHUNK], 0.0)
-        solve = inverse(link, row, col)
-        solve_ref[head] = solve
-        both = dot(
-            solve, jnp.concatenate([beta * value, (beta * decay_in) * key], axis=1), NN, P_FWD
-        )
-        entry = state[head] * keep
-        state_ref[0, head] = entry
-        carried = dot(
-            jnp.concatenate([both[:, HEAD:], decay_in * query], axis=0), entry, NT, P_FWD
-        )
-        delta = both[:, :HEAD] - carried[:CHUNK]
-        delta_ref[:, cols] = delta
-        raw = carried[CHUNK:] + dot(grams[CHUNK:] * ratio, delta, NN, P_FWD)
-        state[head] = decay_all * entry + dot(delta * decay_out, key, TN, P_FWD)
+    each = range(heads)
+    columns = [slice(head * HEAD, (head + 1) * HEAD) for head in each]
+    queries = [unit(active[:, cols])[0] * HEAD**-0.5 for cols in columns]
+    keys = [unit(active[:, width + head * HEAD : width + (head + 1) * HEAD])[0] for head in each]
+    values = [active[:, 2 * width + head * HEAD : 2 * width + (head + 1) * HEAD] for head in each]
+    betas = [lane_column(beta_all, heads + head) for head in each]
+    spans = [decays(cumulative, cumulative_rows, head, masks) for head in each]
+    grams = [
+        dot(jnp.concatenate([key, query], axis=0), key, NT, P_FWD)
+        for key, query in zip(keys, queries)
+    ]
+    links = [
+        jnp.where(masks[1], beta * span[0] * gram[:CHUNK], 0.0)
+        for beta, span, gram in zip(betas, spans, grams)
+    ]
+    solves = inverses(links, row, col)
+    boths = [
+        dot(
+            solve,
+            jnp.concatenate([beta * value, (beta * span[1]) * key], axis=1),
+            NN,
+            P_FWD,
+        )
+        for solve, beta, value, key, span in zip(solves, betas, values, keys, spans)
+    ]
+    entries = [state[head] * keep for head in each]
+    carried = [
+        dot(jnp.concatenate([both[:, HEAD:], span[1] * query], axis=0), entry, NT, P_FWD)
+        for both, span, query, entry in zip(boths, spans, queries, entries)
+    ]
+    deltas = [both[:, :HEAD] - carry[:CHUNK] for both, carry in zip(boths, carried)]
+    states = [
+        span[3] * entry + dot(delta * span[2], key, TN, P_FWD)
+        for span, entry, delta, key in zip(spans, entries, deltas, keys)
+    ]
+    raws = [
+        carry[CHUNK:] + dot(gram[CHUNK:] * span[0], delta, NN, P_FWD)
+        for carry, gram, span, delta in zip(carried, grams, spans, deltas)
+    ]
+    for head, cols in zip(each, columns):
+        solve_ref[head] = solves[head]
+        state_ref[0, head] = entries[head]
+        state[head] = states[head]
+        delta_ref[:, cols] = deltas[head]
+        raw = raws[head]
         raw_ref[:, cols] = raw
         scale = lax.rsqrt(jnp.mean(raw * raw, axis=-1, keepdims=True) + EPS)
         gate = main_ref[:, 3 * width + head * HEAD : 3 * width + (head + 1) * HEAD]
         mixed = raw * scale * gain_ref[...] * (gate * jax.nn.sigmoid(gate))
         mixed_ref[:, cols] = mixed.astype(mixed_ref.dtype)
+
+
+def carry_along(step, chunks, count, top_ref, live_ref, full_out, scratch):
+    *scratch, out_sems = scratch
+    full = scratch[0]
+    gather = gather_of(Group(count), GATHER_SHARE, scratch)
+
+    def out(piece):
+        rows = gather.rows(piece)
+        return pltpu.make_async_copy(full.at[:, rows], full_out.at[:, rows], out_sems.at[piece])
+
+    def begin(piece):
+        rows = gather.rows(piece)
+        full[lax.axis_index("heads"), rows] = (
+            live_ref[rows] * top_ref[rows].astype(F32)
+        ).astype(BF16)
+        gather.phase(piece, 0)
+
+    def end(piece):
+        gather.phase(piece, gather.last)
+        out(piece).start()
+
+    def tick(time, _):
+        during(time, begin)
+        for phase in range(1, gather.last):
+            during(time - phase, functools.partial(gather.phase, step=phase))
+        during(time - gather.last, end)
+        return 0
+
+    ticks = PIECES + gather.last
+
+    @pl.when(step == 0)
+    def _():
+        meet(count)
+
+    lax.fori_loop(step * ticks // chunks, (step + 1) * ticks // chunks, tick, 0)
+
+    @pl.when(step == chunks - 1)
+    def _():
+        gather.drain()
+
+        def finish(piece, _):
+            out(piece).wait()
+            return 0
+
+        lax.fori_loop(0, PIECES, finish, 0)
 
 
 def backward_kernel(
@@ -188,12 +277,10 @@
     cumulative_rows = jnp.transpose(cumulative)
     lane = grid_index((CHUNK, 128), 1)
     last_row = grid_index((CHUNK, 1), 0) == CHUNK - 1
-    dcumulative = jnp.zeros((CHUNK, 128), F32)
-    dbeta_all = jnp.zeros((CHUNK, 128), F32)
     gain = gain_ref[...]
-    dgain = jnp.zeros((1, HEAD), F32)
-    dconv_parts = [[], [], []]
-    for head in range(heads):
+    dgains, dlogs, dbetas, dparts = ([None] * heads for _ in range(4))
+
+    def work(head):
         cols = slice(head * HEAD, (head + 1) * HEAD)
         gate = main_ref[:, 3 * width + head * HEAD : 3 * width + (head + 1) * HEAD]
         raw = raw_ref[:, cols]
@@ -203,7 +290,7 @@
         sigmoid_gate = jax.nn.sigmoid(gate)
         gated = gate * sigmoid_gate
         product = grad * normed
-        dgain = dgain + jnp.sum(product * gated, axis=0, keepdims=True)
+        dgains[head] = jnp.sum(product * gated, axis=0, keepdims=True)
         dgate = product * gain * (sigmoid_gate * (1.0 + gate * (1.0 - sigmoid_gate)))
         dmain_ref[:, 3 * width + head * HEAD : 3 * width + (head + 1) * HEAD] = dgate.astype(
             dmain_ref.dtype
@@ -220,22 +307,32 @@
         delta = delta_ref[:, cols]
         dlater = dstate[head]
         gram = dot(query, key, NT, P_BWD) * ratio
+        yield
         key_dlater = dot(key, dlater, NT, P_BWD)
+        yield
         ddelta = dot(gram, draw, TN, P_BWD) + decay_out * key_dlater
+        yield
         dright = dot(solve_ref[head], ddelta, TN, P_BWD)
+        yield
         pairs = dot(jnp.concatenate([dright, draw], axis=0), delta, NT, P_BWD)
+        yield
         dlink = jnp.where(masks[1], -pairs[:CHUNK] * ratio, 0.0)
         dgram = pairs[CHUNK:] * ratio
         on_entry = dot(jnp.concatenate([dright, draw], axis=0), entry, NN, P_BWD)
+        yield
         key_entry = dot(key, entry, NT, P_BWD)
+        yield
         on_key = dot(jnp.concatenate([dlink, dgram], axis=0), key, NN, P_BWD)
+        yield
         dquery = decay_in * on_entry[CHUNK:] + on_key[CHUNK:]
         link_key = on_key[:CHUNK]
         key_read = beta * (link_key - decay_in * on_entry[:CHUNK])
         key_tail = decay_out * dot(delta, dlater, NN, P_BWD)
+        yield
         key_write = (
             dot(beta * dlink, key, TN, P_BWD) + dot(dgram, query, TN, P_BWD) + key_tail
         )
+        yield
         dkey = key_read + key_write
         dvalue = beta * dright
         dbeta = jnp.sum(
@@ -246,19 +343,29 @@
             jnp.sum(entry * dlater, axis=-1, keepdims=True), axis=0, keepdims=True
         ) + jnp.sum(jnp.sum(key * key_tail, axis=-1, keepdims=True), axis=0, keepdims=True)
         dlog = dlog + jnp.where(last_row, ending, 0.0)
-        dcumulative = jnp.where(lane == head, dlog, dcumulative)
-        dbeta_all = jnp.where(lane == heads + head, dbeta, dbeta_all)
+        dlogs[head], dbetas[head] = dlog, dbeta
         dstate[head] = keep * (
             decay_all * dlater
             + dot(decay_in * draw, query, TN, P_BWD)
             - dot((beta * decay_in) * dright, key, TN, P_BWD)
         )
+        yield
         dquery = (HEAD**-0.5 * query_scale) * (
             dquery - query_unit * jnp.sum(dquery * query_unit, axis=-1, keepdims=True)
         )
         dkey = key_scale * (dkey - key * jnp.sum(dkey * key, axis=-1, keepdims=True))
-        for kind, part in enumerate((dquery, dkey, dvalue)):
-            dconv_parts[kind].append(part)
+        dparts[head] = (dquery, dkey, dvalue)
+
+    works = [work(head) for head in range(heads)]
+    while works:
+        works = [each for each in works if next(each, "end") != "end"]
+    dcumulative = jnp.zeros((CHUNK, 128), F32)
+    dbeta_all = jnp.zeros((CHUNK, 128), F32)
+    for head in range(heads):
+        dcumulative = jnp.where(lane == head, dlogs[head], dcumulative)
+        dbeta_all = jnp.where(lane == heads + head, dbetas[head], dbeta_all)
+    dgain = functools.reduce(jnp.add, dgains)
+    dconv_parts = [[dparts[head][kind] for head in range(heads)] for kind in range(3)]
     dactive = jnp.concatenate([p for parts in dconv_parts for p in parts], axis=1)
     dconvolved = dactive * slope
     padded = jnp.concatenate([dconvolved, head_rows[...]], axis=0)
@@ -294,13 +401,15 @@
     return pl.BlockSpec(shape, lambda i: (0,) * len(shape))
 
 
-def mixer_forward(longer, main, conv, params, gain):
+def mixer_forward(longer, main, conv, params, gain, top, live, count):
     rows, width = main.shape[0], conv.shape[1] // 3
     heads, chunks = width // HEAD, rows // CHUNK
+    own, features = top.shape
+    nz, nx = grid_sizes(count)
     rowed = functools.partial(row_block, chunks=chunks, backward=False)
     shape = jax.ShapeDtypeStruct
     return pl.pallas_call(
-        functools.partial(forward_kernel, heads),
+        functools.partial(forward_kernel, heads, count, chunks),
         grid=(chunks,),
         in_specs=[
             pl.BlockSpec(memory_space=pltpu.SMEM),
@@ -308,6 +417,8 @@
             whole_block((4, 3 * width)),
             whole_block((2, 128)),
             whole_block((1, HEAD)),
+            whole_block((own, features)),
+            whole_block((own, 1)),
         ],
         out_specs=[
             rowed(width),
@@ -316,6 +427,7 @@
             rowed(width),
             pl.BlockSpec((heads, CHUNK, CHUNK), lambda i: (0, i, 0)),
             pl.BlockSpec((1, heads, HEAD, HEAD), lambda i: (i, 0, 0, 0)),
+            pl.BlockSpec(memory_space=pl.ANY),
         ],
         out_shape=[
             shape((rows, width), BF16),
@@ -324,17 +436,18 @@
             shape((rows, width), F32),
             shape((heads, rows, CHUNK), F32),
             shape((chunks, heads, HEAD, HEAD), F32),
+            shape((count, own, features), BF16),
         ],
         scratch_shapes=[
             pltpu.VMEM((heads, HEAD, HEAD), F32),
             pltpu.VMEM((8, 3 * width), F32),
-        ],
-        compiler_params=pltpu.CompilerParams(vmem_limit_bytes=48 * 2**20),
-        cost_estimate=pl.CostEstimate(
-            flops=10**11, bytes_accessed=2**20, transcendentals=0
-        ),
+            *gather_scratch(nz, nx, own, features),
+            pltpu.SemaphoreType.DMA((PIECES,)),
+        ],
+        compiler_params=linked(4),
+        cost_estimate=lasting(95),
         name="mixer_forward",
-    )(longer, main, conv, params, gain)
+    )(longer, main, conv, params, gain, top, live)
 
 
 def mixer_backward(longer, grad, main, saved, conv, params, gain):
@@ -896,12 +1009,22 @@
 
 
 def branch_kernel(
-    count, mixed_ref, weight_ref, input_ref, live_ref, gain_ref, middle_out, full_out, *scratch
+    count, mixed_ref, weight_ref, input_ref, live_ref, gain_ref, gate_weight_ref, up_weight_ref,
+    down_weight_ref, grad_ref, middle_out, full_out, dgate_out, dup_out, hidden_out, *scratch
 ):
+    *scratch, grads, grad_sems, dgate, dup, hidden, feed_sems = scratch
     group = Group(count)
     scatter = scatter_of(group, PAIR_SHARE, scratch[:SCATTER_COUNT])
     gather = gather_of(group, PAIR_SHARE, scratch[SCATTER_COUNT:-1])
     parts, full, out_sems = scratch[0], scratch[SCATTER_COUNT], scratch[-1]
+
+    def fetch(piece):
+        slot = piece % 2
+        return pltpu.make_async_copy(
+            grad_ref.at[:, gather.rows(piece)], grads.at[slot], grad_sems.at[slot]
+        )
+
+    fetch(0).start()
     meet(count)
 
     def prepare(piece):
@@ -918,31 +1041,79 @@
         middle_out[rows] = values
         return values * inverse_rms(values) * gain_ref[...]
 
-    sum_and_gather(
-        scatter, gather, full, full_out, out_sems, prepare, middle, lambda piece: None
-    )
-
-
-def branch_and_norm(mixed, weight, rows, live, gain, count):
+    def copies(piece):
+        rows = gather.rows(piece)
+        return [
+            pltpu.make_async_copy(ref.at[:, rows], out.at[:, rows], feed_sems.at[piece, index])
+            for index, (ref, out) in enumerate(
+                ((dgate, dgate_out), (dup, dup_out), (hidden, hidden_out))
+            )
+        ]
+
+    def ready(piece):
+        rows = gather.rows(piece)
+        fetch(piece).wait()
+        pl.when(piece + 1 < PIECES)(lambda: fetch(piece + 1).start())
+        left, grad = joined(full[:, rows]), joined(grads[piece % 2])
+        total = gate_weight_ref.shape[1]
+        for first in range(0, total, 256):
+            cols = slice(first, min(first + 256, total))
+
+            def product(a, b, dims):
+                return lax.dot_general(a, b, (dims, ((), ())), preferred_element_type=F32)
+
+            gate = product(left, gate_weight_ref[:, cols], NN)
+            up = product(left, up_weight_ref[:, cols], NN)
+            dhidden = product(grad, down_weight_ref[cols, :], NT)
+            sigmoid = jax.nn.sigmoid(gate)
+            active = gate * sigmoid
+            hidden[:, rows, cols] = split((active * up).astype(BF16), count)
+            dup[:, rows, cols] = split((dhidden * active).astype(BF16), count)
+            slope = sigmoid * (1.0 + gate * (1.0 - sigmoid))
+            dgate[:, rows, cols] = split((dhidden * up * slope).astype(BF16), count)
+        for copy in copies(piece):
+            copy.start()
+
+    sum_and_gather(scatter, gather, full, full_out, out_sems, prepare, middle, ready)
+
+    def finish(piece, _):
+        for copy in copies(piece):
+            copy.wait()
+        return 0
+
+    lax.fori_loop(0, PIECES, finish, 0)
+
+
+def branch_and_feed(
+    mixed, weight, rows, live, gain, gate_weight, up_weight, down_weight, grad, count
+):
     own, features = rows.shape
+    hidden = gate_weight.shape[1]
     nz, nx = grid_sizes(count)
     return pl.pallas_call(
         functools.partial(branch_kernel, count),
         out_shape=[
             jax.ShapeDtypeStruct((own, features), F32),
             jax.ShapeDtypeStruct((count, own, features), BF16),
-        ],
-        in_specs=[VMEM_SPEC] * 5,
-        out_specs=[VMEM_SPEC, ANY_SPEC],
+            *[jax.ShapeDtypeStruct((count, own, hidden), BF16)] * 3,
+        ],
+        in_specs=[VMEM_SPEC] * 8 + [ANY_SPEC],
+        out_specs=[VMEM_SPEC] + [ANY_SPEC] * 4,
         scratch_shapes=[
             *scatter_scratch(nz, nx, own, features, PAIR_SHARE),
             *gather_scratch(nz, nx, own, features),
             pltpu.SemaphoreType.DMA((PIECES,)),
+            pltpu.VMEM((2, count, own // PIECES, features), BF16),
+            pltpu.SemaphoreType.DMA((2,)),
+            *[pltpu.VMEM((count, own, hidden), BF16)] * 3,
+            pltpu.SemaphoreType.DMA((PIECES, 3)),
         ],
         compiler_params=linked(1),
         cost_estimate=lasting(180),
-        name="branch_and_norm",
-    )(split(mixed, count), weight, rows, live, gain)
+        name="branch_and_feed",
+    )(
+        split(mixed, count), weight, rows, live, gain, gate_weight, up_weight, down_weight, grad
+    )
 
 
 def feed_back_kernel(
@@ -1019,7 +1190,7 @@
         cost_estimate=lasting(180),
         name="feed_back",
     )(
-        split(dgate, count), split(dup, count), gate_weight, up_weight, top, middle, live, gain,
+        dgate, dup, gate_weight, up_weight, top, middle, live, gain,
         out_weight,
     )
 
@@ -1167,7 +1338,7 @@
 
 def input_back_kernel(
     count, grad_ref, weight_ref, normed_ref, later_ref, input_ref, gain_ref, small_ref,
-    wout_ref, grad_out, small_out, dweight_out, *scratch
+    wout_ref, grad_out, small_out, dmain_out, drest_out, *scratch
 ):
     parts, rest = scratch[0], scratch[SCATTER_COUNT:]
     values = rest[0]
@@ -1225,10 +1396,12 @@
         weight_share(replicas.core, replicas.line(k))
         replicas.cores(k)
 
-    order = range(replicas.lines - 1, -1, -1)
-    steps = [functools.partial(other_core, k) for k in order]
-    steps += [functools.partial(this_core, k) for k in order]
-    steps += [replicas.over_y, replicas.back]
+    steps = []
+    for k in range(replicas.lines - 1, -1, -1):
+        steps += [functools.partial(other_core, k), functools.partial(this_core, k)]
+    while len(steps) < PIECES - 1:
+        steps.append(lambda: None)
+    steps.append(replicas.over_y)
 
     def tick(time, _):
         during(time + 1, begin)
@@ -1240,12 +1413,20 @@
         return 0
 
     lax.fori_loop(-1, max(PIECES + scatter.last - 1, len(steps)), tick, 0)
+    replicas.back()
     copies = sum_small(small_out, near, near_send, near_recv, "heads", 3)
     copies += sum_small(small_out, far, far_send, far_recv, "dp", 8)
     replicas.home()
+    part = dmain_out.shape[3]
+    outs = []
+    for index, (total, share) in enumerate(replicas.totals()):
+        for kind in range(4):
+            outs.append((total.at[:, pl.ds(kind * part, part)], dmain_out.at[kind, share], index))
+        rest_cols = pl.ds(4 * part, drest_out.shape[2])
+        outs.append((total.at[:, rest_cols], drest_out.at[share], index))
     outs = [
-        pltpu.make_async_copy(total, dweight_out.at[share], out_sems.at[index])
-        for index, (total, share) in enumerate(replicas.totals())
+        pltpu.make_async_copy(source, target, out_sems.at[index, place % 5])
+        for place, (source, target, index) in enumerate(outs)
     ]
     for copy in outs:
         copy.start()
@@ -1262,17 +1443,19 @@
 ):
     own, features = rows.shape
     nz, nx = grid_sizes(count)
-    cols = weight.shape[1] + grad_wout.shape[1]
+    width, share = grad_wout.shape[1], features // replica_count
+    cols = weight.shape[1] + width
     dma = pltpu.SemaphoreType.DMA
     return pl.pallas_call(
         functools.partial(input_back_kernel, count),
         out_shape=[
             jax.ShapeDtypeStruct((own, features), F32),
             jax.ShapeDtypeStruct(small.shape, F32),
-            jax.ShapeDtypeStruct((replica_count, features // replica_count, cols), BF16),
+            jax.ShapeDtypeStruct((4, replica_count, share, width), BF16),
+            jax.ShapeDtypeStruct((replica_count, share, cols - 4 * width), BF16),
         ],
         in_specs=[VMEM_SPEC] * 8,
-        out_specs=[VMEM_SPEC, VMEM_SPEC, ANY_SPEC],
+        out_specs=[VMEM_SPEC, VMEM_SPEC, ANY_SPEC, ANY_SPEC],
         scratch_shapes=[
             *scatter_scratch(nz, nx, own, features, SCATTER_SHARE),
             *Replicas.scratch(features, cols, replica_count),
@@ -1283,7 +1466,7 @@
             dma((replica_count,)),
             dma((replica_count,)),
             pltpu.VMEM((features // replica_count, weight.shape[1]), BF16),
-            dma((replica_count,)),
+            dma((replica_count, 5)),
         ],
         compiler_params=linked(3),
         cost_estimate=lasting(120),
@@ -1295,14 +1478,8 @@
     return lax.dot_general(left, right, (dims, ((), ())), preferred_element_type=F32)
 
 
-def gather_rows(values):
-    return lax.all_gather(values, "heads", axis=0, tiled=True)
-
-
 def scatter_rows(values):
-    return lax.psum_scatter(
-        values.astype(BF16), "heads", scatter_dimension=0, tiled=True
-    ).astype(F32)
+    return lax.psum_scatter(values, "heads", scatter_dimension=0, tiled=True).astype(F32)
 
 
 def on_device(
@@ -1341,33 +1518,30 @@
     full_normed1, projected = project(
         block_in, norm1_gain[None], weight, count, lax.axis_size("dp")
     )
-    projected, grad_feed = lax.optimization_barrier(
-        (projected, (live_own * cotangent.astype(F32)).astype(BF16))
-    )
-    grad_feed = gather_rows(grad_feed)
     projected = projected.reshape(all_rows, -1)
     taps = jnp.transpose(conv_weight, (1, 0, 2)).reshape(4, 3 * width)
     params = jnp.pad(gate_params, ((0, 0), (0, 128 - heads)))
     gain_row = out_gain[None]
-    mixed, *saved = mixer_forward(longer, projected, taps, params, gain_row)
-    mixed, grad_feed = lax.optimization_barrier((mixed, grad_feed))
-    middle, full_normed2 = branch_and_norm(
-        mixed, w_out, block_in, live_own, norm2_gain[None], count
-    )
-    full_normed2 = full_normed2.reshape(all_rows, features)
+    mixed, *saved, grad_feed = mixer_forward(
+        longer, projected, taps, params, gain_row, cotangent, live_own, count
+    )
     gate_weight, up_weight = w_gate_up[:, 0], w_gate_up[:, 1]
-    gate_pre = matmul(full_normed2, gate_weight, NN)
-    up_pre = matmul(full_normed2, up_weight, NN)
-    hidden = (jax.nn.silu(gate_pre) * up_pre).astype(BF16)
-    grad_hidden = matmul(grad_feed, w_down, NT)
-    sigmoid_gate = jax.nn.sigmoid(gate_pre)
-    grad_gate = grad_hidden * up_pre * sigmoid_gate * (1.0 + gate_pre * (1.0 - sigmoid_gate))
-    grad_gate = grad_gate.astype(BF16)
-    grad_up = (grad_hidden * gate_pre * sigmoid_gate).astype(BF16)
+    middle, full_normed2, grad_gate, grad_up, hidden = branch_and_feed(
+        mixed,
+        w_out,
+        block_in,
+        live_own,
+        norm2_gain[None],
+        gate_weight,
+        up_weight,
+        w_down,
+        grad_feed,
+        count,
+    )
     early = (
-        matmul(full_normed2, grad_gate, TN).astype(BF16),
-        matmul(full_normed2, grad_up, TN).astype(BF16),
-        matmul(hidden, grad_feed, TN).astype(BF16),
+        matmul(joined(full_normed2), joined(grad_gate), TN).astype(BF16),
+        matmul(joined(full_normed2), joined(grad_up), TN).astype(BF16),
+        matmul(joined(hidden), joined(grad_feed), TN).astype(BF16),
     )
     grad_gate, grad_up, early, hidden = lax.optimization_barrier(
         (grad_gate, grad_up, early, hidden)
@@ -1386,13 +1560,14 @@
     )
     early = lax.psum(early, "dp")
     hidden, grad_mixed, early = lax.optimization_barrier((hidden, grad_mixed, early))
-    feed = scatter_rows(matmul(hidden, w_down, NN))
+    feed = matmul(joined(hidden), w_down, NN).astype(BF16)
+    feed, grad_mixed = lax.optimization_barrier((feed, grad_mixed))
+    feed = scatter_rows(feed)
     grad_mix = grad_mix.reshape(all_rows, features)
     grad_wout = matmul(grad_mix, mixed, TN).astype(BF16)
     dprojected, dtaps, dparams, dgain = mixer_backward(
         longer, grad_mixed.reshape(all_rows, width), projected, saved, taps, params, gain_row
     )
-    dprojected, feed = lax.optimization_barrier((dprojected, feed))
     layer_out = (middle + live_own * feed).astype(BF16)
 
     def row(values):
@@ -1408,7 +1583,7 @@
         ],
         axis=0,
     )
-    grad_in, small, grad_weight = input_back(
+    grad_in, small, grad_main, grad_rest = input_back(
         dprojected,
         weight,
         full_normed1,
@@ -1420,19 +1595,18 @@
         count,
         lax.axis_size("dp"),
     )
-    cols = weight.shape[1]
-    grad_weight = grad_weight.reshape(features, -1)
-    grad_weight, grad_wout = grad_weight[:, :cols].astype(F32), grad_weight[:, cols:].T
+    grad_main = grad_main.reshape(4, features, width)
+    grad_rest = grad_rest.reshape(features, -1)
     return (
         layer_out,
         grad_in,
         small[0],
-        grad_weight[:, : 4 * width].reshape(w_qkvg.shape),
+        jnp.transpose(grad_main, (1, 0, 2)).astype(F32),
         jnp.transpose(small[3:7, : 3 * width].reshape(4, 3, width), (1, 0, 2)),
-        grad_weight[:, 4 * width : 4 * width + 2 * heads].reshape(w_gates.shape),
+        grad_rest[:, : 2 * heads].reshape(w_gates.shape).astype(F32),
         small[7, :256].reshape(2, 128)[:, :heads],
         small[2, : out_gain.shape[0]],
-        grad_wout.astype(F32),
+        grad_rest[:, 128:].T.astype(F32),
         small[1],
         jnp.stack([early[0], early[1]], axis=1).astype(F32),
         early[2].astype(F32),

time: 1100 us -> 976 us (0.89)
  waiting for transfers between devices: 104 us -> 0.04 us
  matrix products: 85.1 us -> 45 us
  Pallas kernels: 796 us -> 831 us
  local copies, waits for them, and re-layouts: 70.9 us -> 55.7 us
    reduce_scatter x1, waiting for transfers between devices: 87.8 us -> 0.01 us  [scatter_rows(): lax.psum_scatter(values, 'heads', scatter_dimension=0, tiled=True)]
    dot_general x8 -> x5, matrix products: 85.1 us -> 45 us  [matmul(): lax.dot_general(left, right, (dims, ((), ())), preferred_element_type=F32)]
    pallas_call x1, Pallas kernels: 167 us -> 206 us  [input_back(): pl.pallas_call(functools.partial(input_back_kernel, count), out_shape=[ja...]
    pallas_call x2, Pallas kernels: 282 us -> 302 us  [the longest x1 186 us: branch_and_feed(): pl.pallas_call(functools.partial(branch_kernel, count), out_shape=[jax.Sh...]
    all_gather x1 -> x0, waiting for transfers between devices: 16.2 us -> none  [gather_rows(): return lax.all_gather(values, 'heads', axis=0, tiled=True)]
    convert_element_type x0 -> x2, local copies, waits for them, and re-layouts: none -> 15.9 us  [the longest x1 15.3 us: on_device(): jnp.transpose(grad_main, (1, 0, 2)).astype(F32)]
    pallas_call x1, Pallas kernels: 192 us -> 178 us  [feed_back(): pl.pallas_call(functools.partial(feed_back_kernel, count), out_shape=[jax...]
    reshape x2 -> x0, local copies, waits for them, and re-layouts: 11.3 us -> none  [the longest x1 10.6 us: on_device(): grad_weight[:, :4 * width].reshape(w_qkvg.shape)]
  transfers between devices with their start and end apart: 3 -> 2, of which waited for: 2 -> 0; matrix products, arithmetic and copies ran while one was open for 3% -> 5% of each run, Pallas kernels for 32% -> 45%
where the time goes in v4:
time: 976 us; the launch traced here: 966 us
  Pallas kernels  831 us (85%)
  local copies, waits for them, and re-layouts  55.7 us (6%)
  matrix products  45 us (5%)
  other arithmetic  18 us (2%)
  between operations  15.7 us (2%)
    pallas_call x1, Pallas kernels, input_back(): pl.pallas_call(functools.partial(input_back_kernel, count), out_shape=[ja...  206 us
    pallas_call x1, Pallas kernels, branch_and_feed(): pl.pallas_call(functools.partial(branch_kernel, count), out_shape=[jax.Sh...  186 us
    pallas_call x1, Pallas kernels, feed_back(): pl.pallas_call(functools.partial(feed_back_kernel, count), out_shape=[jax...  178 us
    pallas_call x1, Pallas kernels, mixer_forward(): pl.pallas_call(functools.partial(forward_kernel, heads, count, chunks), g...  116 us
    pallas_call x1, Pallas kernels, project(): pl.pallas_call(functools.partial(project_kernel, count), out_shape=[jax.S...  98.4 us
    pallas_call x1, Pallas kernels, mixer_backward(): pl.pallas_call(functools.partial(backward_kernel, heads, chunks), grid=(c...  46.7 us
    dot_general x5, matrix products, matmul(): lax.dot_general(left, right, (dims, ((), ())), preferred_element_type=F32)  45 us
  transfers between devices with their start and end apart: 2, of which 0 were waited for; matrix products, arithmetic and copies ran while one was open for 5% of the time, Pallas kernels for 45%

profile of v4, /device:TPU:1, one launch (start us, length us, event | category | flops | bytes accessed | tf_op | source)
XLA Modules:
  0.0 965.9 jit_solution(11921989792647806152)
XLA Ops:
  7.2 0.0 all-reduce.7.cloned.1.call-start
  7.2 1.3 fusion.4
  8.5 0.7 reshape.94
  9.3 0.3 copy.44
  9.6 0.0 copy-start.6
  9.6 5.4 copy.60
  15.0 0.0 copy-done.6
  15.0 2.3 fusion.2
  17.4 4.6 copy.57
  21.9 2.8 copy.56
  24.7 0.0 copy-done.14
  24.7 0.6 pad.16.params_ref
  26.6 0.7 fusion.1.live_ref
  27.3 0.1 broadcast_in_dim.25
  27.3 7.8 concatenate.6.weight_ref
  35.2 98.4 %project.1 = (bf16[4,8,256,512]{3,2,1,0:T(8,128)(2,1)}, f32[8,256,1152]{2,1,0:T(8,128)}) custom-call(bf16[256,2048]{1,0:T(8,128)(2,1)} %input_ref.3, f32[1,2048]{1,0:T(1,128)} %bitcast.83, bf16[2048,1152]{1,0:T(8,128)(2,1)} %concatenate.6.weight_ref), custom_call_target="tpu_custom_call" | custom-call | flops 109999996928 | bytes 1048576 | tf_op jit(solution)/shard_map/project/pallas_call | solution.py:947
  133.6 115.8 %mixer_forward.1 = (bf16[2048,256]{1,0:T(8,128)(2,1)}, f32[2048,768]{1,0:T(8,128)}, f32[2048,256]{1,0:T(8,128)}, f32[2048,256]{1,0:T(8,128)}, f32[2,2048,256]{2,...) custom-call(s32[1]{0:T(128)} %bitcast.longer_ref, f32[2048,1152]{1,0:T(8,128)} %bitcast.85, ...), custom_call_target="tpu_custom_call" | custom-call | flops 104500002816 | bytes 1048576 | tf_op jit(solution)/shard_map/mixer_forward/pallas_call | solution.py:411
  249.3 186.0 %branch_and_feed.1 = (f32[256,2048]{1,0:T(8,128)}, bf16[8,256,2048]{2,1,0:T(8,128)(2,1)}, bf16[8,256,704]{2,1,0:T(8,128)(2,1)}, bf16[8,256,704]{2,1,0:T(8,128)(2,1)}, bf16[8,256,704]{2,1,0:T(8,128)(2,1)}) custom-call(bf16[8,256,256]{2,1,0:T(8,128)(2,1)} %bitcast.90, bf16[256,2048]{1,0:T(8,128)(2,1)} %out_weight_ref.1, bf16[256,2048]{1,0:T(8,128)(2,1)} %input_ref.3, ...), custom_call_target="tpu_custom_call" | custom-call | flops 198000001024 | bytes 1048576 | tf_op jit(solution)/shard_map/branch_and_feed/pallas_call | solution.py:1093
  435.4 0.0 copy-start.16
  435.4 0.0 copy-start.17
  435.4 10.8 %bitcast_convert_fusion = bf16[704,2048]{1,0:T(8,128)(2,1)} fusion(bf16[8,256,704]{2,1,0:T(8,128)(2,1)} %get-tuple-element.66, bf16[8,256,2048]{2,1,0:T(8,128)(2,1)} %get-tuple-element.53.grad_ref), kind=kOutput, calls=%fused_computation.3 | convolution fusion | flops 5907021824 | bytes 14155776 | tf_op jit(solution)/shard_map/dot_general | solution.py:1478
  446.2 0.0 copy-done.16
  446.2 0.0 copy-done.17
  446.2 8.0 bitcast_convert_fusion.2
  454.2 0.0 copy-done.18
  454.2 7.8 bitcast_convert_fusion.1
  462.1 0.0 all-reduce.7.cloned.1.call-update
  462.1 0.0 reduce-scatter.2.cloned.1.call-start
  462.1 178.3 %feed_back.1 = (f32[256,2048]{1,0:T(8,128)}, f32[1,2048]{1,0:T(1,128)}, bf16[8,256,2048]{2,1,0:T(8,128)(2,1)}, f32[8,256,256]{2,1,0:T(8,128)}) custom-call(bf16[8,256,704]{2,1,0:T(8,128)(2,1)} %get-tuple-element.60.dgate_ref, bf16[8,256,704]{2,1,0:T(8,128)(2,1)} %get-tuple-element.61.dup_ref, bf16[2048,704]{1,0:T(8,128)(2,1)} %bitcast.72, ...), custom_call_target="tpu_custom_call" | custom-call | flops 198000001024 | bytes 1048576 | tf_op jit(solution)/shard_map/feed_back/pallas_call | solution.py:1174
  640.5 0.6 select_convert_fusion
  641.1 7.2 convolution_convert_fusion.1.wout_ref
  648.3 0.0 copy-done.15
  648.3 11.1 %convolution_convert_fusion = bf16[2048,2048]{1,0:T(8,128)(2,1)} fusion(bf16[2048,704]{1,0:T(8,128)(2,1)} %bitcast.89, bf16[704,2048]{1,0:T(8,128)(2,1)S(1)} %copy-done.15), kind=kOutput, calls=%fused_computation.1 | convolution fusion | flops 5909774336 | bytes 14155776 | tf_op jit(solution)/shard_map/dot_general | solution.py:1478
  659.4 0.0 copy-start.5
  659.4 0.0 reduce-scatter.2.cloned.1.call-update
  659.4 0.6 copy-done
  660.0 0.0 copy-done.1
  660.1 0.0 copy-done.2
  660.1 0.9 copy-done.3
  661.0 0.3 copy-done.5
  661.3 1.6 copy-done.4
  662.9 46.7 %mixer_backward.1 = (bf16[2048,1152]{1,0:T(8,128)(2,1)}, f32[4,768]{1,0:T(4,128)S(1)}, f32[2,128]{1,0:T(2,128)S(1)}, f32[1,128]{1,0:T(1,128)S(1)}) custom-call(s32[1]{0:T(128)} %bitcast.longer_ref, f32[2048,256]{1,0:T(8,128)S(1)} %bitcast.65, f32[2048,1152]{1,0:T(8,128)} %bitcast.86, f32[2048,768]{1,0:T(8,128)} %get-tuple-element.70.conv_out_ref, ...), custom_call_target="tpu_custom_call" | custom-call | flops 60000002048 | bytes 1048576 | tf_op jit(solution)/shard_map/mixer_backward/pallas_call | solution.py:458
  709.7 0.0 copy-done.12
  709.7 0.7 concatenate.7.small_ref
  710.4 206.0 %input_back.1 = (f32[256,2048]{1,0:T(8,128)}, f32[8,2048]{1,0:T(8,128)}, bf16[4,4,512,256]{3,2,1,0:T(8,128)(2,1)}, bf16[4,512,384]{2,1,0:T(8,128)(2,1)}) custom-call(bf16[8,256,1152]{2,1,0:T(8,128)(2,1)} %bitcast.88, bf16[2048,1152]{1,0:T(8,128)(2,1)} %concatenate.6.weight_ref, bf16[4,8,256,512]{3,2,1,0:T(8,128)(2,1)} %get-tuple-element.76.normed_ref, ...), custom_call_target="tpu_custom_call" | custom-call | flops 131999997952 | bytes 1048576 | tf_op jit(solution)/shard_map/input_back/pallas_call | solution.py:1449
  916.4 1.3 slice.43
  917.7 1.3 slice.41
  919.0 1.3 slice.49
  920.3 1.1 slice_convert_fusion
  921.4 0.3 copy.61
  921.8 0.6 copy.59
  922.4 0.6 reshape.105
  923.1 5.3 convert_element_type.86
  928.3 0.0 copy-done.7
  928.3 1.0 bitcast_convert_fusion.3
  929.3 0.0 copy-start.8
  929.4 15.3 %copy.63 = f32[4,2048,256]{2,0,1:T(4,128)} copy(f32[4,2048,256]{2,1,0:T(8,128)S(1)} %bitcast_convert_fusion.3) | data formatting | bytes 16777216 | tf_op jit(solution)/shard_map/convert_element_type | solution.py:1604
  944.6 1.2 slice_bitcast_fusion
  945.8 1.5 fusion.3
  947.4 5.2 maximum_convert_fusion
  952.5 1.6 convert_bitcast_fusion
  954.1 0.8 copy-done.10
  954.9 2.6 add_convert_fusion
  957.5 1.3 copy.68
  (24 shorter events, 0.1 us)
Async XLA Ops:
  7.2 641.1 %all-reduce.7.cloned.1.call-start = ((), (), s32[]{:S(2)}) async-start(), calls=%async_computation.2 | async-start | bytes 17301504 | tf_op jit(solution)/shard_map/psum | solution.py:1561
  9.6 5.4 copy-start.6
  21.9 2.8 copy-start.14
  435.4 10.9 %copy-start.16 = (bf16[8,256,2048]{2,1,0:T(8,128)(2,1)S(1)}, bf16[8,256,2048]{2,1,0:T(8,128)(2,1)}, u32[]{:S(2)}) copy-start(bf16[8,256,2048]{2,1,0:T(8,128)(2,1)} %get-tuple-element.57) | copy-start | bytes 25165828
  435.4 10.9 %copy-start.17 = (bf16[8,256,704]{2,1,0:T(8,128)(2,1)S(1)}, bf16[8,256,704]{2,1,0:T(8,128)(2,1)}, u32[]{:S(2)}) copy-start(bf16[8,256,704]{2,1,0:T(8,128)(2,1)} %get-tuple-element.60.dgate_ref) | copy-start | bytes 8650756
  446.2 8.0 copy-start.18
  462.1 492.0 %reduce-scatter.2.cloned.1.call-start = ((), (), s32[]{:S(2)}) async-start(), calls=%async_computation.1 | async-start | bytes 9437184 | tf_op jit(solution)/shard_map/reduce_scatter | solution.py:1482
  641.1 7.2 copy-start.15
  659.4 0.7 copy-start
  659.4 0.7 copy-start.1
  659.4 0.7 copy-start.2
  659.4 1.6 copy-start.3
  659.4 1.9 copy-start.5
  661.3 1.6 copy-start.4
  662.9 46.8 %copy-start.12 = (f32[1,2048]{1,0:T(1,128)S(1)}, f32[1,2048]{1,0:T(1,128)}, u32[]{:S(2)}) copy-start(f32[1,2048]{1,0:T(1,128)} %get-tuple-element.78) | copy-start | bytes 24580
  923.1 5.3 copy-start.7
  929.3 18.0 %copy-start.8 = (bf16[2048,704]{0,1:T(8,128)(2,1)S(1)}, bf16[2048,704]{0,1:T(8,128)(2,1)}, u32[]{:S(2)}) copy-start(bf16[2048,704]{0,1:T(8,128)(2,1)} %get-tuple-element.87) | copy-start | bytes 8650756
  929.3 18.0 %copy-start.9 = (bf16[2048,704]{0,1:T(8,128)(2,1)S(1)}, bf16[2048,704]{0,1:T(8,128)(2,1)}, u32[]{:S(2)}) copy-start(bf16[2048,704]{0,1:T(8,128)(2,1)} %get-tuple-element.88) | copy-start | bytes 8650756
  952.5 2.3 copy-start.10
  952.5 2.3 copy-start.13
  954.9 2.7 copy-start.11
Sparse Core Ops, SparseCore 0:
  462.2 177.4 all-reduce.6
  659.5 226.8 reduce-scatter.1

commit v5 on v4

--- a/solution.py
+++ b/solution.py
@@ -116,7 +116,8 @@
 ):
     step = pl.program_id(0)
     first_row = step * CHUNK
-    carry_along(step, chunks, count, top_ref, live_ref, full_out, scratch)
+    run, close = gather_along(step, chunks, count, top_ref, live_ref, full_out, scratch)
+    run(2 * step)
     longer = longer_ref[0]
     width = heads * HEAD
 
@@ -161,6 +162,7 @@
         for beta, span, gram in zip(betas, spans, grams)
     ]
     solves = inverses(links, row, col)
+    run(2 * step + 1)
     boths = [
         dot(
             solve,
@@ -195,9 +197,21 @@
         gate = main_ref[:, 3 * width + head * HEAD : 3 * width + (head + 1) * HEAD]
         mixed = raw * scale * gain_ref[...] * (gate * jax.nn.sigmoid(gate))
         mixed_ref[:, cols] = mixed.astype(mixed_ref.dtype)
-
-
-def carry_along(step, chunks, count, top_ref, live_ref, full_out, scratch):
+    pl.when(step == chunks - 1)(close)
+
+
+def spread_ticks(tick, first, ticks, halves):
+    def run(half):
+        def one(index, _):
+            tick(first + index)
+            return 0
+
+        lax.fori_loop(half * ticks // halves, (half + 1) * ticks // halves, one, 0)
+
+    return run
+
+
+def gather_along(step, chunks, count, top_ref, live_ref, full_out, scratch):
     *scratch, out_sems = scratch
     full = scratch[0]
     gather = gather_of(Group(count), GATHER_SHARE, scratch)
@@ -217,23 +231,13 @@
         gather.phase(piece, gather.last)
         out(piece).start()
 
-    def tick(time, _):
+    def tick(time):
         during(time, begin)
         for phase in range(1, gather.last):
             during(time - phase, functools.partial(gather.phase, step=phase))
         during(time - gather.last, end)
-        return 0
-
-    ticks = PIECES + gather.last
-
-    @pl.when(step == 0)
-    def _():
-        meet(count)
-
-    lax.fori_loop(step * ticks // chunks, (step + 1) * ticks // chunks, tick, 0)
-
-    @pl.when(step == chunks - 1)
-    def _():
+
+    def close():
         gather.drain()
 
         def finish(piece, _):
@@ -242,14 +246,49 @@
 
         lax.fori_loop(0, PIECES, finish, 0)
 
+    pl.when(step == 0)(functools.partial(meet, count))
+    return spread_ticks(tick, 0, PIECES + gather.last, 2 * chunks), close
+
+
+def scatter_along(step, chunks, count, hidden_ref, weight_ref, middle_ref, live_ref, out, scratch):
+    parts = scratch[0]
+    scatter = scatter_of(Group(count), SCATTER_SHARE, scratch)
+
+    def begin(piece):
+        rows = scatter.rows(piece)
+
+        def store(cols, value):
+            parts[:, rows, cols] = split(value.astype(BF16), count)
+
+        wide_dot([(joined(hidden_ref[:, rows]), weight_ref)], NN, 512, store)
+        scatter.phase(piece, 0)
+
+    def end(piece):
+        total = scatter.phase(piece, scatter.last)
+        rows = scatter.rows(piece)
+        out[rows] = (middle_ref[rows] + live_ref[rows] * total).astype(BF16)
+
+    def tick(time):
+        during(time + 1, begin)
+        for phase in range(1, scatter.last):
+            during(time - phase + 1, functools.partial(scatter.phase, step=phase))
+        during(time - scatter.last + 1, end)
+
+    pl.when(step == 0)(functools.partial(meet, count))
+    return spread_ticks(tick, -1, PIECES + scatter.last, 2 * chunks), scatter.drain
+
 
 def backward_kernel(
-    heads, chunks, longer_ref, grad_ref, main_ref, conv_out_ref, raw_ref, delta_ref,
-    solve_ref, state_ref, conv_ref, params_ref, gain_ref,
-    dmain_ref, dconv_ref, dparams_ref, dgain_ref, dstate, head_rows,
+    heads, chunks, count, longer_ref, grad_ref, main_ref, conv_out_ref, raw_ref, delta_ref,
+    solve_ref, state_ref, conv_ref, params_ref, gain_ref, hidden_ref, down_ref, middle_ref, live_ref,
+    dmain_ref, dconv_ref, dparams_ref, dgain_ref, layer_ref, dstate, head_rows, *scratch
 ):
     step = pl.program_id(0)
     first_row = (chunks - 1 - step) * CHUNK
+    run, close = scatter_along(
+        step, chunks, count, hidden_ref, down_ref, middle_ref, live_ref, layer_ref, scratch
+    )
+    run(2 * step)
     longer = longer_ref[0]
     width = heads * HEAD
 
@@ -357,8 +396,12 @@
         dparts[head] = (dquery, dkey, dvalue)
 
     works = [work(head) for head in range(heads)]
+    turns = 0
     while works:
         works = [each for each in works if next(each, "end") != "end"]
+        turns += 1
+        if turns == 6:
+            run(2 * step + 1)
     dcumulative = jnp.zeros((CHUNK, 128), F32)
     dbeta_all = jnp.zeros((CHUNK, 128), F32)
     for head in range(heads):
@@ -389,6 +432,7 @@
         dmain_ref.dtype
     )
     dgain_ref[...] += dgain
+    pl.when(step == chunks - 1)(close)
 
 
 def row_block(width, chunks, backward):
@@ -450,13 +494,17 @@
     )(longer, main, conv, params, gain, top, live)
 
 
-def mixer_backward(longer, grad, main, saved, conv, params, gain):
+def mixer_backward(
+    longer, grad, main, saved, conv, params, gain, hidden, down_weight, middle, live, count
+):
     rows, width = main.shape[0], conv.shape[1] // 3
     heads, chunks = width // HEAD, rows // CHUNK
+    own, features = middle.shape
+    nz, nx = grid_sizes(count)
     rowed = functools.partial(row_block, chunks=chunks, backward=True)
     shape = jax.ShapeDtypeStruct
     return pl.pallas_call(
-        functools.partial(backward_kernel, heads, chunks),
+        functools.partial(backward_kernel, heads, chunks, count),
         grid=(chunks,),
         in_specs=[
             pl.BlockSpec(memory_space=pltpu.SMEM),
@@ -470,29 +518,36 @@
             whole_block((4, 3 * width)),
             whole_block((2, 128)),
             whole_block((1, HEAD)),
+            whole_block(hidden.shape),
+            whole_block(down_weight.shape),
+            whole_block((own, features)),
+            whole_block((own, 1)),
         ],
         out_specs=[
             rowed(4 * width + 128),
             whole_block((4, 3 * width)),
             whole_block((2, 128)),
             whole_block((1, HEAD)),
+            whole_block((own, features)),
         ],
         out_shape=[
             shape((rows, 4 * width + 128), BF16),
             shape((4, 3 * width), F32),
             shape((2, 128), F32),
             shape((1, HEAD), F32),
+            shape((own, features), BF16),
         ],
         scratch_shapes=[
             pltpu.VMEM((heads, HEAD, HEAD), F32),
             pltpu.VMEM((8, 3 * width), F32),
+            *scatter_scratch(nz, nx, own, features, SCATTER_SHARE),
         ],
-        compiler_params=pltpu.CompilerParams(vmem_limit_bytes=48 * 2**20),
-        cost_estimate=pl.CostEstimate(
-            flops=6 * 10**10, bytes_accessed=2**20, transcendentals=0
-        ),
+        compiler_params=linked(5),
+        cost_estimate=lasting(100),
         name="mixer_backward",
-    )(longer, grad, main, *saved, conv, params, gain)
+    )(
+        longer, grad, main, *saved, conv, params, gain, hidden, down_weight, middle, live
+    )
 
 
 MESH = pl.DeviceIdType.MESH
@@ -857,7 +912,7 @@
 
 VMEM_SPEC = pl.BlockSpec(memory_space=pltpu.VMEM)
 ANY_SPEC = pl.BlockSpec(memory_space=pl.ANY)
-PAIR_SHARE, GATHER_SHARE, SCATTER_SHARE = 3, 1, 2
+PAIR_SHARE, GATHER_SHARE, SCATTER_SHARE = 2, 1, 2
 
 
 def lasting(microseconds):
@@ -880,7 +935,9 @@
     return values.reshape(parts, values.shape[0] // parts, values.shape[1])
 
 
-def project_kernel(count, rows_ref, gain_ref, weight_ref, full_out, projected_out, *scratch):
+def project_kernel(
+    count, rows_ref, gain_ref, weight_ref, gates_ref, full_out, projected_out, *scratch
+):
     full, staged, full_sems, staged_sems = scratch[0], *scratch[GATHER_COUNT:]
     group = Group(count)
     gather = gather_of(group, GATHER_SHARE, scratch[:GATHER_COUNT])
@@ -918,7 +975,12 @@
         def store(cols, value):
             staged[:, rows, cols] = split(value, count)
 
-        wide_dot([(joined(full[:, rows]), weight_ref)], NN, 256, store)
+        left = joined(full[:, rows])
+        wide_dot([(left, weight_ref)], NN, 256, store)
+        value = lax.dot_general(
+            left, gates_ref[...], (NN, ((), ())), preferred_element_type=F32
+        )
+        staged[:, rows, weight_ref.shape[1] :] = split(value, count)
         staged_copy(piece).start()
 
     def tick(time, _):
@@ -940,9 +1002,9 @@
     lax.fori_loop(0, PIECES, finish, 0)
 
 
-def project(rows, gain, weight, count, shares):
+def project(rows, gain, weight, gates, count, shares):
     own, features = rows.shape
-    cols = weight.shape[1]
+    cols = weight.shape[1] + gates.shape[1]
     nz, nx = grid_sizes(count)
     return pl.pallas_call(
         functools.partial(project_kernel, count),
@@ -950,7 +1012,7 @@
             jax.ShapeDtypeStruct((shares, count, own, features // shares), BF16),
             jax.ShapeDtypeStruct((count, own, cols), F32),
         ],
-        in_specs=[VMEM_SPEC] * 3,
+        in_specs=[VMEM_SPEC] * 4,
         out_specs=[ANY_SPEC] * 2,
         scratch_shapes=[
             *gather_scratch(nz, nx, own, features),
@@ -961,15 +1023,11 @@
         compiler_params=linked(0),
         cost_estimate=lasting(100),
         name="project",
-    )(rows, gain, weight)
-
-
-def sum_and_gather(scatter, gather, full, full_out, out_sems, prepare, middle, ready):
+    )(rows, gain, weight, gates)
+
+
+def sum_and_gather(scatter, gather, full, prepare, middle, ready, job=None):
     own = lax.axis_index("heads")
-
-    def out(piece):
-        rows = gather.rows(piece)
-        return pltpu.make_async_copy(full.at[:, rows], full_out.at[:, rows], out_sems.at[piece])
 
     def begin(piece):
         prepare(piece)
@@ -982,11 +1040,12 @@
 
     def end(piece):
         gather.phase(piece, gather.last)
-        out(piece).start()
         ready(piece)
 
     def tick(time, _):
         during(time + 1, begin)
+        if job is not None:
+            job(time + 1)
         for step in range(1, scatter.last):
             during(time - step + 1, functools.partial(scatter.phase, step=step))
         during(time - scatter.last + 1, turn)
@@ -1001,12 +1060,6 @@
     scatter.drain()
     gather.drain()
 
-    def finish(piece, _):
-        out(piece).wait()
-        return 0
-
-    lax.fori_loop(0, PIECES, finish, 0)
-
 
 def branch_kernel(
     count, mixed_ref, weight_ref, input_ref, live_ref, gain_ref, gate_weight_ref, up_weight_ref,
@@ -1015,8 +1068,8 @@
     *scratch, grads, grad_sems, dgate, dup, hidden, feed_sems = scratch
     group = Group(count)
     scatter = scatter_of(group, PAIR_SHARE, scratch[:SCATTER_COUNT])
-    gather = gather_of(group, PAIR_SHARE, scratch[SCATTER_COUNT:-1])
-    parts, full, out_sems = scratch[0], scratch[SCATTER_COUNT], scratch[-1]
+    gather = gather_of(group, PAIR_SHARE, scratch[SCATTER_COUNT:])
+    parts, full = scratch[0], scratch[SCATTER_COUNT]
 
     def fetch(piece):
         slot = piece % 2
@@ -1046,7 +1099,7 @@
         return [
             pltpu.make_async_copy(ref.at[:, rows], out.at[:, rows], feed_sems.at[piece, index])
             for index, (ref, out) in enumerate(
-                ((dgate, dgate_out), (dup, dup_out), (hidden, hidden_out))
+                ((dgate, dgate_out), (dup, dup_out), (hidden, hidden_out), (full, full_out))
             )
         ]
 
@@ -1074,7 +1127,7 @@
         for copy in copies(piece):
             copy.start()
 
-    sum_and_gather(scatter, gather, full, full_out, out_sems, prepare, middle, ready)
+    sum_and_gather(scatter, gather, full, prepare, middle, ready)
 
     def finish(piece, _):
         for copy in copies(piece):
@@ -1102,11 +1155,10 @@
         scratch_shapes=[
             *scatter_scratch(nz, nx, own, features, PAIR_SHARE),
             *gather_scratch(nz, nx, own, features),
-            pltpu.SemaphoreType.DMA((PIECES,)),
             pltpu.VMEM((2, count, own // PIECES, features), BF16),
             pltpu.SemaphoreType.DMA((2,)),
             *[pltpu.VMEM((count, own, hidden), BF16)] * 3,
-            pltpu.SemaphoreType.DMA((PIECES, 3)),
+            pltpu.SemaphoreType.DMA((PIECES, 4)),
         ],
         compiler_params=linked(1),
         cost_estimate=lasting(180),
@@ -1116,16 +1168,75 @@
     )
 
 
+TILE = 256
+
+
+class TileJob:
+    def __init__(self, rows_ref, tile, factors, staged, outs, fetch_sem, out_sems):
+        self.rows_ref, self.tile, self.factors = rows_ref, tile, factors
+        self.staged, self.outs = staged, outs
+        self.fetch_sem, self.out_sems = fetch_sem, out_sems
+        self.count = rows_ref.shape[2] // TILE
+
+    def span(self, index):
+        return pl.ds(pl.multiple_of(index * TILE, TILE), TILE)
+
+    def fetch(self, index):
+        return pltpu.make_async_copy(
+            self.rows_ref.at[:, :, self.span(index)], self.tile, self.fetch_sem
+        )
+
+    def results(self, index):
+        return [
+            pltpu.make_async_copy(
+                self.staged.at[which], out.at[self.span(index)], self.out_sems.at[which]
+            )
+            for which, out in enumerate(self.outs)
+        ]
+
+    def wait_results(self, index):
+        for copy in self.results(index):
+            copy.wait()
+
+    def run(self, index):
+        self.fetch(index).wait()
+        left = joined(self.tile[...])
+        pl.when(index > 0)(lambda: self.wait_results(index - 1))
+        for which, factor in enumerate(self.factors):
+            self.staged[which] = lax.dot_general(
+                left, joined(factor[...]), (TN, ((), ())), preferred_element_type=F32
+            ).astype(BF16)
+        for copy in self.results(index):
+            copy.start()
+        pl.when(index + 1 < self.count)(lambda: self.fetch(index + 1).start())
+
+
 def feed_back_kernel(
     count, dgate_ref, dup_ref, gate_weight_ref, up_weight_ref, top_ref, middle_ref, live_ref,
-    gain_ref, out_weight_ref, dmiddle_out, dgain_out, full_out, dmixed_out, *scratch
+    gain_ref, out_weight_ref, mixed_ref, hidden_ref, normed_ref, grad_feed_ref,
+    dmiddle_out, dgain_out, dmixed_out, dweight_out, dgate_weight, dup_weight, ddown_weight,
+    *scratch
 ):
+    *scratch, total_out, tile, grad_tile, staged, grad_staged, fetch_sems, out_sems = scratch
     group = Group(count)
     scatter = scatter_of(group, PAIR_SHARE, scratch[:SCATTER_COUNT])
-    gather = gather_of(group, PAIR_SHARE, scratch[SCATTER_COUNT:-1])
-    parts, full, out_sems = scratch[0], scratch[SCATTER_COUNT], scratch[-1]
+    gather = gather_of(group, PAIR_SHARE, scratch[SCATTER_COUNT:])
+    parts, full = scratch[0], scratch[SCATTER_COUNT]
+    jobs = (
+        TileJob(
+            normed_ref, tile, (dgate_ref, dup_ref), staged, (dgate_weight, dup_weight),
+            fetch_sems.at[0], out_sems.at[0],
+        ),
+        TileJob(
+            grad_feed_ref, grad_tile, (hidden_ref,), grad_staged, (ddown_weight,),
+            fetch_sems.at[1], out_sems.at[1],
+        ),
+    )
+    for each in jobs:
+        each.fetch(0).start()
     meet(count)
     dgain_out[...] = jnp.zeros(dgain_out.shape, F32)
+    total_out[...] = jnp.zeros(total_out.shape, F32)
 
     def prepare(piece):
         rows = gather.rows(piece)
@@ -1158,40 +1269,66 @@
 
     def ready(piece):
         rows = gather.rows(piece)
+        left, mixed = joined(full[:, rows]), joined(mixed_ref[:, rows])
 
         def store(cols, value):
             dmixed_out[:, rows, cols] = split(value, count)
 
-        wide_dot([(joined(full[:, rows]), out_weight_ref)], NT, 256, store)
-
-    sum_and_gather(scatter, gather, full, full_out, out_sems, prepare, middle, ready)
-
-
-def feed_back(dgate, dup, gate_weight, up_weight, top, middle, live, gain, out_weight, count):
+        wide_dot([(left, out_weight_ref)], NT, 256, store)
+        for first in range(0, left.shape[1], 256):
+            total_out[first : first + 256] += lax.dot_general(
+                left[:, first : first + 256], mixed, (TN, ((), ())), preferred_element_type=F32
+            )
+
+    def job(time):
+        for which, each in enumerate(jobs):
+            pl.when((time % 2 == which) & (time < 2 * each.count))(
+                functools.partial(each.run, time // 2)
+            )
+
+    sum_and_gather(scatter, gather, full, prepare, middle, ready, job)
+    last = PIECES + scatter.last + gather.last
+    lax.fori_loop(last, max(2 * jobs[0].count, last), lambda time, _: (job(time), 0)[1], 0)
+    for each in jobs:
+        each.wait_results(each.count - 1)
+    dweight_out[...] = total_out[...].astype(BF16)
+
+
+def feed_back(
+    dgate, dup, gate_weight, up_weight, top, middle, live, gain, out_weight, mixed, hidden,
+    normed, grad_feed, count,
+):
     own, features = middle.shape
     nz, nx = grid_sizes(count)
-    width = out_weight.shape[0]
+    width, units = out_weight.shape[0], gate_weight.shape[1]
     return pl.pallas_call(
         functools.partial(feed_back_kernel, count),
         out_shape=[
             jax.ShapeDtypeStruct((own, features), F32),
             jax.ShapeDtypeStruct((1, features), F32),
-            jax.ShapeDtypeStruct((count, own, features), BF16),
             jax.ShapeDtypeStruct((count, own, width), F32),
+            jax.ShapeDtypeStruct((features, width), BF16),
+            *[jax.ShapeDtypeStruct((features, units), BF16)] * 3,
         ],
-        in_specs=[VMEM_SPEC] * 9,
-        out_specs=[VMEM_SPEC, VMEM_SPEC, ANY_SPEC, VMEM_SPEC],
+        in_specs=[VMEM_SPEC] * 11 + [ANY_SPEC] * 2,
+        out_specs=[VMEM_SPEC] * 4 + [ANY_SPEC] * 3,
         scratch_shapes=[
             *scatter_scratch(nz, nx, own, features, PAIR_SHARE),
             *gather_scratch(nz, nx, own, features),
-            pltpu.SemaphoreType.DMA((PIECES,)),
+            pltpu.VMEM((features, width), F32),
+            pltpu.VMEM((count, own, TILE), BF16),
+            pltpu.VMEM((count, own, TILE), BF16),
+            pltpu.VMEM((2, TILE, units), BF16),
+            pltpu.VMEM((1, TILE, units), BF16),
+            pltpu.SemaphoreType.DMA((2,)),
+            pltpu.SemaphoreType.DMA((2, 2)),
         ],
         compiler_params=linked(2),
         cost_estimate=lasting(180),
         name="feed_back",
     )(
-        dgate, dup, gate_weight, up_weight, top, middle, live, gain,
-        out_weight,
+        dgate, dup, gate_weight, up_weight, top, middle, live, gain, out_weight,
+        split(mixed, count), hidden, normed, grad_feed,
     )
 
 
@@ -1337,7 +1474,7 @@
 
 
 def input_back_kernel(
-    count, grad_ref, weight_ref, normed_ref, later_ref, input_ref, gain_ref, small_ref,
+    count, grad_ref, weight_ref, gates_ref, normed_ref, later_ref, input_ref, gain_ref, small_ref,
     wout_ref, grad_out, small_out, dmain_out, drest_out, *scratch
 ):
     parts, rest = scratch[0], scratch[SCATTER_COUNT:]
@@ -1356,7 +1493,10 @@
         def store(cols, value):
             parts[:, rows, cols] = split(value.astype(BF16), count)
 
-        wide_dot([(joined(grad_ref[:, rows]), weight_ref)], NT, 256, store)
+        left, edge = joined(grad_ref[:, rows]), weight_ref.shape[1]
+        wide_dot(
+            [(left[:, :edge], weight_ref), (left[:, edge:], gates_ref)], NT, 256, store
+        )
         scatter.phase(piece, 0)
 
     def end(piece):
@@ -1439,12 +1579,12 @@
 
 
 def input_back(
-    grad, weight, normed, later, rows, gain, small, grad_wout, count, replica_count
+    grad, weight, gates, normed, later, rows, gain, small, grad_wout, count, replica_count
 ):
     own, features = rows.shape
     nz, nx = grid_sizes(count)
     width, share = grad_wout.shape[1], features // replica_count
-    cols = weight.shape[1] + width
+    cols = grad.shape[1] + width
     dma = pltpu.SemaphoreType.DMA
     return pl.pallas_call(
         functools.partial(input_back_kernel, count),
@@ -1454,7 +1594,7 @@
             jax.ShapeDtypeStruct((4, replica_count, share, width), BF16),
             jax.ShapeDtypeStruct((replica_count, share, cols - 4 * width), BF16),
         ],
-        in_specs=[VMEM_SPEC] * 8,
+        in_specs=[VMEM_SPEC] * 9,
         out_specs=[VMEM_SPEC, VMEM_SPEC, ANY_SPEC, ANY_SPEC],
         scratch_shapes=[
             *scatter_scratch(nz, nx, own, features, SCATTER_SHARE),
@@ -1465,21 +1605,30 @@
             pltpu.VMEM((replica_count, *small.shape), F32),
             dma((replica_count,)),
             dma((replica_count,)),
-            pltpu.VMEM((features // replica_count, weight.shape[1]), BF16),
+            pltpu.VMEM((share, grad.shape[1]), BF16),
             dma((replica_count, 5)),
         ],
         compiler_params=linked(3),
         cost_estimate=lasting(120),
         name="input_back",
-    )(split(grad, count), weight, normed, later, rows, gain, small, grad_wout)
-
-
-def matmul(left, right, dims):
-    return lax.dot_general(left, right, (dims, ((), ())), preferred_element_type=F32)
-
-
-def scatter_rows(values):
-    return lax.psum_scatter(values, "heads", scatter_dimension=0, tiled=True).astype(F32)
+    )(split(grad, count), weight, gates, normed, later, rows, gain, small, grad_wout)
+
+
+def spread_kernel(given_ref, out_ref):
+    for kind in range(given_ref.shape[0]):
+        out_ref[:, kind, :] = given_ref[kind].astype(F32)
+
+
+def by_rows(values):
+    kinds, rows, cols = values.shape
+    return pl.pallas_call(
+        spread_kernel,
+        grid=(rows // 256,),
+        in_specs=[pl.BlockSpec((kinds, 256, cols), lambda i: (0, i, 0))],
+        out_specs=pl.BlockSpec((256, kinds, cols), lambda i: (i, 0, 0)),
+        out_shape=jax.ShapeDtypeStruct((rows, kinds, cols), F32),
+        name="by_rows",
+    )(values)
 
 
 def on_device(
@@ -1507,16 +1656,12 @@
     row_index = first_row + jnp.arange(own_rows, dtype=jnp.int32)
     live_own = jnp.where(longer[0] > 0, True, row_index < seq_counts[0, 0] * SEQ_SHORT)
     live_own = live_own.astype(F32)[:, None]
-    weight = jnp.concatenate(
-        [
-            w_qkvg.reshape(features, 4 * width),
-            w_gates.reshape(features, 2 * heads),
-            jnp.zeros((features, 128 - 2 * heads), BF16),
-        ],
-        axis=1,
+    weight = w_qkvg.reshape(features, 4 * width)
+    gates_weight = jnp.pad(
+        w_gates.reshape(features, 2 * heads), ((0, 0), (0, 128 - 2 * heads))
     )
     full_normed1, projected = project(
-        block_in, norm1_gain[None], weight, count, lax.axis_size("dp")
+        block_in, norm1_gain[None], weight, gates_weight, count, lax.axis_size("dp")
     )
     projected = projected.reshape(all_rows, -1)
     taps = jnp.transpose(conv_weight, (1, 0, 2)).reshape(4, 3 * width)
@@ -1538,15 +1683,7 @@
         grad_feed,
         count,
     )
-    early = (
-        matmul(joined(full_normed2), joined(grad_gate), TN).astype(BF16),
-        matmul(joined(full_normed2), joined(grad_up), TN).astype(BF16),
-        matmul(joined(hidden), joined(grad_feed), TN).astype(BF16),
-    )
-    grad_gate, grad_up, early, hidden = lax.optimization_barrier(
-        (grad_gate, grad_up, early, hidden)
-    )
-    grad_middle, grad_gain2, grad_mix, grad_mixed = feed_back(
+    grad_middle, grad_gain2, grad_mixed, grad_wout, *early = feed_back(
         grad_gate,
         grad_up,
         gate_weight,
@@ -1556,19 +1693,27 @@
         live_own,
         norm2_gain[None],
         w_out,
+        mixed,
+        hidden,
+        full_normed2,
+        grad_feed,
         count,
     )
-    early = lax.psum(early, "dp")
-    hidden, grad_mixed, early = lax.optimization_barrier((hidden, grad_mixed, early))
-    feed = matmul(joined(hidden), w_down, NN).astype(BF16)
-    feed, grad_mixed = lax.optimization_barrier((feed, grad_mixed))
-    feed = scatter_rows(feed)
-    grad_mix = grad_mix.reshape(all_rows, features)
-    grad_wout = matmul(grad_mix, mixed, TN).astype(BF16)
-    dprojected, dtaps, dparams, dgain = mixer_backward(
-        longer, grad_mixed.reshape(all_rows, width), projected, saved, taps, params, gain_row
-    )
-    layer_out = (middle + live_own * feed).astype(BF16)
+    early = lax.optimization_barrier(lax.psum(lax.optimization_barrier(early), "dp"))
+    dprojected, dtaps, dparams, dgain, layer_out = mixer_backward(
+        longer,
+        grad_mixed.reshape(all_rows, width),
+        projected,
+        saved,
+        taps,
+        params,
+        gain_row,
+        hidden,
+        w_down,
+        middle,
+        live_own,
+        count,
+    )
 
     def row(values):
         return jnp.pad(values, ((0, 0), (0, features - values.shape[1])))
@@ -1586,6 +1731,7 @@
     grad_in, small, grad_main, grad_rest = input_back(
         dprojected,
         weight,
+        gates_weight,
         full_normed1,
         grad_middle,
         block_in,
@@ -1601,7 +1747,7 @@
         layer_out,
         grad_in,
         small[0],
-        jnp.transpose(grad_main, (1, 0, 2)).astype(F32),
+        by_rows(grad_main),
         jnp.transpose(small[3:7, : 3 * width].reshape(4, 3, width), (1, 0, 2)),
         grad_rest[:, : 2 * heads].reshape(w_gates.shape).astype(F32),
         small[7, :256].reshape(2, 128)[:, :heads],
@@ -1609,7 +1755,7 @@
         grad_rest[:, 128:].T.astype(F32),
         small[1],
         jnp.stack([early[0], early[1]], axis=1).astype(F32),
-        early[2].astype(F32),
+        early[2].T.astype(F32),
     )
 
 

time: 976 us -> 1010 us (1.035)
  Pallas kernels: 831 us -> 914 us
  matrix products: 45 us -> 0 us
    pallas_call x1 -> x2, Pallas kernels: 46.7 us -> 137 us  [the longest x1 129 us: mixer_backward(): pl.pallas_call(functools.partial(backward_kernel, heads, chunks, count),...]
    dot_general x5 -> x0, matrix products: 45 us -> none  [matmul(): lax.dot_general(left, right, (dims, ((), ())), preferred_element_type=F32)]
    unnamed x44 -> x21, local copies, waits for them, and re-layouts: 19.3 us -> 35.6 us
    convert_element_type x1 -> x0, local copies, waits for them, and re-layouts: 15.3 us -> none  [on_device(): jnp.transpose(grad_main, (1, 0, 2)).astype(F32)]
    pallas_call x1, Pallas kernels: 186 us -> 172 us  [branch_and_feed(): pl.pallas_call(functools.partial(branch_kernel, count), out_shape=[jax.Sh...]
  transfers between devices with their start and end apart: 2 -> 1, of which waited for: 0 -> 0; matrix products, arithmetic and copies ran while one was open for 5% -> 1% of each run, Pallas kernels for 45% -> 34%
where the time goes in v5:
time: 1010 us; the launch traced here: 999 us
  Pallas kernels  914 us (90%)
  local copies, waits for them, and re-layouts  53.8 us (5%)
  between operations  15.9 us (2%)
  other arithmetic  14.8 us (1%)
    pallas_call x1, Pallas kernels, input_back(): pl.pallas_call(functools.partial(input_back_kernel, count), out_shape=[ja...  203 us
    pallas_call x1, Pallas kernels, feed_back(): pl.pallas_call(functools.partial(feed_back_kernel, count), out_shape=[jax...  188 us
    pallas_call x1, Pallas kernels, branch_and_feed(): pl.pallas_call(functools.partial(branch_kernel, count), out_shape=[jax.Sh...  172 us
    pallas_call x1, Pallas kernels, mixer_backward(): pl.pallas_call(functools.partial(backward_kernel, heads, chunks, count),...  129 us
    pallas_call x1, Pallas kernels, mixer_forward(): pl.pallas_call(functools.partial(forward_kernel, heads, count, chunks), g...  116 us
    pallas_call x1, Pallas kernels, project(): pl.pallas_call(functools.partial(project_kernel, count), out_shape=[jax.S...  98.3 us
    unnamed x21, local copies, waits for them, and re-layouts  35.6 us
  transfers between devices with their start and end apart: 1, of which 0 were waited for; matrix products, arithmetic and copies ran while one was open for 1% of the time, Pallas kernels for 34%

profile of v5, /device:TPU:1, one launch (start us, length us, event | category | flops | bytes accessed | tf_op | source)
XLA Modules:
  0.0 998.8 jit_solution(15027606701266941946)
XLA Ops:
  7.2 0.0 all-reduce.8.cloned.1.call-start
  7.2 1.3 fusion.4
  8.5 0.0 copy-start.3
  8.5 5.3 copy.51
  13.8 0.0 copy-done.3
  13.8 0.3 copy.40
  14.1 5.0 fusion.2
  19.2 4.6 copy.47
  23.7 0.0 copy-start.5
  23.7 2.8 copy.48
  27.8 0.9 pad.20.gates_ref
  28.7 0.0 copy-done.5
  28.7 0.6 pad.21.params_ref
  29.3 0.7 fusion.1.live_ref
  30.0 98.3 %project.1 = (bf16[4,8,256,512]{3,2,1,0:T(8,128)(2,1)}, f32[8,256,1152]{2,1,0:T(8,128)}) custom-call(bf16[256,2048]{1,0:T(8,128)(2,1)} %input_ref.3, f32[1,2048]{1,0:T(1,128)} %bitcast.60, bf16[2048,1024]{1,0:T(8,128)(2,1)} %bitcast.41, bf16[2048,128]{1,0:T(8,128)(2,1)} %pad.20.gates_ref), custom_call_target="tpu_custom_call" | custom-call | flops 109999996928 | bytes 1048576 | tf_op jit(solution)/shard_map/project/pallas_call | solution.py:1009
  128.3 115.9 %mixer_forward.1 = (bf16[2048,256]{1,0:T(8,128)(2,1)}, f32[2048,768]{1,0:T(8,128)}, f32[2048,256]{1,0:T(8,128)}, f32[2048,256]{1,0:T(8,128)}, f32[2,2048,256]{2,...) custom-call(s32[1]{0:T(128)} %bitcast.longer_ref, f32[2048,1152]{1,0:T(8,128)} %bitcast.64, ...), custom_call_target="tpu_custom_call" | custom-call | flops 104500002816 | bytes 1048576 | tf_op jit(solution)/shard_map/mixer_forward/pallas_call | solution.py:455
  244.3 171.8 %branch_and_feed.1 = (f32[256,2048]{1,0:T(8,128)}, bf16[8,256,2048]{2,1,0:T(8,128)(2,1)}, bf16[8,256,704]{2,1,0:T(8,128)(2,1)}, bf16[8,256,704]{2,1,0:T(8,128)(2,1)}, bf16[8,256,704]{2,1,0:T(8,128)(2,1)}) custom-call(bf16[8,256,256]{2,1,0:T(8,128)(2,1)} %bitcast.68, bf16[256,2048]{1,0:T(8,128)(2,1)} %out_weight_ref.1, bf16[256,2048]{1,0:T(8,128)(2,1)} %input_ref.3, ...), custom_call_target="tpu_custom_call" | custom-call | flops 198000001024 | bytes 1048576 | tf_op jit(solution)/shard_map/branch_and_feed/pallas_call | solution.py:1146
  416.0 188.0 %feed_back.1 = (f32[256,2048]{1,0:T(8,128)}, f32[1,2048]{1,0:T(1,128)}, f32[8,256,256]{2,1,0:T(8,128)}, bf16[2048,256]{1,0:T(8,128)(2,1)}, bf16[2048,704]{1,0:T(...) custom-call(bf16[8,256,704]{2,1,0:T(8,128)(2,1)} %get-tuple-element.51.dgate_ref, ...), custom_call_target="tpu_custom_call" | custom-call | flops 198000001024 | bytes 1048576 | tf_op jit(solution)/shard_map/feed_back/pallas_call | solution.py:1304
  604.1 0.0 all-reduce.8.cloned.1.call-update
  604.1 0.0 copy-start.4
  604.1 128.9 %mixer_backward.1 = (bf16[2048,1152]{1,0:T(8,128)(2,1)}, f32[4,768]{1,0:T(4,128)}, f32[2,128]{1,0:T(2,128)}, f32[1,128]{1,0:T(1,128)}, bf16[256,2048]{1,0:T(8,128)(2,1)}) custom-call(s32[1]{0:T(128)} %bitcast.longer_ref, f32[2048,256]{1,0:T(8,128)} %bitcast.67, f32[2048,1152]{1,0:T(8,128)} %bitcast.65, f32[2048,768]{1,0:T(8,128)} %get-tuple-element.57.conv_out_ref, ...), custom_call_target="tpu_custom_call" | custom-call | flops 109999996928 | bytes 1048576 | tf_op jit(solution)/shard_map/mixer_backward/pallas_call | solution.py:506
  733.1 0.7 pad.23
  733.8 0.6 pad.22
  734.4 0.7 pad.24
  735.1 0.0 copy-done.4
  735.1 0.7 concatenate.3.small_ref
  735.8 203.0 %input_back.1 = (f32[256,2048]{1,0:T(8,128)}, f32[8,2048]{1,0:T(8,128)}, bf16[4,4,512,256]{3,2,1,0:T(8,128)(2,1)}, bf16[4,512,384]{2,1,0:T(8,128)(2,1)}) custom-call(bf16[8,256,1152]{2,1,0:T(8,128)(2,1)} %bitcast.66, bf16[2048,1024]{1,0:T(8,128)(2,1)} %bitcast.42, bf16[2048,128]{1,0:T(8,128)(2,1)} %pad.20.gates_ref, ...), custom_call_target="tpu_custom_call" | custom-call | flops 131999997952 | bytes 1048576 | tf_op jit(solution)/shard_map/input_back/pallas_call | solution.py:1589
  938.8 1.3 slice.41
  940.2 1.3 slice.43
  941.4 8.2 by_rows.1
  949.6 1.3 slice.49
  950.9 0.6 copy.50
  951.6 1.1 slice_convert_fusion
  952.7 0.3 copy.52
  953.0 0.7 reshape.92
  953.7 1.2 slice_bitcast_fusion
  954.9 1.5 fusion.3
  956.4 1.6 convert_bitcast_fusion.1
  958.0 0.0 all-reduce.8.cloned.1.call-done
  958.0 8.3 maximum_convert_fusion
  966.3 0.0 copy-start
  966.3 12.3 %copy.45 = f32[2048,2,704]{0,2,1:T(8,128)} copy(f32[2048,2,704]{2,0,1:T(8,128)} %maximum_convert_fusion) | data formatting | bytes 23068672
  978.6 0.0 copy-done
  978.6 3.1 convert_bitcast_fusion
  981.8 0.0 copy-start.2
  981.8 6.4 copy.46
  988.2 0.0 copy-start.1
  988.2 0.0 copy-done.2
  988.2 1.0 copy.58
  989.2 1.0 copy-done.1
  990.2 1.3 copy.59
  (2 shorter events, 0.0 us)
Async XLA Ops:
  7.2 950.8 %all-reduce.8.cloned.1.call-start = ((), (), s32[]{:S(2)}) async-start(), calls=%async_computation | async-start | bytes 18874368 | tf_op jit(solution)/shard_map/psum | solution.py:1702
  8.5 5.3 copy-start.3
  23.7 5.0 copy-start.5
  604.1 131.0 %copy-start.4 = (f32[1,2048]{1,0:T(1,128)S(1)}, f32[1,2048]{1,0:T(1,128)}, u32[]{:S(2)}) copy-start(f32[1,2048]{1,0:T(1,128)} %get-tuple-element.66) | copy-start | bytes 24580
  966.3 12.3 %copy-start = (bf16[2048,704]{1,0:T(8,128)(2,1)S(1)}, bf16[2048,704]{1,0:T(8,128)(2,1)}, u32[]{:S(2)}) copy-start(bf16[2048,704]{1,0:T(8,128)(2,1)} %get-tuple-element.83) | copy-start | bytes 8650756
  981.8 6.4 copy-start.2
  988.2 2.0 copy-start.1
Sparse Core Ops, SparseCore 0:
  604.2 205.7 all-reduce.7

commit v6 on v5

--- a/solution.py
+++ b/solution.py
@@ -1,4 +1,5 @@
 import functools
+import math
 import jax
 import jax.numpy as jnp
 from jax import lax
@@ -214,28 +215,25 @@
 def gather_along(step, chunks, count, top_ref, live_ref, full_out, scratch):
     *scratch, out_sems = scratch
     full = scratch[0]
-    gather = gather_of(Group(count), GATHER_SHARE, scratch)
+    group = Group(count)
+    gather = gather_of(group, GATHER_SHARE, scratch)
 
     def out(piece):
         rows = gather.rows(piece)
-        return pltpu.make_async_copy(full.at[:, rows], full_out.at[:, rows], out_sems.at[piece])
-
-    def begin(piece):
+        return pltpu.make_async_copy(
+            full.at[:, :, rows], full_out.at[:, :, rows], out_sems.at[piece]
+        )
+
+    def prepare(piece):
         rows = gather.rows(piece)
-        full[lax.axis_index("heads"), rows] = (
-            live_ref[rows] * top_ref[rows].astype(F32)
-        ).astype(BF16)
-        gather.phase(piece, 0)
-
-    def end(piece):
-        gather.phase(piece, gather.last)
-        out(piece).start()
+        full[group.z, group.x, rows] = (live_ref[rows] * top_ref[rows].astype(F32)).astype(BF16)
+
+    before, within, behind = gather_ticks(gather, prepare, lambda piece: out(piece).start())
 
     def tick(time):
-        during(time, begin)
-        for phase in range(1, gather.last):
-            during(time - phase, functools.partial(gather.phase, step=phase))
-        during(time - gather.last, end)
+        before(time)
+        at_each_z(group, functools.partial(within, time))
+        behind(time)
 
     def close():
         gather.drain()
@@ -252,27 +250,27 @@
 
 def scatter_along(step, chunks, count, hidden_ref, weight_ref, middle_ref, live_ref, out, scratch):
     parts = scratch[0]
-    scatter = scatter_of(Group(count), SCATTER_SHARE, scratch)
-
-    def begin(piece):
+    group = Group(count)
+    scatter = scatter_of(group, SCATTER_SHARE, scratch)
+
+    def prepare(piece):
         rows = scatter.rows(piece)
 
         def store(cols, value):
-            parts[:, rows, cols] = split(value.astype(BF16), count)
+            parts[:, :, rows, cols] = split(value.astype(BF16), group.deep, group.nx)
 
         wide_dot([(joined(hidden_ref[:, rows]), weight_ref)], NN, 512, store)
-        scatter.phase(piece, 0)
-
-    def end(piece):
-        total = scatter.phase(piece, scatter.last)
+
+    def end(piece, total):
         rows = scatter.rows(piece)
         out[rows] = (middle_ref[rows] + live_ref[rows] * total).astype(BF16)
 
+    before, within, behind = scatter_ticks(scatter, prepare, end)
+
     def tick(time):
-        during(time + 1, begin)
-        for phase in range(1, scatter.last):
-            during(time - phase + 1, functools.partial(scatter.phase, step=phase))
-        during(time - scatter.last + 1, end)
+        before(time)
+        at_each_z(group, functools.partial(within, time))
+        behind(time)
 
     pl.when(step == 0)(functools.partial(meet, count))
     return spread_ticks(tick, -1, PIECES + scatter.last, 2 * chunks), scatter.drain
@@ -480,7 +478,7 @@
             shape((rows, width), F32),
             shape((heads, rows, CHUNK), F32),
             shape((chunks, heads, HEAD, HEAD), F32),
-            shape((count, own, features), BF16),
+            shape((nz, nx, own, features), BF16),
         ],
         scratch_shapes=[
             pltpu.VMEM((heads, HEAD, HEAD), F32),
@@ -562,16 +560,17 @@
 class Group:
     def __init__(self, count):
         self.deep, self.nx = grid_sizes(count)
-        self.size = count
         me = lax.axis_index("heads")
         self.z, self.x = me // self.nx, me % self.nx
-        self.own = me
-
-    def slot(self, z, j):
-        return z * self.nx + (self.x + j) % self.nx
-
-    def device(self, z, j):
-        return {"heads": self.slot(z, j)}
+
+    def column(self, j):
+        return (self.x + j) % self.nx
+
+    def over_x(self, j):
+        return {"heads": self.z * self.nx + self.column(j)}
+
+    def along_z(self, z):
+        return {"heads": z * self.nx + self.x}
 
 
 def meet(count, replicas=1):
@@ -597,259 +596,340 @@
     pl.when((piece >= 0) & (piece < PIECES))(functools.partial(work, piece))
 
 
-class Sender:
-    draining = False
-
-    def push(self, source, target, send_sem, recv_sem, device, condition=None):
-        copy = pltpu.make_async_remote_copy(
-            source, target, send_sem, recv_sem, device_id=device, device_id_type=MESH
-        )
-        act = copy.wait_send if self.draining else copy.start
-        if condition is None:
-            act()
-        else:
-            pl.when(condition)(act)
-
-    def place(self, piece):
+def push(source, target, send_sem, recv_sem, device):
+    pltpu.make_async_remote_copy(
+        source, target, send_sem, recv_sem, device_id=device, device_id_type=MESH
+    ).start()
+
+
+class Gather:
+    def __init__(self, group, full, cols, sems, x_first):
+        self.group, self.full, self.cols, self.x_first = group, full, cols, x_first
+        self.part = full.shape[2] // PIECES
+        self.line_send, self.line_recv, self.x_send, self.x_recv = sems
+        self.last = group.deep
+
+    @staticmethod
+    def sems(deep, nx):
+        dma = pltpu.SemaphoreType.DMA
+        return [dma((PIECES, 2)), dma((PIECES, deep)), dma((PIECES, nx)), dma((PIECES, nx))]
+
+    def at(self, piece, z, column):
         rows = pl.ds(pl.multiple_of(piece * self.part, self.part), self.part)
-        return rows, self.cols
-
-    def drain(self):
-        def one(piece, _):
-            for step in range(self.last + 1):
-                self.phase(piece, step)
-            return 0
-
-        self.draining = True
-        lax.fori_loop(0, PIECES, one, 0)
-        self.draining = False
-
-
-class Gather(Sender):
-    def __init__(self, group, full, cols, send_sems, recv_sems, x_first):
-        self.group, self.full, self.cols, self.x_first = group, full, cols, x_first
-        self.part = full.shape[1] // PIECES
-        self.send_sems, self.recv_sems = send_sems, recv_sems
-        self.last = group.deep
-
-    @staticmethod
-    def sems(size):
-        return [
-            pltpu.SemaphoreType.DMA((PIECES, 3, size)),
-            pltpu.SemaphoreType.DMA((PIECES, size)),
-        ]
-
-    def send(self, piece, slot, way, mark, device, condition):
-        place = self.full.at[slot, *self.place(piece)]
-        self.push(
+        return self.full.at[z, column, rows, self.cols]
+
+    def columns(self):
+        return slice(None) if self.x_first else self.group.x
+
+    def push_line(self, piece, z, way, zz):
+        place = self.at(piece, z, self.columns())
+        push(
             place,
             place,
-            self.send_sems.at[piece, way, mark],
-            self.recv_sems.at[piece, slot],
-            device,
-            condition,
-        )
-
-    def receive(self, piece, slot):
-        if not self.draining:
-            arrived(self.full.at[slot, *self.place(piece)], self.recv_sems.at[piece, slot])
-
-    def send_up(self, piece, slot, here=True):
-        group = self.group
-        self.send(
-            piece, slot, 0, slot, group.device(group.z + 1, 0), here & (group.z + 1 < group.deep)
-        )
-
-    def send_down(self, piece, slot, here=True):
-        group = self.group
-        self.send(piece, slot, 1, slot, group.device(group.z - 1, 0), here & (group.z > 0))
-
-    def send_x(self, piece, slot, here=None):
-        group = self.group
-        for j in range(1, group.nx):
-            mark = (slot // group.nx) * group.nx + (slot + j) % group.nx
-            self.send(piece, slot, 2, mark, group.device(group.z, j), here)
-
-    def phase(self, piece, step):
-        group = self.group
-        if step == 0:
-            self.send_up(piece, group.own)
-            self.send_down(piece, group.own)
-            self.send_x(piece, group.own)
+            self.line_send.at[piece, way],
+            self.line_recv.at[piece, z],
+            self.group.along_z(zz + (1 if way == 0 else -1)),
+        )
+
+    def push_x(self, piece, z):
+        place = self.at(piece, z, self.group.x)
+        for j in range(1, self.group.nx):
+            push(
+                place,
+                place,
+                self.x_send.at[piece, j],
+                self.x_recv.at[piece, self.group.nx - j],
+                self.group.over_x(j),
+            )
+
+    def own_line(self, piece, zz):
+        if zz + 1 < self.group.deep:
+            self.push_line(piece, zz, 0, zz)
+        if zz > 0:
+            self.push_line(piece, zz, 1, zz)
+
+    def begin(self, piece):
+        self.push_x(piece, self.group.z)
+        if not self.x_first:
+            group = self.group
+            pl.when(group.z + 1 < group.deep)(lambda: self.push_line(piece, group.z, 0, group.z))
+            pl.when(group.z > 0)(lambda: self.push_line(piece, group.z, 1, group.z))
+
+    def phase(self, piece, step, zz):
+        deep, nx = self.group.deep, self.group.nx
+        if self.x_first:
+            if step == 1:
+                for j in range(1, nx):
+                    arrived(self.at(piece, zz, self.group.column(j)), self.x_recv.at[piece, j])
+                self.own_line(piece, zz)
+                return
+            step -= 1
+        elif step == deep:
+            for j in range(1, nx):
+                place = self.at(piece, slice(None), self.group.column(j))
+                arrived(place, self.x_recv.at[piece, j])
             return
-        if self.x_first and step == 1:
-            for j in range(1, group.nx):
-                slot = group.slot(group.z, j)
-                self.receive(piece, slot)
-                self.send_up(piece, slot)
-                self.send_down(piece, slot)
-        if step < group.deep:
-            for j in range(group.nx if self.x_first else 1):
-                below, above = group.z - step, group.z + step
-                for z, here, forward in (
-                    (below, below >= 0, self.send_up),
-                    (above, above < group.deep, self.send_down),
-                ):
-                    slot = group.slot(z, j)
-                    pl.when(here)(functools.partial(self.receive, piece, slot))
-                    forward(piece, slot, here)
-                    if not self.x_first:
-                        self.send_x(piece, slot, here)
-        elif not self.x_first:
-            for j in range(1, group.nx):
-                for z in range(group.deep):
-                    self.receive(piece, group.slot(z, j))
-
-
-class Scatter(Sender):
-    last = 3
+        for z, way in ((zz - step, 0), (zz + step, 1)):
+            if 0 <= z < deep:
+                arrived(self.at(piece, z, self.columns()), self.line_recv.at[piece, z])
+                if 0 <= zz + (1 if way == 0 else -1) < deep:
+                    self.push_line(piece, z, way, zz)
+                if not self.x_first:
+                    self.push_x(piece, z)
+
+    def drain(self, piece, zz):
+        deep, nx = self.group.deep, self.group.nx
+        if zz + 1 < deep:
+            place = self.at(piece, pl.ds(0, zz + 1), self.columns())
+            arrived(place, self.line_send.at[piece, 0])
+        if zz > 0:
+            place = self.at(piece, pl.ds(zz, deep - zz), self.columns())
+            arrived(place, self.line_send.at[piece, 1])
+        z = zz if self.x_first else slice(None)
+        for j in range(1, nx):
+            arrived(self.at(piece, z, self.group.x), self.x_send.at[piece, j])
+
+
+class Scatter:
+    last = 4
 
     def __init__(self, group, parts, cols, scratch, z_first):
         self.group, self.parts, self.cols, self.z_first = group, parts, cols, z_first
-        self.part = parts.shape[1] // PIECES
-        self.over_x, self.line, *sems = scratch
+        self.part = parts.shape[2] // PIECES
+        self.landed_x, self.line, *sems = scratch
         self.x_send, self.x_recv, self.z_send, self.z_recv = sems
 
     @staticmethod
     def scratch(deep, nx, rows, cols, z_first):
         dma = pltpu.SemaphoreType.DMA
         return [
-            pltpu.VMEM((1 if z_first else deep, max(nx - 1, 1), rows, cols), BF16),
+            pltpu.VMEM((max(nx - 1, 1), 1 if z_first else deep, rows, cols), BF16),
             pltpu.VMEM((deep + 1, nx if z_first else 1, rows, cols), BF16),
-            *[dma((PIECES, deep, nx))] * 2,
-            *[dma((PIECES, 2, deep * nx))] * 2,
+            *[dma((PIECES, nx))] * 2,
+            *[dma((PIECES, 2))] * 2,
         ]
 
-    def landing(self, piece):
-        return self.place(piece)[0]
-
-    def line_at(self, piece, slot, way):
+    def rows(self, piece):
+        return pl.ds(pl.multiple_of(piece * self.part, self.part), self.part)
+
+    def columns(self):
+        return slice(None) if self.z_first else pl.ds(self.group.x, 1)
+
+    def at(self, piece, z, column):
+        return self.parts.at[z, column, self.rows(piece), self.cols]
+
+    def line_at(self, piece, way, zz):
+        first, size = (zz + 1, self.group.deep - zz) if way == 0 else (0, zz + 1)
+        return self.line.at[pl.ds(first, size), :, self.rows(piece)]
+
+    def push_line(self, piece, way, zz):
+        deep = self.group.deep
+        first, size = (zz + 1, deep - 1 - zz) if way == 0 else (0, zz)
+        if size == 0:
+            return
+        after = zz + 1 if way == 0 else zz - 1
+        push(
+            self.at(piece, pl.ds(first, size), self.columns()),
+            self.line_at(piece, way, after),
+            self.z_send.at[piece, way],
+            self.z_recv.at[piece, way],
+            self.group.along_z(after),
+        )
+
+    def ends(self, piece, zz):
+        if zz == 0:
+            self.push_line(piece, 0, zz)
+        if zz == self.group.deep - 1:
+            self.push_line(piece, 1, zz)
+
+    def hand_on(self, piece, near, zz):
+        deep = self.group.deep
+        if zz == 0 or zz == deep - 1:
+            return
+        way = 0 if (zz < deep // 2) == near else 1
+        arrived(self.line_at(piece, way, zz), self.z_recv.at[piece, way])
+        first, size = (zz + 1, deep - 1 - zz) if way == 0 else (0, zz)
+        shift = 1 if way == 0 else 0
+        ours = self.at(piece, pl.ds(first, size), self.columns())
+        landed = self.line.at[pl.ds(first + shift, size), :, self.rows(piece)]
+        ours[...] = (ours[...].astype(F32) + landed[...].astype(F32)).astype(BF16)
+        self.push_line(piece, way, zz)
+
+    def wait_ends(self, piece, zz):
+        deep = self.group.deep
+        if deep == 1:
+            return
+        if zz == 0:
+            arrived(self.line_at(piece, 1, zz), self.z_recv.at[piece, 1])
+        if zz == deep - 1:
+            arrived(self.line_at(piece, 0, zz), self.z_recv.at[piece, 0])
+
+    def total_line(self, piece, column):
+        group, rows = self.group, self.rows(piece)
+        total = self.parts[group.z, column, rows, self.cols].astype(F32)
+        index = column if self.z_first else 0
+        for here, place in ((group.z > 0, group.z + 1), (group.z + 1 < group.deep, group.z)):
+            landed = self.line[place, index, rows]
+            total = total + jnp.where(here, landed.astype(F32), 0.0)
+        return total
+
+    def begin(self, piece):
+        if not self.z_first:
+            for j in range(1, self.group.nx):
+                push(
+                    self.at(piece, slice(None), self.group.column(j)),
+                    self.landed_x.at[self.group.nx - j - 1, :, self.rows(piece)],
+                    self.x_send.at[piece, j],
+                    self.x_recv.at[piece, self.group.nx - j],
+                    self.group.over_x(j),
+                )
+
+    def begin_line(self, piece, zz):
+        if self.z_first:
+            self.ends(piece, zz)
+
+    def wait_x(self, piece, j):
+        landed = self.landed_x.at[j - 1, :, self.rows(piece)]
+        arrived(landed, self.x_recv.at[piece, j])
+        return landed[...].astype(F32)
+
+    def phase(self, piece, step, zz):
         nx = self.group.nx
-        z = slot // nx + (1 if way == 0 else 0)
-        return self.line.at[z, slot % nx if self.z_first else 0, self.landing(piece)]
-
-    def step_line(self, piece, slot, way, device, add):
-        part = (slot, *self.place(piece))
-        if add and not self.draining:
-            landed = self.line_at(piece, slot, way)
-            arrived(landed, self.z_recv.at[piece, way, slot])
-            total = self.parts[part].astype(F32) + landed[...].astype(F32)
-            self.parts[part] = total.astype(BF16)
-        self.push(
-            self.parts.at[part],
-            self.line_at(piece, slot, way),
-            self.z_send.at[piece, way, slot],
-            self.z_recv.at[piece, way, slot],
-            device,
-        )
-
-    def walk(self, piece, columns, ends):
-        group = self.group
-        deep = group.deep
-
-        def one_way(way):
-            for k in range(deep - 1, 0, -1):
-                target = group.z + k if way == 0 else group.z - k
-                inside = target < deep if way == 0 else target >= 0
-                first = group.z == 0 if way == 0 else group.z == deep - 1
-                condition = inside & (first if ends else jnp.logical_not(first))
-                device = group.device(group.z + (1 if way == 0 else -1), 0)
-                for j in range(columns):
-                    slot = group.slot(target, j)
-                    pl.when(condition)(
-                        functools.partial(self.step_line, piece, slot, way, device, not ends)
-                    )
-
-        if ends or self.draining:
-            one_way(0)
-            one_way(1)
+        if self.z_first:
+            if step < 3:
+                self.hand_on(piece, step == 1, zz)
+            elif step == 3:
+                self.wait_ends(piece, zz)
             return
-
-        def both(first, second):
-            one_way(first)
-            one_way(second)
-
-        low = group.z < deep // 2
-        pl.when(low)(functools.partial(both, 0, 1))
-        pl.when(jnp.logical_not(low))(functools.partial(both, 1, 0))
-
-    def total_line(self, piece, slot):
-        group = self.group
-        total = self.parts[(slot, *self.place(piece))].astype(F32)
-        for way, here in ((0, group.z > 0), (1, group.z + 1 < group.deep)):
-            landed = self.line_at(piece, slot, way)
-            pl.when(here)(
-                functools.partial(arrived, landed, self.z_recv.at[piece, way, slot])
+        if step == 1:
+            ours = self.at(piece, slice(None), self.group.x)
+            total = ours[...].astype(F32)
+            for j in range(1, nx):
+                total = total + self.wait_x(piece, j)
+            ours[...] = total.astype(BF16)
+            self.ends(piece, zz)
+        elif step < 4:
+            self.hand_on(piece, step == 2, zz)
+        else:
+            self.wait_ends(piece, zz)
+
+    def third(self, piece):
+        if not self.z_first:
+            return
+        group, rows = self.group, self.rows(piece)
+        for j in range(1, group.nx):
+            column = group.column(j)
+            total = self.total_line(piece, column).astype(BF16)
+            self.parts[group.z, column, rows, self.cols] = total
+            push(
+                self.at(piece, pl.ds(group.z, 1), column),
+                self.landed_x.at[group.nx - j - 1, :, rows],
+                self.x_send.at[piece, j],
+                self.x_recv.at[piece, group.nx - j],
+                group.over_x(j),
             )
-            total = total + jnp.where(here, landed[...].astype(F32), 0.0)
+
+    def total(self, piece):
+        total = self.total_line(piece, self.group.x)
+        if self.z_first:
+            for j in range(1, self.group.nx):
+                total = total + self.wait_x(piece, j)[0]
         return total
 
-    def send_x(self, piece, index, z, j):
-        group = self.group
-        self.push(
-            self.parts.at[group.slot(z, j), *self.place(piece)],
-            self.over_x.at[index, j - 1, self.landing(piece)],
-            self.x_send.at[piece, index, j],
-            self.x_recv.at[piece, index, j],
-            group.device(group.z, j),
-        )
-
-    def add_x(self, piece, index, total):
+    def drain(self, piece, zz):
+        deep = self.group.deep
+        for way, size in ((0, deep - 1 - zz), (1, zz)):
+            if size > 0:
+                place = self.at(piece, pl.ds(0, size), self.columns())
+                arrived(place, self.z_send.at[piece, way])
+        z = pl.ds(0, 1 if self.z_first else deep)
         for j in range(1, self.group.nx):
-            landed = self.over_x.at[index, j - 1, self.landing(piece)]
-            arrived(landed, self.x_recv.at[piece, index, j])
-            total = total + landed[...].astype(F32)
-        return total
-
-    def phase(self, piece, step):
-        group = self.group
-        if self.z_first:
-            if step == 0:
-                self.walk(piece, group.nx, True)
-            elif step == 1:
-                self.walk(piece, group.nx, False)
-            elif step == 2:
-                for j in range(1, group.nx):
-                    slot = group.slot(group.z, j)
-                    if not self.draining:
-                        total = self.total_line(piece, slot)
-                        self.parts[(slot, *self.place(piece))] = total.astype(BF16)
-                    self.send_x(piece, 0, group.z, j)
-            elif not self.draining:
-                return self.add_x(piece, 0, self.total_line(piece, group.own))
-        elif step == 0:
-            for z in range(group.deep):
-                for j in range(1, group.nx):
-                    self.send_x(piece, z, z, j)
-        elif step == 1:
-            for z in range(group.deep):
-                part = (group.slot(z, 0), *self.place(piece))
-                if not self.draining:
-                    total = self.add_x(piece, z, self.parts[part].astype(F32))
-                    self.parts[part] = total.astype(BF16)
-            self.walk(piece, 1, True)
-        elif step == 2:
-            self.walk(piece, 1, False)
-        elif not self.draining:
-            return self.total_line(piece, group.own)
-        return None
+            arrived(self.at(piece, z, self.group.x), self.x_send.at[piece, j])
 
 
 class Both:
     def __init__(self, first, second):
         self.both = (first, second)
+        self.group = first.group
         self.part, self.last = first.part, first.last
 
     def rows(self, piece):
         return pl.ds(pl.multiple_of(piece * self.part, self.part), self.part)
 
-    def phase(self, piece, step):
-        out = [each.phase(piece, step) for each in self.both]
-        return None if out[0] is None else jnp.concatenate(out, axis=1)
+    def begin(self, piece):
+        for each in self.both:
+            each.begin(piece)
+
+    def begin_line(self, piece, zz):
+        for each in self.both:
+            each.begin_line(piece, zz)
+
+    def phase(self, piece, step, zz):
+        for each in self.both:
+            each.phase(piece, step, zz)
+
+    def third(self, piece):
+        for each in self.both:
+            each.third(piece)
+
+    def total(self, piece):
+        return jnp.concatenate([each.total(piece) for each in self.both], axis=1)
 
     def drain(self):
-        for each in self.both:
-            each.drain()
+        def at(zz):
+            def one(piece, _):
+                for each in self.both:
+                    each.drain(piece, zz)
+                return 0
+
+            lax.fori_loop(0, PIECES, one, 0)
+
+        at_each_z(self.group, at)
+
+
+def at_each_z(group, work):
+    for zz in range(group.deep):
+        pl.when(group.z == zz)(functools.partial(work, zz))
+
+
+def scatter_ticks(scatter, prepare, finish, after=None):
+    def before(time):
+        def begin(piece):
+            prepare(piece)
+            scatter.begin(piece)
+
+        during(time + 1, begin)
+
+    def within(time, zz):
+        for step in range(scatter.last, 0, -1):
+            during(time - step + 1, functools.partial(scatter.phase, step=step, zz=zz))
+        during(time + 1, functools.partial(scatter.begin_line, zz=zz))
+
+    def behind(time):
+        during(time - 2, scatter.third)
+        during(time - scatter.last + 1, lambda piece: finish(piece, scatter.total(piece)))
+
+    return before, within, behind
+
+
+def gather_ticks(gather, prepare, ready):
+    def before(time):
+        if prepare is not None:
+
+            def begin(piece):
+                prepare(piece)
+                gather.begin(piece)
+
+            during(time, begin)
+
+    def within(time, zz):
+        for step in range(gather.last, 0, -1):
+            during(time - step, functools.partial(gather.phase, step=step, zz=zz))
+
+    def behind(time):
+        during(time - gather.last, ready)
+
+    return before, within, behind
 
 
 def cut(cols, share):
@@ -859,15 +939,15 @@
 
 def gather_of(group, share, scratch):
     full, *sems = scratch
-    first, second = cut(full.shape[2], share)
+    first, second = cut(full.shape[3], share)
     return Both(
-        Gather(group, full, first, *sems[:2], False), Gather(group, full, second, *sems[2:], True)
+        Gather(group, full, first, sems[:4], False), Gather(group, full, second, sems[4:], True)
     )
 
 
 def scatter_of(group, share, scratch):
     parts, *rest = scratch
-    first, second = cut(parts.shape[2], share)
+    first, second = cut(parts.shape[3], share)
     return Both(
         Scatter(group, parts, first, rest[:6], False),
         Scatter(group, parts, second, rest[6:], True),
@@ -875,19 +955,19 @@
 
 
 def gather_scratch(nz, nx, rows, cols):
-    return [pltpu.VMEM((nz * nx, rows, cols), BF16), *Gather.sems(nz * nx), *Gather.sems(nz * nx)]
+    return [pltpu.VMEM((nz, nx, rows, cols), BF16), *Gather.sems(nz, nx), *Gather.sems(nz, nx)]
 
 
 def scatter_scratch(nz, nx, rows, cols, share):
     first, second = cut(cols, share)
     return [
-        pltpu.VMEM((nz * nx, rows, cols), BF16),
+        pltpu.VMEM((nz, nx, rows, cols), BF16),
         *Scatter.scratch(nz, nx, rows, first.size, False),
         *Scatter.scratch(nz, nx, rows, second.size, True),
     ]
 
 
-SCATTER_COUNT, GATHER_COUNT = 13, 5
+SCATTER_COUNT, GATHER_COUNT = 13, 9
 
 
 def inverse_rms(rows):
@@ -928,11 +1008,11 @@
 
 
 def joined(values):
-    return values.reshape(values.shape[0] * values.shape[1], values.shape[2])
-
-
-def split(values, parts):
-    return values.reshape(parts, values.shape[0] // parts, values.shape[1])
+    return values.reshape(-1, values.shape[-1])
+
+
+def split(values, *parts):
+    return values.reshape(*parts, values.shape[0] // math.prod(parts), values.shape[1])
 
 
 def project_kernel(
@@ -942,14 +1022,13 @@
     group = Group(count)
     gather = gather_of(group, GATHER_SHARE, scratch[:GATHER_COUNT])
     meet(count)
-
-    shares, share = full_out.shape[0], full_out.shape[3]
+    shares, share = full_out.shape[0], full_out.shape[4]
 
     def full_copy(piece, index):
         rows = gather.rows(piece)
         return pltpu.make_async_copy(
-            full.at[:, rows, pl.ds(index * share, share)],
-            full_out.at[index, :, rows],
+            full.at[:, :, rows, pl.ds(index * share, share)],
+            full_out.at[index, :, :, rows],
             full_sems.at[piece, index],
         )
 
@@ -959,15 +1038,13 @@
             staged.at[:, rows], projected_out.at[:, rows], staged_sems.at[piece]
         )
 
-    def begin(piece):
+    def prepare(piece):
         rows = rows_ref[gather.rows(piece)].astype(F32)
-        full[group.own, gather.rows(piece)] = (
+        full[group.z, group.x, gather.rows(piece)] = (
             rows * inverse_rms(rows) * gain_ref[...]
         ).astype(BF16)
-        gather.phase(piece, 0)
 
     def ready(piece):
-        gather.phase(piece, gather.last)
         rows = gather.rows(piece)
         for index in range(shares):
             full_copy(piece, index).start()
@@ -975,7 +1052,7 @@
         def store(cols, value):
             staged[:, rows, cols] = split(value, count)
 
-        left = joined(full[:, rows])
+        left = joined(full[:, :, rows])
         wide_dot([(left, weight_ref)], NN, 256, store)
         value = lax.dot_general(
             left, gates_ref[...], (NN, ((), ())), preferred_element_type=F32
@@ -983,11 +1060,12 @@
         staged[:, rows, weight_ref.shape[1] :] = split(value, count)
         staged_copy(piece).start()
 
+    before, within, behind = gather_ticks(gather, prepare, ready)
+
     def tick(time, _):
-        during(time, begin)
-        for step in range(1, gather.last):
-            during(time - step, functools.partial(gather.phase, step=step))
-        during(time - gather.last, ready)
+        before(time)
+        at_each_z(group, functools.partial(within, time))
+        behind(time)
         return 0
 
     lax.fori_loop(0, PIECES + gather.last, tick, 0)
@@ -1009,7 +1087,7 @@
     return pl.pallas_call(
         functools.partial(project_kernel, count),
         out_shape=[
-            jax.ShapeDtypeStruct((shares, count, own, features // shares), BF16),
+            jax.ShapeDtypeStruct((shares, nz, nx, own, features // shares), BF16),
             jax.ShapeDtypeStruct((count, own, cols), F32),
         ],
         in_specs=[VMEM_SPEC] * 4,
@@ -1026,43 +1104,39 @@
     )(rows, gain, weight, gates)
 
 
-def sum_and_gather(scatter, gather, full, prepare, middle, ready, job=None):
-    own = lax.axis_index("heads")
-
-    def begin(piece):
-        prepare(piece)
-        scatter.phase(piece, 0)
-
-    def turn(piece):
-        total = scatter.phase(piece, scatter.last)
-        full[own, gather.rows(piece)] = middle(piece, total).astype(BF16)
-        gather.phase(piece, 0)
-
-    def end(piece):
-        gather.phase(piece, gather.last)
-        ready(piece)
+def sum_and_gather(scatter, gather, prepare, middle, ready, job=None):
+    group = gather.group
+    full = gather.both[0].full
+
+    def turn(piece, total):
+        full[group.z, group.x, gather.rows(piece)] = middle(piece, total).astype(BF16)
+        gather.begin(piece)
+
+    late = scatter.last - 1
+    before, sum_within, sum_behind = scatter_ticks(scatter, prepare, turn)
+    _, gather_within, gather_behind = gather_ticks(gather, None, ready)
 
     def tick(time, _):
-        during(time + 1, begin)
+        before(time)
+
+        def within(zz):
+            gather_within(time - late, zz)
+            sum_within(time, zz)
+
+        at_each_z(group, within)
+        sum_behind(time)
+        gather_behind(time - late)
         if job is not None:
             job(time + 1)
-        for step in range(1, scatter.last):
-            during(time - step + 1, functools.partial(scatter.phase, step=step))
-        during(time - scatter.last + 1, turn)
-        for step in range(1, gather.last):
-            during(
-                time - scatter.last + 1 - step, functools.partial(gather.phase, step=step)
-            )
-        during(time - scatter.last + 1 - gather.last, end)
         return 0
 
-    lax.fori_loop(-1, PIECES + scatter.last + gather.last - 1, tick, 0)
+    lax.fori_loop(-1, PIECES + late + gather.last, tick, 0)
     scatter.drain()
     gather.drain()
 
 
 def branch_kernel(
-    count, mixed_ref, weight_ref, input_ref, live_ref, gain_ref, gate_weight_ref, up_weight_ref,
+    count, mixed_ref, weight_ref, input_ref, live_ref, gain_ref, feed_weight_ref,
     down_weight_ref, grad_ref, middle_out, full_out, dgate_out, dup_out, hidden_out, *scratch
 ):
     *scratch, grads, grad_sems, dgate, dup, hidden, feed_sems = scratch
@@ -1074,7 +1148,7 @@
     def fetch(piece):
         slot = piece % 2
         return pltpu.make_async_copy(
-            grad_ref.at[:, gather.rows(piece)], grads.at[slot], grad_sems.at[slot]
+            grad_ref.at[:, :, gather.rows(piece)], grads.at[slot], grad_sems.at[slot]
         )
 
     fetch(0).start()
@@ -1084,7 +1158,7 @@
         rows = gather.rows(piece)
 
         def store(cols, value):
-            parts[:, rows, cols] = split(value.astype(BF16), count)
+            parts[:, :, rows, cols] = split(value.astype(BF16), group.deep, group.nx)
 
         wide_dot([(joined(mixed_ref[:, rows]), weight_ref)], NN, 512, store)
 
@@ -1099,7 +1173,11 @@
         return [
             pltpu.make_async_copy(ref.at[:, rows], out.at[:, rows], feed_sems.at[piece, index])
             for index, (ref, out) in enumerate(
-                ((dgate, dgate_out), (dup, dup_out), (hidden, hidden_out), (full, full_out))
+                ((dgate, dgate_out), (dup, dup_out), (hidden, hidden_out))
+            )
+        ] + [
+            pltpu.make_async_copy(
+                full.at[:, :, rows], full_out.at[:, :, rows], feed_sems.at[piece, 3]
             )
         ]
 
@@ -1107,16 +1185,16 @@
         rows = gather.rows(piece)
         fetch(piece).wait()
         pl.when(piece + 1 < PIECES)(lambda: fetch(piece + 1).start())
-        left, grad = joined(full[:, rows]), joined(grads[piece % 2])
-        total = gate_weight_ref.shape[1]
+        left, grad = joined(full[:, :, rows]), joined(grads[piece % 2])
+        total = feed_weight_ref.shape[1]
         for first in range(0, total, 256):
             cols = slice(first, min(first + 256, total))
 
             def product(a, b, dims):
                 return lax.dot_general(a, b, (dims, ((), ())), preferred_element_type=F32)
 
-            gate = product(left, gate_weight_ref[:, cols], NN)
-            up = product(left, up_weight_ref[:, cols], NN)
+            gate = product(left, feed_weight_ref[0, cols], NT)
+            up = product(left, feed_weight_ref[1, cols], NT)
             dhidden = product(grad, down_weight_ref[cols, :], NT)
             sigmoid = jax.nn.sigmoid(gate)
             active = gate * sigmoid
@@ -1127,7 +1205,7 @@
         for copy in copies(piece):
             copy.start()
 
-    sum_and_gather(scatter, gather, full, prepare, middle, ready)
+    sum_and_gather(scatter, gather, prepare, middle, ready)
 
     def finish(piece, _):
         for copy in copies(piece):
@@ -1137,25 +1215,23 @@
     lax.fori_loop(0, PIECES, finish, 0)
 
 
-def branch_and_feed(
-    mixed, weight, rows, live, gain, gate_weight, up_weight, down_weight, grad, count
-):
+def branch_and_feed(mixed, weight, rows, live, gain, feed_weight, down_weight, grad, count):
     own, features = rows.shape
-    hidden = gate_weight.shape[1]
+    hidden = feed_weight.shape[1]
     nz, nx = grid_sizes(count)
     return pl.pallas_call(
         functools.partial(branch_kernel, count),
         out_shape=[
             jax.ShapeDtypeStruct((own, features), F32),
-            jax.ShapeDtypeStruct((count, own, features), BF16),
+            jax.ShapeDtypeStruct((nz, nx, own, features), BF16),
             *[jax.ShapeDtypeStruct((count, own, hidden), BF16)] * 3,
         ],
-        in_specs=[VMEM_SPEC] * 8 + [ANY_SPEC],
+        in_specs=[VMEM_SPEC] * 7 + [ANY_SPEC],
         out_specs=[VMEM_SPEC] + [ANY_SPEC] * 4,
         scratch_shapes=[
             *scatter_scratch(nz, nx, own, features, PAIR_SHARE),
             *gather_scratch(nz, nx, own, features),
-            pltpu.VMEM((2, count, own // PIECES, features), BF16),
+            pltpu.VMEM((2, nz, nx, own // PIECES, features), BF16),
             pltpu.SemaphoreType.DMA((2,)),
             *[pltpu.VMEM((count, own, hidden), BF16)] * 3,
             pltpu.SemaphoreType.DMA((PIECES, 4)),
@@ -1163,9 +1239,7 @@
         compiler_params=linked(1),
         cost_estimate=lasting(180),
         name="branch_and_feed",
-    )(
-        split(mixed, count), weight, rows, live, gain, gate_weight, up_weight, down_weight, grad
-    )
+    )(split(mixed, count), weight, rows, live, gain, feed_weight, down_weight, grad)
 
 
 TILE = 256
@@ -1176,20 +1250,20 @@
         self.rows_ref, self.tile, self.factors = rows_ref, tile, factors
         self.staged, self.outs = staged, outs
         self.fetch_sem, self.out_sems = fetch_sem, out_sems
-        self.count = rows_ref.shape[2] // TILE
+        self.count = rows_ref.shape[3] // TILE
 
     def span(self, index):
         return pl.ds(pl.multiple_of(index * TILE, TILE), TILE)
 
     def fetch(self, index):
         return pltpu.make_async_copy(
-            self.rows_ref.at[:, :, self.span(index)], self.tile, self.fetch_sem
+            self.rows_ref.at[:, :, :, self.span(index)], self.tile, self.fetch_sem
         )
 
     def results(self, index):
         return [
             pltpu.make_async_copy(
-                self.staged.at[which], out.at[self.span(index)], self.out_sems.at[which]
+                self.staged.at[which], out.at[:, self.span(index)], self.out_sems.at[which]
             )
             for which, out in enumerate(self.outs)
         ]
@@ -1203,19 +1277,19 @@
         left = joined(self.tile[...])
         pl.when(index > 0)(lambda: self.wait_results(index - 1))
         for which, factor in enumerate(self.factors):
-            self.staged[which] = lax.dot_general(
+            product = lax.dot_general(
                 left, joined(factor[...]), (TN, ((), ())), preferred_element_type=F32
-            ).astype(BF16)
+            )
+            self.staged[which] = jnp.transpose(product).astype(BF16)
         for copy in self.results(index):
             copy.start()
         pl.when(index + 1 < self.count)(lambda: self.fetch(index + 1).start())
 
 
 def feed_back_kernel(
-    count, dgate_ref, dup_ref, gate_weight_ref, up_weight_ref, top_ref, middle_ref, live_ref,
+    count, dgate_ref, dup_ref, feed_weight_ref, top_ref, middle_ref, live_ref,
     gain_ref, out_weight_ref, mixed_ref, hidden_ref, normed_ref, grad_feed_ref,
-    dmiddle_out, dgain_out, dmixed_out, dweight_out, dgate_weight, dup_weight, ddown_weight,
-    *scratch
+    dmiddle_out, dgain_out, dmixed_out, dweight_out, dfeed_out, *scratch
 ):
     *scratch, total_out, tile, grad_tile, staged, grad_staged, fetch_sems, out_sems = scratch
     group = Group(count)
@@ -1224,11 +1298,11 @@
     parts, full = scratch[0], scratch[SCATTER_COUNT]
     jobs = (
         TileJob(
-            normed_ref, tile, (dgate_ref, dup_ref), staged, (dgate_weight, dup_weight),
+            normed_ref, tile, (dgate_ref, dup_ref), staged, (dfeed_out.at[0], dfeed_out.at[1]),
             fetch_sems.at[0], out_sems.at[0],
         ),
         TileJob(
-            grad_feed_ref, grad_tile, (hidden_ref,), grad_staged, (ddown_weight,),
+            grad_feed_ref, grad_tile, (hidden_ref,), grad_staged, (dfeed_out.at[2],),
             fetch_sems.at[1], out_sems.at[1],
         ),
     )
@@ -1242,14 +1316,14 @@
         rows = gather.rows(piece)
 
         def store(cols, value):
-            parts[:, rows, cols] = split(value.astype(BF16), count)
+            parts[:, :, rows, cols] = split(value.astype(BF16), group.deep, group.nx)
 
         wide_dot(
             [
-                (joined(dgate_ref[:, rows]), gate_weight_ref),
-                (joined(dup_ref[:, rows]), up_weight_ref),
+                (joined(dgate_ref[:, rows]), feed_weight_ref.at[0]),
+                (joined(dup_ref[:, rows]), feed_weight_ref.at[1]),
             ],
-            NT,
+            NN,
             256,
             store,
         )
@@ -1269,7 +1343,7 @@
 
     def ready(piece):
         rows = gather.rows(piece)
-        left, mixed = joined(full[:, rows]), joined(mixed_ref[:, rows])
+        left, mixed = joined(full[:, :, rows]), joined(mixed_ref[:, rows])
 
         def store(cols, value):
             dmixed_out[:, rows, cols] = split(value, count)
@@ -1286,7 +1360,7 @@
                 functools.partial(each.run, time // 2)
             )
 
-    sum_and_gather(scatter, gather, full, prepare, middle, ready, job)
+    sum_and_gather(scatter, gather, prepare, middle, ready, job)
     last = PIECES + scatter.last + gather.last
     lax.fori_loop(last, max(2 * jobs[0].count, last), lambda time, _: (job(time), 0)[1], 0)
     for each in jobs:
@@ -1295,12 +1369,12 @@
 
 
 def feed_back(
-    dgate, dup, gate_weight, up_weight, top, middle, live, gain, out_weight, mixed, hidden,
-    normed, grad_feed, count,
+    dgate, dup, feed_weight, top, middle, live, gain, out_weight, mixed, hidden, normed, grad_feed,
+    count,
 ):
     own, features = middle.shape
     nz, nx = grid_sizes(count)
-    width, units = out_weight.shape[0], gate_weight.shape[1]
+    width, units = out_weight.shape[0], feed_weight.shape[1]
     return pl.pallas_call(
         functools.partial(feed_back_kernel, count),
         out_shape=[
@@ -1308,18 +1382,18 @@
             jax.ShapeDtypeStruct((1, features), F32),
             jax.ShapeDtypeStruct((count, own, width), F32),
             jax.ShapeDtypeStruct((features, width), BF16),
-            *[jax.ShapeDtypeStruct((features, units), BF16)] * 3,
+            jax.ShapeDtypeStruct((3, units, features), BF16),
         ],
-        in_specs=[VMEM_SPEC] * 11 + [ANY_SPEC] * 2,
-        out_specs=[VMEM_SPEC] * 4 + [ANY_SPEC] * 3,
+        in_specs=[VMEM_SPEC] * 10 + [ANY_SPEC] * 2,
+        out_specs=[VMEM_SPEC] * 4 + [ANY_SPEC],
         scratch_shapes=[
             *scatter_scratch(nz, nx, own, features, PAIR_SHARE),
             *gather_scratch(nz, nx, own, features),
             pltpu.VMEM((features, width), F32),
-            pltpu.VMEM((count, own, TILE), BF16),
-            pltpu.VMEM((count, own, TILE), BF16),
-            pltpu.VMEM((2, TILE, units), BF16),
-            pltpu.VMEM((1, TILE, units), BF16),
+            pltpu.VMEM((nz, nx, own, TILE), BF16),
+            pltpu.VMEM((nz, nx, own, TILE), BF16),
+            pltpu.VMEM((2, units, TILE), BF16),
+            pltpu.VMEM((1, units, TILE), BF16),
             pltpu.SemaphoreType.DMA((2,)),
             pltpu.SemaphoreType.DMA((2, 2)),
         ],
@@ -1327,12 +1401,12 @@
         cost_estimate=lasting(180),
         name="feed_back",
     )(
-        dgate, dup, gate_weight, up_weight, top, middle, live, gain, out_weight,
+        dgate, dup, feed_weight, top, middle, live, gain, out_weight,
         split(mixed, count), hidden, normed, grad_feed,
     )
 
 
-class Replicas(Sender):
+class Replicas:
     def __init__(self, values, from_core, from_y, over_back, over_home, sems):
         self.values, self.from_core, self.from_y = values, from_core, from_y
         self.over_back, self.over_home = over_back, over_home
@@ -1361,6 +1435,17 @@
 
     def line(self, k):
         return (self.y + k) % self.lines
+
+    draining = False
+
+    def push(self, source, target, send_sem, recv_sem, device):
+        copy = pltpu.make_async_remote_copy(
+            source, target, send_sem, recv_sem, device_id=device, device_id_type=MESH
+        )
+        if self.draining:
+            copy.wait_send()
+        else:
+            copy.start()
 
     def drain(self):
         self.draining = True
@@ -1480,27 +1565,26 @@
     parts, rest = scratch[0], scratch[SCATTER_COUNT:]
     values = rest[0]
     near, near_send, near_recv, far, far_send, far_recv, staged, out_sems = rest[9:]
-    scatter = scatter_of(Group(count), SCATTER_SHARE, scratch[:SCATTER_COUNT])
+    group = Group(count)
+    scatter = scatter_of(group, SCATTER_SHARE, scratch[:SCATTER_COUNT])
     replicas = Replicas(*rest[:5], rest[5:9])
     meet(count, lax.axis_size("dp"))
     small_out[...] = small_ref[...]
     width = grad_ref.shape[2]
     values[:, :, width:] = split(wout_ref[...], values.shape[0])
 
-    def begin(piece):
+    def prepare(piece):
         rows = scatter.rows(piece)
 
         def store(cols, value):
-            parts[:, rows, cols] = split(value.astype(BF16), count)
+            parts[:, :, rows, cols] = split(value.astype(BF16), group.deep, group.nx)
 
         left, edge = joined(grad_ref[:, rows]), weight_ref.shape[1]
         wide_dot(
             [(left[:, :edge], weight_ref), (left[:, edge:], gates_ref)], NT, 256, store
         )
-        scatter.phase(piece, 0)
-
-    def end(piece):
-        dnormed = scatter.phase(piece, scatter.last)
+
+    def end(piece, dnormed):
         rows = scatter.rows(piece)
         given = input_ref[rows].astype(F32)
         scale = inverse_rms(given)
@@ -1543,11 +1627,12 @@
         steps.append(lambda: None)
     steps.append(replicas.over_y)
 
+    before, within, behind = scatter_ticks(scatter, prepare, end)
+
     def tick(time, _):
-        during(time + 1, begin)
-        for step in range(1, scatter.last):
-            during(time - step + 1, functools.partial(scatter.phase, step=step))
-        during(time - scatter.last + 1, end)
+        before(time)
+        at_each_z(group, functools.partial(within, time))
+        behind(time)
         for index, step in enumerate(steps):
             pl.when(time == index)(step)
         return 0
@@ -1670,24 +1755,22 @@
     mixed, *saved, grad_feed = mixer_forward(
         longer, projected, taps, params, gain_row, cotangent, live_own, count
     )
-    gate_weight, up_weight = w_gate_up[:, 0], w_gate_up[:, 1]
+    feed_weight = jnp.transpose(w_gate_up, (1, 2, 0))
     middle, full_normed2, grad_gate, grad_up, hidden = branch_and_feed(
         mixed,
         w_out,
         block_in,
         live_own,
         norm2_gain[None],
-        gate_weight,
-        up_weight,
+        feed_weight,
         w_down,
         grad_feed,
         count,
     )
-    grad_middle, grad_gain2, grad_mixed, grad_wout, *early = feed_back(
+    grad_middle, grad_gain2, grad_mixed, grad_wout, early = feed_back(
         grad_gate,
         grad_up,
-        gate_weight,
-        up_weight,
+        feed_weight,
         cotangent,
         middle,
         live_own,
@@ -1699,7 +1782,7 @@
         grad_feed,
         count,
     )
-    early = lax.optimization_barrier(lax.psum(lax.optimization_barrier(early), "dp"))
+    early = lax.psum(early, "dp")
     dprojected, dtaps, dparams, dgain, layer_out = mixer_backward(
         longer,
         grad_mixed.reshape(all_rows, width),
@@ -1754,8 +1837,8 @@
         small[2, : out_gain.shape[0]],
         grad_rest[:, 128:].T.astype(F32),
         small[1],
-        jnp.stack([early[0], early[1]], axis=1).astype(F32),
-        early[2].T.astype(F32),
+        jnp.transpose(early[:2].astype(F32), (2, 0, 1)),
+        early[2].astype(F32),
     )
 
 

time: 1010 us -> 861 us (0.85)
  Pallas kernels: 914 us -> 797 us
  local copies, waits for them, and re-layouts: 53.8 us -> 21.6 us
    pallas_call x1, Pallas kernels: 203 us -> 168 us  [input_back(): pl.pallas_call(functools.partial(input_back_kernel, count), out_shape=[ja...]
    pallas_call x1, Pallas kernels: 129 us -> 101 us  [mixer_backward(): pl.pallas_call(functools.partial(backward_kernel, heads, chunks, count),...]
    unnamed x21 -> x15, local copies, waits for them, and re-layouts: 35.6 us -> 8.55 us
    pallas_call x1, Pallas kernels: 188 us -> 165 us  [feed_back(): pl.pallas_call(functools.partial(feed_back_kernel, count), out_shape=[jax...]
    pallas_call x1, Pallas kernels: 116 us -> 96.6 us  [mixer_forward(): pl.pallas_call(functools.partial(forward_kernel, heads, count, chunks), g...]
  transfers between devices with their start and end apart: 1 -> 1, of which waited for: 0 -> 0; matrix products, arithmetic and copies ran while one was open for 1% -> 2% of each run, Pallas kernels for 34% -> 33%
where the time goes in v6:
time: 861 us; the launch traced here: 852 us
  Pallas kernels  797 us (93%)
  local copies, waits for them, and re-layouts  21.6 us (3%)
  other arithmetic  17.3 us (2%)
  between operations  15.7 us (2%)
    pallas_call x1, Pallas kernels, input_back(): pl.pallas_call(functools.partial(input_back_kernel, count), out_shape=[ja...  168 us
    pallas_call x1, Pallas kernels, branch_and_feed(): pl.pallas_call(functools.partial(branch_kernel, count), out_shape=[jax.Sh...  166 us
    pallas_call x1, Pallas kernels, feed_back(): pl.pallas_call(functools.partial(feed_back_kernel, count), out_shape=[jax...  165 us
    pallas_call x1, Pallas kernels, mixer_backward(): pl.pallas_call(functools.partial(backward_kernel, heads, chunks, count),...  101 us
    pallas_call x1, Pallas kernels, mixer_forward(): pl.pallas_call(functools.partial(forward_kernel, heads, count, chunks), g...  96.6 us
    pallas_call x1, Pallas kernels, project(): pl.pallas_call(functools.partial(project_kernel, count), out_shape=[jax.S...  93.8 us
  transfers between devices with their start and end apart: 1, of which 0 were waited for; matrix products, arithmetic and copies ran while one was open for 2% of the time, Pallas kernels for 33%

profile of v6, /device:TPU:1, one launch (start us, length us, event | category | flops | bytes accessed | tf_op | source)
XLA Modules:
  0.0 852.0 jit_solution(3788811445260479773)
XLA Ops:
  7.2 0.0 all-reduce.7.cloned.1.call-start
  7.2 1.3 fusion.4
  8.5 0.0 copy-start.2
  8.5 0.0 copy-start.4
  8.5 5.3 copy.37
  13.8 0.0 copy-done.2
  13.8 0.3 copy.32
  15.5 0.9 pad.20.gates_ref
  16.4 0.0 copy-done.4
  16.4 0.6 pad.21.params_ref
  16.9 0.7 fusion.2.live_ref
  17.6 93.8 %project.1 = (bf16[4,4,2,256,512]{4,3,2,1,0:T(8,128)(2,1)}, f32[8,256,1152]{2,1,0:T(8,128)}) custom-call(bf16[256,2048]{1,0:T(8,128)(2,1)} %input_ref.3, f32[1,2048]{1,0:T(1,128)} %bitcast.58, bf16[2048,1024]{1,0:T(8,128)(2,1)} %bitcast.43, bf16[2048,128]{1,0:T(8,128)(2,1)} %pad.20.gates_ref), custom_call_target="tpu_custom_call" | custom-call | flops 109999996928 | bytes 1048576 | tf_op jit(solution)/shard_map/project/pallas_call | solution.py:1087
  111.5 96.6 %mixer_forward.1 = (bf16[2048,256]{1,0:T(8,128)(2,1)}, f32[2048,768]{1,0:T(8,128)}, f32[2048,256]{1,0:T(8,128)}, f32[2048,256]{1,0:T(8,128)}, f32[2,2048,256]{2,...) custom-call(s32[1]{0:T(128)} %bitcast.longer_ref, f32[2048,1152]{1,0:T(8,128)} %bitcast.62, ...), custom_call_target="tpu_custom_call" | custom-call | flops 104500002816 | bytes 1048576 | tf_op jit(solution)/shard_map/mixer_forward/pallas_call | solution.py:453
  208.0 165.5 %branch_and_feed.1 = (f32[256,2048]{1,0:T(8,128)}, bf16[4,2,256,2048]{3,2,1,0:T(8,128)(2,1)}, bf16[8,256,704]{2,1,0:T(8,128)(2,1)}, bf16[8,256,704]{2,1,0:T(8,128)(2,1)}, bf16[8,256,704]{2,1,0:T(8,128)(2,1)}) custom-call(bf16[8,256,256]{2,1,0:T(8,128)(2,1)} %bitcast.66, bf16[256,2048]{1,0:T(8,128)(2,1)} %out_weight_ref.1, bf16[256,2048]{1,0:T(8,128)(2,1)} %input_ref.3, ...), custom_call_target="tpu_custom_call" | custom-call | flops 198000001024 | bytes 1048576 | tf_op jit(solution)/shard_map/branch_and_feed/pallas_call | solution.py:1222
  373.6 164.5 %feed_back.1 = (f32[256,2048]{1,0:T(8,128)}, f32[1,2048]{1,0:T(1,128)}, f32[8,256,256]{2,1,0:T(8,128)}, bf16[2048,256]{1,0:T(8,128)(2,1)}, bf16[3,704,2048]{2,1,0:T(8,128)(2,1)}) custom-call(bf16[8,256,704]{2,1,0:T(8,128)(2,1)} %get-tuple-element.43.dgate_ref, bf16[8,256,704]{2,1,0:T(8,128)(2,1)} %get-tuple-element.44.dup_ref, ...), custom_call_target="tpu_custom_call" | custom-call | flops 198000001024 | bytes 1048576 | tf_op jit(solution)/shard_map/feed_back/pallas_call | solution.py:1378
  538.1 0.0 all-reduce.7.cloned.1.call-update
  538.1 0.0 copy-start.3
  538.1 100.7 %mixer_backward.1 = (bf16[2048,1152]{1,0:T(8,128)(2,1)}, f32[4,768]{1,0:T(4,128)}, f32[2,128]{1,0:T(2,128)}, f32[1,128]{1,0:T(1,128)}, bf16[256,2048]{1,0:T(8,128)(2,1)}) custom-call(s32[1]{0:T(128)} %bitcast.longer_ref, f32[2048,256]{1,0:T(8,128)} %bitcast.65, f32[2048,1152]{1,0:T(8,128)} %bitcast.63, f32[2048,768]{1,0:T(8,128)} %get-tuple-element.49.conv_out_ref, ...), custom_call_target="tpu_custom_call" | custom-call | flops 109999996928 | bytes 1048576 | tf_op jit(solution)/shard_map/mixer_backward/pallas_call | solution.py:504
  638.8 0.7 pad.23
  639.5 0.6 pad.22
  640.1 0.6 pad.24
  640.8 0.0 copy-done.3
  640.8 0.7 concatenate.3.small_ref
  641.5 167.8 %input_back.1 = (f32[256,2048]{1,0:T(8,128)}, f32[8,2048]{1,0:T(8,128)}, bf16[4,4,512,256]{3,2,1,0:T(8,128)(2,1)}, bf16[4,512,384]{2,1,0:T(8,128)(2,1)}) custom-call(bf16[8,256,1152]{2,1,0:T(8,128)(2,1)} %bitcast.64, bf16[2048,1024]{1,0:T(8,128)(2,1)} %bitcast.44, bf16[2048,128]{1,0:T(8,128)(2,1)} %pad.20.gates_ref, ...), custom_call_target="tpu_custom_call" | custom-call | flops 131999997952 | bytes 1048576 | tf_op jit(solution)/shard_map/input_back/pallas_call | solution.py:1674
  809.3 1.3 slice.39
  810.7 1.3 slice.41
  811.9 8.4 by_rows.1
  820.4 1.3 slice.49
  821.7 0.6 copy.36
  822.3 1.1 slice_convert_fusion
  823.4 0.3 copy.38
  823.8 0.7 reshape.94
  824.4 1.2 slice_bitcast_fusion.1
  825.6 1.5 fusion.3
  827.1 1.6 convert_bitcast_fusion.1
  828.7 0.0 all-reduce.7.cloned.1.call-done
  828.7 8.7 %convert_bitcast_fusion = f32[2048,2,704]{0,2,1:T(8,128)} fusion(bf16[3,704,2048]{2,1,0:T(8,128)(2,1)} %all-reduce.7.cloned.1.call-done), kind=kLoop, calls=%fused_computation | loop fusion | flops 2883584 | bytes 17301504 | tf_op jit(solution)/shard_map/transpose | solution.py:1840
  837.4 0.0 copy-start.1
  837.4 0.0 copy-start
  837.4 5.3 fusion
  842.6 0.0 copy-done.1
  842.6 1.0 copy.42
  843.6 0.0 copy-done
  843.6 1.3 copy.43
  (2 shorter events, 0.0 us)
Async XLA Ops:
  7.2 821.5 %all-reduce.7.cloned.1.call-start = ((), (), s32[]{:S(2)}) async-start(), calls=%async_computation | async-start | bytes 17301504 | tf_op jit(solution)/shard_map/psum | solution.py:1785
  8.5 5.3 copy-start.2
  8.5 7.8 copy-start.4
  538.1 102.7 %copy-start.3 = (f32[1,2048]{1,0:T(1,128)S(1)}, f32[1,2048]{1,0:T(1,128)}, u32[]{:S(2)}) copy-start(f32[1,2048]{1,0:T(1,128)} %get-tuple-element.58) | copy-start | bytes 24580
  837.4 5.3 copy-start.1
  837.4 6.2 copy-start
Sparse Core Ops, SparseCore 0:
  538.2 185.3 all-reduce.6

commit v7 on v6

--- a/solution.py
+++ b/solution.py
@@ -995,6 +995,30 @@
 PAIR_SHARE, GATHER_SHARE, SCATTER_SHARE = 2, 1, 2
 
 
+class Late:
+    def __init__(self, given, held, sem):
+        self.held = held
+        self.copy = pltpu.make_async_copy(given, held, sem)
+        self.copy.start()
+
+    def wait(self):
+        self.copy.wait()
+
+
+def late_all(given, scratch):
+    return [
+        Late(ref, held, sem)
+        for ref, held, sem in zip(given, scratch[: len(given)], scratch[len(given) :])
+    ]
+
+
+def late_scratch(*values):
+    return [
+        *[pltpu.VMEM(value.shape, value.dtype) for value in values],
+        *[pltpu.SemaphoreType.DMA] * len(values),
+    ]
+
+
 def lasting(microseconds):
     return pl.CostEstimate(
         flops=int(microseconds * 1.1e9), bytes_accessed=2**20, transcendentals=0
@@ -1016,12 +1040,17 @@
 
 
 def project_kernel(
-    count, rows_ref, gain_ref, weight_ref, gates_ref, full_out, projected_out, *scratch
+    count, rows_ref, gain_ref, weight_ref, gates_ref, full_out, projected_out, weight_out, *scratch
 ):
-    full, staged, full_sems, staged_sems = scratch[0], *scratch[GATHER_COUNT:]
+    full = scratch[0]
+    staged, full_sems, staged_sems, given, weight, given_sem, out_sem = scratch[GATHER_COUNT:]
+    late = Late(weight_ref, given, given_sem)
     group = Group(count)
     gather = gather_of(group, GATHER_SHARE, scratch[:GATHER_COUNT])
     meet(count)
+    weight_copy = pltpu.make_async_copy(weight, weight_out, out_sem)
+    kinds, width = given.shape[1:]
+    blocks = given.shape[0] // 256
     shares, share = full_out.shape[0], full_out.shape[4]
 
     def full_copy(piece, index):
@@ -1053,23 +1082,35 @@
             staged[:, rows, cols] = split(value, count)
 
         left = joined(full[:, :, rows])
-        wide_dot([(left, weight_ref)], NN, 256, store)
+        wide_dot([(left, weight)], NN, 256, store)
         value = lax.dot_general(
             left, gates_ref[...], (NN, ((), ())), preferred_element_type=F32
         )
-        staged[:, rows, weight_ref.shape[1] :] = split(value, count)
+        staged[:, rows, kinds * width :] = split(value, count)
         staged_copy(piece).start()
 
     before, within, behind = gather_ticks(gather, prepare, ready)
+
+    def lay_out(block, _):
+        rows = pl.ds(pl.multiple_of(block * 256, 256), 256)
+        for kind in range(kinds):
+            weight[rows, kind * width : (kind + 1) * width] = given[rows, kind, :]
+        return 0
 
     def tick(time, _):
         before(time)
+        pl.when(time == 0)(late.wait)
+        lax.fori_loop(
+            jnp.minimum(time * 2, blocks), jnp.minimum(time * 2 + 2, blocks), lay_out, 0
+        )
+        pl.when(time == 4)(weight_copy.start)
         at_each_z(group, functools.partial(within, time))
         behind(time)
         return 0
 
     lax.fori_loop(0, PIECES + gather.last, tick, 0)
     gather.drain()
+    weight_copy.wait()
 
     def finish(piece, _):
         for index in range(shares):
@@ -1082,21 +1123,26 @@
 
 def project(rows, gain, weight, gates, count, shares):
     own, features = rows.shape
-    cols = weight.shape[1] + gates.shape[1]
+    kinds, width = weight.shape[1:]
+    cols = kinds * width + gates.shape[1]
     nz, nx = grid_sizes(count)
     return pl.pallas_call(
         functools.partial(project_kernel, count),
         out_shape=[
             jax.ShapeDtypeStruct((shares, nz, nx, own, features // shares), BF16),
             jax.ShapeDtypeStruct((count, own, cols), F32),
+            jax.ShapeDtypeStruct((features, kinds * width), BF16),
         ],
-        in_specs=[VMEM_SPEC] * 4,
-        out_specs=[ANY_SPEC] * 2,
+        in_specs=[VMEM_SPEC, VMEM_SPEC, ANY_SPEC, VMEM_SPEC],
+        out_specs=[ANY_SPEC] * 3,
         scratch_shapes=[
             *gather_scratch(nz, nx, own, features),
             pltpu.VMEM((count, own, cols), F32),
             pltpu.SemaphoreType.DMA((PIECES, shares)),
             pltpu.SemaphoreType.DMA((PIECES,)),
+            pltpu.VMEM(weight.shape, BF16),
+            pltpu.VMEM((features, kinds * width), BF16),
+            *[pltpu.SemaphoreType.DMA] * 2,
         ],
         compiler_params=linked(0),
         cost_estimate=lasting(100),
@@ -1137,9 +1183,11 @@
 
 def branch_kernel(
     count, mixed_ref, weight_ref, input_ref, live_ref, gain_ref, feed_weight_ref,
-    down_weight_ref, grad_ref, middle_out, full_out, dgate_out, dup_out, hidden_out, *scratch
+    down_weight_ref, grad_ref, middle_out, full_out, dgate_out, dup_out, hidden_out, *all_scratch
 ):
-    *scratch, grads, grad_sems, dgate, dup, hidden, feed_sems = scratch
+    *scratch, grads, grad_sems, dgate, dup, hidden, feed_sems = all_scratch[:-4]
+    lates = late_all((feed_weight_ref, down_weight_ref), all_scratch[-4:])
+    feed_weight_ref, down_weight_ref = (late.held for late in lates)
     group = Group(count)
     scatter = scatter_of(group, PAIR_SHARE, scratch[:SCATTER_COUNT])
     gather = gather_of(group, PAIR_SHARE, scratch[SCATTER_COUNT:])
@@ -1183,6 +1231,8 @@
 
     def ready(piece):
         rows = gather.rows(piece)
+        for late in lates:
+            pl.when(piece == 0)(late.wait)
         fetch(piece).wait()
         pl.when(piece + 1 < PIECES)(lambda: fetch(piece + 1).start())
         left, grad = joined(full[:, :, rows]), joined(grads[piece % 2])
@@ -1226,7 +1276,7 @@
             jax.ShapeDtypeStruct((nz, nx, own, features), BF16),
             *[jax.ShapeDtypeStruct((count, own, hidden), BF16)] * 3,
         ],
-        in_specs=[VMEM_SPEC] * 7 + [ANY_SPEC],
+        in_specs=[VMEM_SPEC] * 5 + [ANY_SPEC] * 3,
         out_specs=[VMEM_SPEC] + [ANY_SPEC] * 4,
         scratch_shapes=[
             *scatter_scratch(nz, nx, own, features, PAIR_SHARE),
@@ -1235,6 +1285,7 @@
             pltpu.SemaphoreType.DMA((2,)),
             *[pltpu.VMEM((count, own, hidden), BF16)] * 3,
             pltpu.SemaphoreType.DMA((PIECES, 4)),
+            *late_scratch(feed_weight, down_weight),
         ],
         compiler_params=linked(1),
         cost_estimate=lasting(180),
@@ -1289,9 +1340,13 @@
 def feed_back_kernel(
     count, dgate_ref, dup_ref, feed_weight_ref, top_ref, middle_ref, live_ref,
     gain_ref, out_weight_ref, mixed_ref, hidden_ref, normed_ref, grad_feed_ref,
-    dmiddle_out, dgain_out, dmixed_out, dweight_out, dfeed_out, *scratch
+    dmiddle_out, dgain_out, dmixed_out, dweight_out, dfeed_out, *all_scratch
 ):
-    *scratch, total_out, tile, grad_tile, staged, grad_staged, fetch_sems, out_sems = scratch
+    lates = late_all((out_weight_ref, mixed_ref, hidden_ref), all_scratch[-6:])
+    out_weight_ref, mixed_ref, hidden_ref = (late.held for late in lates)
+    *scratch, total_out, tile, grad_tile, staged, grad_staged, fetch_sems, out_sems = (
+        all_scratch[:-6]
+    )
     group = Group(count)
     scatter = scatter_of(group, PAIR_SHARE, scratch[:SCATTER_COUNT])
     gather = gather_of(group, PAIR_SHARE, scratch[SCATTER_COUNT:])
@@ -1343,6 +1398,8 @@
 
     def ready(piece):
         rows = gather.rows(piece)
+        for late in lates[:2]:
+            pl.when(piece == 0)(late.wait)
         left, mixed = joined(full[:, :, rows]), joined(mixed_ref[:, rows])
 
         def store(cols, value):
@@ -1355,6 +1412,7 @@
             )
 
     def job(time):
+        pl.when(time == 1)(lates[2].wait)
         for which, each in enumerate(jobs):
             pl.when((time % 2 == which) & (time < 2 * each.count))(
                 functools.partial(each.run, time // 2)
@@ -1384,7 +1442,7 @@
             jax.ShapeDtypeStruct((features, width), BF16),
             jax.ShapeDtypeStruct((3, units, features), BF16),
         ],
-        in_specs=[VMEM_SPEC] * 10 + [ANY_SPEC] * 2,
+        in_specs=[VMEM_SPEC] * 7 + [ANY_SPEC] * 5,
         out_specs=[VMEM_SPEC] * 4 + [ANY_SPEC],
         scratch_shapes=[
             *scatter_scratch(nz, nx, own, features, PAIR_SHARE),
@@ -1396,6 +1454,7 @@
             pltpu.VMEM((1, units, TILE), BF16),
             pltpu.SemaphoreType.DMA((2,)),
             pltpu.SemaphoreType.DMA((2, 2)),
+            *late_scratch(out_weight, split(mixed, count), hidden),
         ],
         compiler_params=linked(2),
         cost_estimate=lasting(180),
@@ -1559,9 +1618,13 @@
 
 
 def input_back_kernel(
-    count, grad_ref, weight_ref, gates_ref, normed_ref, later_ref, input_ref, gain_ref, small_ref,
-    wout_ref, grad_out, small_out, dmain_out, drest_out, *scratch
+    count, grad_ref, weight_ref, gates_ref, later_ref, input_ref, gain_ref, dgain_ref, dnorm_ref,
+    dtaps_ref, dparams_ref, wout_ref, normed_ref, grad_out, norm1_out, norm2_out, gain_out,
+    taps_out, params_out, dmain_out, drest_out, *scratch
 ):
+    *scratch, small_out, normed, normed_sem = scratch
+    late = Late(normed_ref, normed, normed_sem)
+    normed_ref = normed
     parts, rest = scratch[0], scratch[SCATTER_COUNT:]
     values = rest[0]
     near, near_send, near_recv, far, far_send, far_recv, staged, out_sems = rest[9:]
@@ -1569,7 +1632,12 @@
     scatter = scatter_of(group, SCATTER_SHARE, scratch[:SCATTER_COUNT])
     replicas = Replicas(*rest[:5], rest[5:9])
     meet(count, lax.axis_size("dp"))
-    small_out[...] = small_ref[...]
+    small_out[...] = jnp.zeros(small_out.shape, F32)
+    small_out[1:2] = dnorm_ref[...]
+    small_out[2:3, : dgain_ref.shape[1]] = dgain_ref[...]
+    small_out[3:7, : dtaps_ref.shape[1]] = dtaps_ref[...]
+    for row in range(2):
+        small_out[7:8, 128 * row : 128 * (row + 1)] = dparams_ref[row : row + 1]
     width = grad_ref.shape[2]
     values[:, :, width:] = split(wout_ref[...], values.shape[0])
 
@@ -1595,7 +1663,9 @@
             scaled - normed * jnp.mean(scaled * normed, axis=-1, keepdims=True)
         )
 
-    def weight_share(core, y):
+    def weight_share(core, y, first=False):
+        if first:
+            late.wait()
         share = replicas.share(core, y)
         left = joined(normed_ref[share])
         grads = joined(grad_ref[...])
@@ -1613,7 +1683,7 @@
         lax.fori_loop(0, staged.shape[0] // 64, some, 0)
 
     def other_core(k):
-        weight_share(1 - replicas.core, replicas.line(k))
+        weight_share(1 - replicas.core, replicas.line(k), k == replicas.lines - 1)
         replicas.start(k)
 
     def this_core(k):
@@ -1623,7 +1693,7 @@
     steps = []
     for k in range(replicas.lines - 1, -1, -1):
         steps += [functools.partial(other_core, k), functools.partial(this_core, k)]
-    while len(steps) < PIECES - 1:
+    while len(steps) < 5:
         steps.append(lambda: None)
     steps.append(replicas.over_y)
 
@@ -1641,6 +1711,14 @@
     replicas.back()
     copies = sum_small(small_out, near, near_send, near_recv, "heads", 3)
     copies += sum_small(small_out, far, far_send, far_recv, "dp", 8)
+    norm1_out[...] = small_out[0:1]
+    norm2_out[...] = small_out[1:2]
+    gain_out[...] = small_out[2:3, : gain_out.shape[1]]
+    kind_width = taps_out.shape[2]
+    for kind in range(taps_out.shape[0]):
+        taps_out[kind] = small_out[3:7, kind * kind_width : (kind + 1) * kind_width]
+    for row in range(2):
+        params_out[row : row + 1] = small_out[7:8, 128 * row : 128 * (row + 1)]
     replicas.home()
     part = dmain_out.shape[3]
     outs = []
@@ -1664,7 +1742,8 @@
 
 
 def input_back(
-    grad, weight, gates, normed, later, rows, gain, small, grad_wout, count, replica_count
+    grad, weight, gates, later, rows, gain, dgain, dnorm, dtaps, dparams, grad_wout, normed, count,
+    replica_count,
 ):
     own, features = rows.shape
     nz, nx = grid_sizes(count)
@@ -1675,28 +1754,37 @@
         functools.partial(input_back_kernel, count),
         out_shape=[
             jax.ShapeDtypeStruct((own, features), F32),
-            jax.ShapeDtypeStruct(small.shape, F32),
+            *[jax.ShapeDtypeStruct((1, features), F32)] * 2,
+            jax.ShapeDtypeStruct(dgain.shape, F32),
+            jax.ShapeDtypeStruct((3, 4, width), F32),
+            jax.ShapeDtypeStruct(dparams.shape, F32),
             jax.ShapeDtypeStruct((4, replica_count, share, width), BF16),
             jax.ShapeDtypeStruct((replica_count, share, cols - 4 * width), BF16),
         ],
-        in_specs=[VMEM_SPEC] * 9,
-        out_specs=[VMEM_SPEC, VMEM_SPEC, ANY_SPEC, ANY_SPEC],
+        in_specs=[VMEM_SPEC] * 11 + [ANY_SPEC],
+        out_specs=[VMEM_SPEC] * 6 + [ANY_SPEC] * 2,
         scratch_shapes=[
             *scatter_scratch(nz, nx, own, features, SCATTER_SHARE),
             *Replicas.scratch(features, cols, replica_count),
-            pltpu.VMEM((count, *small.shape), F32),
+            pltpu.VMEM((count, 8, features), F32),
             dma((count,)),
             dma((count,)),
-            pltpu.VMEM((replica_count, *small.shape), F32),
+            pltpu.VMEM((replica_count, 8, features), F32),
             dma((replica_count,)),
             dma((replica_count,)),
             pltpu.VMEM((share, grad.shape[1]), BF16),
             dma((replica_count, 5)),
+            pltpu.VMEM((8, features), F32),
+            pltpu.VMEM(normed.shape, BF16),
+            dma,
         ],
         compiler_params=linked(3),
         cost_estimate=lasting(120),
         name="input_back",
-    )(split(grad, count), weight, gates, normed, later, rows, gain, small, grad_wout)
+    )(
+        split(grad, count), weight, gates, later, rows, gain, dgain, dnorm, dtaps, dparams,
+        grad_wout, normed,
+    )
 
 
 def spread_kernel(given_ref, out_ref):
@@ -1741,12 +1829,11 @@
     row_index = first_row + jnp.arange(own_rows, dtype=jnp.int32)
     live_own = jnp.where(longer[0] > 0, True, row_index < seq_counts[0, 0] * SEQ_SHORT)
     live_own = live_own.astype(F32)[:, None]
-    weight = w_qkvg.reshape(features, 4 * width)
     gates_weight = jnp.pad(
         w_gates.reshape(features, 2 * heads), ((0, 0), (0, 128 - 2 * heads))
     )
-    full_normed1, projected = project(
-        block_in, norm1_gain[None], weight, gates_weight, count, lax.axis_size("dp")
+    full_normed1, projected, weight = project(
+        block_in, norm1_gain[None], w_qkvg, gates_weight, count, lax.axis_size("dp")
     )
     projected = projected.reshape(all_rows, -1)
     taps = jnp.transpose(conv_weight, (1, 0, 2)).reshape(4, 3 * width)
@@ -1798,29 +1885,19 @@
         count,
     )
 
-    def row(values):
-        return jnp.pad(values, ((0, 0), (0, features - values.shape[1])))
-
-    small = jnp.concatenate(
-        [
-            jnp.zeros((1, features), F32),
-            grad_gain2,
-            row(dgain),
-            row(dtaps),
-            row(dparams.reshape(1, 256)),
-        ],
-        axis=0,
-    )
-    grad_in, small, grad_main, grad_rest = input_back(
+    grad_in, grad_gain1, grad_gain2, dgain, grad_conv, dparams, grad_main, grad_rest = input_back(
         dprojected,
         weight,
         gates_weight,
-        full_normed1,
         grad_middle,
         block_in,
         norm1_gain[None],
-        small,
+        dgain,
+        grad_gain2,
+        dtaps,
+        dparams,
         grad_wout,
+        full_normed1,
         count,
         lax.axis_size("dp"),
     )
@@ -1829,14 +1906,14 @@
     return (
         layer_out,
         grad_in,
-        small[0],
+        grad_gain1[0],
         by_rows(grad_main),
-        jnp.transpose(small[3:7, : 3 * width].reshape(4, 3, width), (1, 0, 2)),
+        grad_conv,
         grad_rest[:, : 2 * heads].reshape(w_gates.shape).astype(F32),
-        small[7, :256].reshape(2, 128)[:, :heads],
-        small[2, : out_gain.shape[0]],
+        dparams[:, :heads],
+        dgain[0],
         grad_rest[:, 128:].T.astype(F32),
-        small[1],
+        grad_gain2[0],
         jnp.transpose(early[:2].astype(F32), (2, 0, 1)),
         early[2].astype(F32),
     )

time: 861 us -> 834 us (0.969)
  Pallas kernels: 797 us -> 779 us
    pallas_call x1, Pallas kernels: 168 us -> 144 us  [input_back(): pl.pallas_call(functools.partial(input_back_kernel, count), out_shape=[ja...]
  transfers between devices with their start and end apart: 1 -> 1, of which waited for: 0 -> 0; matrix products, arithmetic and copies ran while one was open for 2% -> 1% of each run, Pallas kernels for 33% -> 32%
where the time goes in v7:
time: 834 us; the launch traced here: 823 us
  Pallas kernels  779 us (93%)
  between operations  15.7 us (2%)
  other arithmetic  14.7 us (2%)
  local copies, waits for them, and re-layouts  13.2 us (2%)
    pallas_call x1, Pallas kernels, branch_and_feed(): pl.pallas_call(functools.partial(branch_kernel, count), out_shape=[jax.Sh...  165 us
    pallas_call x1, Pallas kernels, feed_back(): pl.pallas_call(functools.partial(feed_back_kernel, count), out_shape=[jax...  165 us
    pallas_call x1, Pallas kernels, input_back(): pl.pallas_call(functools.partial(input_back_kernel, count), out_shape=[ja...  144 us
    pallas_call x1, Pallas kernels, mixer_backward(): pl.pallas_call(functools.partial(backward_kernel, heads, chunks, count),...  107 us
    pallas_call x1, Pallas kernels, mixer_forward(): pl.pallas_call(functools.partial(forward_kernel, heads, count, chunks), g...  97.3 us
    pallas_call x1, Pallas kernels, project(): pl.pallas_call(functools.partial(project_kernel, count), out_shape=[jax.S...  92.5 us
  transfers between devices with their start and end apart: 1, of which 0 were waited for; matrix products, arithmetic and copies ran while one was open for 1% of the time, Pallas kernels for 32%

profile of v7, /device:TPU:1, one launch (start us, length us, event | category | flops | bytes accessed | tf_op | source)
XLA Modules:
  0.0 822.7 jit_solution(7052396378233316326)
XLA Ops:
  7.2 0.0 all-reduce.4.cloned.1.call-start
  7.2 1.3 fusion.3
  8.5 0.7 reshape.74
  9.3 0.3 copy.31
  9.6 1.3 pad.9.params_ref
  12.1 0.9 pad.8.gates_ref
  13.0 0.7 fusion.2.live_ref
  13.7 92.5 %project.1 = (bf16[4,4,2,256,512]{4,3,2,1,0:T(8,128)(2,1)}, f32[8,256,1152]{2,1,0:T(8,128)}, bf16[2048,1024]{1,0:T(8,128)(2,1)}) custom-call(bf16[256,2048]{1,0:T(8,128)(2,1)} %input_ref.3, f32[1,2048]{1,0:T(1,128)} %bitcast.45, bf16[2048,4,256]{2,1,0:T(4,128)(2,1)} %weight_ref.2, bf16[2048,128]{1,0:T(8,128)(2,1)} %pad.8.gates_ref), custom_call_target="tpu_custom_call" | custom-call | flops 109999996928 | bytes 1048576 | tf_op jit(solution)/shard_map/project/pallas_call | solution.py:1129
  106.2 97.3 %mixer_forward.1 = (bf16[2048,256]{1,0:T(8,128)(2,1)}, f32[2048,768]{1,0:T(8,128)}, f32[2048,256]{1,0:T(8,128)}, f32[2048,256]{1,0:T(8,128)}, f32[2,2048,256]{2,...) custom-call(s32[1]{0:T(128)} %bitcast.longer_ref, f32[2048,1152]{1,0:T(8,128)} %bitcast.49, ...), custom_call_target="tpu_custom_call" | custom-call | flops 104500002816 | bytes 1048576 | tf_op jit(solution)/shard_map/mixer_forward/pallas_call | solution.py:453
  203.5 165.1 %branch_and_feed.1 = (f32[256,2048]{1,0:T(8,128)}, bf16[4,2,256,2048]{3,2,1,0:T(8,128)(2,1)}, bf16[8,256,704]{2,1,0:T(8,128)(2,1)}, bf16[8,256,704]{2,1,0:T(8,128)(2,1)}, bf16[8,256,704]{2,1,0:T(8,128)(2,1)}) custom-call(bf16[8,256,256]{2,1,0:T(8,128)(2,1)} %bitcast.53, bf16[256,2048]{1,0:T(8,128)(2,1)} %out_weight_ref.1, bf16[256,2048]{1,0:T(8,128)(2,1)} %input_ref.3, ...), custom_call_target="tpu_custom_call" | custom-call | flops 198000001024 | bytes 1048576 | tf_op jit(solution)/shard_map/branch_and_feed/pallas_call | solution.py:1272
  368.6 164.8 %feed_back.1 = (f32[256,2048]{1,0:T(8,128)}, f32[1,2048]{1,0:T(1,128)}, f32[8,256,256]{2,1,0:T(8,128)}, bf16[2048,256]{1,0:T(8,128)(2,1)}, bf16[3,704,2048]{2,1,0:T(8,128)(2,1)}) custom-call(bf16[8,256,704]{2,1,0:T(8,128)(2,1)} %get-tuple-element.48.dgate_ref, bf16[8,256,704]{2,1,0:T(8,128)(2,1)} %get-tuple-element.49.dup_ref, ...), custom_call_target="tpu_custom_call" | custom-call | flops 198000001024 | bytes 1048576 | tf_op jit(solution)/shard_map/feed_back/pallas_call | solution.py:1436
  533.4 0.0 all-reduce.4.cloned.1.call-update
  533.4 107.2 %mixer_backward.1 = (bf16[2048,1152]{1,0:T(8,128)(2,1)}, f32[4,768]{1,0:T(4,128)}, f32[2,128]{1,0:T(2,128)}, f32[1,128]{1,0:T(1,128)}, bf16[256,2048]{1,0:T(8,128)(2,1)}) custom-call(s32[1]{0:T(128)} %bitcast.longer_ref, f32[2048,256]{1,0:T(8,128)} %bitcast.52, f32[2048,1152]{1,0:T(8,128)} %bitcast.50, f32[2048,768]{1,0:T(8,128)} %get-tuple-element.54.conv_out_ref, ...), custom_call_target="tpu_custom_call" | custom-call | flops 109999996928 | bytes 1048576 | tf_op jit(solution)/shard_map/mixer_backward/pallas_call | solution.py:504
  640.6 144.0 %input_back.1 = (f32[256,2048]{1,0:T(8,128)}, f32[1,2048]{1,0:T(1,128)}, f32[1,2048]{1,0:T(1,128)}, f32[1,128]{1,0:T(1,128)}, f32[3,4,256]{2,1,0:T(4,128)}, /*in...) custom-call(bf16[8,256,1152]{2,1,0:T(8,128)(2,1)} %bitcast.51, ...), custom_call_target="tpu_custom_call" | custom-call | flops 131999997952 | bytes 1048576 | tf_op jit(solution)/shard_map/input_back/pallas_call | solution.py:1753
  784.6 1.3 slice.29
  785.9 1.1 slice_convert_fusion
  787.1 0.3 copy.36
  787.4 0.8 copy.35
  788.2 0.6 reshape.82
  788.9 8.2 by_rows.1
  797.1 1.6 convert_bitcast_fusion.1
  798.7 0.0 all-reduce.4.cloned.1.call-done
  798.7 0.0 copy-start
  798.7 5.4 fusion
  804.0 0.4 copy-done
  804.4 0.0 copy-start.2
  804.4 0.0 copy-start.1
  804.4 6.0 convert_bitcast_fusion
  810.4 0.0 copy-done.2
  810.4 0.0 copy-start.5
  810.4 0.0 copy-start.3
  810.4 0.0 copy-start.6
  810.4 0.0 copy-start.7
  810.4 0.0 copy-start.4
  810.4 1.0 copy.45
  811.4 0.0 copy-done.1
  811.4 1.3 copy.46
  812.7 0.0 copy-done.5
  812.7 0.6 copy.47
  813.3 0.0 copy-done.3
  813.3 0.6 copy.48
  813.9 0.0 copy-done.6
  813.9 0.6 copy.49
  814.5 0.0 copy-done.7
  814.5 0.5 copy.50
  815.0 0.0 copy-done.4
  815.0 0.6 copy.51
Async XLA Ops:
  7.2 791.5 %all-reduce.4.cloned.1.call-start = ((), (), s32[]{:S(2)}) async-start(), calls=%async_computation | async-start | bytes 17301504 | tf_op jit(solution)/shard_map/psum | solution.py:1872
  798.7 5.7 copy-start
  804.4 6.0 copy-start.2
  804.4 7.0 copy-start.1
  810.4 2.3 copy-start.5
  810.4 2.9 copy-start.3
  810.4 3.5 copy-start.6
  810.4 4.1 copy-start.7
  810.4 4.6 copy-start.4
Sparse Core Ops, SparseCore 0:
  533.5 187.1 all-reduce.3

commit v8 on v7

--- a/solution.py
+++ b/solution.py
@@ -242,10 +242,10 @@
             out(piece).wait()
             return 0
 
-        lax.fori_loop(0, PIECES, finish, 0)
+        lax.fori_loop(0, gather.pieces, finish, 0)
 
     pl.when(step == 0)(functools.partial(meet, count))
-    return spread_ticks(tick, 0, PIECES + gather.last, 2 * chunks), close
+    return spread_ticks(tick, 0, gather.pieces + gather.last, 2 * chunks), close
 
 
 def scatter_along(step, chunks, count, hidden_ref, weight_ref, middle_ref, live_ref, out, scratch):
@@ -273,7 +273,7 @@
         behind(time)
 
     pl.when(step == 0)(functools.partial(meet, count))
-    return spread_ticks(tick, -1, PIECES + scatter.last, 2 * chunks), scatter.drain
+    return spread_ticks(tick, -1, scatter.pieces + scatter.last, 2 * chunks), scatter.drain
 
 
 def backward_kernel(
@@ -483,8 +483,8 @@
         scratch_shapes=[
             pltpu.VMEM((heads, HEAD, HEAD), F32),
             pltpu.VMEM((8, 3 * width), F32),
-            *gather_scratch(nz, nx, own, features),
-            pltpu.SemaphoreType.DMA((PIECES,)),
+            *gather_scratch(nz, nx, own, features, FEW),
+            pltpu.SemaphoreType.DMA((pieces_of(own, FEW),)),
         ],
         compiler_params=linked(4),
         cost_estimate=lasting(95),
@@ -538,7 +538,7 @@
         scratch_shapes=[
             pltpu.VMEM((heads, HEAD, HEAD), F32),
             pltpu.VMEM((8, 3 * width), F32),
-            *scatter_scratch(nz, nx, own, features, SCATTER_SHARE),
+            *scatter_scratch(nz, nx, own, features, SCATTER_SHARE, FEW),
         ],
         compiler_params=linked(5),
         cost_estimate=lasting(100),
@@ -549,7 +549,11 @@
 
 
 MESH = pl.DeviceIdType.MESH
-PIECES = 8
+MANY, FEW = 16, 8
+
+
+def pieces_of(rows, most):
+    return min(most, rows // 16)
 
 
 def grid_sizes(count):
@@ -592,8 +596,8 @@
     pltpu.make_async_copy(ref, ref, sem).wait()
 
 
-def during(piece, work):
-    pl.when((piece >= 0) & (piece < PIECES))(functools.partial(work, piece))
+def during(piece, pieces, work):
+    pl.when((piece >= 0) & (piece < pieces))(functools.partial(work, piece))
 
 
 def push(source, target, send_sem, recv_sem, device):
@@ -605,14 +609,15 @@
 class Gather:
     def __init__(self, group, full, cols, sems, x_first):
         self.group, self.full, self.cols, self.x_first = group, full, cols, x_first
-        self.part = full.shape[2] // PIECES
         self.line_send, self.line_recv, self.x_send, self.x_recv = sems
+        self.pieces = self.x_send.shape[0]
+        self.part = full.shape[2] // self.pieces
         self.last = group.deep
 
     @staticmethod
-    def sems(deep, nx):
+    def sems(deep, nx, pieces):
         dma = pltpu.SemaphoreType.DMA
-        return [dma((PIECES, 2)), dma((PIECES, deep)), dma((PIECES, nx)), dma((PIECES, nx))]
+        return [dma((pieces, 2)), dma((pieces, deep)), dma((pieces, nx)), dma((pieces, nx))]
 
     def at(self, piece, z, column):
         rows = pl.ds(pl.multiple_of(piece * self.part, self.part), self.part)
@@ -695,18 +700,19 @@
 
     def __init__(self, group, parts, cols, scratch, z_first):
         self.group, self.parts, self.cols, self.z_first = group, parts, cols, z_first
-        self.part = parts.shape[2] // PIECES
         self.landed_x, self.line, *sems = scratch
         self.x_send, self.x_recv, self.z_send, self.z_recv = sems
+        self.pieces = self.x_send.shape[0]
+        self.part = parts.shape[2] // self.pieces
 
     @staticmethod
-    def scratch(deep, nx, rows, cols, z_first):
+    def scratch(deep, nx, rows, cols, z_first, pieces):
         dma = pltpu.SemaphoreType.DMA
         return [
             pltpu.VMEM((max(nx - 1, 1), 1 if z_first else deep, rows, cols), BF16),
             pltpu.VMEM((deep + 1, nx if z_first else 1, rows, cols), BF16),
-            *[dma((PIECES, nx))] * 2,
-            *[dma((PIECES, 2))] * 2,
+            *[dma((pieces, nx))] * 2,
+            *[dma((pieces, 2))] * 2,
         ]
 
     def rows(self, piece):
@@ -851,7 +857,7 @@
     def __init__(self, first, second):
         self.both = (first, second)
         self.group = first.group
-        self.part, self.last = first.part, first.last
+        self.part, self.pieces, self.last = first.part, first.pieces, first.last
 
     def rows(self, piece):
         return pl.ds(pl.multiple_of(piece * self.part, self.part), self.part)
@@ -882,7 +888,7 @@
                     each.drain(piece, zz)
                 return 0
 
-            lax.fori_loop(0, PIECES, one, 0)
+            lax.fori_loop(0, self.pieces, one, 0)
 
         at_each_z(self.group, at)
 
@@ -898,16 +904,16 @@
             prepare(piece)
             scatter.begin(piece)
 
-        during(time + 1, begin)
+        during(time + 1, scatter.pieces, begin)
 
     def within(time, zz):
-        for step in range(scatter.last, 0, -1):
-            during(time - step + 1, functools.partial(scatter.phase, step=step, zz=zz))
-        during(time + 1, functools.partial(scatter.begin_line, zz=zz))
+        during(time + 1, scatter.pieces, functools.partial(scatter.begin_line, zz=zz))
+        for step in range(1, scatter.last + 1):
+            during(time - step + 1, scatter.pieces, functools.partial(scatter.phase, step=step, zz=zz))
 
     def behind(time):
-        during(time - 2, scatter.third)
-        during(time - scatter.last + 1, lambda piece: finish(piece, scatter.total(piece)))
+        during(time - 2, scatter.pieces, scatter.third)
+        during(time - scatter.last + 1, scatter.pieces, lambda piece: finish(piece, scatter.total(piece)))
 
     return before, within, behind
 
@@ -920,14 +926,14 @@
                 prepare(piece)
                 gather.begin(piece)
 
-            during(time, begin)
+            during(time, gather.pieces, begin)
 
     def within(time, zz):
-        for step in range(gather.last, 0, -1):
-            during(time - step, functools.partial(gather.phase, step=step, zz=zz))
+        for step in range(1, gather.last + 1):
+            during(time - step, gather.pieces, functools.partial(gather.phase, step=step, zz=zz))
 
     def behind(time):
-        during(time - gather.last, ready)
+        during(time - gather.last, gather.pieces, ready)
 
     return before, within, behind
 
@@ -954,16 +960,18 @@
     )
 
 
-def gather_scratch(nz, nx, rows, cols):
-    return [pltpu.VMEM((nz, nx, rows, cols), BF16), *Gather.sems(nz, nx), *Gather.sems(nz, nx)]
-
-
-def scatter_scratch(nz, nx, rows, cols, share):
+def gather_scratch(nz, nx, rows, cols, most):
+    sems = Gather.sems(nz, nx, pieces_of(rows, most))
+    return [pltpu.VMEM((nz, nx, rows, cols), BF16), *sems, *sems]
+
+
+def scatter_scratch(nz, nx, rows, cols, share, most):
     first, second = cut(cols, share)
+    pieces = pieces_of(rows, most)
     return [
         pltpu.VMEM((nz, nx, rows, cols), BF16),
-        *Scatter.scratch(nz, nx, rows, first.size, False),
-        *Scatter.scratch(nz, nx, rows, second.size, True),
+        *Scatter.scratch(nz, nx, rows, first.size, False, pieces),
+        *Scatter.scratch(nz, nx, rows, second.size, True, pieces),
     ]
 
 
@@ -992,7 +1000,7 @@
 
 VMEM_SPEC = pl.BlockSpec(memory_space=pltpu.VMEM)
 ANY_SPEC = pl.BlockSpec(memory_space=pl.ANY)
-PAIR_SHARE, GATHER_SHARE, SCATTER_SHARE = 2, 1, 2
+PAIR_SHARE, GATHER_SHARE, SCATTER_SHARE = 3, 1, 2
 
 
 class Late:
@@ -1108,7 +1116,7 @@
         behind(time)
         return 0
 
-    lax.fori_loop(0, PIECES + gather.last, tick, 0)
+    lax.fori_loop(0, gather.pieces + gather.last, tick, 0)
     gather.drain()
     weight_copy.wait()
 
@@ -1118,7 +1126,7 @@
         staged_copy(piece).wait()
         return 0
 
-    lax.fori_loop(0, PIECES, finish, 0)
+    lax.fori_loop(0, gather.pieces, finish, 0)
 
 
 def project(rows, gain, weight, gates, count, shares):
@@ -1136,10 +1144,10 @@
         in_specs=[VMEM_SPEC, VMEM_SPEC, ANY_SPEC, VMEM_SPEC],
         out_specs=[ANY_SPEC] * 3,
         scratch_shapes=[
-            *gather_scratch(nz, nx, own, features),
+            *gather_scratch(nz, nx, own, features, FEW),
             pltpu.VMEM((count, own, cols), F32),
-            pltpu.SemaphoreType.DMA((PIECES, shares)),
-            pltpu.SemaphoreType.DMA((PIECES,)),
+            pltpu.SemaphoreType.DMA((pieces_of(own, FEW), shares)),
+            pltpu.SemaphoreType.DMA((pieces_of(own, FEW),)),
             pltpu.VMEM(weight.shape, BF16),
             pltpu.VMEM((features, kinds * width), BF16),
             *[pltpu.SemaphoreType.DMA] * 2,
@@ -1166,8 +1174,8 @@
         before(time)
 
         def within(zz):
+            sum_within(time, zz)
             gather_within(time - late, zz)
-            sum_within(time, zz)
 
         at_each_z(group, within)
         sum_behind(time)
@@ -1176,7 +1184,7 @@
             job(time + 1)
         return 0
 
-    lax.fori_loop(-1, PIECES + late + gather.last, tick, 0)
+    lax.fori_loop(-1, gather.pieces + late + gather.last, tick, 0)
     scatter.drain()
     gather.drain()
 
@@ -1234,7 +1242,7 @@
         for late in lates:
             pl.when(piece == 0)(late.wait)
         fetch(piece).wait()
-        pl.when(piece + 1 < PIECES)(lambda: fetch(piece + 1).start())
+        pl.when(piece + 1 < gather.pieces)(lambda: fetch(piece + 1).start())
         left, grad = joined(full[:, :, rows]), joined(grads[piece % 2])
         total = feed_weight_ref.shape[1]
         for first in range(0, total, 256):
@@ -1262,7 +1270,7 @@
             copy.wait()
         return 0
 
-    lax.fori_loop(0, PIECES, finish, 0)
+    lax.fori_loop(0, gather.pieces, finish, 0)
 
 
 def branch_and_feed(mixed, weight, rows, live, gain, feed_weight, down_weight, grad, count):
@@ -1279,12 +1287,12 @@
         in_specs=[VMEM_SPEC] * 5 + [ANY_SPEC] * 3,
         out_specs=[VMEM_SPEC] + [ANY_SPEC] * 4,
         scratch_shapes=[
-            *scatter_scratch(nz, nx, own, features, PAIR_SHARE),
-            *gather_scratch(nz, nx, own, features),
-            pltpu.VMEM((2, nz, nx, own // PIECES, features), BF16),
+            *scatter_scratch(nz, nx, own, features, PAIR_SHARE, MANY),
+            *gather_scratch(nz, nx, own, features, MANY),
+            pltpu.VMEM((2, nz, nx, own // pieces_of(own, MANY), features), BF16),
             pltpu.SemaphoreType.DMA((2,)),
             *[pltpu.VMEM((count, own, hidden), BF16)] * 3,
-            pltpu.SemaphoreType.DMA((PIECES, 4)),
+            pltpu.SemaphoreType.DMA((pieces_of(own, MANY), 4)),
             *late_scratch(feed_weight, down_weight),
         ],
         compiler_params=linked(1),
@@ -1419,7 +1427,7 @@
             )
 
     sum_and_gather(scatter, gather, prepare, middle, ready, job)
-    last = PIECES + scatter.last + gather.last
+    last = gather.pieces + scatter.last + gather.last
     lax.fori_loop(last, max(2 * jobs[0].count, last), lambda time, _: (job(time), 0)[1], 0)
     for each in jobs:
         each.wait_results(each.count - 1)
@@ -1445,8 +1453,8 @@
         in_specs=[VMEM_SPEC] * 7 + [ANY_SPEC] * 5,
         out_specs=[VMEM_SPEC] * 4 + [ANY_SPEC],
         scratch_shapes=[
-            *scatter_scratch(nz, nx, own, features, PAIR_SHARE),
-            *gather_scratch(nz, nx, own, features),
+            *scatter_scratch(nz, nx, own, features, PAIR_SHARE, MANY),
+            *gather_scratch(nz, nx, own, features, MANY),
             pltpu.VMEM((features, width), F32),
             pltpu.VMEM((nz, nx, own, TILE), BF16),
             pltpu.VMEM((nz, nx, own, TILE), BF16),
@@ -1707,7 +1715,7 @@
             pl.when(time == index)(step)
         return 0
 
-    lax.fori_loop(-1, max(PIECES + scatter.last - 1, len(steps)), tick, 0)
+    lax.fori_loop(-1, max(scatter.pieces + scatter.last - 1, len(steps)), tick, 0)
     replicas.back()
     copies = sum_small(small_out, near, near_send, near_recv, "heads", 3)
     copies += sum_small(small_out, far, far_send, far_recv, "dp", 8)
@@ -1764,7 +1772,7 @@
         in_specs=[VMEM_SPEC] * 11 + [ANY_SPEC],
         out_specs=[VMEM_SPEC] * 6 + [ANY_SPEC] * 2,
         scratch_shapes=[
-            *scatter_scratch(nz, nx, own, features, SCATTER_SHARE),
+            *scatter_scratch(nz, nx, own, features, SCATTER_SHARE, FEW),
             *Replicas.scratch(features, cols, replica_count),
             pltpu.VMEM((count, 8, features), F32),
             dma((count,)),

time: 834 us -> 828 us (level)
    pallas_call x1, Pallas kernels: 144 us -> 158 us  [input_back(): pl.pallas_call(functools.partial(input_back_kernel, count), out_shape=[ja...]
where the time goes in v8:
time: 828 us; the launch traced here: 824 us
  Pallas kernels  781 us (94%)
  between operations  15.7 us (2%)
  other arithmetic  14.7 us (2%)
  local copies, waits for them, and re-layouts  13.2 us (2%)
    pallas_call x1, Pallas kernels, branch_and_feed(): pl.pallas_call(functools.partial(branch_kernel, count), out_shape=[jax.Sh...  163 us
    pallas_call x1, Pallas kernels, feed_back(): pl.pallas_call(functools.partial(feed_back_kernel, count), out_shape=[jax...  160 us
    pallas_call x1, Pallas kernels, input_back(): pl.pallas_call(functools.partial(input_back_kernel, count), out_shape=[ja...  158 us
    pallas_call x1, Pallas kernels, mixer_backward(): pl.pallas_call(functools.partial(backward_kernel, heads, chunks, count),...  99.5 us
    pallas_call x1, Pallas kernels, mixer_forward(): pl.pallas_call(functools.partial(forward_kernel, heads, count, chunks), g...  99.4 us
    pallas_call x1, Pallas kernels, project(): pl.pallas_call(functools.partial(project_kernel, count), out_shape=[jax.S...  93 us
  transfers between devices with their start and end apart: 1, of which 0 were waited for; matrix products, arithmetic and copies ran while one was open for 1% of the time, Pallas kernels for 32%

profile of v8, /device:TPU:1, one launch (start us, length us, event | category | flops | bytes accessed | tf_op | source)
XLA Modules:
  0.0 824.3 jit_solution(4039370817727567225)
XLA Ops:
  7.2 0.0 all-reduce.4.cloned.1.call-start
  7.2 1.3 fusion.3
  8.5 0.7 reshape.74
  9.3 0.3 copy.31
  9.6 1.3 pad.9.params_ref
  12.1 0.9 pad.8.gates_ref
  13.0 0.7 fusion.2.live_ref
  13.7 93.0 %project.1 = (bf16[4,4,2,256,512]{4,3,2,1,0:T(8,128)(2,1)}, f32[8,256,1152]{2,1,0:T(8,128)}, bf16[2048,1024]{1,0:T(8,128)(2,1)}) custom-call(bf16[256,2048]{1,0:T(8,128)(2,1)} %input_ref.3, f32[1,2048]{1,0:T(1,128)} %bitcast.45, bf16[2048,4,256]{2,1,0:T(4,128)(2,1)} %weight_ref.2, bf16[2048,128]{1,0:T(8,128)(2,1)} %pad.8.gates_ref), custom_call_target="tpu_custom_call" | custom-call | flops 109999996928 | bytes 1048576 | tf_op jit(solution)/shard_map/project/pallas_call | solution.py:1137
  106.8 99.4 %mixer_forward.1 = (bf16[2048,256]{1,0:T(8,128)(2,1)}, f32[2048,768]{1,0:T(8,128)}, f32[2048,256]{1,0:T(8,128)}, f32[2048,256]{1,0:T(8,128)}, f32[2,2048,256]{2,...) custom-call(s32[1]{0:T(128)} %bitcast.longer_ref, f32[2048,1152]{1,0:T(8,128)} %bitcast.49, ...), custom_call_target="tpu_custom_call" | custom-call | flops 104500002816 | bytes 1048576 | tf_op jit(solution)/shard_map/mixer_forward/pallas_call | solution.py:453
  206.1 162.6 %branch_and_feed.1 = (f32[256,2048]{1,0:T(8,128)}, bf16[4,2,256,2048]{3,2,1,0:T(8,128)(2,1)}, bf16[8,256,704]{2,1,0:T(8,128)(2,1)}, bf16[8,256,704]{2,1,0:T(8,128)(2,1)}, bf16[8,256,704]{2,1,0:T(8,128)(2,1)}) custom-call(bf16[8,256,256]{2,1,0:T(8,128)(2,1)} %bitcast.53, bf16[256,2048]{1,0:T(8,128)(2,1)} %out_weight_ref.1, bf16[256,2048]{1,0:T(8,128)(2,1)} %input_ref.3, ...), custom_call_target="tpu_custom_call" | custom-call | flops 198000001024 | bytes 1048576 | tf_op jit(solution)/shard_map/branch_and_feed/pallas_call | solution.py:1280
  368.8 159.6 %feed_back.1 = (f32[256,2048]{1,0:T(8,128)}, f32[1,2048]{1,0:T(1,128)}, f32[8,256,256]{2,1,0:T(8,128)}, bf16[2048,256]{1,0:T(8,128)(2,1)}, bf16[3,704,2048]{2,1,0:T(8,128)(2,1)}) custom-call(bf16[8,256,704]{2,1,0:T(8,128)(2,1)} %get-tuple-element.48.dgate_ref, bf16[8,256,704]{2,1,0:T(8,128)(2,1)} %get-tuple-element.49.dup_ref, ...), custom_call_target="tpu_custom_call" | custom-call | flops 198000001024 | bytes 1048576 | tf_op jit(solution)/shard_map/feed_back/pallas_call | solution.py:1444
  528.3 0.0 all-reduce.4.cloned.1.call-update
  528.4 99.5 %mixer_backward.1 = (bf16[2048,1152]{1,0:T(8,128)(2,1)}, f32[4,768]{1,0:T(4,128)}, f32[2,128]{1,0:T(2,128)}, f32[1,128]{1,0:T(1,128)}, bf16[256,2048]{1,0:T(8,128)(2,1)}) custom-call(s32[1]{0:T(128)} %bitcast.longer_ref, f32[2048,256]{1,0:T(8,128)} %bitcast.52, f32[2048,1152]{1,0:T(8,128)} %bitcast.50, f32[2048,768]{1,0:T(8,128)} %get-tuple-element.54.conv_out_ref, ...), custom_call_target="tpu_custom_call" | custom-call | flops 109999996928 | bytes 1048576 | tf_op jit(solution)/shard_map/mixer_backward/pallas_call | solution.py:504
  627.8 158.4 %input_back.1 = (f32[256,2048]{1,0:T(8,128)}, f32[1,2048]{1,0:T(1,128)}, f32[1,2048]{1,0:T(1,128)}, f32[1,128]{1,0:T(1,128)}, f32[3,4,256]{2,1,0:T(4,128)}, /*in...) custom-call(bf16[8,256,1152]{2,1,0:T(8,128)(2,1)} %bitcast.51, ...), custom_call_target="tpu_custom_call" | custom-call | flops 131999997952 | bytes 1048576 | tf_op jit(solution)/shard_map/input_back/pallas_call | solution.py:1761
  786.3 1.3 slice.29
  787.6 1.1 slice_convert_fusion
  788.7 0.3 copy.36
  789.0 0.8 copy.35
  789.9 0.6 reshape.82
  790.5 8.2 by_rows.1
  798.7 1.6 convert_bitcast_fusion.1
  800.3 0.0 all-reduce.4.cloned.1.call-done
  800.3 0.0 copy-start
  800.3 5.4 fusion
  805.7 0.4 copy-done
  806.0 0.0 copy-start.2
  806.0 0.0 copy-start.1
  806.0 6.0 convert_bitcast_fusion
  812.0 0.0 copy-done.2
  812.0 0.0 copy-start.5
  812.0 0.0 copy-start.3
  812.1 0.0 copy-start.6
  812.1 0.0 copy-start.7
  812.1 0.0 copy-start.4
  812.1 1.0 copy.45
  813.0 0.0 copy-done.1
  813.1 1.3 copy.46
  814.4 0.0 copy-done.5
  814.4 0.6 copy.47
  815.0 0.0 copy-done.3
  815.0 0.6 copy.48
  815.6 0.0 copy-done.6
  815.6 0.6 copy.49
  816.1 0.0 copy-done.7
  816.1 0.5 copy.50
  816.7 0.0 copy-done.4
  816.7 0.6 copy.51
Async XLA Ops:
  7.2 793.1 %all-reduce.4.cloned.1.call-start = ((), (), s32[]{:S(2)}) async-start(), calls=%async_computation | async-start | bytes 17301504 | tf_op jit(solution)/shard_map/psum | solution.py:1880
  800.3 5.7 copy-start
  806.0 6.0 copy-start.2
  806.0 7.0 copy-start.1
  812.0 2.3 copy-start.5
  812.0 2.9 copy-start.3
  812.1 3.5 copy-start.6
  812.1 4.1 copy-start.7
  812.1 4.6 copy-start.4
Sparse Core Ops, SparseCore 0:
  528.5 193.5 all-reduce.3

commit v9 on v8

--- a/solution.py
+++ b/solution.py
@@ -1701,7 +1701,7 @@
     steps = []
     for k in range(replicas.lines - 1, -1, -1):
         steps += [functools.partial(other_core, k), functools.partial(this_core, k)]
-    while len(steps) < 5:
+    while len(steps) < 7:
         steps.append(lambda: None)
     steps.append(replicas.over_y)
 
@@ -1795,21 +1795,41 @@
     )
 
 
-def spread_kernel(given_ref, out_ref):
-    for kind in range(given_ref.shape[0]):
-        out_ref[:, kind, :] = given_ref[kind].astype(F32)
-
-
-def by_rows(values):
-    kinds, rows, cols = values.shape
+def results_kernel(main_ref, rest_ref, feed_ref, main_out, wout_out, gate_up_out, down_out):
+    for kind in range(main_ref.shape[0]):
+        main_out[:, kind, :] = main_ref[kind].astype(F32)
+    wout_out[...] = jnp.transpose(rest_ref[:, 128:].astype(F32))
+    gate_up_out[...] = feed_ref[:2].astype(F32)
+    down_out[...] = feed_ref[2].astype(F32)
+
+
+def results(main, rest, feed):
+    kinds, features, width = main.shape
+    units = feed.shape[1]
+    step = 256
     return pl.pallas_call(
-        spread_kernel,
-        grid=(rows // 256,),
-        in_specs=[pl.BlockSpec((kinds, 256, cols), lambda i: (0, i, 0))],
-        out_specs=pl.BlockSpec((256, kinds, cols), lambda i: (i, 0, 0)),
-        out_shape=jax.ShapeDtypeStruct((rows, kinds, cols), F32),
-        name="by_rows",
-    )(values)
+        results_kernel,
+        grid=(features // step,),
+        in_specs=[
+            pl.BlockSpec((kinds, step, width), lambda i: (0, i, 0)),
+            pl.BlockSpec((step, rest.shape[1]), lambda i: (i, 0)),
+            pl.BlockSpec((3, units, step), lambda i: (0, 0, i)),
+        ],
+        out_specs=[
+            pl.BlockSpec((step, kinds, width), lambda i: (i, 0, 0)),
+            pl.BlockSpec((width, step), lambda i: (0, i)),
+            pl.BlockSpec((2, units, step), lambda i: (0, 0, i)),
+            pl.BlockSpec((units, step), lambda i: (0, i)),
+        ],
+        out_shape=[
+            jax.ShapeDtypeStruct((features, kinds, width), F32),
+            jax.ShapeDtypeStruct((width, features), F32),
+            jax.ShapeDtypeStruct((2, units, features), F32),
+            jax.ShapeDtypeStruct((units, features), F32),
+        ],
+        compiler_params=pltpu.CompilerParams(vmem_limit_bytes=48 * 2**20),
+        name="results",
+    )(main, rest, feed)
 
 
 def on_device(
@@ -1911,19 +1931,20 @@
     )
     grad_main = grad_main.reshape(4, features, width)
     grad_rest = grad_rest.reshape(features, -1)
+    grad_qkvg, grad_out_weight, grad_gate_up, grad_down = results(grad_main, grad_rest, early)
     return (
         layer_out,
         grad_in,
         grad_gain1[0],
-        by_rows(grad_main),
+        grad_qkvg,
         grad_conv,
         grad_rest[:, : 2 * heads].reshape(w_gates.shape).astype(F32),
         dparams[:, :heads],
         dgain[0],
-        grad_rest[:, 128:].T.astype(F32),
+        grad_out_weight,
         grad_gain2[0],
-        jnp.transpose(early[:2].astype(F32), (2, 0, 1)),
-        early[2].astype(F32),
+        jnp.transpose(grad_gate_up, (2, 0, 1)),
+        grad_down,
     )
 
 

time: 828 us -> 824 us (level)
  other arithmetic: 14.7 us -> 1.8 us
  transfers between devices with their start and end apart: 1 -> 1, of which waited for: 0 -> 0; matrix products, arithmetic and copies ran while one was open for 1% -> 0% of each run, Pallas kernels for 32% -> 32%
where the time goes in v9:
time: 824 us; the launch traced here: 820 us
  Pallas kernels  788 us (96%)
  between operations  15.6 us (2%)
  local copies, waits for them, and re-layouts  14.3 us (2%)
    pallas_call x1, Pallas kernels, branch_and_feed(): pl.pallas_call(functools.partial(branch_kernel, count), out_shape=[jax.Sh...  163 us
    pallas_call x1, Pallas kernels, input_back(): pl.pallas_call(functools.partial(input_back_kernel, count), out_shape=[ja...  161 us
    pallas_call x1, Pallas kernels, feed_back(): pl.pallas_call(functools.partial(feed_back_kernel, count), out_shape=[jax...  160 us
    pallas_call x1, Pallas kernels, mixer_backward(): pl.pallas_call(functools.partial(backward_kernel, heads, chunks, count),...  99.8 us
    pallas_call x1, Pallas kernels, mixer_forward(): pl.pallas_call(functools.partial(forward_kernel, heads, count, chunks), g...  99.4 us
    pallas_call x1, Pallas kernels, project(): pl.pallas_call(functools.partial(project_kernel, count), out_shape=[jax.S...  93 us
  transfers between devices with their start and end apart: 1, of which 0 were waited for; matrix products, arithmetic and copies ran while one was open for 0% of the time, Pallas kernels for 32%

profile of v9, /device:TPU:1, one launch (start us, length us, event | category | flops | bytes accessed | tf_op | source)
XLA Modules:
  0.0 820.2 jit_solution(4035181138165879457)
XLA Ops:
  7.2 0.0 all-reduce.4.cloned.1.call-start
  7.2 1.3 fusion.2
  8.5 0.7 reshape.72
  9.3 0.3 copy.29
  9.6 1.3 pad.9.params_ref
  12.1 0.9 pad.8.gates_ref
  13.0 0.7 fusion.1.live_ref
  13.7 93.0 %project.1 = (bf16[4,4,2,256,512]{4,3,2,1,0:T(8,128)(2,1)}, f32[8,256,1152]{2,1,0:T(8,128)}, bf16[2048,1024]{1,0:T(8,128)(2,1)}) custom-call(bf16[256,2048]{1,0:T(8,128)(2,1)} %input_ref.3, f32[1,2048]{1,0:T(1,128)} %bitcast.38, bf16[2048,4,256]{2,1,0:T(4,128)(2,1)} %weight_ref.2, bf16[2048,128]{1,0:T(8,128)(2,1)} %pad.8.gates_ref), custom_call_target="tpu_custom_call" | custom-call | flops 109999996928 | bytes 1048576 | tf_op jit(solution)/shard_map/project/pallas_call | solution.py:1137
  106.7 99.4 %mixer_forward.1 = (bf16[2048,256]{1,0:T(8,128)(2,1)}, f32[2048,768]{1,0:T(8,128)}, f32[2048,256]{1,0:T(8,128)}, f32[2048,256]{1,0:T(8,128)}, f32[2,2048,256]{2,...) custom-call(s32[1]{0:T(128)} %bitcast.longer_ref, f32[2048,1152]{1,0:T(8,128)} %bitcast.42, ...), custom_call_target="tpu_custom_call" | custom-call | flops 104500002816 | bytes 1048576 | tf_op jit(solution)/shard_map/mixer_forward/pallas_call | solution.py:453
  206.1 162.6 %branch_and_feed.1 = (f32[256,2048]{1,0:T(8,128)}, bf16[4,2,256,2048]{3,2,1,0:T(8,128)(2,1)}, bf16[8,256,704]{2,1,0:T(8,128)(2,1)}, bf16[8,256,704]{2,1,0:T(8,128)(2,1)}, bf16[8,256,704]{2,1,0:T(8,128)(2,1)}) custom-call(bf16[8,256,256]{2,1,0:T(8,128)(2,1)} %bitcast.46, bf16[256,2048]{1,0:T(8,128)(2,1)} %out_weight_ref.1, bf16[256,2048]{1,0:T(8,128)(2,1)} %input_ref.3, ...), custom_call_target="tpu_custom_call" | custom-call | flops 198000001024 | bytes 1048576 | tf_op jit(solution)/shard_map/branch_and_feed/pallas_call | solution.py:1280
  368.8 159.6 %feed_back.1 = (f32[256,2048]{1,0:T(8,128)}, f32[1,2048]{1,0:T(1,128)}, f32[8,256,256]{2,1,0:T(8,128)}, bf16[2048,256]{1,0:T(8,128)(2,1)}, bf16[3,704,2048]{2,1,0:T(8,128)(2,1)}) custom-call(bf16[8,256,704]{2,1,0:T(8,128)(2,1)} %get-tuple-element.52.dgate_ref, bf16[8,256,704]{2,1,0:T(8,128)(2,1)} %get-tuple-element.53.dup_ref, ...), custom_call_target="tpu_custom_call" | custom-call | flops 198000001024 | bytes 1048576 | tf_op jit(solution)/shard_map/feed_back/pallas_call | solution.py:1444
  528.4 0.0 all-reduce.4.cloned.1.call-update
  528.4 99.8 %mixer_backward.1 = (bf16[2048,1152]{1,0:T(8,128)(2,1)}, f32[4,768]{1,0:T(4,128)}, f32[2,128]{1,0:T(2,128)}, f32[1,128]{1,0:T(1,128)}, bf16[256,2048]{1,0:T(8,128)(2,1)}) custom-call(s32[1]{0:T(128)} %bitcast.longer_ref, f32[2048,256]{1,0:T(8,128)} %bitcast.45, f32[2048,1152]{1,0:T(8,128)} %bitcast.43, f32[2048,768]{1,0:T(8,128)} %get-tuple-element.58.conv_out_ref, ...), custom_call_target="tpu_custom_call" | custom-call | flops 109999996928 | bytes 1048576 | tf_op jit(solution)/shard_map/mixer_backward/pallas_call | solution.py:504
  628.2 160.6 %input_back.1 = (f32[256,2048]{1,0:T(8,128)}, f32[1,2048]{1,0:T(1,128)}, f32[1,2048]{1,0:T(1,128)}, f32[1,128]{1,0:T(1,128)}, f32[3,4,256]{2,1,0:T(4,128)}, /*in...) custom-call(bf16[8,256,1152]{2,1,0:T(8,128)(2,1)} %bitcast.44, ...), custom_call_target="tpu_custom_call" | custom-call | flops 131999997952 | bytes 1048576 | tf_op jit(solution)/shard_map/input_back/pallas_call | solution.py:1761
  788.8 1.1 slice_convert_fusion
  789.9 0.3 copy.30
  790.2 0.7 reshape.80
  790.9 0.0 all-reduce.4.cloned.1.call-done.feed_ref
  790.9 0.0 copy-start
  790.9 2.2 copy-done
  793.1 0.0 copy-start.1
  793.1 1.4 copy-done.1
  794.5 0.0 copy-start.3
  794.5 0.0 copy-start.2
  794.5 13.4 %results.1 = (f32[2048,4,256]{2,1,0:T(4,128)}, f32[256,2048]{1,0:T(8,128)}, f32[2,704,2048]{2,1,0:T(8,128)}, f32[704,2048]{1,0:T(8,128)}) custom-call(bf16[4,2048,256]{2,1,0:T(8,128)(2,1)S(1)} %bitcast.25, bf16[2048,384]{1,0:T(8,128)(2,1)S(1)} %bitcast.27, bf16[3,704,2048]{2,1,0:T(8,128)(2,1)} %all-reduce.4.cloned.1.call-done.feed_ref), custom_call_target="tpu_custom_call" | custom-call | tf_op jit(solution)/shard_map/results/pallas_call | solution.py:1810
  807.9 0.0 copy-start.6
  807.9 0.0 copy-start.4
  807.9 0.0 copy-start.7
  807.9 0.0 copy-start.8
  807.9 0.0 copy-start.5
  807.9 0.0 copy-done.3
  807.9 1.0 copy.39
  808.9 0.0 copy-done.2
  808.9 1.3 copy.40
  810.2 0.0 copy-done.6
  810.2 0.6 copy.41
  810.8 0.0 copy-done.4
  810.8 0.6 copy.42
  811.4 0.0 copy-done.7
  811.5 0.6 copy.43
  812.0 0.0 copy-done.8
  812.0 0.5 copy.44
  812.5 0.0 copy-done.5
  812.5 0.6 copy.45
Async XLA Ops:
  7.2 783.7 %all-reduce.4.cloned.1.call-start = ((), (), s32[]{:S(2)}) async-start(), calls=%async_computation | async-start | bytes 17301504 | tf_op jit(solution)/shard_map/psum | solution.py:1900
  790.9 2.2 copy-start
  793.1 1.4 copy-start.1
  794.5 13.5 %copy-start.3 = (bf16[256,2048]{1,0:T(8,128)(2,1)S(1)}, bf16[256,2048]{1,0:T(8,128)(2,1)}, u32[]{:S(2)}) copy-start(bf16[256,2048]{1,0:T(8,128)(2,1)} %get-tuple-element.112) | copy-start | bytes 3145732
  794.5 14.4 %copy-start.2 = (f32[256,2048]{1,0:T(8,128)S(1)}, f32[256,2048]{1,0:T(8,128)}, u32[]{:S(2)}) copy-start(f32[256,2048]{1,0:T(8,128)} %get-tuple-element.113) | copy-start | bytes 6291460
  807.9 2.3 copy-start.6
  807.9 2.9 copy-start.4
  807.9 3.5 copy-start.7
  807.9 4.1 copy-start.8
  807.9 4.6 copy-start.5
Sparse Core Ops, SparseCore 0:
  528.5 193.5 all-reduce.3

commit v10 on v9

--- a/solution.py
+++ b/solution.py
@@ -1605,24 +1605,36 @@
             yield self.over_home.at[k], self.share(1 - self.core, self.line(k))
 
 
-def sum_small(small, seen, send_sems, recv_sems, axis, rows):
-    me, size = lax.axis_index(axis), lax.axis_size(axis)
-    copies = []
-    seen[me] = small[...]
-    for k in range(1, size):
-        copy = pltpu.make_async_remote_copy(
-            seen.at[me], seen.at[me], send_sems.at[k], recv_sems.at[size - k],
-            device_id={axis: (me + k) % size}, device_id_type=MESH,
-        )
-        copy.start()
-        copies.append(copy)
-    for k in range(1, size):
-        arrived(seen.at[(me + k) % size], recv_sems.at[k])
-    total = seen[0]
-    for other in range(1, size):
-        total = total + seen[other]
-    small[...] = jnp.where(grid_index(total.shape, 0) < rows, total, small[...])
-    return copies
+class SmallSum:
+    def __init__(self, small, seen, send_sems, recv_sems, axis, cols):
+        self.small, self.seen, self.cols = small, seen, pl.ds(0, cols)
+        self.send_sems, self.recv_sems, self.axis = send_sems, recv_sems, axis
+        self.me, self.size = lax.axis_index(axis), lax.axis_size(axis)
+
+    def copy(self, k):
+        place = self.seen.at[self.me, :, self.cols]
+        return pltpu.make_async_remote_copy(
+            place, place, self.send_sems.at[k], self.recv_sems.at[self.size - k],
+            device_id={self.axis: (self.me + k) % self.size}, device_id_type=MESH,
+        )
+
+    def start(self):
+        self.seen[self.me, :, self.cols] = self.small[:, self.cols]
+        for k in range(1, self.size):
+            self.copy(k).start()
+
+    def finish(self):
+        for k in range(1, self.size):
+            landed = self.seen.at[(self.me + k) % self.size, :, self.cols]
+            arrived(landed, self.recv_sems.at[k])
+        total = self.seen[0, :, self.cols]
+        for other in range(1, self.size):
+            total = total + self.seen[other, :, self.cols]
+        self.small[:, self.cols] = total
+
+    def drain(self):
+        for k in range(1, self.size):
+            self.copy(k).wait_send()
 
 
 def input_back_kernel(
@@ -1630,22 +1642,27 @@
     dtaps_ref, dparams_ref, wout_ref, normed_ref, grad_out, norm1_out, norm2_out, gain_out,
     taps_out, params_out, dmain_out, drest_out, *scratch
 ):
-    *scratch, small_out, normed, normed_sem = scratch
+    *scratch, small, normed, normed_sem = scratch
     late = Late(normed_ref, normed, normed_sem)
     normed_ref = normed
     parts, rest = scratch[0], scratch[SCATTER_COUNT:]
     values = rest[0]
-    near, near_send, near_recv, far, far_send, far_recv, staged, out_sems = rest[9:]
+    small_scratch, staged, out_sems = rest[9:15], *rest[15:]
     group = Group(count)
     scatter = scatter_of(group, SCATTER_SHARE, scratch[:SCATTER_COUNT])
     replicas = Replicas(*rest[:5], rest[5:9])
     meet(count, lax.axis_size("dp"))
-    small_out[...] = jnp.zeros(small_out.shape, F32)
-    small_out[1:2] = dnorm_ref[...]
-    small_out[2:3, : dgain_ref.shape[1]] = dgain_ref[...]
-    small_out[3:7, : dtaps_ref.shape[1]] = dtaps_ref[...]
-    for row in range(2):
-        small_out[7:8, 128 * row : 128 * (row + 1)] = dparams_ref[row : row + 1]
+    tall = norm1_out.shape[1] // 8
+    edges = [tall, 2 * tall, 2 * tall + 128]
+    small[...] = jnp.zeros(small.shape, F32)
+    norm1_out[...] = jnp.zeros(norm1_out.shape, F32)
+    for row in range(8):
+        small[row : row + 1, edges[0] : edges[1]] = dnorm_ref[:, row * tall : (row + 1) * tall]
+    small[0:1, edges[1] : edges[2]] = dgain_ref[...]
+    small[0:4, edges[2] :] = dtaps_ref[...]
+    small[4:6, edges[2] : edges[2] + 128] = dparams_ref[...]
+    near = SmallSum(small, *small_scratch[:3], "heads", edges[2])
+    far = SmallSum(small, *small_scratch[3:6], "dp", small.shape[1])
     width = grad_ref.shape[2]
     values[:, :, width:] = split(wout_ref[...], values.shape[0])
 
@@ -1665,7 +1682,7 @@
         given = input_ref[rows].astype(F32)
         scale = inverse_rms(given)
         normed = given * scale
-        small_out[0:1] += jnp.sum(dnormed * normed, axis=0, keepdims=True)
+        norm1_out[...] += jnp.sum(dnormed * normed, axis=0, keepdims=True)
         scaled = dnormed * gain_ref[...]
         grad_out[rows] = later_ref[rows] + scale * (
             scaled - normed * jnp.mean(scaled * normed, axis=-1, keepdims=True)
@@ -1716,17 +1733,23 @@
         return 0
 
     lax.fori_loop(-1, max(scatter.pieces + scatter.last - 1, len(steps)), tick, 0)
+    for row in range(8):
+        small[row : row + 1, : edges[0]] = norm1_out[:, row * tall : (row + 1) * tall]
+    near.start()
     replicas.back()
-    copies = sum_small(small_out, near, near_send, near_recv, "heads", 3)
-    copies += sum_small(small_out, far, far_send, far_recv, "dp", 8)
-    norm1_out[...] = small_out[0:1]
-    norm2_out[...] = small_out[1:2]
-    gain_out[...] = small_out[2:3, : gain_out.shape[1]]
+    near.finish()
+    far.start()
+    far.finish()
+    for row in range(8):
+        cols = slice(row * tall, (row + 1) * tall)
+        norm1_out[:, cols] = small[row : row + 1, : edges[0]]
+        norm2_out[:, cols] = small[row : row + 1, edges[0] : edges[1]]
+    gain_out[...] = small[0:1, edges[1] : edges[2]]
     kind_width = taps_out.shape[2]
     for kind in range(taps_out.shape[0]):
-        taps_out[kind] = small_out[3:7, kind * kind_width : (kind + 1) * kind_width]
-    for row in range(2):
-        params_out[row : row + 1] = small_out[7:8, 128 * row : 128 * (row + 1)]
+        first = edges[2] + kind * kind_width
+        taps_out[kind] = small[0:4, first : first + kind_width]
+    params_out[...] = small[4:6, edges[2] : edges[2] + 128]
     replicas.home()
     part = dmain_out.shape[3]
     outs = []
@@ -1743,8 +1766,8 @@
         copy.start()
     scatter.drain()
     replicas.drain()
-    for copy in copies:
-        copy.wait_send()
+    near.drain()
+    far.drain()
     for copy in outs:
         copy.wait()
 
@@ -1757,6 +1780,7 @@
     nz, nx = grid_sizes(count)
     width, share = grad_wout.shape[1], features // replica_count
     cols = grad.shape[1] + width
+    small_cols = features // 4 + 128 + dtaps.shape[1]
     dma = pltpu.SemaphoreType.DMA
     return pl.pallas_call(
         functools.partial(input_back_kernel, count),
@@ -1774,15 +1798,15 @@
         scratch_shapes=[
             *scatter_scratch(nz, nx, own, features, SCATTER_SHARE, FEW),
             *Replicas.scratch(features, cols, replica_count),
-            pltpu.VMEM((count, 8, features), F32),
+            pltpu.VMEM((count, 8, small_cols), F32),
             dma((count,)),
             dma((count,)),
-            pltpu.VMEM((replica_count, 8, features), F32),
+            pltpu.VMEM((replica_count, 8, small_cols), F32),
             dma((replica_count,)),
             dma((replica_count,)),
             pltpu.VMEM((share, grad.shape[1]), BF16),
             dma((replica_count, 5)),
-            pltpu.VMEM((8, features), F32),
+            pltpu.VMEM((8, small_cols), F32),
             pltpu.VMEM(normed.shape, BF16),
             dma,
         ],

time: 824 us -> 817 us (level)
  Pallas kernels: 788 us -> 775 us
    pallas_call x1, Pallas kernels: 161 us -> 147 us  [input_back(): pl.pallas_call(functools.partial(input_back_kernel, count), out_shape=[ja...]
  transfers between devices with their start and end apart: 1 -> 1, of which waited for: 0 -> 0; matrix products, arithmetic and copies ran while one was open for 0% -> 0% of each run, Pallas kernels for 32% -> 31%
where the time goes in v10:
time: 817 us; the launch traced here: 807 us
  Pallas kernels  775 us (95%)
  between operations  15.6 us (2%)
  local copies, waits for them, and re-layouts  14.3 us (2%)
    pallas_call x1, Pallas kernels, branch_and_feed(): pl.pallas_call(functools.partial(branch_kernel, count), out_shape=[jax.Sh...  163 us
    pallas_call x1, Pallas kernels, feed_back(): pl.pallas_call(functools.partial(feed_back_kernel, count), out_shape=[jax...  160 us
    pallas_call x1, Pallas kernels, input_back(): pl.pallas_call(functools.partial(input_back_kernel, count), out_shape=[ja...  147 us
    pallas_call x1, Pallas kernels, mixer_backward(): pl.pallas_call(functools.partial(backward_kernel, heads, chunks, count),...  99.8 us
    pallas_call x1, Pallas kernels, mixer_forward(): pl.pallas_call(functools.partial(forward_kernel, heads, count, chunks), g...  99.4 us
    pallas_call x1, Pallas kernels, project(): pl.pallas_call(functools.partial(project_kernel, count), out_shape=[jax.S...  93 us
  transfers between devices with their start and end apart: 1, of which 0 were waited for; matrix products, arithmetic and copies ran while one was open for 0% of the time, Pallas kernels for 31%

profile of v10, /device:TPU:1, one launch (start us, length us, event | category | flops | bytes accessed | tf_op | source)
XLA Modules:
  0.0 806.8 jit_solution(15102132763492378561)
XLA Ops:
  7.2 0.0 all-reduce.4.cloned.1.call-start
  7.2 1.3 fusion.2
  8.5 0.7 reshape.72
  9.3 0.3 copy.29
  9.6 1.3 pad.9.params_ref
  12.1 0.9 pad.8.gates_ref
  13.0 0.7 fusion.1.live_ref
  13.7 93.0 %project.1 = (bf16[4,4,2,256,512]{4,3,2,1,0:T(8,128)(2,1)}, f32[8,256,1152]{2,1,0:T(8,128)}, bf16[2048,1024]{1,0:T(8,128)(2,1)}) custom-call(bf16[256,2048]{1,0:T(8,128)(2,1)} %input_ref.3, f32[1,2048]{1,0:T(1,128)} %bitcast.38, bf16[2048,4,256]{2,1,0:T(4,128)(2,1)} %weight_ref.2, bf16[2048,128]{1,0:T(8,128)(2,1)} %pad.8.gates_ref), custom_call_target="tpu_custom_call" | custom-call | flops 109999996928 | bytes 1048576 | tf_op jit(solution)/shard_map/project/pallas_call | solution.py:1137
  106.7 99.4 %mixer_forward.1 = (bf16[2048,256]{1,0:T(8,128)(2,1)}, f32[2048,768]{1,0:T(8,128)}, f32[2048,256]{1,0:T(8,128)}, f32[2048,256]{1,0:T(8,128)}, f32[2,2048,256]{2,...) custom-call(s32[1]{0:T(128)} %bitcast.longer_ref, f32[2048,1152]{1,0:T(8,128)} %bitcast.42, ...), custom_call_target="tpu_custom_call" | custom-call | flops 104500002816 | bytes 1048576 | tf_op jit(solution)/shard_map/mixer_forward/pallas_call | solution.py:453
  206.1 162.6 %branch_and_feed.1 = (f32[256,2048]{1,0:T(8,128)}, bf16[4,2,256,2048]{3,2,1,0:T(8,128)(2,1)}, bf16[8,256,704]{2,1,0:T(8,128)(2,1)}, bf16[8,256,704]{2,1,0:T(8,128)(2,1)}, bf16[8,256,704]{2,1,0:T(8,128)(2,1)}) custom-call(bf16[8,256,256]{2,1,0:T(8,128)(2,1)} %bitcast.46, bf16[256,2048]{1,0:T(8,128)(2,1)} %out_weight_ref.1, bf16[256,2048]{1,0:T(8,128)(2,1)} %input_ref.3, ...), custom_call_target="tpu_custom_call" | custom-call | flops 198000001024 | bytes 1048576 | tf_op jit(solution)/shard_map/branch_and_feed/pallas_call | solution.py:1280
  368.8 159.6 %feed_back.1 = (f32[256,2048]{1,0:T(8,128)}, f32[1,2048]{1,0:T(1,128)}, f32[8,256,256]{2,1,0:T(8,128)}, bf16[2048,256]{1,0:T(8,128)(2,1)}, bf16[3,704,2048]{2,1,0:T(8,128)(2,1)}) custom-call(bf16[8,256,704]{2,1,0:T(8,128)(2,1)} %get-tuple-element.52.dgate_ref, bf16[8,256,704]{2,1,0:T(8,128)(2,1)} %get-tuple-element.53.dup_ref, ...), custom_call_target="tpu_custom_call" | custom-call | flops 198000001024 | bytes 1048576 | tf_op jit(solution)/shard_map/feed_back/pallas_call | solution.py:1444
  528.4 0.0 all-reduce.4.cloned.1.call-update
  528.4 99.8 %mixer_backward.1 = (bf16[2048,1152]{1,0:T(8,128)(2,1)}, f32[4,768]{1,0:T(4,128)}, f32[2,128]{1,0:T(2,128)}, f32[1,128]{1,0:T(1,128)}, bf16[256,2048]{1,0:T(8,128)(2,1)}) custom-call(s32[1]{0:T(128)} %bitcast.longer_ref, f32[2048,256]{1,0:T(8,128)} %bitcast.45, f32[2048,1152]{1,0:T(8,128)} %bitcast.43, f32[2048,768]{1,0:T(8,128)} %get-tuple-element.58.conv_out_ref, ...), custom_call_target="tpu_custom_call" | custom-call | flops 109999996928 | bytes 1048576 | tf_op jit(solution)/shard_map/mixer_backward/pallas_call | solution.py:504
  628.2 147.2 %input_back.1 = (f32[256,2048]{1,0:T(8,128)}, f32[1,2048]{1,0:T(1,128)}, f32[1,2048]{1,0:T(1,128)}, f32[1,128]{1,0:T(1,128)}, f32[3,4,256]{2,1,0:T(4,128)}, /*in...) custom-call(bf16[8,256,1152]{2,1,0:T(8,128)(2,1)} %bitcast.44, ...), custom_call_target="tpu_custom_call" | custom-call | flops 131999997952 | bytes 1048576 | tf_op jit(solution)/shard_map/input_back/pallas_call | solution.py:1785
  775.4 1.1 slice_convert_fusion
  776.5 0.3 copy.30
  776.9 0.7 reshape.80
  777.5 0.0 all-reduce.4.cloned.1.call-done.feed_ref
  777.5 0.0 copy-start
  777.5 2.2 copy-done
  779.7 0.0 copy-start.1
  779.7 1.4 copy-done.1
  781.1 0.0 copy-start.3
  781.1 0.0 copy-start.2
  781.1 13.4 %results.1 = (f32[2048,4,256]{2,1,0:T(4,128)}, f32[256,2048]{1,0:T(8,128)}, f32[2,704,2048]{2,1,0:T(8,128)}, f32[704,2048]{1,0:T(8,128)}) custom-call(bf16[4,2048,256]{2,1,0:T(8,128)(2,1)S(1)} %bitcast.25, bf16[2048,384]{1,0:T(8,128)(2,1)S(1)} %bitcast.27, bf16[3,704,2048]{2,1,0:T(8,128)(2,1)} %all-reduce.4.cloned.1.call-done.feed_ref), custom_call_target="tpu_custom_call" | custom-call | tf_op jit(solution)/shard_map/results/pallas_call | solution.py:1834
  794.5 0.0 copy-start.6
  794.5 0.0 copy-start.4
  794.5 0.0 copy-start.7
  794.5 0.0 copy-start.8
  794.6 0.0 copy-start.5
  794.6 0.0 copy-done.3
  794.6 1.0 copy.39
  795.6 0.0 copy-done.2
  795.6 1.3 copy.40
  796.9 0.0 copy-done.6
  796.9 0.6 copy.41
  797.5 0.0 copy-done.4
  797.5 0.6 copy.42
  798.1 0.0 copy-done.7
  798.1 0.6 copy.43
  798.6 0.0 copy-done.8
  798.6 0.5 copy.44
  799.2 0.0 copy-done.5
  799.2 0.6 copy.45
Async XLA Ops:
  7.2 770.3 %all-reduce.4.cloned.1.call-start = ((), (), s32[]{:S(2)}) async-start(), calls=%async_computation | async-start | bytes 17301504 | tf_op jit(solution)/shard_map/psum | solution.py:1924
  777.5 2.2 copy-start
  779.7 1.4 copy-start.1
  781.1 13.5 %copy-start.3 = (bf16[256,2048]{1,0:T(8,128)(2,1)S(1)}, bf16[256,2048]{1,0:T(8,128)(2,1)}, u32[]{:S(2)}) copy-start(bf16[256,2048]{1,0:T(8,128)(2,1)} %get-tuple-element.112) | copy-start | bytes 3145732
  781.1 14.4 %copy-start.2 = (f32[256,2048]{1,0:T(8,128)S(1)}, f32[256,2048]{1,0:T(8,128)}, u32[]{:S(2)}) copy-start(f32[256,2048]{1,0:T(8,128)} %get-tuple-element.113) | copy-start | bytes 6291460
  794.5 2.3 copy-start.6
  794.5 2.9 copy-start.4
  794.5 3.5 copy-start.7
  794.5 4.1 copy-start.8
  794.6 4.6 copy-start.5
Sparse Core Ops, SparseCore 0:
  528.5 193.4 all-reduce.3

commit v11 on v10

--- a/solution.py
+++ b/solution.py
@@ -359,7 +359,7 @@
         yield
         key_entry = dot(key, entry, NT, P_BWD)
         yield
-        on_key = dot(jnp.concatenate([dlink, dgram], axis=0), key, NN, P_BWD)
+        on_key = dot(jnp.concatenate([dlink, dgram], axis=0), key, NN, TOP)
         yield
         dquery = decay_in * on_entry[CHUNK:] + on_key[CHUNK:]
         link_key = on_key[:CHUNK]
@@ -367,7 +367,7 @@
         key_tail = decay_out * dot(delta, dlater, NN, P_BWD)
         yield
         key_write = (
-            dot(beta * dlink, key, TN, P_BWD) + dot(dgram, query, TN, P_BWD) + key_tail
+            dot(beta * dlink, key, TN, TOP) + dot(dgram, query, TN, TOP) + key_tail
         )
         yield
         dkey = key_read + key_write

time: 817 us -> 819 us (level)
  no operation moved by 1% of the time
where the time goes in v11:
time: 819 us; the launch traced here: 810 us
  Pallas kernels  779 us (95%)
  between operations  15.6 us (2%)
  local copies, waits for them, and re-layouts  14.3 us (2%)
    pallas_call x1, Pallas kernels, branch_and_feed(): pl.pallas_call(functools.partial(branch_kernel, count), out_shape=[jax.Sh...  163 us
    pallas_call x1, Pallas kernels, feed_back(): pl.pallas_call(functools.partial(feed_back_kernel, count), out_shape=[jax...  160 us
    pallas_call x1, Pallas kernels, input_back(): pl.pallas_call(functools.partial(input_back_kernel, count), out_shape=[ja...  144 us
    pallas_call x1, Pallas kernels, mixer_backward(): pl.pallas_call(functools.partial(backward_kernel, heads, chunks, count),...  106 us
    pallas_call x1, Pallas kernels, mixer_forward(): pl.pallas_call(functools.partial(forward_kernel, heads, count, chunks), g...  99.4 us
    pallas_call x1, Pallas kernels, project(): pl.pallas_call(functools.partial(project_kernel, count), out_shape=[jax.S...  93 us
  transfers between devices with their start and end apart: 1, of which 0 were waited for; matrix products, arithmetic and copies ran while one was open for 0% of the time, Pallas kernels for 31%

profile of v11, /device:TPU:1, one launch (start us, length us, event | category | flops | bytes accessed | tf_op | source)
XLA Modules:
  0.0 810.4 jit_solution(10268225031267078311)
XLA Ops:
  7.2 0.0 all-reduce.4.cloned.1.call-start
  7.2 1.3 fusion.2
  8.5 0.7 reshape.72
  9.3 0.3 copy.29
  9.6 1.3 pad.9.params_ref
  12.1 0.9 pad.8.gates_ref
  13.0 0.7 fusion.1.live_ref
  13.7 93.0 %project.1 = (bf16[4,4,2,256,512]{4,3,2,1,0:T(8,128)(2,1)}, f32[8,256,1152]{2,1,0:T(8,128)}, bf16[2048,1024]{1,0:T(8,128)(2,1)}) custom-call(bf16[256,2048]{1,0:T(8,128)(2,1)} %input_ref.3, f32[1,2048]{1,0:T(1,128)} %bitcast.38, bf16[2048,4,256]{2,1,0:T(4,128)(2,1)} %weight_ref.2, bf16[2048,128]{1,0:T(8,128)(2,1)} %pad.8.gates_ref), custom_call_target="tpu_custom_call" | custom-call | flops 109999996928 | bytes 1048576 | tf_op jit(solution)/shard_map/project/pallas_call | solution.py:1137
  106.7 99.4 %mixer_forward.1 = (bf16[2048,256]{1,0:T(8,128)(2,1)}, f32[2048,768]{1,0:T(8,128)}, f32[2048,256]{1,0:T(8,128)}, f32[2048,256]{1,0:T(8,128)}, f32[2,2048,256]{2,...) custom-call(s32[1]{0:T(128)} %bitcast.longer_ref, f32[2048,1152]{1,0:T(8,128)} %bitcast.42, ...), custom_call_target="tpu_custom_call" | custom-call | flops 104500002816 | bytes 1048576 | tf_op jit(solution)/shard_map/mixer_forward/pallas_call | solution.py:453
  206.1 162.6 %branch_and_feed.1 = (f32[256,2048]{1,0:T(8,128)}, bf16[4,2,256,2048]{3,2,1,0:T(8,128)(2,1)}, bf16[8,256,704]{2,1,0:T(8,128)(2,1)}, bf16[8,256,704]{2,1,0:T(8,128)(2,1)}, bf16[8,256,704]{2,1,0:T(8,128)(2,1)}) custom-call(bf16[8,256,256]{2,1,0:T(8,128)(2,1)} %bitcast.46, bf16[256,2048]{1,0:T(8,128)(2,1)} %out_weight_ref.1, bf16[256,2048]{1,0:T(8,128)(2,1)} %input_ref.3, ...), custom_call_target="tpu_custom_call" | custom-call | flops 198000001024 | bytes 1048576 | tf_op jit(solution)/shard_map/branch_and_feed/pallas_call | solution.py:1280
  368.8 159.6 %feed_back.1 = (f32[256,2048]{1,0:T(8,128)}, f32[1,2048]{1,0:T(1,128)}, f32[8,256,256]{2,1,0:T(8,128)}, bf16[2048,256]{1,0:T(8,128)(2,1)}, bf16[3,704,2048]{2,1,0:T(8,128)(2,1)}) custom-call(bf16[8,256,704]{2,1,0:T(8,128)(2,1)} %get-tuple-element.52.dgate_ref, bf16[8,256,704]{2,1,0:T(8,128)(2,1)} %get-tuple-element.53.dup_ref, ...), custom_call_target="tpu_custom_call" | custom-call | flops 198000001024 | bytes 1048576 | tf_op jit(solution)/shard_map/feed_back/pallas_call | solution.py:1444
  528.4 0.0 all-reduce.4.cloned.1.call-update
  528.4 106.2 %mixer_backward.1 = (bf16[2048,1152]{1,0:T(8,128)(2,1)}, f32[4,768]{1,0:T(4,128)}, f32[2,128]{1,0:T(2,128)}, f32[1,128]{1,0:T(1,128)}, bf16[256,2048]{1,0:T(8,128)(2,1)}) custom-call(s32[1]{0:T(128)} %bitcast.longer_ref, f32[2048,256]{1,0:T(8,128)} %bitcast.45, f32[2048,1152]{1,0:T(8,128)} %bitcast.43, f32[2048,768]{1,0:T(8,128)} %get-tuple-element.58.conv_out_ref, ...), custom_call_target="tpu_custom_call" | custom-call | flops 109999996928 | bytes 1048576 | tf_op jit(solution)/shard_map/mixer_backward/pallas_call | solution.py:504
  634.6 144.5 %input_back.1 = (f32[256,2048]{1,0:T(8,128)}, f32[1,2048]{1,0:T(1,128)}, f32[1,2048]{1,0:T(1,128)}, f32[1,128]{1,0:T(1,128)}, f32[3,4,256]{2,1,0:T(4,128)}, /*in...) custom-call(bf16[8,256,1152]{2,1,0:T(8,128)(2,1)} %bitcast.44, ...), custom_call_target="tpu_custom_call" | custom-call | flops 131999997952 | bytes 1048576 | tf_op jit(solution)/shard_map/input_back/pallas_call | solution.py:1785
  779.0 1.1 slice_convert_fusion
  780.2 0.3 copy.30
  780.5 0.7 reshape.80
  781.2 0.0 all-reduce.4.cloned.1.call-done.feed_ref
  781.2 0.0 copy-start
  781.2 2.2 copy-done
  783.3 0.0 copy-start.1
  783.3 1.4 copy-done.1
  784.8 0.0 copy-start.3
  784.8 0.0 copy-start.2
  784.8 13.4 %results.1 = (f32[2048,4,256]{2,1,0:T(4,128)}, f32[256,2048]{1,0:T(8,128)}, f32[2,704,2048]{2,1,0:T(8,128)}, f32[704,2048]{1,0:T(8,128)}) custom-call(bf16[4,2048,256]{2,1,0:T(8,128)(2,1)S(1)} %bitcast.25, bf16[2048,384]{1,0:T(8,128)(2,1)S(1)} %bitcast.27, bf16[3,704,2048]{2,1,0:T(8,128)(2,1)} %all-reduce.4.cloned.1.call-done.feed_ref), custom_call_target="tpu_custom_call" | custom-call | tf_op jit(solution)/shard_map/results/pallas_call | solution.py:1834
  798.2 0.0 copy-start.6
  798.2 0.0 copy-start.4
  798.2 0.0 copy-start.7
  798.2 0.0 copy-start.8
  798.2 0.0 copy-start.5
  798.2 0.0 copy-done.3
  798.2 1.0 copy.39
  799.2 0.0 copy-done.2
  799.2 1.3 copy.40
  800.5 0.0 copy-done.6
  800.5 0.6 copy.41
  801.1 0.0 copy-done.4
  801.1 0.6 copy.42
  801.7 0.0 copy-done.7
  801.7 0.6 copy.43
  802.3 0.0 copy-done.8
  802.3 0.5 copy.44
  802.8 0.0 copy-done.5
  802.8 0.6 copy.45
Async XLA Ops:
  7.2 774.0 %all-reduce.4.cloned.1.call-start = ((), (), s32[]{:S(2)}) async-start(), calls=%async_computation | async-start | bytes 17301504 | tf_op jit(solution)/shard_map/psum | solution.py:1924
  781.2 2.2 copy-start
  783.3 1.4 copy-start.1
  784.8 13.5 %copy-start.3 = (bf16[256,2048]{1,0:T(8,128)(2,1)S(1)}, bf16[256,2048]{1,0:T(8,128)(2,1)}, u32[]{:S(2)}) copy-start(bf16[256,2048]{1,0:T(8,128)(2,1)} %get-tuple-element.112) | copy-start | bytes 3145732
  784.8 14.4 %copy-start.2 = (f32[256,2048]{1,0:T(8,128)S(1)}, f32[256,2048]{1,0:T(8,128)}, u32[]{:S(2)}) copy-start(f32[256,2048]{1,0:T(8,128)} %get-tuple-element.113) | copy-start | bytes 6291460
  798.2 2.3 copy-start.6
  798.2 2.9 copy-start.4
  798.2 3.5 copy-start.7
  798.2 4.1 copy-start.8
  798.2 4.6 copy-start.5
Sparse Core Ops, SparseCore 0:
  528.5 190.5 all-reduce.3
